TPU v7x, 128 devices: a whole 4x4x4 slice. The times are simulated.
128 devices in a mesh: dp: 16 (over x, z), tensor: 8 (over y, core).
Axes of the slice: x: 4, y: 4, z: 4, core: 2. Of those that a mesh axis runs over, the one named last changes fastest.
Arguments:
- tokens: bfloat16 [8192, 4096], P('dp', 'tensor'), may hold values from -6 to 6
- norm_gain: float32 [4096], replicated, may hold values from 0.1 to 1.9
- doc_ids: int32 [8192], P('dp'), may hold values from 0 to 8191, as said below
- panel_plan: int32 [256], P('dp'), may hold values from 0 to 255, as said below
- query_weight: bfloat16 [4096, 4096], P(None, 'tensor'), may hold values from -0.09375 to 0.09375
- key_weight: bfloat16 [4096, 1024], P(None, 'tensor'), may hold values from -0.09375 to 0.09375
- value_weight: bfloat16 [4096, 1024], P(None, 'tensor'), may hold values from -0.09375 to 0.09375
- out_weight: bfloat16 [4096, 4096], P('tensor'), may hold values from -0.5 to 0.5
- cotangent: bfloat16 [8192, 4096], P('dp', 'tensor'), may hold values from -6 to 6
Outputs:
- output: bfloat16 [8192, 4096], P('dp', 'tensor')
- grad_tokens: bfloat16 [8192, 4096], P('dp', 'tensor')
- grad_query: bfloat16 [4096, 4096], P(None, 'tensor')
- grad_key: bfloat16 [4096, 1024], P(None, 'tensor')
- grad_value: bfloat16 [4096, 1024], P(None, 'tensor')
Inputs may be any that keep to these rules, and one draw needn't show every extreme that they name: A permutation: loader panel i goes to device panel_plan[i] // 16 of dp, into slot panel_plan[i] % 16; the 16 panels of one device of dp go to 16 different devices. `doc_ids`: in planned order each document is a run of consecutive rows inside one block of 512 rows, and its id is the planned row index of its first row; the last planned row is a document of its own.
All inputs are finite; a program needn't handle non-finite values.
Results may differ from a plain program's by a relative error of at most 0.02.
Values may be sent and summed in bfloat16 or wider, within the bound.
No kernel may reach another device: no remote copies, remote signals or barrier semaphores. Data moves between devices by JAX's collectives and lax.ppermute only.
A program may use at most 128 MiB of HBM per device.

v0:
```python
import jax
import jax.numpy as jnp
from jax import lax
from jax.sharding import PartitionSpec as P

HD = 128


NORM_EPSILON = 1e-05
ROPE_THETA = 500000.0


def rotate_half(values):
    half_width = values.shape[-1] // 2
    return jnp.concatenate([-values[..., half_width:], values[..., :half_width]], axis=-1)


def rotate(values, cosine, sine_table):
    return values * cosine + rotate_half(values) * sine_table


def rotate_back(values, cosine, sine_table):
    return values * cosine - rotate_half(values) * sine_table


def rotary_tables(positions):
    half_width = HD // 2
    frequency = ROPE_THETA ** (-2.0 * jnp.arange(half_width, dtype=jnp.float32) / HD)
    angles = positions.astype(jnp.float32)[:, None] * frequency[None, :]
    angles = jnp.concatenate([angles, angles], axis=1)
    return (jnp.cos(angles)[:, None, :], jnp.sin(angles)[:, None, :])


def place_rows(array, index, device_count):
    empty_buffer = jnp.zeros((device_count,) + array.shape[1:], array.dtype)
    return empty_buffer.at[index].set(array)


def project_heads(normed, query_weight, key_weight, value_weight, cosine, sine_table):
    row_count = normed.shape[0]
    queries = jnp.dot(normed, query_weight, preferred_element_type=jnp.float32).reshape(
        row_count, -1, HD
    )
    key_rows = jnp.dot(normed, key_weight, preferred_element_type=jnp.float32).reshape(
        row_count, -1, HD
    )
    values = jnp.dot(normed, value_weight, preferred_element_type=jnp.float32).astype(jnp.bfloat16)
    queries = rotate(queries, cosine, sine_table).astype(jnp.bfloat16).reshape(row_count, -1)
    key_rows = rotate(key_rows, cosine, sine_table).astype(jnp.bfloat16).reshape(row_count, -1)
    return (queries, key_rows, values)


def attend(queries, key_rows, values, doc_rows):
    row_count = queries.shape[0]
    kv_count = key_rows.shape[1] // HD
    grouped = queries.reshape(row_count, kv_count, -1, HD)
    key_heads = key_rows.reshape(row_count, kv_count, HD)
    scores = jnp.einsum(
        "qkgd,skd->kgqs", grouped, key_heads, preferred_element_type=jnp.float32
    ) * HD ** (-0.5)
    ordinal = jnp.arange(row_count)
    allowed = (doc_rows[:, None] == doc_rows[None, :]) & (ordinal[None, :] <= ordinal[:, None])
    weights = jnp.where(allowed, jnp.exp(scores), 0.0)
    shares = weights / jnp.sum(weights, axis=-1, keepdims=True)
    rounded = shares.astype(jnp.bfloat16)
    attended = jnp.einsum(
        "kgqs,skd->qkgd",
        rounded,
        values.reshape(row_count, kv_count, HD),
        preferred_element_type=jnp.float32,
    )
    return (attended.astype(jnp.bfloat16).reshape(row_count, -1), shares, rounded)


def attend_back(grad_attended, queries, key_rows, values, shares, rounded, cosine, sine_table):
    row_count = queries.shape[0]
    kv_count = key_rows.shape[1] // HD
    grouped = queries.reshape(row_count, kv_count, -1, HD)
    grouped_grad = grad_attended.reshape(row_count, kv_count, -1, HD)
    key_heads = key_rows.reshape(row_count, kv_count, HD)
    value_heads = values.reshape(row_count, kv_count, HD)
    share_grad = jnp.einsum(
        "qkgd,skd->kgqs", grouped_grad, value_heads, preferred_element_type=jnp.float32
    )
    row_dot = jnp.sum(share_grad * shares, axis=-1, keepdims=True)
    dscore = (shares * (share_grad - row_dot) * HD ** (-0.5)).astype(jnp.bfloat16)
    value_grad = jnp.einsum(
        "kgqs,qkgd->skd", rounded, grouped_grad, preferred_element_type=jnp.float32
    )
    query_grad = jnp.einsum(
        "kgqs,skd->qkgd", dscore, key_heads, preferred_element_type=jnp.float32
    ).reshape(row_count, -1, HD)
    key_grad = jnp.einsum("kgqs,qkgd->skd", dscore, grouped, preferred_element_type=jnp.float32)
    query_grad = (
        rotate_back(query_grad, cosine, sine_table).astype(jnp.bfloat16).reshape(row_count, -1)
    )
    key_grad = rotate_back(key_grad, cosine, sine_table).astype(jnp.bfloat16).reshape(row_count, -1)
    return (query_grad, key_grad, value_grad.astype(jnp.bfloat16).reshape(row_count, -1))


def per_device(
    tokens,
    norm_gain,
    doc_ids,
    panel_plan,
    query_weight,
    key_weight,
    value_weight,
    out_weight,
    cotangent,
):
    device_count = lax.axis_size("dp")
    panel_count = panel_plan.shape[0]
    panel_rows = doc_ids.shape[0] // panel_count
    shard_width = tokens.shape[1]
    targets = panel_plan // panel_count
    slot_ids = panel_plan % panel_count
    marker = jnp.zeros((device_count,), jnp.int32).at[targets].set(slot_ids + 1)
    arrived = (
        lax.all_to_all(
            place_rows(tokens.reshape(panel_count, panel_rows, shard_width), targets, device_count),
            "dp",
            split_axis=0,
            concat_axis=0,
            tiled=True,
        ),
        lax.all_to_all(
            place_rows(
                cotangent.reshape(panel_count, panel_rows, shard_width), targets, device_count
            ),
            "dp",
            split_axis=0,
            concat_axis=0,
            tiled=True,
        ),
        lax.all_to_all(
            place_rows(doc_ids.reshape(panel_count, panel_rows), targets, device_count),
            "dp",
            split_axis=0,
            concat_axis=0,
            tiled=True,
        ),
        lax.all_to_all(marker, "dp", split_axis=0, concat_axis=0, tiled=True),
    )
    chosen = arrived[3][None, :] == jnp.arange(1, panel_count + 1, dtype=jnp.int32)[:, None]
    source = jnp.sum(
        jnp.where(chosen, jnp.arange(device_count, dtype=jnp.int32)[None, :], 0), axis=1
    )
    here_tokens = arrived[0][source].reshape(-1, shard_width)
    here_cot = arrived[1][source].reshape(-1, shard_width)
    here_docs = arrived[2][source].reshape(-1)
    row_count = here_docs.shape[0]
    first_row = lax.axis_index("dp") * row_count
    positions = first_row + jnp.arange(row_count, dtype=jnp.int32) - here_docs
    full_tokens, full_cot = (
        lax.all_gather(here_tokens, "tensor", axis=1, tiled=True),
        lax.all_gather(here_cot, "tensor", axis=1, tiled=True),
    )
    widened = full_tokens.astype(jnp.float32)
    inverse = lax.rsqrt(jnp.mean(widened * widened, axis=1, keepdims=True) + NORM_EPSILON)
    scaled = widened * inverse
    normed = (scaled * norm_gain).astype(jnp.bfloat16)
    cosine, sine_table = rotary_tables(positions)
    queries, key_rows, values = project_heads(
        normed, query_weight, key_weight, value_weight, cosine, sine_table
    )
    attended, shares, rounded = attend(queries, key_rows, values, here_docs)
    head_term = jnp.dot(attended, out_weight, preferred_element_type=jnp.float32)
    summed = lax.psum_scatter(
        head_term.astype(jnp.bfloat16), "tensor", scatter_dimension=1, tiled=True
    ).astype(jnp.float32)
    output_rows = (here_tokens.astype(jnp.float32) + summed).astype(jnp.bfloat16)
    grad_attended = jnp.einsum(
        "rd,cd->rc", full_cot, out_weight, preferred_element_type=jnp.float32
    ).astype(jnp.bfloat16)
    query_grad, key_grad, value_grad = attend_back(
        grad_attended, queries, key_rows, values, shares, rounded, cosine, sine_table
    )
    grad_query_w = jnp.einsum("rd,rc->dc", normed, query_grad, preferred_element_type=jnp.float32)
    grad_key_w = jnp.einsum("rd,rc->dc", normed, key_grad, preferred_element_type=jnp.float32)
    grad_value_w = jnp.einsum("rd,rc->dc", normed, value_grad, preferred_element_type=jnp.float32)
    input_term = jnp.einsum(
        "rc,dc->rd", query_grad, query_weight, preferred_element_type=jnp.float32
    )
    input_term = input_term + jnp.einsum(
        "rc,dc->rd", key_grad, key_weight, preferred_element_type=jnp.float32
    )
    input_term = input_term + jnp.einsum(
        "rc,dc->rd", value_grad, value_weight, preferred_element_type=jnp.float32
    )
    shard_start = lax.axis_index("tensor") * shard_width
    dnormed = lax.psum(input_term.astype(jnp.bfloat16), "tensor").astype(jnp.float32)
    dscaled = dnormed * norm_gain
    mean_term = jnp.mean(dscaled * scaled, axis=1, keepdims=True)
    grad_full = inverse * (dscaled - scaled * mean_term)
    grad_share = lax.dynamic_slice_in_dim(grad_full, shard_start, shard_width, 1)
    grad_rows = (here_cot.astype(jnp.float32) + grad_share).astype(jnp.bfloat16)
    grad_query_w, grad_key_w, grad_value_w = (
        lax.psum(grad_query_w.astype(jnp.bfloat16), "dp").astype(jnp.float32),
        lax.psum(grad_key_w.astype(jnp.bfloat16), "dp").astype(jnp.float32),
        lax.psum(grad_value_w.astype(jnp.bfloat16), "dp").astype(jnp.float32),
    )
    scale = (row_count * device_count) ** (-0.5)
    returned = (
        lax.all_to_all(
            place_rows(
                output_rows.reshape(panel_count, panel_rows, shard_width), source, device_count
            ),
            "dp",
            split_axis=0,
            concat_axis=0,
            tiled=True,
        ),
        lax.all_to_all(
            place_rows(
                grad_rows.reshape(panel_count, panel_rows, shard_width), source, device_count
            ),
            "dp",
            split_axis=0,
            concat_axis=0,
            tiled=True,
        ),
    )
    output = returned[0][targets].reshape(-1, shard_width)
    grad_tokens = returned[1][targets].reshape(-1, shard_width)
    return (
        output,
        grad_tokens,
        (grad_query_w * scale).astype(jnp.bfloat16),
        (grad_key_w * scale).astype(jnp.bfloat16),
        (grad_value_w * scale).astype(jnp.bfloat16),
    )


def solution(mesh):
    in_specs = (
        P("dp", "tensor"),
        P(),
        P("dp"),
        P("dp"),
        P(None, "tensor"),
        P(None, "tensor"),
        P(None, "tensor"),
        P("tensor", None),
        P("dp", "tensor"),
    )
    out_specs = (
        P("dp", "tensor"),
        P("dp", "tensor"),
        P(None, "tensor"),
        P(None, "tensor"),
        P(None, "tensor"),
    )
    return jax.shard_map(
        per_device, mesh=mesh, in_specs=in_specs, out_specs=out_specs, check_vma=False
    )
```

profile of v0, /device:TPU:1, one launch (start us, length us, event | category | flops | bytes accessed | tf_op | source)
XLA Modules:
  0.0 398.8 jit_solution(17089606910186697582)
XLA Ops:
  7.2 0.8 fusion.53
  8.0 0.6 scatter_custom_fusion
  8.6 0.7 copy.40
  9.3 8.4 %all-to-all-start = ((s32[16,1,1]{2,1,0:T(1,128)}), s32[16,1,1]{2,1,0:T(1,128)S(1)}, u32[]{:S(2)}, u32[]{:S(2)}) async-start(s32[16,1,1]{2,1,0:T(1,128)} %copy.40), calls=%async_computation | async-start | bytes 16384 | tf_op jit(solution)/shard_map/all_to_all | solution.py:143
  17.7 0.8 broadcast.159.clone.1
  18.6 2.9 scatter_fusion
  21.5 2.6 all-to-all-done
  24.1 4.1 %all-to-all-start.1 = ((bf16[16,32,512]{2,1,0:T(8,128)(2,1)}), bf16[16,32,512]{2,1,0:T(8,128)(2,1)S(1)}, u32[]{:S(2)}, u32[]{:S(2)}) async-start(bf16[16,32,512]{2,1,0:T(8,128)(2,1)} %scatter_fusion), calls=%async_computation.1 | async-start | bytes 1048576 | tf_op jit(solution)/shard_map/all_to_all | solution.py:120
  28.8 8.2 %all-to-all-done.1 = bf16[16,32,512]{2,1,0:T(8,128)(2,1)S(1)} async-done(((bf16[16,32,512]{2,1,0:T(8,128)(2,1)}), bf16[16,32,512]{2,1,0:T(8,128)(2,1)S(1)}, u32[]{:S(2)}, u32[]{:S(2)}) %all-to-all-start.1) | async-done | bytes 524320 | tf_op jit(solution)/shard_map/all_to_all | solution.py:120
  37.0 1.4 gather_fusion
  38.5 1.1 scatter_fusion.2
  39.6 13.1 %all_to_all.41 = bf16[16,32,512]{2,1,0:T(8,128)(2,1)S(1)} all-to-all(bf16[16,32,512]{2,1,0:T(8,128)(2,1)S(1)} %scatter_fusion.2), channel_id=1, replica_groups=mesh['dp'=16,'tensor'=8] {'dp'}, dimensions={0} | all-to-all | bytes 1048576 | tf_op jit(solution)/shard_map/all_to_all | solution.py:127
  52.7 1.4 gather_fusion.3
  54.2 1.2 scatter_custom_fusion.2
  55.4 3.5 all-to-all-start.2
  58.8 0.6 all-reduce.4.cloned.1.call-start
  59.4 5.7 %all-to-all-done.2 = s32[16,1,32]{2,1,0:T(1,128)S(1)} async-done(((s32[16,1,32]{2,1,0:T(1,128)}), s32[16,1,32]{2,1,0:T(1,128)S(1)}, u32[]{:S(2)}, u32[]{:S(2)}) %all-to-all-start.2) | async-done | bytes 2080 | tf_op jit(solution)/shard_map/all_to_all | solution.py:136
  65.1 0.6 gather_fusion.1
  65.8 0.7 fusion.50
  66.5 0.9 fusion.33
  67.4 4.5 %all-gather.3.cloned.1.call-done = bf16[512,4096]{1,0:T(8,128)(2,1)} async-done(((bf16[512,512]{1,0:T(8,128)(2,1)}), bf16[512,4096]{1,0:T(8,128)(2,1)}) %all-gather.3.cloned.1.call-update) | async-done | bytes 4194320 | tf_op jit(solution)/shard_map/all_gather | solution.py:156
  72.0 3.2 fusion
  75.4 1.7 fusion.60
  77.1 1.0 fusion.36
  78.1 2.6 fusion.59
  81.3 0.4 copy-done.15
  81.7 3.1 fusion.6
  84.8 2.0 fusion.25
  86.8 19.5 %all-gather.5.cloned.1.call-done = bf16[512,4096]{1,0:T(8,128)(2,1)} async-done(((bf16[512,512]{1,0:T(8,128)(2,1)}), bf16[512,4096]{1,0:T(8,128)(2,1)}) %all-gather.5.cloned.1.call-update) | async-done | bytes 4194320 | tf_op jit(solution)/shard_map/all_gather | solution.py:157
  106.3 6.0 %convolution_convert_fusion.4 = bf16[512,512]{0,1:T(8,128)(2,1)S(1)} fusion(bf16[512,4096]{1,0:T(8,128)(2,1)} %all-gather.5.cloned.1.call-done, bf16[512,4096]{1,0:T(8,128)(2,1)} %param.16), kind=kOutput, calls=%fused_computation.42 | convolution fusion | flops 2147745792 | bytes 8912896 | tf_op jit(solution)/shard_map/rd,cd->rc/dot_general | solution.py:173
  112.3 1.7 fusion.1
  114.0 1.3 fusion.7
  115.3 0.4 fusion.61
  115.8 0.9 convolution_bitcast_fusion
  116.7 1.3 fusion.22
  118.6 1.6 copy-done.7
  120.2 2.4 fusion.62
  122.7 1.0 fusion.43
  123.7 1.3 fusion.48
  125.0 3.3 add_convert_fusion
  128.6 0.4 copy-done.22
  129.0 5.0 %convolution_convert_fusion.3 = bf16[4096,128]{1,0:T(8,128)(2,1)} fusion(bf16[512,1,128]{0,2,1:T(8,128)(2,1)S(1)} %fusion.43, f32[4096]{0:T(1024)S(1)} %copy-done.22, f32[512]{0:T(512)S(1)} %add_rsqrt_fusion, bf16[512,4096]{1,0:T(8,128)(2,1)} %all-gather.3.cloned.1.call-done), kind=kOutput, calls=%fused_computation.22 | convolution fusion | flops 545783808 | bytes 5392384 | tf_op jit(solution)/shard_map/rd,rc->dc/dot_general | solution.py:180
  134.0 2.9 convolution_convert_fusion.2
  136.9 4.7 %convolution_convert_fusion = bf16[4096,512]{1,0:T(8,128)(2,1)} fusion(bf16[512,512]{0,1:T(8,128)(2,1)S(1)} %fusion.29, f32[4096]{0:T(1024)S(1)} %copy-done.22, f32[512]{0:T(512)S(1)} %add_rsqrt_fusion, bf16[512,4096]{1,0:T(8,128)(2,1)S(1)} %copy-done.3), kind=kOutput, calls=%fused_computation.19 | convolution fusion | flops 2157969408 | bytes 8931328 | tf_op jit(solution)/shard_map/rd,rc->dc/dot_general | solution.py:179
  141.7 0.9 copy-done.17
  142.6 3.7 fusion.13
  146.3 4.4 %convolution_convert_fusion.1 = bf16[512,4096]{1,0:T(8,128)(2,1)} fusion(bf16[512,512]{0,1:T(8,128)(2,1)S(1)} %bitcast.165, bf16[512,4096]{1,0:T(8,128)(2,1)S(1)} %copy-done.8), kind=kOutput, calls=%fused_computation.20 | convolution fusion | flops 2149580800 | bytes 8912896 | tf_op jit(solution)/shard_map/dot_general | solution.py:168
  150.7 48.2 %all-reduce.4.cloned.1.call-done = bf16[512,4096]{1,0:T(8,128)(2,1)} async-done(((bf16[512,4096]{1,0:T(8,128)(2,1)}), bf16[512,4096]{1,0:T(8,128)(2,1)}) %all-reduce.4.cloned.1.call-update) | async-done | bytes 4194320 | tf_op jit(solution)/shard_map/psum | solution.py:192
  198.9 5.7 %multiply_reduce_fusion = (f32[512]{0:T(512)S(1)}, f32[512,4096]{1,0:T(8,128)S(1)}, f32[512,4096]{1,0:T(8,128)S(1)}) fusion(f32[4096]{0:T(1024)S(1)} %copy-done.22, bf16[512,4096]{1,0:T(8,128)(2,1)} %all-reduce.4.cloned.1.call-done, f32[512]{0:T(512)S(1)} %add_rsqrt_fusion, bf16[512,4096]{1,0:T(8,128)(2,1)} %all-gather.3.cloned.1.call-done), kind=kLoop, calls=%fused_computation.15 | loop fusion | flops 12582400 | bytes 25186304 | tf_op jit(solution)/shard_map/reduce_sum | solution.py:194
  204.9 0.8 broadcast.159.clone.2
  205.7 2.6 scatter_fusion.3
  208.3 6.9 %all-to-all-start.5 = ((bf16[16,32,512]{2,1,0:T(8,128)(2,1)}), bf16[16,32,512]{2,1,0:T(8,128)(2,1)S(1)}, u32[]{:S(2)}, u32[]{:S(2)}) async-start(bf16[16,32,512]{2,1,0:T(8,128)(2,1)} %scatter_fusion.3), calls=%async_computation.6 | async-start | bytes 1048576 | tf_op jit(solution)/shard_map/all_to_all | solution.py:214
  215.3 13.6 %all-to-all-done.5 = bf16[16,32,512]{2,1,0:T(8,128)(2,1)S(1)} async-done(((bf16[16,32,512]{2,1,0:T(8,128)(2,1)}), bf16[16,32,512]{2,1,0:T(8,128)(2,1)S(1)}, u32[]{:S(2)}, u32[]{:S(2)}) %all-to-all-start.5) | async-done | bytes 524320 | tf_op jit(solution)/shard_map/all_to_all | solution.py:214
  228.9 1.4 gather_fusion.4
  230.3 103.0 %all-reduce.6.cloned.1.call-done = (bf16[4096,512]{1,0:T(8,128)(2,1)}, bf16[4096,128]{1,0:T(8,128)(2,1)}, bf16[4096,128]{1,0:T(8,128)(2,1)}) async-done(((bf16[4096,512]{1,0:T(8,128)(2,1)}, bf16[4096,128]{1,0:T(8,128)(2,1)}, bf16[4096,128]{1,0:T(8,128)(2,1)}), (bf16[4096,512]{1,0:T(8,128)(2,1)}, bf16[4096,128]{1,0:T(8,128)(2,1)}, bf16[4096,128]{1,0:T(8,128)(2,1)})) %all-reduce.6.cloned.1.call-update) | async-done | bytes 6291472 | tf_op jit(solution)/shard_map/psum | solution.py:199
  333.3 5.1 %multiply_convert_fusion = bf16[4096,512]{1,0:T(8,128)(2,1)} fusion(bf16[4096,512]{1,0:T(8,128)(2,1)} %get-tuple-element.5), kind=kLoop, calls=%fused_computation.14 | loop fusion | flops 6291456 | bytes 8388608 | tf_op jit(solution)/shard_map/convert_element_type | solution.py:229
  338.4 31.9 %reduce-scatter.2.cloned.1.call-done = bf16[512,512]{1,0:T(8,128)(2,1)} async-done(((bf16[512,4096]{1,0:T(8,128)(2,1)}), bf16[512,512]{1,0:T(8,128)(2,1)}) %reduce-scatter.2.cloned.1.call-update) | async-done | bytes 524304 | tf_op jit(solution)/shard_map/reduce_scatter | solution.py:169
  370.3 1.2 add_convert_fusion.2
  371.5 0.8 broadcast.159.clone
  372.3 2.6 scatter_fusion.1
  374.9 6.7 %all-to-all-start.3 = ((bf16[16,32,512]{2,1,0:T(8,128)(2,1)}), bf16[16,32,512]{2,1,0:T(8,128)(2,1)S(1)}, u32[]{:S(2)}, u32[]{:S(2)}) async-start(bf16[16,32,512]{2,1,0:T(8,128)(2,1)} %scatter_fusion.1), calls=%async_computation.4 | async-start | bytes 1048576 | tf_op jit(solution)/shard_map/all_to_all | solution.py:205
  381.6 2.9 multiply_convert_fusion.2
  384.5 6.1 %all-to-all-done.3 = bf16[16,32,512]{2,1,0:T(8,128)(2,1)S(1)} async-done(((bf16[16,32,512]{2,1,0:T(8,128)(2,1)}), bf16[16,32,512]{2,1,0:T(8,128)(2,1)S(1)}, u32[]{:S(2)}, u32[]{:S(2)}) %all-to-all-start.3) | async-done | bytes 524320 | tf_op jit(solution)/shard_map/all_to_all | solution.py:205
  390.6 1.4 gather_fusion.2
  (83 shorter events, 3.0 us)
Async XLA Ops:
  7.2 68.0 %copy-start = (bf16[4096,128]{1,0:T(8,128)(2,1)S(1)}, bf16[4096,128]{1,0:T(8,128)(2,1)}, u32[]{:S(2)}) copy-start(bf16[4096,128]{1,0:T(8,128)(2,1)} %param.14) | copy-start | bytes 3145732
  7.2 31.3 %copy-start.18 = (bf16[512,512]{1,0:T(8,128)(2,1)S(1)}, bf16[512,512]{1,0:T(8,128)(2,1)}, u32[]{:S(2)}) copy-start(bf16[512,512]{1,0:T(8,128)(2,1)} %param.17) | copy-start | bytes 1572868
  9.3 14.8 %all-to-all-start = ((s32[16,1,1]{2,1,0:T(1,128)}), s32[16,1,1]{2,1,0:T(1,128)S(1)}, u32[]{:S(2)}, u32[]{:S(2)}) async-start(s32[16,1,1]{2,1,0:T(1,128)} %copy.40), calls=%async_computation | async-start | bytes 16384 | tf_op jit(solution)/shard_map/all_to_all | solution.py:143
  18.6 35.5 %copy-start.25 = (s32[512]{0:T(512)S(1)}, s32[512]{0:T(512)}, u32[]{:S(2)}) copy-start(s32[512]{0:T(512)} %param.11) | copy-start | bytes 6148
  24.1 12.9 %all-to-all-start.1 = ((bf16[16,32,512]{2,1,0:T(8,128)(2,1)}), bf16[16,32,512]{2,1,0:T(8,128)(2,1)S(1)}, u32[]{:S(2)}, u32[]{:S(2)}) async-start(bf16[16,32,512]{2,1,0:T(8,128)(2,1)} %scatter_fusion), calls=%async_computation.1 | async-start | bytes 1048576 | tf_op jit(solution)/shard_map/all_to_all | solution.py:120
  28.1 43.8 %all-gather.3.cloned.1.call-start = ((), (), s32[]{:S(2)}) async-start(), calls=%async_computation.7 | async-start | bytes 4718592 | tf_op jit(solution)/shard_map/all_gather | solution.py:156
  28.8 9.6 %copy-start.23 = (s32[16]{0:T(128)}, s32[16]{0:T(128)S(1)}, u32[]{:S(2)}) copy-start(s32[16]{0:T(128)S(1)} %fusion.54) | copy-start | bytes 196
  38.4 68.0 %all-gather.5.cloned.1.call-start = ((), (), s32[]{:S(2)}) async-start(), calls=%async_computation.9 | async-start | bytes 4718592 | tf_op jit(solution)/shard_map/all_gather | solution.py:157
  38.5 36.7 %copy-start.20 = (f32[4096]{0:T(1024)S(1)}, f32[4096]{0:T(1024)}, u32[]{:S(2)}) copy-start(f32[4096]{0:T(1024)} %param.10) | copy-start | bytes 49156
  55.4 9.8 %all-to-all-start.2 = ((s32[16,1,32]{2,1,0:T(1,128)}), s32[16,1,32]{2,1,0:T(1,128)S(1)}, u32[]{:S(2)}, u32[]{:S(2)}) async-start(s32[16,1,32]{2,1,0:T(1,128)} %bitcast.6), calls=%async_computation.2 | async-start | bytes 16384 | tf_op jit(solution)/shard_map/all_to_all | solution.py:136
  58.8 140.1 %all-reduce.4.cloned.1.call-start = ((), (), s32[]{:S(2)}) async-start(), calls=%async_computation.10 | async-start | bytes 8388608 | tf_op jit(solution)/shard_map/psum | solution.py:192
  72.0 3.4 copy-start.2
  75.4 2.7 copy-start.6
  78.1 2.7 copy-start.10
  80.7 1.0 copy-start.15
  81.0 3.8 copy-start.13
  81.0 3.8 copy-start.21
  106.3 6.0 %copy-start.9 = (f32[512,512,4]{1,0,2:T(8,128)S(1)}, f32[512,512,4]{1,0,2:T(8,128)}, u32[]{:S(2)}) copy-start(f32[512,512,4]{1,0,2:T(8,128)} %get-tuple-element.27) | copy-start | bytes 12582916
  106.3 6.0 %copy-start.16 = (pred[512,512]{0,1:T(8,128)(4,1)S(1)}, pred[512,512]{0,1:T(8,128)(4,1)}, u32[]{:S(2)}) copy-start(pred[512,512]{0,1:T(8,128)(4,1)} %fusion.33) | copy-start | bytes 786436
  106.3 6.0 %copy-start.26 = (bf16[512,128,1]{1,0,2:T(8,128)(2,1)S(1)}, bf16[512,128,1]{1,0,2:T(8,128)(2,1)}, u32[]{:S(2)}) copy-start(bf16[512,128,1]{1,0,2:T(8,128)(2,1)} %fusion.25) | copy-start | bytes 393220
  116.7 1.4 copy-start.11
  118.0 2.2 copy-start.7
  120.2 2.5 copy-start.19
  123.7 1.3 copy-start.14
  128.3 0.7 copy-start.22
  128.3 205.0 %all-reduce.6.cloned.1.call-start = ((), (), s32[]{:S(2)}) async-start(), calls=%async_computation.11 | async-start | bytes 12582912 | tf_op jit(solution)/shard_map/psum | solution.py:199
  129.0 5.0 %copy-start.3 = (bf16[512,4096]{1,0:T(8,128)(2,1)S(1)}, bf16[512,4096]{1,0:T(8,128)(2,1)}, u32[]{:S(2)}) copy-start(bf16[512,4096]{1,0:T(8,128)(2,1)} %all-gather.3.cloned.1.call-done) | copy-start | bytes 12582916
  141.6 1.0 copy-start.17
  141.6 1.0 copy-start.27
  141.6 228.6 %reduce-scatter.2.cloned.1.call-start = ((), (), s32[]{:S(2)}) async-start(), calls=%async_computation.8 | async-start | bytes 4718592 | tf_op jit(solution)/shard_map/reduce_scatter | solution.py:169
  142.6 3.7 copy-start.8
  150.7 53.9 %copy-start.5 = (bf16[16,32,512]{2,1,0:T(8,128)(2,1)S(1)}, bf16[16,32,512]{2,1,0:T(8,128)(2,1)}, u32[]{:S(2)}) copy-start(bf16[16,32,512]{2,1,0:T(8,128)(2,1)} %gather_fusion.3) | copy-start | bytes 1572868
  150.7 55.0 %copy-start.24 = (s32[16]{0:T(128)S(1)}, s32[16]{0:T(128)}, u32[]{:S(2)}) copy-start(s32[16]{0:T(128)} %copy-done.23) | copy-start | bytes 196
  208.3 20.6 %all-to-all-start.5 = ((bf16[16,32,512]{2,1,0:T(8,128)(2,1)}), bf16[16,32,512]{2,1,0:T(8,128)(2,1)S(1)}, u32[]{:S(2)}, u32[]{:S(2)}) async-start(bf16[16,32,512]{2,1,0:T(8,128)(2,1)} %scatter_fusion.3), calls=%async_computation.6 | async-start | bytes 1048576 | tf_op jit(solution)/shard_map/all_to_all | solution.py:214
  333.3 37.0 %copy-start.4 = (bf16[16,32,512]{2,1,0:T(8,128)(2,1)S(1)}, bf16[16,32,512]{2,1,0:T(8,128)(2,1)}, u32[]{:S(2)}) copy-start(bf16[16,32,512]{2,1,0:T(8,128)(2,1)} %gather_fusion) | copy-start | bytes 1572868
  338.4 43.2 %copy-start.12 = (bf16[4096,128]{1,0:T(8,128)(2,1)S(1)}, bf16[4096,128]{1,0:T(8,128)(2,1)}, u32[]{:S(2)}) copy-start(bf16[4096,128]{1,0:T(8,128)(2,1)} %get-tuple-element.6) | copy-start | bytes 3145732
  371.4 20.5 %copy-start.1 = (bf16[4096,128]{1,0:T(8,128)(2,1)S(1)}, bf16[4096,128]{1,0:T(8,128)(2,1)}, u32[]{:S(2)}) copy-start(bf16[4096,128]{1,0:T(8,128)(2,1)} %param.14) | copy-start | bytes 3145732
  374.9 15.7 %all-to-all-start.3 = ((bf16[16,32,512]{2,1,0:T(8,128)(2,1)}), bf16[16,32,512]{2,1,0:T(8,128)(2,1)S(1)}, u32[]{:S(2)}, u32[]{:S(2)}) async-start(bf16[16,32,512]{2,1,0:T(8,128)(2,1)} %scatter_fusion.1), calls=%async_computation.4 | async-start | bytes 1048576 | tf_op jit(solution)/shard_map/all_to_all | solution.py:205
Sparse Core Ops, SparseCore 0:
  38.5 33.4 all-gather.2
  74.2 32.0 all-gather.4
  128.4 70.4 all-reduce.3
  203.1 130.1 all-reduce.5
  335.7 34.5 reduce-scatter.1
where the time goes:
time: 406 us; the launch traced here: 399 us
  waiting for transfers between devices  243 us (60%)
  matrix products  47.3 us (12%)
  starting transfers between devices  30.5 us (8%)
  other arithmetic  25.9 us (6%)
  local copies, waits for them, and re-layouts  24 us (6%)
  between operations  14.6 us (4%)
  blocking collectives  13.1 us (3%)
    psum x1, waiting for transfers between devices, per_device(): lax.psum(grad_query_w.astype(jnp.bfloat16), 'dp').astype(jnp.float32)  103 us
    psum x1, waiting for transfers between devices, per_device(): lax.psum(input_term.astype(jnp.bfloat16), 'tensor').astype(jnp.float32)  48.2 us
    reduce_scatter x1, waiting for transfers between devices, per_device(): lax.psum_scatter(head_term.astype(jnp.bfloat16), 'tensor', scatter_dimens...  31.9 us
    all_gather x1, waiting for transfers between devices, per_device(): lax.all_gather(here_cot, 'tensor', axis=1, tiled=True)  19.5 us
    all_to_all x1, waiting for transfers between devices, per_device(): lax.all_to_all(place_rows(grad_rows.reshape(panel_count, panel_rows, shar...  13.6 us
    all_to_all x1, blocking collectives, per_device(): lax.all_to_all(place_rows(cotangent.reshape(panel_count, panel_rows, shar...  13.1 us
    scatter x5, local copies, waits for them, and re-layouts, place_rows(): return empty_buffer.at[index].set(array)  10.3 us
    all_to_all x1, starting transfers between devices, per_device(): lax.all_to_all(marker, 'dp', split_axis=0, concat_axis=0, tiled=True)  8.43 us
  transfers between devices with their start and end apart: 10, of which 10 were waited for; matrix products, arithmetic and copies ran while one was open for 16% of the time, Pallas kernels for 0%

commit v1 on v0

v1 whole, which is shorter than its diff:
```python
import functools

import jax
import jax.numpy as jnp
from jax import lax
from jax.experimental import pallas as pl
from jax.experimental.pallas import tpu as pltpu
from jax.sharding import Mesh
from jax.sharding import PartitionSpec as P

HD = 128
NORM_EPSILON = 1e-05
ROPE_THETA = 500000.0
SCORE_SCALE = HD ** (-0.5)
STEPS = (0, -1, 1, 2)
BF = jnp.bfloat16
F32 = jnp.float32
VMEM_LIMIT = 48 * 1024 * 1024


def params():
    return pltpu.CompilerParams(vmem_limit_bytes=VMEM_LIMIT)


def cost(flops, moved):
    return pl.CostEstimate(flops=int(flops), bytes_accessed=int(moved), transcendentals=0)


def nn(a, b):
    return lax.dot_general(a, b, (((1,), (0,)), ((), ())), preferred_element_type=F32)


def nt(a, b):
    return lax.dot_general(a, b, (((1,), (1,)), ((), ())), preferred_element_type=F32)


def place_kernel(plan_ref, rows_ref, out_ref):
    count = rows_ref.shape[0]
    for panel in range(count):
        out_ref[plan_ref[panel] // count] = rows_ref[panel]


def place(plan, panels):
    return pl.pallas_call(
        place_kernel,
        out_shape=jax.ShapeDtypeStruct(panels.shape, panels.dtype),
        in_specs=[
            pl.BlockSpec(memory_space=pltpu.SMEM),
            pl.BlockSpec(memory_space=pltpu.VMEM),
        ],
        out_specs=pl.BlockSpec(memory_space=pltpu.VMEM),
        compiler_params=params(),
        cost_estimate=cost(0, 2 * panels.size * 2),
        name="place",
    )(plan, panels)


def place_meta_kernel(plan_ref, rows_ref, docs_ref, out_ref):
    count, rows, width = rows_ref.shape
    for panel in range(count):
        target = plan_ref[panel] // count
        slot = plan_ref[panel] % count
        out_ref[target, :, :width] = rows_ref[panel]
        doc = docs_ref[panel]
        high = (doc // 128).astype(F32)
        low = (doc % 128).astype(F32)
        lane = lax.broadcasted_iota(jnp.int32, (rows, 128), 1)
        extra = jnp.where(lane == 0, high, 0.0)
        extra = jnp.where(lane == 1, low, extra)
        extra = jnp.where(lane == 2, slot.astype(F32), extra)
        out_ref[target, :, width:] = extra.astype(BF)


def place_meta(plan, panels, docs):
    count, rows, width = panels.shape
    return pl.pallas_call(
        place_meta_kernel,
        out_shape=jax.ShapeDtypeStruct((count, rows, width + 128), panels.dtype),
        in_specs=[
            pl.BlockSpec(memory_space=pltpu.SMEM),
            pl.BlockSpec(memory_space=pltpu.VMEM),
            pl.BlockSpec(memory_space=pltpu.VMEM),
        ],
        out_specs=pl.BlockSpec(memory_space=pltpu.VMEM),
        compiler_params=params(),
        cost_estimate=cost(0, 2 * panels.size * 2),
        name="place_meta",
    )(plan, panels, docs.reshape(count, rows, 1))


def project_kernel(
    idx_ref, mine_ref, other_ref, gain_ref, wq_ref, wk_ref, wv_ref,
    turned_ref, raw_ref, inverse_ref, acc_ref, squares_ref,
):
    step = pl.program_id(0)
    last = pl.num_programs(0) - 1
    width = mine_ref.shape[2]

    @pl.when(step == 0)
    def _():
        acc_ref[...] = jnp.zeros_like(acc_ref)
        squares_ref[...] = jnp.zeros_like(squares_ref)

    def work(piece):
        wide = piece.astype(F32)
        squares_ref[...] += jnp.sum(wide * wide, axis=1, keepdims=True)
        gained = (wide * gain_ref[0]).astype(BF)
        turned_ref[0] = gained.T
        q_cols = wq_ref.shape[1]
        kv_cols = wk_ref.shape[1]
        acc_ref[:, :q_cols] += nn(gained, wq_ref[...])
        acc_ref[:, q_cols : q_cols + kv_cols] += nn(gained, wk_ref[...])
        acc_ref[:, q_cols + kv_cols :] += nn(gained, wv_ref[...])

    half = pl.num_programs(0) // 2

    @pl.when(step < half)
    def _():
        work(mine_ref[0])

    @pl.when(step >= half)
    def _():
        work(other_ref[0])

    @pl.when(step == last)
    def _():
        features = width * (last + 1)
        inverse = lax.rsqrt(squares_ref[...] / features + NORM_EPSILON)
        inverse_ref[...] = inverse
        raw_ref[...] = acc_ref[...] * inverse


def project(idx, mine, other, gain, wq, wk, wv):
    parts, rows, width = mine.shape
    pieces = 2 * parts
    cols = wq.shape[1] + wk.shape[1] + wv.shape[1]
    grid_spec = pltpu.PrefetchScalarGridSpec(
        num_scalar_prefetch=1,
        grid=(pieces,),
        in_specs=[
            pl.BlockSpec((1, rows, width), lambda j, idx: (jnp.minimum(j, parts - 1), 0, 0)),
            pl.BlockSpec((1, rows, width), lambda j, idx: (jnp.maximum(j - parts, 0), 0, 0)),
            pl.BlockSpec((1, 1, width), lambda j, idx: (idx[j], 0, 0)),
            pl.BlockSpec((width, wq.shape[1]), lambda j, idx: (idx[j], 0)),
            pl.BlockSpec((width, wk.shape[1]), lambda j, idx: (idx[j], 0)),
            pl.BlockSpec((width, wv.shape[1]), lambda j, idx: (idx[j], 0)),
        ],
        out_specs=[
            pl.BlockSpec((1, width, rows), lambda j, idx: (j, 0, 0)),
            pl.BlockSpec((rows, cols), lambda j, idx: (0, 0)),
            pl.BlockSpec((rows, 1), lambda j, idx: (0, 0)),
        ],
        scratch_shapes=[pltpu.VMEM((rows, cols), F32), pltpu.VMEM((rows, 1), F32)],
    )
    return pl.pallas_call(
        project_kernel,
        grid_spec=grid_spec,
        out_shape=[
            jax.ShapeDtypeStruct((pieces, width, rows), BF),
            jax.ShapeDtypeStruct((rows, cols), F32),
            jax.ShapeDtypeStruct((rows, 1), F32),
        ],
        compiler_params=params(),
        cost_estimate=cost(2 * rows * width * pieces * cols, 2 * pieces * width * (2 * rows + cols)),
        name="project",
    )(idx, mine, other, gain.reshape(pieces, 1, width), wq, wk, wv)


def attend_kernel(
    q_raw_ref, k_raw_ref, v_raw_ref, cosine_ref, sine_ref, where_col_ref, where_row_ref,
    q_ref, k_ref, k_turned_ref, v_ref, shares_ref, attended_ref, v_turned_ref,
):
    cosine = cosine_ref[...]
    sine = sine_ref[...]

    def rotate(u):
        return u * cosine + pltpu.roll(u, HD // 2, 1) * sine

    @pl.when(pl.program_id(0) == 0)
    def _():
        key = rotate(k_raw_ref[...])
        k_ref[...] = key.astype(BF)
        k_turned_ref[...] = key.T.astype(BF)
        v_ref[...] = v_raw_ref[...].astype(BF)
        v_turned_ref[...] = v_raw_ref[...].T.astype(BF)

    query = rotate(q_raw_ref[...]).astype(BF)
    q_ref[...] = query
    scores = nt(k_ref[...], query) * SCORE_SCALE
    doc_s = where_col_ref[:, 0:1]
    at_s = where_col_ref[:, 1:2]
    doc_g = where_row_ref[0:1, :]
    at_g = where_row_ref[1:2, :]
    allowed = (doc_s == doc_g) & (at_s <= at_g)
    weights = jnp.where(allowed, jnp.exp(scores), 0.0)
    total = jnp.sum(weights, axis=0, keepdims=True)
    shares = (weights * (1.0 / total)).astype(BF)
    shares_ref[0] = shares
    attended_ref[...] = nn(v_turned_ref[...], shares).T.astype(BF)


def attend(raw, cosine, sine, where_col, where_row):
    rows = raw.shape[0]
    heads = raw.shape[1] // HD - 2
    whole = lambda shape: pl.BlockSpec(shape, lambda h: (0,) * len(shape))
    head = pl.BlockSpec((rows, HD), lambda h: (0, h))
    return pl.pallas_call(
        attend_kernel,
        grid=(heads,),
        in_specs=[
            head,
            pl.BlockSpec((rows, HD), lambda h: (0, heads)),
            pl.BlockSpec((rows, HD), lambda h: (0, heads + 1)),
            whole((rows, HD)),
            whole((rows, HD)),
            whole(where_col.shape),
            whole(where_row.shape),
        ],
        out_specs=[
            head,
            whole((rows, HD)),
            whole((HD, rows)),
            whole((rows, HD)),
            pl.BlockSpec((1, rows, rows), lambda h: (h, 0, 0)),
            head,
        ],
        out_shape=[
            jax.ShapeDtypeStruct((rows, heads * HD), BF),
            jax.ShapeDtypeStruct((rows, HD), BF),
            jax.ShapeDtypeStruct((HD, rows), BF),
            jax.ShapeDtypeStruct((rows, HD), BF),
            jax.ShapeDtypeStruct((heads, rows, rows), BF),
            jax.ShapeDtypeStruct((rows, heads * HD), BF),
        ],
        scratch_shapes=[pltpu.VMEM((HD, rows), BF)],
        compiler_params=params(),
        cost_estimate=cost(4 * heads * rows * rows * HD, 2 * heads * rows * rows),
        name="attend",
    )(raw, raw, raw, cosine, sine, where_col, where_row)


def back_kernel(
    idx_ref, mine_ref, other_ref, wo_ref, q_ref, k_ref, k_turned_ref, v_ref, shares_ref,
    raw_ref, inverse_ref, cosine_ref, sine_ref,
    grad_ref, scaled_ref, dots_ref, acc_ref, *, scale,
):
    step = pl.program_id(0)
    last = pl.num_programs(0) - 1
    half = pl.num_programs(0) // 2

    @pl.when(step == 0)
    def _():
        acc_ref[...] = jnp.zeros_like(acc_ref)

    @pl.when(step < half)
    def _():
        acc_ref[...] += nt(mine_ref[0], wo_ref[...])

    @pl.when(step >= half)
    def _():
        acc_ref[...] += nt(other_ref[0], wo_ref[...])

    @pl.when(step == last)
    def _():
        cosine = cosine_ref[...]
        sine = sine_ref[...]
        heads = shares_ref.shape[0]
        rows = q_ref.shape[0]
        factor = inverse_ref[...] * scale
        ones = jnp.ones((8, HD), F32)
        dots_ref[...] = jnp.zeros_like(dots_ref)

        def rotate_back(u):
            return u * cosine - pltpu.roll(u, HD // 2, 1) * sine

        def emit(at, grad):
            cols = slice(at * HD, (at + 1) * HD)
            rounded = grad.astype(BF)
            grad_ref[:, cols] = rounded
            scaled_ref[:, cols] = (grad * factor).astype(BF)
            product = rounded.astype(F32) * raw_ref[:, cols]
            dots_ref[...] += lax.dot_general(
                ones, product, (((1,), (1,)), ((), ())),
                preferred_element_type=F32, precision=lax.Precision.HIGHEST,
            )

        key_grad = jnp.zeros((rows, HD), F32)
        value_grad = jnp.zeros((rows, HD), F32)
        for h in range(heads):
            cols = slice(h * HD, (h + 1) * HD)
            grad_attended = acc_ref[:, cols].astype(BF)
            shares = shares_ref[h]
            share_grad = nt(v_ref[...], grad_attended)
            wide = shares.astype(F32)
            row_dot = jnp.sum(share_grad * wide, axis=0, keepdims=True)
            dscore = (wide * (share_grad - row_dot) * SCORE_SCALE).astype(BF)
            key_grad += nn(dscore, q_ref[:, cols])
            value_grad += nn(shares, grad_attended)
            emit(h, rotate_back(nn(k_turned_ref[...], dscore).T))
        emit(heads, rotate_back(key_grad))
        emit(heads + 1, value_grad)


def back(idx, mine, other, wo, q, k, k_turned, v, shares, raw, inverse, cosine, sine, scale):
    parts, rows, width = mine.shape
    cols = wo.shape[0]
    whole = lambda array: pl.BlockSpec(array.shape, lambda j, idx: (0,) * array.ndim)
    grid_spec = pltpu.PrefetchScalarGridSpec(
        num_scalar_prefetch=1,
        grid=(2 * parts,),
        in_specs=[
            pl.BlockSpec((1, rows, width), lambda j, idx: (jnp.minimum(j, parts - 1), 0, 0)),
            pl.BlockSpec((1, rows, width), lambda j, idx: (jnp.maximum(j - parts, 0), 0, 0)),
            pl.BlockSpec((cols, width), lambda j, idx: (0, idx[j])),
        ]
        + [whole(a) for a in (q, k, k_turned, v, shares, raw, inverse, cosine, sine)],
        out_specs=[
            pl.BlockSpec(raw.shape, lambda j, idx: (0, 0)),
            pl.BlockSpec(raw.shape, lambda j, idx: (0, 0)),
            pl.BlockSpec((8, rows), lambda j, idx: (0, 0)),
        ],
        scratch_shapes=[pltpu.VMEM((rows, cols), F32)],
    )
    return pl.pallas_call(
        functools.partial(back_kernel, scale=scale),
        grid_spec=grid_spec,
        out_shape=[
            jax.ShapeDtypeStruct(raw.shape, BF),
            jax.ShapeDtypeStruct(raw.shape, BF),
            jax.ShapeDtypeStruct((8, rows), F32),
        ],
        compiler_params=params(),
        cost_estimate=cost(
            4 * parts * rows * width * cols + 8 * cols * rows * rows, 4 * parts * width * (rows + cols)
        ),
        name="back",
    )(idx, mine, other, wo, q, k, k_turned, v, shares, raw, inverse, cosine, sine)


def weight_grad_kernel(idx_ref, turned_ref, scaled_ref, q_ref, k_ref, v_ref):
    turned = turned_ref[0]
    q_cols = q_ref.shape[1]
    kv_cols = k_ref.shape[1]
    q_ref[...] = nn(turned, scaled_ref[:, :q_cols]).astype(BF)
    both = nn(turned, scaled_ref[:, q_cols:]).astype(BF)
    k_ref[...] = both[:, :kv_cols]
    v_ref[...] = both[:, kv_cols:]


def weight_grad(idx, turned, scaled, q_cols, kv_cols):
    pieces, width, rows = turned.shape
    widths = (q_cols, kv_cols, kv_cols)
    grid_spec = pltpu.PrefetchScalarGridSpec(
        num_scalar_prefetch=1,
        grid=(pieces,),
        in_specs=[
            pl.BlockSpec((1, width, rows), lambda j, idx: (j, 0, 0)),
            pl.BlockSpec(scaled.shape, lambda j, idx: (0, 0)),
        ],
        out_specs=[pl.BlockSpec((width, w), lambda j, idx: (idx[j], 0)) for w in widths],
    )
    return pl.pallas_call(
        weight_grad_kernel,
        grid_spec=grid_spec,
        out_shape=[jax.ShapeDtypeStruct((pieces * width, w), BF) for w in widths],
        compiler_params=params(),
        cost_estimate=cost(
            2 * pieces * width * rows * sum(widths), 2 * pieces * width * (rows + sum(widths))
        ),
        name="weight_grad",
    )(idx, turned, scaled)


def out_term_kernel(idx_ref, attended_ref, wo_ref, out_ref):
    out_ref[0] = nn(attended_ref[...], wo_ref[...]).astype(BF)


def out_terms(idx, attended, wo, width):
    rows, cols = attended.shape
    parts = idx.shape[0]
    grid_spec = pltpu.PrefetchScalarGridSpec(
        num_scalar_prefetch=1,
        grid=(parts,),
        in_specs=[
            pl.BlockSpec((rows, cols), lambda j, idx: (0, 0)),
            pl.BlockSpec((cols, width), lambda j, idx: (0, idx[j])),
        ],
        out_specs=pl.BlockSpec((1, rows, width), lambda j, idx: (j, 0, 0)),
    )
    return pl.pallas_call(
        out_term_kernel,
        grid_spec=grid_spec,
        out_shape=jax.ShapeDtypeStruct((parts, rows, width), BF),
        compiler_params=params(),
        cost_estimate=cost(2 * parts * rows * cols * width, 2 * parts * width * (rows + cols)),
        name="out_terms",
    )(idx, attended, wo)


def input_term_kernel(idx_ref, grad_ref, dots_ref, wq_ref, wk_ref, wv_ref, out_ref):
    q_cols = wq_ref.shape[1]
    kv_cols = wk_ref.shape[1]
    rows = grad_ref.shape[0]
    term = nt(grad_ref[:, :q_cols], wq_ref[...])
    term += nt(grad_ref[:, q_cols : q_cols + kv_cols], wk_ref[...])
    term += nt(grad_ref[:, q_cols + kv_cols :], wv_ref[...])
    out_ref[0, :rows] = term.astype(BF)
    dots = dots_ref[0:1, :]
    high = dots.astype(BF).astype(F32)
    line = lax.broadcasted_iota(jnp.int32, (16, dots.shape[1]), 0)
    extra = jnp.where(line == 0, high, jnp.where(line == 1, dots - high, 0.0))
    out_ref[0, rows:] = extra.astype(BF)


def input_terms(idx, grad, dots, wq, wk, wv, width):
    rows, cols = grad.shape
    parts = idx.shape[0]
    grid_spec = pltpu.PrefetchScalarGridSpec(
        num_scalar_prefetch=1,
        grid=(parts,),
        in_specs=[
            pl.BlockSpec((rows, cols), lambda j, idx: (0, 0)),
            pl.BlockSpec(dots.shape, lambda j, idx: (0, 0)),
        ]
        + [pl.BlockSpec((width, w.shape[1]), lambda j, idx: (idx[j], 0)) for w in (wq, wk, wv)],
        out_specs=pl.BlockSpec((1, rows + 16, width), lambda j, idx: (j, 0, 0)),
    )
    return pl.pallas_call(
        input_term_kernel,
        grid_spec=grid_spec,
        out_shape=jax.ShapeDtypeStruct((parts, rows + 16, width), BF),
        compiler_params=params(),
        cost_estimate=cost(2 * parts * rows * cols * width, 2 * parts * width * (rows + cols)),
        name="input_terms",
    )(idx, grad, dots, wq, wk, wv)


def shift(array, step):
    size = lax.axis_size("y")
    return lax.ppermute(array, "y", [(i, (i + step) % size) for i in range(size)])


def swap(array):
    return lax.ppermute(array, "core", [(0, 1), (1, 0)])


def gather_pieces(piece):
    half = piece.shape[0] // 2
    below = shift(piece, 1)
    above = shift(piece, -1)
    far_top = shift(below[:half], 1)
    far_end = shift(above[half:], -1)
    mine = jnp.stack([piece, below, above, jnp.concatenate([far_top, far_end], axis=0)])
    return mine, swap(mine)


def sum_pieces(other_terms, mine_terms):
    wide = lambda a: a.astype(F32)
    sums = (wide(mine_terms) + wide(swap(other_terms))).astype(BF)
    rows = sums.shape[1]
    half = rows // 32 * 16
    relay_top = shift(sums[3, :half], 1)
    relay_end = shift(sums[3, half:], -1)
    up = jnp.concatenate([(wide(sums[2, :half]) + wide(relay_top)).astype(BF), sums[2, half:]], axis=0)
    down = jnp.concatenate([sums[1, :half], (wide(sums[1, half:]) + wide(relay_end)).astype(BF)], axis=0)
    return wide(sums[0]) + wide(shift(up, 1)) + wide(shift(down, -1))


def exchange(panels):
    return lax.all_to_all(panels, ("x", "z"), split_axis=0, concat_axis=0, tiled=True)


def per_device(
    tokens, norm_gain, doc_ids, panel_plan, wq, wk, wv, wo, cotangent,
):
    y, core = lax.axis_index("y"), lax.axis_index("core")
    ys, cores = lax.axis_size("y"), lax.axis_size("core")
    block = lax.axis_index("x") * lax.axis_size("z") + lax.axis_index("z")
    dp = lax.axis_size("x") * lax.axis_size("z")
    count = panel_plan.shape[0]
    rows, width = tokens.shape
    panel = rows // count
    features = norm_gain.shape[0]

    around = (y + jnp.array(STEPS, jnp.int32)) % ys
    idx_mine = around * cores + core
    idx_other = around * cores + (1 - core)
    idx = jnp.concatenate([idx_mine, idx_other])

    here_tokens = exchange(place(panel_plan, tokens.reshape(count, panel, width))).reshape(rows, width)
    arrived = exchange(
        place_meta(panel_plan, cotangent.reshape(count, panel, width), doc_ids.reshape(count, panel))
    )
    here_cot = arrived[:, :, :width].reshape(rows, width)
    meta = arrived[:, :, width : width + 3].reshape(rows, 3).astype(jnp.int32)
    docs = meta[:, 0] * 128 + meta[:, 1]
    at = block * rows + meta[:, 2] * panel + jnp.arange(rows, dtype=jnp.int32) % panel
    positions = (at - docs).astype(F32)
    frequency = ROPE_THETA ** (-2.0 * jnp.arange(HD // 2, dtype=F32) / HD)
    angles = positions[:, None] * frequency[None, :]
    cosine, sine = jnp.cos(angles), jnp.sin(angles)
    cosine = jnp.concatenate([cosine, cosine], axis=1)
    sine = jnp.concatenate([-sine, sine], axis=1)
    where_row = jnp.stack([docs, at])
    where_col = where_row.T

    tok_mine, tok_other = gather_pieces(here_tokens)
    cot_mine, cot_other = gather_pieces(here_cot)
    turned, raw, inverse = project(idx, tok_mine, tok_other, norm_gain, wq, wk, wv)
    q, k, k_turned, v, shares, attended = attend(raw, cosine, sine, where_col, where_row)

    out_sum = sum_pieces(
        out_terms(idx_other, attended, wo, width), out_terms(idx_mine, attended, wo, width)
    )
    output_rows = (here_tokens.astype(F32) + out_sum).astype(BF)

    scale = (rows * dp) ** (-0.5)
    grad, scaled, dots = back(
        idx, cot_mine, cot_other, wo, q, k, k_turned, v, shares, raw, inverse, cosine, sine, scale
    )
    grads = weight_grad(idx, turned, scaled, wq.shape[1], wk.shape[1])
    grad_query, grad_key, grad_value = lax.psum(tuple(grads), ("x", "z"))

    in_sum = sum_pieces(
        input_terms(idx_other, grad, dots, wq, wk, wv, width),
        input_terms(idx_mine, grad, dots, wq, wk, wv, width),
    )
    mean_term = ((in_sum[rows] + in_sum[rows + 1]) / features)[:, None]
    own = y * cores + core
    own_gain = lax.dynamic_slice_in_dim(norm_gain, own * width, width, 0)
    own_scaled = here_tokens.astype(F32) * inverse
    grad_rows = here_cot.astype(F32) + inverse * (in_sum[:rows] * own_gain - own_scaled * mean_term)
    grad_rows = grad_rows.astype(BF)

    targets = panel_plan // count
    output = exchange(output_rows.reshape(dp, panel, width))[targets].reshape(rows, width)
    grad_tokens = exchange(grad_rows.reshape(dp, panel, width))[targets].reshape(rows, width)
    return output, grad_tokens, grad_query, grad_key, grad_value


def solution(mesh):
    axes = ("x", "z", "y", "core")
    split = Mesh(mesh.devices.reshape(4, 4, 4, 2), axes)
    dp, tensor = ("x", "z"), ("y", "core")
    in_specs = (
        P(dp, tensor),
        P(),
        P(dp),
        P(dp),
        P(None, tensor),
        P(None, tensor),
        P(None, tensor),
        P(tensor, None),
        P(dp, tensor),
    )
    out_specs = (
        P(dp, tensor),
        P(dp, tensor),
        P(None, tensor),
        P(None, tensor),
        P(None, tensor),
    )
    return jax.shard_map(
        per_device, mesh=split, in_specs=in_specs, out_specs=out_specs, check_vma=False
    )
```

time: 406 us -> 272 us (0.67); the launches traced: 399 us -> 270 us
  waiting for transfers between devices: 243 us -> 95.6 us
  Pallas kernels: 0 us -> 62.6 us
  matrix products: 47.3 us -> 0 us
  starting transfers between devices: 30.5 us -> 44 us
  other arithmetic: 25.9 us -> 20.2 us
  local copies, waits for them, and re-layouts: 24 us -> 18.6 us
    psum x2 -> x1, waiting for transfers between devices: 151 us -> 36 us  [per_device(): grad_query, grad_key, grad_value = lax.psum(tuple(grads), ('x', 'z'))]
    pallas_call x0 -> x10, Pallas kernels: none -> 62.6 us  [the longest x1 14.5 us: back(): pl.pallas_call(functools.partial(back_kernel, scale=scale), grid_spec=gri...]
    dot_general x17 -> x0, matrix products: 47.3 us -> none  [the longest x1 5.96 us: per_device(): jnp.einsum('rd,cd->rc', full_cot, out_weight, preferred_element_type=jnp....]
    ppermute x0 -> x20, waiting for transfers between devices: none -> 35.4 us  [the longest x16 35.1 us: shift(): lax.ppermute(array, 'y', [(i, (i + step) % size) for i in range(size)])]
    reduce_scatter x1 -> x0, waiting for transfers between devices: 31.9 us -> none  [per_device(): lax.psum_scatter(head_term.astype(jnp.bfloat16), 'tensor', scatter_dimens...]
    ppermute x0 -> x20, starting transfers between devices: none -> 28.4 us  [the longest x16 21.2 us: shift(): lax.ppermute(array, 'y', [(i, (i + step) % size) for i in range(size)])]
    all_gather x2 -> x0, waiting for transfers between devices: 24.1 us -> none  [the longest x1 19.5 us: per_device(): lax.all_gather(here_cot, 'tensor', axis=1, tiled=True)]
    all_to_all x5 -> x3, starting transfers between devices: 29.6 us -> 15.6 us  [exchange(): lax.all_to_all(panels, ('x', 'z'), split_axis=0, concat_axis=0, tiled=True)]
  transfers between devices with their start and end apart: 10 -> 24, of which waited for: 10 -> 13; matrix products, arithmetic and copies ran while one was open for 16% -> 10% of each run, Pallas kernels for 0% -> 23%
where the time goes in v1:
time: 272 us; the launch traced here: 270 us
  waiting for transfers between devices  95.6 us (35%)
  Pallas kernels  62.6 us (23%)
  starting transfers between devices  44 us (16%)
  other arithmetic  20.2 us (7%)
  local copies, waits for them, and re-layouts  18.6 us (7%)
  blocking collectives  15.1 us (6%)
  between operations  14.4 us (5%)
    psum x1, waiting for transfers between devices, per_device(): grad_query, grad_key, grad_value = lax.psum(tuple(grads), ('x', 'z'))  36 us
    ppermute x16, waiting for transfers between devices, shift(): lax.ppermute(array, 'y', [(i, (i + step) % size) for i in range(size)])  35.1 us
    all_to_all x3, waiting for transfers between devices, exchange(): lax.all_to_all(panels, ('x', 'z'), split_axis=0, concat_axis=0, tiled=True)  24.2 us
    ppermute x16, starting transfers between devices, shift(): lax.ppermute(array, 'y', [(i, (i + step) % size) for i in range(size)])  21.2 us
    all_to_all x3, starting transfers between devices, exchange(): lax.all_to_all(panels, ('x', 'z'), split_axis=0, concat_axis=0, tiled=True)  15.6 us
    all_to_all x1, blocking collectives, exchange(): lax.all_to_all(panels, ('x', 'z'), split_axis=0, concat_axis=0, tiled=True)  15.1 us
    pallas_call x1, Pallas kernels, back(): pl.pallas_call(functools.partial(back_kernel, scale=scale), grid_spec=gri...  14.5 us
    unnamed x48, local copies, waits for them, and re-layouts  12.6 us
  transfers between devices with their start and end apart: 24, of which 13 were waited for; matrix products, arithmetic and copies ran while one was open for 10% of the time, Pallas kernels for 23%

profile of v1, /device:TPU:1, one launch (start us, length us, event | category | flops | bytes accessed | tf_op | source)
XLA Modules:
  0.0 270.4 jit_solution(8554512312404857794)
XLA Ops:
  7.2 1.1 copy-done.8
  8.3 0.7 copy-done.9
  8.9 1.4 place.1
  10.4 8.4 %all-to-all-start = ((bf16[16,32,512]{2,1,0:T(8,128)(2,1)}), bf16[16,32,512]{2,1,0:T(8,128)(2,1)S(1)}, u32[]{:S(2)}, u32[]{:S(2)}) async-start(bf16[16,32,512]{2,1,0:T(8,128)(2,1)} %place.1), calls=%async_computation | async-start | bytes 1048576 | tf_op jit(solution)/shard_map/all_to_all | solution.py:470
  18.8 0.2 reshape_reshape.4.docs_ref
  19.0 1.7 place_meta.1
  20.7 8.4 %all-to-all-done = bf16[16,32,512]{2,1,0:T(8,128)(2,1)S(1)} async-done(((bf16[16,32,512]{2,1,0:T(8,128)(2,1)}), bf16[16,32,512]{2,1,0:T(8,128)(2,1)S(1)}, u32[]{:S(2)}, u32[]{:S(2)}) %all-to-all-start) | async-done | bytes 524320 | tf_op jit(solution)/shard_map/all_to_all | solution.py:470
  29.1 3.6 %all-to-all-start.1 = ((bf16[16,32,640]{2,1,0:T(8,128)(2,1)}), bf16[16,32,640]{2,1,0:T(8,128)(2,1)S(1)}, u32[]{:S(2)}, u32[]{:S(2)}) async-start(bf16[16,32,640]{2,1,0:T(8,128)(2,1)} %place_meta.1), calls=%async_computation.1 | async-start | bytes 1310720 | tf_op jit(solution)/shard_map/all_to_all | solution.py:470
  32.7 2.8 %collective-permute-start.1 = (bf16[512,512]{1,0:T(8,128)(2,1)S(1)}, bf16[512,512]{1,0:T(8,128)(2,1)S(1)}, u32[]{:S(2)}, u32[]{:S(2)}) collective-permute-start(bf16[512,512]{1,0:T(8,128)(2,1)S(1)} %bitcast.82), channel_id=1, source_target_pairs={{0,6},{2,0},{4,2},{6,4},{1,7},{3,1},{5,3},{7,5},{8,14},{10,8},{12,... | collective-permute-start | bytes 1572872 | tf_op jit(solution)/shard_map/ppermute | solution.py:440
  35.6 7.1 %all-to-all-done.1 = bf16[16,32,640]{2,1,0:T(8,128)(2,1)S(1)} async-done(((bf16[16,32,640]{2,1,0:T(8,128)(2,1)}), bf16[16,32,640]{2,1,0:T(8,128)(2,1)S(1)}, u32[]{:S(2)}, u32[]{:S(2)}) %all-to-all-start.1) | async-done | bytes 655392 | tf_op jit(solution)/shard_map/all_to_all | solution.py:470
  42.7 2.8 %collective-permute-start.11 = (bf16[512,512]{1,0:T(8,128)(2,1)S(1)}, bf16[512,512]{1,0:T(8,128)(2,1)S(1)}, u32[]{:S(2)}, u32[]{:S(2)}) collective-permute-start(bf16[512,512]{1,0:T(8,128)(2,1)S(1)} %bitcast.85), channel_id=1, source_target_pairs={{0,6},{2,0},{4,2},{6,4},{1,7},{3,1},{5,3},{7,5},{8,14},{10,8},{12,... | collective-permute-start | bytes 1572872 | tf_op jit(solution)/shard_map/ppermute | solution.py:440
  45.5 0.7 slice.109
  46.2 2.7 collective-permute-start.3
  48.9 1.7 slice.108
  50.6 4.8 %collective-permute-done.11 = bf16[512,512]{1,0:T(8,128)(2,1)S(1)} collective-permute-done((bf16[512,512]{1,0:T(8,128)(2,1)S(1)}, bf16[512,512]{1,0:T(8,128)(2,1)S(1)}, u32[]{:S(2)}, u32[]{:S(2)}) %collective-permute-start.11) | collective-permute-done | bytes 524320 | tf_op jit(solution)/shard_map/ppermute | solution.py:440
  55.4 3.5 %collective-permute-start.13 = (bf16[256,512]{1,0:T(8,128)(2,1)S(1)}, bf16[256,512]{1,0:T(8,128)(2,1)S(1)}, u32[]{:S(2)}, u32[]{:S(2)}) collective-permute-start(bf16[256,512]{1,0:T(8,128)(2,1)S(1)} %slice.123), channel_id=1, source_target_pairs={{0,6},{2,0},{4,2},{6,4},{1,7},{3,1},{5,3},{7,5},{8,14},{10,8},{12,... | collective-permute-start | bytes 786440 | tf_op jit(solution)/shard_map/ppermute | solution.py:440
  59.0 2.1 collective-permute-done.3
  61.1 3.0 %collective-permute-done.2 = bf16[256,512]{1,0:T(8,128)(2,1)} collective-permute-done((bf16[256,512]{1,0:T(8,128)(2,1)}, bf16[256,512]{1,0:T(8,128)(2,1)}, u32[]{:S(2)}, u32[]{:S(2)}) %collective-permute-start.2) | collective-permute-done | bytes 262176 | tf_op jit(solution)/shard_map/ppermute | solution.py:440
  64.2 1.1 maximum_bitcast_fusion
  65.2 2.7 pad_maximum_fusion.mine_ref
  67.9 6.7 %collective-permute-start.4 = (bf16[4,512,512]{2,1,0:T(8,128)(2,1)}, bf16[4,512,512]{2,1,0:T(8,128)(2,1)}, u32[]{:S(2)}, u32[]{:S(2)}) collective-permute-start(bf16[4,512,512]{2,1,0:T(8,128)(2,1)} %pad_maximum_fusion.mine_ref), channel_id=1, source_target_pairs={{0,1},{1,0},{2,3},{3,2},{4,5},{5,4},{6,7},{7,6},{8,9},{9,8},{10,11... | collective-permute-start | bytes 6291464 | tf_op jit(solution)/shard_map/ppermute | solution.py:444
  74.7 1.6 pad_maximum_fusion.1.mine_ref
  77.3 1.0 fusion.12
  78.3 0.2 pad_maximum_fusion.6
  78.5 0.3 collective-permute-done.4.other_ref
  78.7 11.2 %project.1 = (bf16[8,512,512]{2,1,0:T(8,128)(2,1)}, f32[512,768]{1,0:T(8,128)S(1)}, f32[512,1]{1,0:T(8,128)S(1)}) custom-call(s32[8]{0:T(128)S(1)} %pad_add_fusion.1.idx_ref, bf16[4,512,512]{2,1,0:T(8,128)(2,1)} %pad_maximum_fusion.mine_ref, bf16[4,512,512]{2,1,0:T(8,128)(2,1)} %collective-permute-done.4.other_ref, f32[8,1,512]{2,1,0:T(1,128)S(1)} %bitcast.81, ...), custom_call_target="tpu_custom_call" | custom-call | flops 3221225472 | bytes 14680064 | tf_op jit(solution)/shard_map/project/pallas_call | solution.py:155
  90.0 4.5 %attend.1 = (bf16[512,512]{1,0:T(8,128)(2,1)S(1)}, bf16[512,128]{1,0:T(8,128)(2,1)S(1)}, bf16[128,512]{1,0:T(8,128)(2,1)S(1)}, bf16[512,128]{1,0:T(8,128)(2,1)S(...) custom-call(f32[512,768]{1,0:T(8,128)S(1)} %get-tuple-element.20.q_raw_ref.k_raw_ref.v_raw_ref.raw_ref, ...), custom_call_target="tpu_custom_call" | custom-call | flops 536870912 | bytes 2097152 | tf_op jit(solution)/shard_map/attend/pallas_call | solution.py:207
  94.5 1.3 copy-done.2
  95.9 5.2 %out_terms.3 = bf16[4,512,512]{2,1,0:T(8,128)(2,1)} custom-call(s32[4]{0:T(128)S(1)} %broadcast_add_fusion.idx_ref, bf16[512,512]{1,0:T(8,128)(2,1)S(1)} %get-tuple-element.21.attended_ref, bf16[512,4096]{1,0:T(8,128)(2,1)} %wo_ref.5), custom_call_target="tpu_custom_call" | custom-call | flops 1073741824 | bytes 4194304 | tf_op jit(solution)/shard_map/out_terms/pallas_call | solution.py:390
  101.0 0.4 collective-permute-start.5
  101.4 14.5 %back.1 = (bf16[512,768]{1,0:T(8,128)(2,1)S(1)}, bf16[512,768]{1,0:T(8,128)(2,1)S(1)}, f32[8,512]{1,0:T(8,128)S(1)}) custom-call(s32[8]{0:T(128)S(1)} %pad_add_fusion.1.idx_ref, bf16[4,512,512]{2,1,0:T(8,128)(2,1)} %pad_maximum_fusion.1.mine_ref, bf16[4,512,512]{2,1,0:T(8,128)(2,1)} %collective-permute-done.14.other_ref, bf16[512,4096]{1,0:T(8,128)(2,1)} %wo_ref.5, ...), custom_call_target="tpu_custom_call" | custom-call | flops 3221225472 | bytes 8388608 | tf_op jit(solution)/shard_map/back/pallas_call | solution.py:324
  115.9 5.9 %input_terms.3 = bf16[4,528,512]{2,1,0:T(8,128)(2,1)} custom-call(s32[4]{0:T(128)S(1)} %broadcast_add_fusion.idx_ref, bf16[512,768]{1,0:T(8,128)(2,1)S(1)} %get-tuple-element.28.grad_ref, f32[8,512]{1,0:T(8,128)S(1)} %get-tuple-element.29.dots_ref, bf16[4096,512]{1,0:T(8,128)(2,1)} %wq_ref.5, bf16[4096,128]{1,0:T(8,128)(2,1)S(1)} %copy-done, ...), custom_call_target="tpu_custom_call" | custom-call | flops 1610612736 | bytes 5242880 | tf_op jit(solution)/shard_map/input_terms/pallas_call | solution.py:428
  122.0 9.1 %weight_grad.1 = (bf16[4096,512]{1,0:T(8,128)(2,1)}, bf16[4096,128]{1,0:T(8,128)(2,1)S(1)}, bf16[4096,128]{1,0:T(8,128)(2,1)S(1)}) custom-call(s32[8]{0:T(128)S(1)} %pad_add_fusion.1.idx_ref, bf16[8,512,512]{2,1,0:T(8,128)(2,1)} %get-tuple-element.30.turned_ref, bf16[512,768]{1,0:T(8,128)(2,1)S(1)} %get-tuple-element.31.scaled_ref), custom_call_target="tpu_custom_call" | custom-call | flops 3221225472 | bytes 10485760 | tf_op jit(solution)/shard_map/weight_grad/pallas_call | solution.py:362
  131.1 1.0 copy-done.5
  132.0 1.0 copy-done.6
  133.0 4.0 %out_terms.2 = bf16[4,512,512]{2,1,0:T(8,128)(2,1)S(1)} custom-call(s32[4]{0:T(128)S(1)} %get-tuple-element.38.idx_ref, bf16[512,512]{1,0:T(8,128)(2,1)S(1)} %get-tuple-element.21.attended_ref, bf16[512,4096]{1,0:T(8,128)(2,1)} %wo_ref.5), custom_call_target="tpu_custom_call" | custom-call | flops 1073741824 | bytes 4194304 | tf_op jit(solution)/shard_map/out_terms/pallas_call | solution.py:390
  137.1 5.0 %input_terms.2 = bf16[4,528,512]{2,1,0:T(8,128)(2,1)S(1)} custom-call(s32[4]{0:T(128)S(1)} %get-tuple-element.38.idx_ref, bf16[512,768]{1,0:T(8,128)(2,1)S(1)} %get-tuple-element.28.grad_ref, f32[8,512]{1,0:T(8,128)S(1)} %get-tuple-element.29.dots_ref, bf16[4096,512]{1,0:T(8,128)(2,1)} %wq_ref.5, bf16[4096,128]{1,0:T(8,128)(2,1)S(1)} %copy-done, ...), custom_call_target="tpu_custom_call" | custom-call | flops 1610612736 | bytes 5242880 | tf_op jit(solution)/shard_map/input_terms/pallas_call | solution.py:428
  142.1 2.3 add_convert_fusion.1
  144.4 3.1 %add_convert_fusion = bf16[4,528,512]{2,1,0:T(8,128)(2,1)S(1)} fusion(bf16[4,528,512]{2,1,0:T(8,128)(2,1)} %collective-permute-done.15, bf16[4,528,512]{2,1,0:T(8,128)(2,1)S(1)} %input_terms.2), kind=kLoop, calls=%fused_computation.2 | loop fusion | flops 4325376 | bytes 6488064 | tf_op jit(solution)/shard_map/convert_element_type | solution.py:459
  147.8 2.7 %collective-permute-start.8 = (bf16[256,512]{1,0:T(8,128)(2,1)S(1)}, bf16[256,512]{1,0:T(8,128)(2,1)S(1)}, u32[]{:S(2)}, u32[]{:S(2)}) collective-permute-start(bf16[256,512]{1,0:T(8,128)(2,1)S(1)} %get-tuple-element.47), channel_id=1, source_target_pairs={{0,6},{2,0},{4,2},{6,4},{1,7},{3,1},{5,3},{7,5},{8,14},{10,8},{12,... | collective-permute-start | bytes 786440 | tf_op jit(solution)/shard_map/ppermute | solution.py:440
  150.6 1.5 collective-permute-start.18
  152.0 4.4 %collective-permute-done.16 = bf16[256,512]{1,0:T(8,128)(2,1)S(1)} collective-permute-done((bf16[256,512]{1,0:T(8,128)(2,1)S(1)}, bf16[256,512]{1,0:T(8,128)(2,1)S(1)}, u32[]{:S(2)}, u32[]{:S(2)}) %collective-permute-start.16) | collective-permute-done | bytes 262176 | tf_op jit(solution)/shard_map/ppermute | solution.py:440
  156.5 0.9 pad_maximum_fusion.2
  157.4 4.1 %collective-permute-done.18 = bf16[272,512]{1,0:T(8,128)(2,1)S(1)} collective-permute-done((bf16[272,512]{1,0:T(8,128)(2,1)S(1)}, bf16[272,512]{1,0:T(8,128)(2,1)S(1)}, u32[]{:S(2)}, u32[]{:S(2)}) %collective-permute-start.18) | collective-permute-done | bytes 278560 | tf_op jit(solution)/shard_map/ppermute | solution.py:440
  161.5 0.8 pad_maximum_fusion.3
  162.4 3.5 %collective-permute-start.19 = (bf16[528,512]{1,0:T(8,128)(2,1)}, bf16[528,512]{1,0:T(8,128)(2,1)}, u32[]{:S(2)}, u32[]{:S(2)}) collective-permute-start(bf16[528,512]{1,0:T(8,128)(2,1)} %pad_maximum_fusion.3), channel_id=1, source_target_pairs={{0,6},{2,0},{4,2},{6,4},{1,7},{3,1},{5,3},{7,5},{8,14},{10,8},{12,... | collective-permute-start | bytes 1622024 | tf_op jit(solution)/shard_map/ppermute | solution.py:440
  166.1 0.8 pad_maximum_fusion.5
  166.9 0.9 pad_maximum_fusion.4
  167.8 1.4 collective-permute-start.7
  169.5 3.8 %collective-permute-done.17 = bf16[528,512]{1,0:T(8,128)(2,1)} collective-permute-done((bf16[528,512]{1,0:T(8,128)(2,1)}, bf16[528,512]{1,0:T(8,128)(2,1)}, u32[]{:S(2)}, u32[]{:S(2)}) %collective-permute-start.17) | collective-permute-done | bytes 540704 | tf_op jit(solution)/shard_map/ppermute | solution.py:440
  173.2 3.1 %collective-permute-done.19 = bf16[528,512]{1,0:T(8,128)(2,1)} collective-permute-done((bf16[528,512]{1,0:T(8,128)(2,1)}, bf16[528,512]{1,0:T(8,128)(2,1)}, u32[]{:S(2)}, u32[]{:S(2)}) %collective-permute-start.19) | collective-permute-done | bytes 540704 | tf_op jit(solution)/shard_map/ppermute | solution.py:440
  176.3 1.5 fusion
  177.8 9.8 %collective-permute-done.9 = bf16[512,512]{1,0:T(8,128)(2,1)} collective-permute-done((bf16[512,512]{1,0:T(8,128)(2,1)}, bf16[512,512]{1,0:T(8,128)(2,1)}, u32[]{:S(2)}, u32[]{:S(2)}) %collective-permute-start.9) | collective-permute-done | bytes 524320 | tf_op jit(solution)/shard_map/ppermute | solution.py:440
  187.6 2.7 %fusion.6 = (bf16[512,512]{1,0:T(8,128)(2,1)}, bf16[512,512]{1,0:T(8,128)(2,1)S(1)}) fusion(f32[528,512]{1,0:T(8,128)S(1)} %fusion, f32[512]{0:T(512)S(1)} %bitcast.94, f32[512]{0:T(512)S(1)} %dynamic_slice.3, f32[512]{0:T(512)S(1)} %reduce, bf16[16,32,512]{2,1,0:T(8,128)(2,1)S(1)} %copy-done.16, bf16[16,32,512]{2,1,0:T(8,128)(2,1)S(1)} %copy-done.14, ...), kind=kLoop, calls=%fused_computation.15 | loop fusion | flops 4194304 | bytes 4724736 | tf_op jit(solution)/shard_map/convert_element_type | solution.py:533
  190.3 15.1 %all_to_all.20 = bf16[16,32,512]{2,1,0:T(8,128)(2,1)S(1)} all-to-all(bf16[16,32,512]{2,1,0:T(8,128)(2,1)S(1)} %bitcast.88), channel_id=1, replica_groups=mesh['x'=4,'z'=4,'y'=4,'core'=2] {'x','z'}, dimensions={0} | all-to-all | bytes 1048576 | tf_op jit(solution)/shard_map/all_to_all | solution.py:470
  205.4 3.6 %all-to-all-start.3 = ((bf16[16,32,512]{2,1,0:T(8,128)(2,1)}), bf16[16,32,512]{2,1,0:T(8,128)(2,1)S(1)}, u32[]{:S(2)}, u32[]{:S(2)}) async-start(bf16[16,32,512]{2,1,0:T(8,128)(2,1)} %bitcast.35), calls=%async_computation.3 | async-start | bytes 1048576 | tf_op jit(solution)/shard_map/all_to_all | solution.py:470
  209.0 1.4 gather_fusion
  210.4 8.7 %all-to-all-done.3 = bf16[16,32,512]{2,1,0:T(8,128)(2,1)S(1)} async-done(((bf16[16,32,512]{2,1,0:T(8,128)(2,1)}), bf16[16,32,512]{2,1,0:T(8,128)(2,1)S(1)}, u32[]{:S(2)}, u32[]{:S(2)}) %all-to-all-start.3) | async-done | bytes 524320 | tf_op jit(solution)/shard_map/all_to_all | solution.py:470
  219.1 1.4 gather_fusion.1
  220.5 36.0 %all-reduce.3.cloned.1.call-done = (bf16[4096,512]{1,0:T(8,128)(2,1)}, bf16[4096,128]{1,0:T(8,128)(2,1)}, bf16[4096,128]{1,0:T(8,128)(2,1)}) async-done(((bf16[4096,512]{1,0:T(8,128)(2,1)}, bf16[4096,128]{1,0:T(8,128)(2,1)}, bf16[4096,128]{1,0:T(8,128)(2,1)}), (bf16[4096,512]{1,0:T(8,128)(2,1)}, bf16[4096,128]{1,0:T(8,128)(2,1)}, bf16[4096,128]{1,0:T(8,128)(2,1)})) %all-reduce.3.cloned.1.call-update) | async-done | bytes 6291472 | tf_op jit(solution)/shard_map/psum | solution.py:522
  256.4 4.6 %copy.27 = bf16[4096,512]{1,0:T(8,128)(2,1)} copy(bf16[4096,512]{1,0:T(8,128)(2,1)} %get-tuple-element.66) | data formatting | bytes 8388608
  261.0 1.0 copy.28
  262.0 0.6 copy-done.17
  262.6 1.0 copy.29
  (88 shorter events, 2.3 us)
Async XLA Ops:
  7.2 11.8 %copy-start.7 = (bf16[512,512]{1,0:T(8,128)(2,1)S(1)}, bf16[512,512]{1,0:T(8,128)(2,1)}, u32[]{:S(2)}) copy-start(bf16[512,512]{1,0:T(8,128)(2,1)} %param.18) | copy-start | bytes 1572868
  7.2 1.1 copy-start.8
  8.3 0.7 copy-start.9
  8.9 9.9 %copy-start.19 = (s32[512]{0:T(512)S(1)}, s32[512]{0:T(512)}, u32[]{:S(2)}) copy-start(s32[512]{0:T(512)} %param.12) | copy-start | bytes 6148
  8.9 10.1 %copy-start.10 = (s32[16]{0:T(128)S(1)}, s32[16]{0:T(128)}, u32[]{:S(2)}) copy-start(s32[16]{0:T(128)} %plan_ref.3) | copy-start | bytes 196
  10.4 18.7 %all-to-all-start = ((bf16[16,32,512]{2,1,0:T(8,128)(2,1)}), bf16[16,32,512]{2,1,0:T(8,128)(2,1)S(1)}, u32[]{:S(2)}, u32[]{:S(2)}) async-start(bf16[16,32,512]{2,1,0:T(8,128)(2,1)} %place.1), calls=%async_computation | async-start | bytes 1048576 | tf_op jit(solution)/shard_map/all_to_all | solution.py:470
  19.0 31.5 %copy-start.20 = (s32[4]{0:T(128)S(1)}, s32[4]{0:T(128)}, u32[]{:S(2)}) copy-start(s32[4]{0:T(128)} %constant.89.clone) | copy-start | bytes 52
  29.1 36.1 %copy-start.13 = (bf16[16,32,512]{2,1,0:T(8,128)(2,1)}, bf16[16,32,512]{2,1,0:T(8,128)(2,1)S(1)}, u32[]{:S(2)}) copy-start(bf16[16,32,512]{2,1,0:T(8,128)(2,1)S(1)} %all-to-all-done) | copy-start | bytes 1572868
  29.1 13.5 %all-to-all-start.1 = ((bf16[16,32,640]{2,1,0:T(8,128)(2,1)}), bf16[16,32,640]{2,1,0:T(8,128)(2,1)S(1)}, u32[]{:S(2)}, u32[]{:S(2)}) async-start(bf16[16,32,640]{2,1,0:T(8,128)(2,1)} %place_meta.1), calls=%async_computation.1 | async-start | bytes 1310720 | tf_op jit(solution)/shard_map/all_to_all | solution.py:470
  32.7 223.7 %all-reduce.3.cloned.1.call-start = ((), (), s32[]{:S(2)}) async-start(), calls=%async_computation.4 | async-start | bytes 12582912 | tf_op jit(solution)/shard_map/psum | solution.py:522
  32.7 12.8 %collective-permute-start.1 = (bf16[512,512]{1,0:T(8,128)(2,1)S(1)}, bf16[512,512]{1,0:T(8,128)(2,1)S(1)}, u32[]{:S(2)}, u32[]{:S(2)}) collective-permute-start(bf16[512,512]{1,0:T(8,128)(2,1)S(1)} %bitcast.82), channel_id=1, source_target_pairs={{0,6},{2,0},{4,2},{6,4},{1,7},{3,1},{5,3},{7,5},{8,14},{10,8},{12,... | collective-permute-start | bytes 1572872 | tf_op jit(solution)/shard_map/ppermute | solution.py:440
  35.6 13.4 %collective-permute-start = (bf16[512,512]{1,0:T(8,128)(2,1)S(1)}, bf16[512,512]{1,0:T(8,128)(2,1)}, u32[]{:S(2)}, u32[]{:S(2)}) collective-permute-start(bf16[512,512]{1,0:T(8,128)(2,1)S(1)} %bitcast.83), channel_id=1, source_target_pairs={{0,2},{2,4},{4,6},{6,0},{1,3},{3,5},{5,7},{7,1},{8,10},{10,12},{12... | collective-permute-start | bytes 1572872 | tf_op jit(solution)/shard_map/ppermute | solution.py:440
  42.7 32.0 %copy-start.15 = (bf16[16,32,512]{2,1,0:T(8,128)(2,1)}, bf16[16,32,512]{2,1,0:T(8,128)(2,1)S(1)}, u32[]{:S(2)}) copy-start(bf16[16,32,512]{2,1,0:T(8,128)(2,1)S(1)} %slice.121) | copy-start | bytes 1572868
  42.7 12.7 %collective-permute-start.11 = (bf16[512,512]{1,0:T(8,128)(2,1)S(1)}, bf16[512,512]{1,0:T(8,128)(2,1)S(1)}, u32[]{:S(2)}, u32[]{:S(2)}) collective-permute-start(bf16[512,512]{1,0:T(8,128)(2,1)S(1)} %bitcast.85), channel_id=1, source_target_pairs={{0,6},{2,0},{4,2},{6,4},{1,7},{3,1},{5,3},{7,5},{8,14},{10,8},{12,... | collective-permute-start | bytes 1572872 | tf_op jit(solution)/shard_map/ppermute | solution.py:440
  45.5 13.4 %collective-permute-start.10 = (bf16[512,512]{1,0:T(8,128)(2,1)S(1)}, bf16[512,512]{1,0:T(8,128)(2,1)S(1)}, u32[]{:S(2)}, u32[]{:S(2)}) collective-permute-start(bf16[512,512]{1,0:T(8,128)(2,1)S(1)} %bitcast.86), channel_id=1, source_target_pairs={{0,2},{2,4},{4,6},{6,0},{1,3},{3,5},{5,7},{7,1},{8,10},{10,12},{12... | collective-permute-start | bytes 1572872 | tf_op jit(solution)/shard_map/ppermute | solution.py:440
  46.2 14.9 %collective-permute-start.3 = (bf16[256,512]{1,0:T(8,128)(2,1)}, bf16[256,512]{1,0:T(8,128)(2,1)}, u32[]{:S(2)}, u32[]{:S(2)}) collective-permute-start(bf16[256,512]{1,0:T(8,128)(2,1)} %slice.109), channel_id=1, source_target_pairs={{0,6},{2,0},{4,2},{6,4},{1,7},{3,1},{5,3},{7,5},{8,14},{10,8},{12,... | collective-permute-start | bytes 786440 | tf_op jit(solution)/shard_map/ppermute | solution.py:440
  50.6 13.6 %collective-permute-start.2 = (bf16[256,512]{1,0:T(8,128)(2,1)}, bf16[256,512]{1,0:T(8,128)(2,1)}, u32[]{:S(2)}, u32[]{:S(2)}) collective-permute-start(bf16[256,512]{1,0:T(8,128)(2,1)} %slice.108), channel_id=1, source_target_pairs={{0,2},{2,4},{4,6},{6,0},{1,3},{3,5},{5,7},{7,1},{8,10},{10,12},{12... | collective-permute-start | bytes 786440 | tf_op jit(solution)/shard_map/ppermute | solution.py:440
  55.4 19.2 %collective-permute-start.13 = (bf16[256,512]{1,0:T(8,128)(2,1)S(1)}, bf16[256,512]{1,0:T(8,128)(2,1)S(1)}, u32[]{:S(2)}, u32[]{:S(2)}) collective-permute-start(bf16[256,512]{1,0:T(8,128)(2,1)S(1)} %slice.123), channel_id=1, source_target_pairs={{0,6},{2,0},{4,2},{6,4},{1,7},{3,1},{5,3},{7,5},{8,14},{10,8},{12,... | collective-permute-start | bytes 786440 | tf_op jit(solution)/shard_map/ppermute | solution.py:440
  58.9 15.7 %collective-permute-start.12 = (bf16[256,512]{1,0:T(8,128)(2,1)S(1)}, bf16[256,512]{1,0:T(8,128)(2,1)S(1)}, u32[]{:S(2)}, u32[]{:S(2)}) collective-permute-start(bf16[256,512]{1,0:T(8,128)(2,1)S(1)} %slice.122), channel_id=1, source_target_pairs={{0,2},{2,4},{4,6},{6,0},{1,3},{3,5},{5,7},{7,1},{8,10},{10,12},{12... | collective-permute-start | bytes 786440 | tf_op jit(solution)/shard_map/ppermute | solution.py:440
  67.9 10.8 %collective-permute-start.4 = (bf16[4,512,512]{2,1,0:T(8,128)(2,1)}, bf16[4,512,512]{2,1,0:T(8,128)(2,1)}, u32[]{:S(2)}, u32[]{:S(2)}) collective-permute-start(bf16[4,512,512]{2,1,0:T(8,128)(2,1)} %pad_maximum_fusion.mine_ref), channel_id=1, source_target_pairs={{0,1},{1,0},{2,3},{3,2},{4,5},{5,4},{6,7},{7,6},{8,9},{9,8},{10,11... | collective-permute-start | bytes 6291464 | tf_op jit(solution)/shard_map/ppermute | solution.py:444
  76.3 25.1 %collective-permute-start.14 = (bf16[4,512,512]{2,1,0:T(8,128)(2,1)}, bf16[4,512,512]{2,1,0:T(8,128)(2,1)}, u32[]{:S(2)}, u32[]{:S(2)}) collective-permute-start(bf16[4,512,512]{2,1,0:T(8,128)(2,1)} %pad_maximum_fusion.1.mine_ref), channel_id=1, source_target_pairs={{0,1},{1,0},{2,3},{3,2},{4,5},{5,4},{6,7},{7,6},{8,9},{9,8},{10,11... | collective-permute-start | bytes 6291464 | tf_op jit(solution)/shard_map/ppermute | solution.py:444
  76.5 2.3 copy-start
  76.5 2.3 copy-start.1
  76.5 2.3 copy-start.11
  90.0 11.4 %copy-start.3 = (f32[512,1]{1,0:T(8,128)}, f32[512,1]{1,0:T(8,128)S(1)}, u32[]{:S(2)}) copy-start(f32[512,1]{1,0:T(8,128)S(1)} %get-tuple-element.22.inverse_ref) | copy-start | bytes 6148
  94.5 1.4 copy-start.2
  101.0 41.1 %collective-permute-start.5 = (bf16[4,512,512]{2,1,0:T(8,128)(2,1)}, bf16[4,512,512]{2,1,0:T(8,128)(2,1)}, u32[]{:S(2)}, u32[]{:S(2)}) collective-permute-start(bf16[4,512,512]{2,1,0:T(8,128)(2,1)} %out_terms.3), channel_id=1, source_target_pairs={{0,1},{1,0},{2,3},{3,2},{4,5},{5,4},{6,7},{7,6},{8,9},{9,8},{10,11... | collective-permute-start | bytes 6291464 | tf_op jit(solution)/shard_map/ppermute | solution.py:444
  121.8 22.6 %collective-permute-start.15 = (bf16[4,528,512]{2,1,0:T(8,128)(2,1)}, bf16[4,528,512]{2,1,0:T(8,128)(2,1)}, u32[]{:S(2)}, u32[]{:S(2)}) collective-permute-start(bf16[4,528,512]{2,1,0:T(8,128)(2,1)} %input_terms.3), channel_id=1, source_target_pairs={{0,1},{1,0},{2,3},{3,2},{4,5},{5,4},{6,7},{7,6},{8,9},{9,8},{10,11... | collective-permute-start | bytes 6488072 | tf_op jit(solution)/shard_map/ppermute | solution.py:444
  131.1 1.0 copy-start.5
  132.0 1.0 copy-start.6
  144.4 21.5 %copy-start.12 = (bf16[4,512,512]{2,1,0:T(8,128)(2,1)}, bf16[4,512,512]{2,1,0:T(8,128)(2,1)S(1)}, u32[]{:S(2)}) copy-start(bf16[4,512,512]{2,1,0:T(8,128)(2,1)S(1)} %add_convert_fusion.1) | copy-start | bytes 6291460
  147.5 8.9 %collective-permute-start.16 = (bf16[256,512]{1,0:T(8,128)(2,1)S(1)}, bf16[256,512]{1,0:T(8,128)(2,1)S(1)}, u32[]{:S(2)}, u32[]{:S(2)}) collective-permute-start(bf16[256,512]{1,0:T(8,128)(2,1)S(1)} %get-tuple-element.40), channel_id=1, source_target_pairs={{0,2},{2,4},{4,6},{6,0},{1,3},{3,5},{5,7},{7,1},{8,10},{10,12},{12... | collective-permute-start | bytes 786440 | tf_op jit(solution)/shard_map/ppermute | solution.py:440
  147.7 18.2 %collective-permute-start.6 = (bf16[256,512]{1,0:T(8,128)(2,1)S(1)}, bf16[256,512]{1,0:T(8,128)(2,1)S(1)}, u32[]{:S(2)}, u32[]{:S(2)}) collective-permute-start(bf16[256,512]{1,0:T(8,128)(2,1)S(1)} %get-tuple-element.46), channel_id=1, source_target_pairs={{0,2},{2,4},{4,6},{6,0},{1,3},{3,5},{5,7},{7,1},{8,10},{10,12},{12... | collective-permute-start | bytes 786440 | tf_op jit(solution)/shard_map/ppermute | solution.py:440
  147.8 18.1 %collective-permute-start.8 = (bf16[256,512]{1,0:T(8,128)(2,1)S(1)}, bf16[256,512]{1,0:T(8,128)(2,1)S(1)}, u32[]{:S(2)}, u32[]{:S(2)}) collective-permute-start(bf16[256,512]{1,0:T(8,128)(2,1)S(1)} %get-tuple-element.47), channel_id=1, source_target_pairs={{0,6},{2,0},{4,2},{6,4},{1,7},{3,1},{5,3},{7,5},{8,14},{10,8},{12,... | collective-permute-start | bytes 786440 | tf_op jit(solution)/shard_map/ppermute | solution.py:440
  150.6 10.9 %collective-permute-start.18 = (bf16[272,512]{1,0:T(8,128)(2,1)S(1)}, bf16[272,512]{1,0:T(8,128)(2,1)S(1)}, u32[]{:S(2)}, u32[]{:S(2)}) collective-permute-start(bf16[272,512]{1,0:T(8,128)(2,1)S(1)} %get-tuple-element.43), channel_id=1, source_target_pairs={{0,6},{2,0},{4,2},{6,4},{1,7},{3,1},{5,3},{7,5},{8,14},{10,8},{12,... | collective-permute-start | bytes 835592 | tf_op jit(solution)/shard_map/ppermute | solution.py:440
  157.3 15.9 %collective-permute-start.17 = (bf16[528,512]{1,0:T(8,128)(2,1)}, bf16[528,512]{1,0:T(8,128)(2,1)}, u32[]{:S(2)}, u32[]{:S(2)}) collective-permute-start(bf16[528,512]{1,0:T(8,128)(2,1)} %pad_maximum_fusion.2), channel_id=1, source_target_pairs={{0,2},{2,4},{4,6},{6,0},{1,3},{3,5},{5,7},{7,1},{8,10},{10,12},{12... | collective-permute-start | bytes 1622024 | tf_op jit(solution)/shard_map/ppermute | solution.py:440
  162.4 6.9 %copy-start.4 = (f32[512,1]{1,0:T(8,128)S(1)}, f32[512,1]{1,0:T(8,128)}, u32[]{:S(2)}) copy-start(f32[512,1]{1,0:T(8,128)} %copy-done.3) | copy-start | bytes 6148
  162.4 14.0 %collective-permute-start.19 = (bf16[528,512]{1,0:T(8,128)(2,1)}, bf16[528,512]{1,0:T(8,128)(2,1)}, u32[]{:S(2)}, u32[]{:S(2)}) collective-permute-start(bf16[528,512]{1,0:T(8,128)(2,1)} %pad_maximum_fusion.3), channel_id=1, source_target_pairs={{0,6},{2,0},{4,2},{6,4},{1,7},{3,1},{5,3},{7,5},{8,14},{10,8},{12,... | collective-permute-start | bytes 1622024 | tf_op jit(solution)/shard_map/ppermute | solution.py:440
  166.9 20.7 %copy-start.14 = (bf16[16,32,512]{2,1,0:T(8,128)(2,1)S(1)}, bf16[16,32,512]{2,1,0:T(8,128)(2,1)}, u32[]{:S(2)}) copy-start(bf16[16,32,512]{2,1,0:T(8,128)(2,1)} %copy-done.13) | copy-start | bytes 1572868
  166.9 20.7 %copy-start.16 = (bf16[16,32,512]{2,1,0:T(8,128)(2,1)S(1)}, bf16[16,32,512]{2,1,0:T(8,128)(2,1)}, u32[]{:S(2)}) copy-start(bf16[16,32,512]{2,1,0:T(8,128)(2,1)} %copy-done.15) | copy-start | bytes 1572868
  166.9 20.7 %collective-permute-start.9 = (bf16[512,512]{1,0:T(8,128)(2,1)}, bf16[512,512]{1,0:T(8,128)(2,1)}, u32[]{:S(2)}, u32[]{:S(2)}) collective-permute-start(bf16[512,512]{1,0:T(8,128)(2,1)} %pad_maximum_fusion.5), channel_id=1, source_target_pairs={{0,6},{2,0},{4,2},{6,4},{1,7},{3,1},{5,3},{7,5},{8,14},{10,8},{12,... | collective-permute-start | bytes 1572872 | tf_op jit(solution)/shard_map/ppermute | solution.py:440
  167.8 19.8 %collective-permute-start.7 = (bf16[512,512]{1,0:T(8,128)(2,1)}, bf16[512,512]{1,0:T(8,128)(2,1)}, u32[]{:S(2)}, u32[]{:S(2)}) collective-permute-start(bf16[512,512]{1,0:T(8,128)(2,1)} %pad_maximum_fusion.4), channel_id=1, source_target_pairs={{0,2},{2,4},{4,6},{6,0},{1,3},{3,5},{5,7},{7,1},{8,10},{10,12},{12... | collective-permute-start | bytes 1572872 | tf_op jit(solution)/shard_map/ppermute | solution.py:440
  205.4 13.7 %all-to-all-start.3 = ((bf16[16,32,512]{2,1,0:T(8,128)(2,1)}), bf16[16,32,512]{2,1,0:T(8,128)(2,1)S(1)}, u32[]{:S(2)}, u32[]{:S(2)}) async-start(bf16[16,32,512]{2,1,0:T(8,128)(2,1)} %bitcast.35), calls=%async_computation.3 | async-start | bytes 1048576 | tf_op jit(solution)/shard_map/all_to_all | solution.py:470
  256.4 4.6 %copy-start.18 = (bf16[4096,128]{1,0:T(8,128)(2,1)S(1)}, bf16[4096,128]{1,0:T(8,128)(2,1)}, u32[]{:S(2)}) copy-start(bf16[4096,128]{1,0:T(8,128)(2,1)} %get-tuple-element.67) | copy-start | bytes 3145732
  261.0 1.6 copy-start.17
Sparse Core Ops, SparseCore 0:
  133.2 123.2 all-reduce.2

commit v2 on v1

v2 whole, which is shorter than its diff:
```python
import functools

import jax
import jax.numpy as jnp
from jax import lax
from jax.experimental import pallas as pl
from jax.experimental.pallas import tpu as pltpu
from jax.sharding import Mesh
from jax.sharding import PartitionSpec as P

HD = 128
NORM_EPSILON = 1e-05
ROPE_THETA = 500000.0
SCORE_SCALE = HD ** (-0.5)
STEPS = (0, -1, 1, 2)
BF = jnp.bfloat16
F32 = jnp.float32
VMEM_LIMIT = 56 * 1024 * 1024


def params():
    return pltpu.CompilerParams(vmem_limit_bytes=VMEM_LIMIT)


def cost(flops, moved):
    return pl.CostEstimate(flops=int(flops), bytes_accessed=int(moved), transcendentals=0)


def nn(a, b):
    return lax.dot_general(a, b, (((1,), (0,)), ((), ())), preferred_element_type=F32)


def nt(a, b):
    return lax.dot_general(a, b, (((1,), (1,)), ((), ())), preferred_element_type=F32)


def place_kernel(plan_ref, rows_ref, out_ref):
    count = rows_ref.shape[0]
    for panel in range(count):
        out_ref[plan_ref[panel] // count] = rows_ref[panel]


def place(plan, panels):
    return pl.pallas_call(
        place_kernel,
        out_shape=jax.ShapeDtypeStruct(panels.shape, panels.dtype),
        in_specs=[
            pl.BlockSpec(memory_space=pltpu.SMEM),
            pl.BlockSpec(memory_space=pltpu.VMEM),
        ],
        out_specs=pl.BlockSpec(memory_space=pltpu.VMEM),
        compiler_params=params(),
        cost_estimate=cost(0, 2 * panels.size * 2),
        name="place",
    )(plan, panels)


def place_meta_kernel(plan_ref, rows_ref, docs_ref, out_ref):
    count, rows, width = rows_ref.shape
    for panel in range(count):
        target = plan_ref[panel] // count
        slot = plan_ref[panel] % count
        out_ref[target, :, :width] = rows_ref[panel]
        doc = docs_ref[panel]
        high = (doc // 128).astype(F32)
        low = (doc % 128).astype(F32)
        lane = lax.broadcasted_iota(jnp.int32, (rows, 128), 1)
        extra = jnp.where(lane == 0, high, 0.0)
        extra = jnp.where(lane == 1, low, extra)
        extra = jnp.where(lane == 2, slot.astype(F32), extra)
        out_ref[target, :, width:] = extra.astype(BF)


def place_meta(plan, panels, docs):
    count, rows, width = panels.shape
    return pl.pallas_call(
        place_meta_kernel,
        out_shape=jax.ShapeDtypeStruct((count, rows, width + 128), panels.dtype),
        in_specs=[
            pl.BlockSpec(memory_space=pltpu.SMEM),
            pl.BlockSpec(memory_space=pltpu.VMEM),
            pl.BlockSpec(memory_space=pltpu.VMEM),
        ],
        out_specs=pl.BlockSpec(memory_space=pltpu.VMEM),
        compiler_params=params(),
        cost_estimate=cost(0, 2 * panels.size * 2),
        name="place_meta",
    )(plan, panels, docs.reshape(count, rows, 1))


NEAR = tuple((step, other) for step in range(3) for other in (0, 1))
FAR = ((3, 0), (3, 1))

SMEM_SPEC = pl.BlockSpec(memory_space=pltpu.SMEM)
HBM_SPEC = pl.BlockSpec(memory_space=pltpu.HBM)


def whole(shape):
    return pl.BlockSpec(tuple(shape), lambda j: (0,) * len(shape))


def part_of(idx_ref, step, other, width):
    at = idx_ref[step] + (idx_ref[4] if not other else 1 - idx_ref[4])
    return pl.ds(pl.multiple_of(at * width, width), width)


class Copies:
    def __init__(self, sems):
        self.sems = sems
        self.count = 0

    def start(self, source, target):
        copy = pltpu.make_async_copy(source, target, self.sems.at[self.count])
        self.count += 1
        copy.start()
        return copy


def fetch_near(copies, pieces, buffer):
    return [[copies.start(pieces[3 * o + s], buffer.at[n])] for n, (s, o) in enumerate(NEAR)]


def fetch_far(copies, pieces, buffer):
    half = buffer.shape[1] // 2
    return [
        [
            copies.start(pieces[2 * n], buffer.at[n, :half]),
            copies.start(pieces[2 * n + 1], buffer.at[n, half:]),
        ]
        for n in range(2)
    ]


def project_steps(
    idx_ref, places, arrivals, copies, buffer, gain_ref, weights, held, turned_ref, raw_ref, fresh
):
    rows, width = buffer.shape[1:]
    for n, (step, other) in enumerate(places):
        part = part_of(idx_ref, step, other, width)
        for ref, target in zip(weights, held):
            arrivals[n].append(copies.start(ref.at[part], target.at[n]))
    squares = jnp.zeros((rows, 1), F32)
    for n, (step, other) in enumerate(places):
        core = idx_ref[4] if not other else 1 - idx_ref[4]
        for copy in arrivals[n]:
            copy.wait()
        wide = buffer[n].astype(F32)
        squares += jnp.sum(wide * wide, axis=1, keepdims=True)
        gained = (wide * gain_ref[pl.ds(idx_ref[step] + core, 1)]).astype(BF)
        turned_ref[step % 3, pl.ds(pl.multiple_of(core * width, width), width)] = gained.T
        at = 0
        for target in held:
            cols = slice(at, at + target.shape[2])
            at += target.shape[2]
            if fresh and n == 0:
                raw_ref[:, cols] = nn(gained, target[n])
            else:
                raw_ref[:, cols] += nn(gained, target[n])
    return squares


def project_near_kernel(*refs):
    idx_ref, pieces = refs[0], refs[1:7]
    gain_ref, wq, wk, wv, turned_ref, raw_ref, squares_ref, buffer, hq, hk, hv, sems = refs[7:]
    copies = Copies(sems)
    arrivals = fetch_near(copies, pieces, buffer)
    squares = project_steps(
        idx_ref, NEAR, arrivals, copies, buffer, gain_ref, (wq, wk, wv), (hq, hk, hv),
        turned_ref, raw_ref, True,
    )
    squares_ref[...] = jnp.broadcast_to(squares, squares_ref.shape)


def project_near(idx, pieces, gain, wq, wk, wv):
    rows, width = pieces[0].shape
    weights = (wq, wk, wv)
    cols = sum(w.shape[1] for w in weights)
    shapes = [
        jax.ShapeDtypeStruct((3, 2 * width, rows), BF),
        jax.ShapeDtypeStruct((rows, cols), F32),
        jax.ShapeDtypeStruct((rows, HD), F32),
    ]
    return pl.pallas_call(
        project_near_kernel,
        grid=(1,),
        in_specs=[SMEM_SPEC] + [HBM_SPEC] * 6 + [whole(gain.shape)] + [HBM_SPEC] * 3,
        out_specs=[whole(a.shape) for a in shapes],
        out_shape=shapes,
        scratch_shapes=[pltpu.VMEM((6, rows, width), BF)]
        + [pltpu.VMEM((6, width, w.shape[1]), BF) for w in weights]
        + [pltpu.SemaphoreType.DMA((24,))],
        compiler_params=params(),
        cost_estimate=cost(12 * rows * width * cols, 12 * width * (2 * rows + cols)),
        name="project_near",
    )(idx, *pieces, gain, *weights)


def attend_kernel(*refs):
    idx_ref, pieces = refs[0], refs[1:5]
    (
        gain_ref, wq, wk, wv, near_raw_ref, near_squares_ref,
        cosine_ref, sine_ref, where_col_ref, where_row_ref,
        turned_ref, raw_ref, inverse_ref, q_ref, k_ref, k_turned_ref, v_ref, shares_ref, attended_ref,
        buffer, hq, hk, hv, sems,
    ) = refs[5:]
    rows, width = buffer.shape[1:]
    copies = Copies(sems)
    arrivals = fetch_far(copies, pieces, buffer)
    raw_ref[...] = near_raw_ref[...]
    squares = project_steps(
        idx_ref, FAR, arrivals, copies, buffer, gain_ref, (wq, wk, wv), (hq, hk, hv),
        turned_ref, raw_ref, False,
    )
    features = wq.shape[0]
    inverse = lax.rsqrt((squares + near_squares_ref[:, 0:1]) / features + NORM_EPSILON)
    inverse_ref[...] = jnp.broadcast_to(inverse, inverse_ref.shape)
    raw_ref[...] = raw_ref[...] * inverse

    cosine = cosine_ref[...]
    sine = sine_ref[...]
    heads = shares_ref.shape[0]

    def rotate(u):
        return u * cosine + pltpu.roll(u, HD // 2, 1) * sine

    key = rotate(raw_ref[:, heads * HD : (heads + 1) * HD])
    k_ref[...] = key.astype(BF)
    k_turned_ref[...] = key.T.astype(BF)
    value = raw_ref[:, (heads + 1) * HD :]
    v_ref[...] = value.astype(BF)
    v_turned = value.T.astype(BF)
    doc_s = where_col_ref[:, 0:1]
    at_s = where_col_ref[:, 1:2]
    doc_g = where_row_ref[0:1, :]
    at_g = where_row_ref[1:2, :]
    allowed = (doc_s == doc_g) & (at_s <= at_g)
    for h in range(heads):
        cols = slice(h * HD, (h + 1) * HD)
        query = rotate(raw_ref[:, cols]).astype(BF)
        q_ref[:, cols] = query
        scores = nt(k_ref[...], query) * SCORE_SCALE
        weights = jnp.where(allowed, jnp.exp(scores), 0.0)
        total = jnp.sum(weights, axis=0, keepdims=True)
        shares = (weights * (1.0 / total)).astype(BF)
        shares_ref[h] = shares
        attended_ref[:, cols] = nn(v_turned, shares).T.astype(BF)


def attend(idx, pieces, gain, wq, wk, wv, near_raw, near_squares, cosine, sine, where_col, where_row):
    width = pieces[0].shape[1]
    rows, cols = near_raw.shape
    weights = (wq, wk, wv)
    heads = wq.shape[1] // HD
    shapes = [
        jax.ShapeDtypeStruct((1, 2 * width, rows), BF),
        jax.ShapeDtypeStruct((rows, cols), F32),
        jax.ShapeDtypeStruct((rows, HD), F32),
        jax.ShapeDtypeStruct((rows, heads * HD), BF),
        jax.ShapeDtypeStruct((rows, HD), BF),
        jax.ShapeDtypeStruct((HD, rows), BF),
        jax.ShapeDtypeStruct((rows, HD), BF),
        jax.ShapeDtypeStruct((heads, rows, rows), BF),
        jax.ShapeDtypeStruct((rows, heads * HD), BF),
    ]
    extras = (near_raw, near_squares, cosine, sine, where_col, where_row)
    return pl.pallas_call(
        attend_kernel,
        grid=(1,),
        in_specs=[SMEM_SPEC] + [HBM_SPEC] * 4 + [whole(gain.shape)] + [HBM_SPEC] * 3
        + [whole(a.shape) for a in extras],
        out_specs=[whole(a.shape) for a in shapes],
        out_shape=shapes,
        scratch_shapes=[pltpu.VMEM((2, rows, width), BF)]
        + [pltpu.VMEM((2, width, w.shape[1]), BF) for w in weights]
        + [pltpu.SemaphoreType.DMA((10,))],
        compiler_params=params(),
        cost_estimate=cost(
            4 * rows * width * cols + 4 * heads * rows * rows * HD, 4 * width * (2 * rows + cols)
        ),
        name="attend",
    )(idx, *pieces, gain, *weights, *extras)


def back_near_kernel(*refs):
    idx_ref, pieces = refs[0], refs[1:7]
    wo_ref, acc_ref, buffer, held, sems = refs[7:]
    width = buffer.shape[2]
    copies = Copies(sems)
    arrivals = fetch_near(copies, pieces, buffer)
    for n, (step, other) in enumerate(NEAR):
        part = part_of(idx_ref, step, other, width)
        arrivals[n].append(copies.start(wo_ref.at[:, part], held.at[n]))
    for n in range(len(NEAR)):
        for copy in arrivals[n]:
            copy.wait()
        if n == 0:
            acc_ref[...] = nt(buffer[n], held[n])
        else:
            acc_ref[...] += nt(buffer[n], held[n])


def back_near(idx, pieces, wo):
    rows, width = pieces[0].shape
    cols = wo.shape[0]
    return pl.pallas_call(
        back_near_kernel,
        grid=(1,),
        in_specs=[SMEM_SPEC] + [HBM_SPEC] * 7,
        out_specs=whole((rows, cols)),
        out_shape=jax.ShapeDtypeStruct((rows, cols), F32),
        scratch_shapes=[
            pltpu.VMEM((6, rows, width), BF),
            pltpu.VMEM((6, cols, width), BF),
            pltpu.SemaphoreType.DMA((12,)),
        ],
        compiler_params=params(),
        cost_estimate=cost(12 * rows * width * cols, 12 * width * (rows + cols)),
        name="back_near",
    )(idx, *pieces, wo)


def back_kernel(*refs, scale):
    idx_ref, pieces = refs[0], refs[1:5]
    inputs = refs[5:17]
    grad_ref, dots_ref, gq_ref, gk_ref, gv_ref = refs[17:22]
    buffer, held, scaled_ref, gq, gk, gv, sems = refs[22:29]
    targets = refs[29:]
    wo_ref, near_ref, far_turned, near_turned = inputs[:4]
    copies = Copies(sems)
    arrivals = fetch_far(copies, pieces, buffer)
    rows, width = buffer.shape[1:]
    for n, (step, other) in enumerate(FAR):
        part = part_of(idx_ref, step, other, width)
        arrivals[n].append(copies.start(wo_ref.at[:, part], held.at[n]))
    acc_ref, turned_ref = targets[:2]
    acc_copy = copies.start(near_ref, acc_ref)
    loads = [copies.start(source, target) for source, target in zip(inputs[4:], targets[2:])]
    turned_loads = [
        copies.start(near_turned, turned_ref.at[:3]),
        copies.start(far_turned, turned_ref.at[3:]),
    ]
    q_ref, k_ref, k_turned_ref, v_ref, shares_ref, raw_ref, inverse_ref, rotary_ref = targets[2:]
    acc_copy.wait()
    for n in range(2):
        for copy in arrivals[n]:
            copy.wait()
        acc_ref[...] += nt(buffer[n], held[n])
    for copy in loads:
        copy.wait()

    cosine = rotary_ref[0]
    sine = rotary_ref[1]
    heads = shares_ref.shape[0]
    factor = inverse_ref[:, 0:1] * scale

    def rotate_back(u):
        return u * cosine - pltpu.roll(u, HD // 2, 1) * sine

    products = jnp.zeros((rows, HD), F32)

    def emit(at, grad):
        cols = slice(at * HD, (at + 1) * HD)
        rounded = grad.astype(BF)
        grad_ref[:, cols] = rounded
        scaled_ref[:, cols] = (grad * factor).astype(BF)
        return rounded.astype(F32) * raw_ref[:, cols]

    parts = turned_ref.shape[0]
    outs = []

    def send(held_ref, out_ref, at):
        tall = turned_ref.shape[1]
        wide = held_ref.shape[2]
        for j in range(parts):
            held_ref[j] = nn(turned_ref[j], scaled_ref[:, at : at + wide]).astype(BF)
            start = pl.multiple_of(idx_ref[j] * width, tall)
            outs.append(copies.start(held_ref.at[j], out_ref.at[pl.ds(start, tall)]))

    key_grad = jnp.zeros((rows, HD), F32)
    value_grad = jnp.zeros((rows, HD), F32)
    for h in range(heads):
        cols = slice(h * HD, (h + 1) * HD)
        grad_attended = acc_ref[:, cols].astype(BF)
        shares = shares_ref[h]
        share_grad = nt(v_ref[...], grad_attended)
        wide = shares.astype(F32)
        row_dot = jnp.sum(share_grad * wide, axis=0, keepdims=True)
        dscore = (wide * (share_grad - row_dot) * SCORE_SCALE).astype(BF)
        key_grad += nn(dscore, q_ref[:, cols])
        value_grad += nn(shares, grad_attended)
        products += emit(h, rotate_back(nn(k_turned_ref[...], dscore).T))
    products += emit(heads, rotate_back(key_grad))
    products += emit(heads + 1, value_grad)
    for copy in turned_loads:
        copy.wait()
    send(gq, gq_ref, 0)
    kv = gk.shape[2]
    for j in range(parts):
        both = nn(turned_ref[j], scaled_ref[:, heads * HD :]).astype(BF)
        gk[j] = both[:, :kv]
        gv[j] = both[:, kv:]
        tall = turned_ref.shape[1]
        start = pl.multiple_of(idx_ref[j] * width, tall)
        outs.append(copies.start(gk.at[j], gk_ref.at[pl.ds(start, tall)]))
        outs.append(copies.start(gv.at[j], gv_ref.at[pl.ds(start, tall)]))
    dots_ref[...] = lax.dot_general(
        jnp.ones((8, HD), F32), products, (((1,), (1,)), ((), ())),
        preferred_element_type=F32, precision=lax.Precision.HIGHEST,
    )
    for copy in outs:
        copy.wait()


def back(idx, pieces, wo, near, far_turned, near_turned, q, k, k_turned, v, shares, raw, inverse, rotary, scale):
    width = pieces[0].shape[1]
    cols, features = wo.shape
    rows = near.shape[0]
    kv_cols = k.shape[1]
    inputs = (wo, near, far_turned, near_turned, q, k, k_turned, v, shares, raw, inverse, rotary)
    loaded = (q, k, k_turned, v, shares, raw, inverse, rotary)
    weight_shapes = [
        jax.ShapeDtypeStruct((features, w), BF) for w in (cols, kv_cols, kv_cols)
    ]
    shapes = [jax.ShapeDtypeStruct(raw.shape, BF), jax.ShapeDtypeStruct((8, rows), F32)]
    return pl.pallas_call(
        functools.partial(back_kernel, scale=scale),
        grid=(1,),
        in_specs=[SMEM_SPEC] + [HBM_SPEC] * 16,
        out_specs=[whole(a.shape) for a in shapes] + [HBM_SPEC] * 3,
        out_shape=shapes + weight_shapes,
        scratch_shapes=[
            pltpu.VMEM((2, rows, width), BF),
            pltpu.VMEM((2, cols, width), BF),
            pltpu.VMEM(raw.shape, BF),
        ]
        + [pltpu.VMEM((4, features // 4, w.shape[1]), BF) for w in weight_shapes]
        + [
            pltpu.SemaphoreType.DMA((40,)),
            pltpu.VMEM(near.shape, F32),
            pltpu.VMEM((4, features // 4, rows), BF),
        ]
        + [pltpu.VMEM(a.shape, a.dtype) for a in loaded],
        compiler_params=params(),
        cost_estimate=cost(
            4 * rows * width * cols + 8 * cols * rows * rows + 2 * rows * features * (cols + 2 * kv_cols),
            2 * features * (rows + cols),
        ),
        name="back",
    )(idx, *pieces, *inputs)


def out_term_kernel(idx_ref, _, attended_ref, wo_ref, out_ref):
    out_ref[0] = nn(attended_ref[...], wo_ref[...]).astype(BF)


def out_terms(idx, after, attended, wo, width):
    rows, cols = attended.shape
    parts = 4
    grid_spec = pltpu.PrefetchScalarGridSpec(
        num_scalar_prefetch=1,
        grid=(parts,),
        in_specs=[
            HBM_SPEC,
            pl.BlockSpec((rows, cols), lambda j, idx: (0, 0)),
            pl.BlockSpec((cols, width), lambda j, idx: (0, idx[j])),
        ],
        out_specs=pl.BlockSpec((1, rows, width), lambda j, idx: (j, 0, 0)),
    )
    return pl.pallas_call(
        out_term_kernel,
        grid_spec=grid_spec,
        out_shape=jax.ShapeDtypeStruct((parts, rows, width), BF),
        compiler_params=params(),
        cost_estimate=cost(40 * parts * rows * cols * width, 40 * parts * width * (rows + cols)),
        name="out_terms",
    )(idx, after, attended, wo)


def input_term_kernel(idx_ref, _, grad_ref, dots_ref, wq_ref, wk_ref, wv_ref, out_ref):
    q_cols = wq_ref.shape[1]
    kv_cols = wk_ref.shape[1]
    rows = grad_ref.shape[0]
    dots = dots_ref[0:1, :]
    high = dots.astype(BF).astype(F32)
    line = lax.broadcasted_iota(jnp.int32, (16, dots.shape[1]), 0)
    extra = jnp.where(line == 0, high, jnp.where(line == 1, dots - high, 0.0))
    term = nt(grad_ref[:, :q_cols], wq_ref[...])
    term += nt(grad_ref[:, q_cols : q_cols + kv_cols], wk_ref[...])
    term += nt(grad_ref[:, q_cols + kv_cols :], wv_ref[...])
    out_ref[0, :rows] = term.astype(BF)
    out_ref[0, rows:] = extra.astype(BF)


def input_terms(idx, after, grad, dots, wq, wk, wv, width):
    rows, cols = grad.shape
    parts = 4
    grid_spec = pltpu.PrefetchScalarGridSpec(
        num_scalar_prefetch=1,
        grid=(parts,),
        in_specs=[
            HBM_SPEC,
            pl.BlockSpec((rows, cols), lambda j, idx: (0, 0)),
            pl.BlockSpec(dots.shape, lambda j, idx: (0, 0)),
        ]
        + [
            pl.BlockSpec((width, w.shape[1]), lambda j, idx: (idx[j], 0))
            for w in (wq, wk, wv)
        ],
        out_specs=pl.BlockSpec((1, rows + 16, width), lambda j, idx: (j, 0, 0)),
    )
    return pl.pallas_call(
        input_term_kernel,
        grid_spec=grid_spec,
        out_shape=jax.ShapeDtypeStruct((parts, rows + 16, width), BF),
        compiler_params=params(),
        cost_estimate=cost(40 * parts * rows * cols * width, 40 * parts * width * (rows + cols)),
        name="input_terms",
    )(idx, after, grad, dots, wq, wk, wv)


def shift(array, step):
    size = lax.axis_size("y")
    return lax.ppermute(array, "y", [(i, (i + step) % size) for i in range(size)])


def swap(array):
    return lax.ppermute(array, "core", [(0, 1), (1, 0)])


def start_gather(piece):
    return piece, shift(piece, 1), shift(piece, -1)


def end_gather(piece, below, above):
    half = piece.shape[0] // 2
    far = (shift(below[:half], 1), shift(above[half:], -1))
    near = (piece, below, above)
    near = near + tuple(swap(a) for a in near)
    return near, far + tuple(swap(a) for a in far)


def sum_pieces(mine_terms, other_terms):
    wide = lambda a: a.astype(F32)
    sums = (wide(mine_terms) + wide(swap(other_terms))).astype(BF)
    rows = sums.shape[1]
    half = rows // 32 * 16
    relay_top = shift(sums[3, :half], 1)
    relay_end = shift(sums[3, half:], -1)
    up = jnp.concatenate([(wide(sums[2, :half]) + wide(relay_top)).astype(BF), sums[2, half:]], axis=0)
    down = jnp.concatenate([sums[1, :half], (wide(sums[1, half:]) + wide(relay_end)).astype(BF)], axis=0)
    return wide(sums[0]) + wide(shift(up, 1)) + wide(shift(down, -1))


def exchange(panels):
    return lax.all_to_all(panels, ("x", "z"), split_axis=0, concat_axis=0, tiled=True)


def per_device(
    tokens, norm_gain, doc_ids, panel_plan, wq, wk, wv, wo, cotangent,
):
    y, core = lax.axis_index("y"), lax.axis_index("core")
    ys, cores = lax.axis_size("y"), lax.axis_size("core")
    block = lax.axis_index("x") * lax.axis_size("z") + lax.axis_index("z")
    dp = lax.axis_size("x") * lax.axis_size("z")
    count = panel_plan.shape[0]
    rows, width = tokens.shape
    panel = rows // count
    features = norm_gain.shape[0]

    around = (y + jnp.array(STEPS, jnp.int32)) % ys
    idx = jnp.concatenate([around * cores, core[None]])

    here_tokens = exchange(place(panel_plan, tokens.reshape(count, panel, width))).reshape(rows, width)
    arrived = exchange(
        place_meta(panel_plan, cotangent.reshape(count, panel, width), doc_ids.reshape(count, panel))
    )
    here_cot = arrived[:, :, :width].reshape(rows, width)
    meta = arrived[:, :, width : width + 3].reshape(rows, 3).astype(jnp.int32)
    docs = meta[:, 0] * 128 + meta[:, 1]
    at = block * rows + meta[:, 2] * panel + jnp.arange(rows, dtype=jnp.int32) % panel
    positions = (at - docs).astype(F32)
    frequency = ROPE_THETA ** (-2.0 * jnp.arange(HD // 2, dtype=F32) / HD)
    angles = positions[:, None] * frequency[None, :]
    cosine, sine = jnp.cos(angles), jnp.sin(angles)
    cosine = jnp.concatenate([cosine, cosine], axis=1)
    sine = jnp.concatenate([-sine, sine], axis=1)
    where_row = jnp.stack([docs, at])
    where_col = where_row.T

    tok_near = start_gather(here_tokens)
    cot_near = start_gather(here_cot)
    tok_pieces = end_gather(*tok_near)
    gain = norm_gain.reshape(features // width, width)
    near_turned, near_raw, near_squares = project_near(idx, tok_pieces[0], gain, wq, wk, wv)
    cot_near, near_raw = lax.optimization_barrier((cot_near, near_raw))
    cot_pieces = end_gather(*cot_near)
    far_turned, raw, inverse, q, k, k_turned, v, shares, attended = attend(
        idx, tok_pieces[1], gain, wq, wk, wv, near_raw, near_squares, cosine, sine, where_col, where_row
    )

    scale = (rows * dp) ** (-0.5)
    cot_nears, shares = lax.optimization_barrier((cot_pieces[0], shares))
    near = back_near(idx, cot_nears, wo)
    rotary = jnp.stack([cosine, sine])
    grad, dots, *grads = back(
        idx, cot_pieces[1], wo, near, far_turned, near_turned, q, k, k_turned, v, shares,
        raw, inverse, rotary, scale,
    )
    grad_query, grad_key, grad_value = lax.psum(tuple(grads), ("x", "z"))

    after = swap(dots)
    idx_mine, idx_other = around * cores + core, around * cores + (1 - core)
    out_sum = sum_pieces(
        *[out_terms(i, after, attended, wo, width) for i in (idx_mine, idx_other)]
    )
    output_rows = (here_tokens.astype(F32) + out_sum).astype(BF)
    in_sum = sum_pieces(
        *[input_terms(i, after, grad, dots, wq, wk, wv, width) for i in (idx_mine, idx_other)]
    )
    inverse = inverse[:, 0:1]
    mean_term = ((in_sum[rows] + in_sum[rows + 1]) / features)[:, None]
    own = y * cores + core
    own_gain = lax.dynamic_slice_in_dim(norm_gain, own * width, width, 0)
    own_scaled = here_tokens.astype(F32) * inverse
    grad_rows = here_cot.astype(F32) + inverse * (in_sum[:rows] * own_gain - own_scaled * mean_term)
    grad_rows = grad_rows.astype(BF)

    targets = panel_plan // count
    output = exchange(output_rows.reshape(dp, panel, width))[targets].reshape(rows, width)
    grad_tokens = exchange(grad_rows.reshape(dp, panel, width))[targets].reshape(rows, width)
    return output, grad_tokens, grad_query, grad_key, grad_value


def solution(mesh):
    axes = ("x", "z", "y", "core")
    split = Mesh(mesh.devices.reshape(4, 4, 4, 2), axes)
    dp, tensor = ("x", "z"), ("y", "core")
    in_specs = (
        P(dp, tensor),
        P(),
        P(dp),
        P(dp),
        P(None, tensor),
        P(None, tensor),
        P(None, tensor),
        P(tensor, None),
        P(dp, tensor),
    )
    out_specs = (
        P(dp, tensor),
        P(dp, tensor),
        P(None, tensor),
        P(None, tensor),
        P(None, tensor),
    )
    return jax.shard_map(
        per_device, mesh=split, in_specs=in_specs, out_specs=out_specs, check_vma=False
    )
```

time: 272 us -> 272 us (level)
  starting transfers between devices: 44 us -> 53.3 us
  other arithmetic: 20.2 us -> 11 us
  waiting for transfers between devices: 95.6 us -> 90.8 us
    ppermute x16, waiting for transfers between devices: 35.1 us -> 45.7 us  [shift(): lax.ppermute(array, 'y', [(i, (i + step) % size) for i in range(size)])]
    psum x1, waiting for transfers between devices: 36 us -> 26.9 us  [per_device(): grad_query, grad_key, grad_value = lax.psum(tuple(grads), ('x', 'z'))]
    ppermute x4 -> x13, starting transfers between devices: 7.23 us -> 14.1 us  [swap(): return lax.ppermute(array, 'core', [(0, 1), (1, 0)])]
    all_to_all x3, waiting for transfers between devices: 24.2 us -> 17.4 us  [exchange(): lax.all_to_all(panels, ('x', 'z'), split_axis=0, concat_axis=0, tiled=True)]
    another operation x4 -> x3, other arithmetic: 5.39 us -> 1.83 us  [per_device(): rotary = jnp.stack([cosine, sine])]
    pallas_call x4, Pallas kernels: 39.4 us -> 36.7 us  [the longest x1 13.2 us: back(): pl.pallas_call(functools.partial(back_kernel, scale=scale), grid=(1,), in...]
    unnamed x48 -> x66, local copies, waits for them, and re-layouts: 12.6 us -> 12 us
  transfers between devices with their start and end apart: 24 -> 33, of which waited for: 13 -> 16; matrix products, arithmetic and copies ran while one was open for 10% -> 7% of each run, Pallas kernels for 23% -> 18%
where the time goes in v2:
time: 272 us; the launch traced here: 271 us
  waiting for transfers between devices  90.8 us (33%)
  Pallas kernels  65.3 us (24%)
  starting transfers between devices  53.3 us (20%)
  local copies, waits for them, and re-layouts  19.3 us (7%)
  blocking collectives  17.1 us (6%)
  between operations  14.6 us (5%)
  other arithmetic  11 us (4%)
    ppermute x16, waiting for transfers between devices, shift(): lax.ppermute(array, 'y', [(i, (i + step) % size) for i in range(size)])  45.7 us
    psum x1, waiting for transfers between devices, per_device(): grad_query, grad_key, grad_value = lax.psum(tuple(grads), ('x', 'z'))  26.9 us
    ppermute x16, starting transfers between devices, shift(): lax.ppermute(array, 'y', [(i, (i + step) % size) for i in range(size)])  22.6 us
    all_to_all x3, waiting for transfers between devices, exchange(): lax.all_to_all(panels, ('x', 'z'), split_axis=0, concat_axis=0, tiled=True)  17.4 us
    all_to_all x1, blocking collectives, exchange(): lax.all_to_all(panels, ('x', 'z'), split_axis=0, concat_axis=0, tiled=True)  17.1 us
    all_to_all x3, starting transfers between devices, exchange(): lax.all_to_all(panels, ('x', 'z'), split_axis=0, concat_axis=0, tiled=True)  16.6 us
    ppermute x13, starting transfers between devices, swap(): return lax.ppermute(array, 'core', [(0, 1), (1, 0)])  14.1 us
    pallas_call x2, Pallas kernels, input_terms(): pl.pallas_call(input_term_kernel, grid_spec=grid_spec, out_shape=jax.Shap...  13.5 us
  transfers between devices with their start and end apart: 33, of which 16 were waited for; matrix products, arithmetic and copies ran while one was open for 7% of the time, Pallas kernels for 18%

profile of v2, /device:TPU:1, one launch (start us, length us, event | category | flops | bytes accessed | tf_op | source)
XLA Modules:
  0.0 271.4 jit_solution(10936126538306514623)
XLA Ops:
  7.2 1.9 place.1
  9.1 8.6 %all-to-all-start = ((bf16[16,32,512]{2,1,0:T(8,128)(2,1)}), bf16[16,32,512]{2,1,0:T(8,128)(2,1)S(1)}, u32[]{:S(2)}, u32[]{:S(2)}) async-start(bf16[16,32,512]{2,1,0:T(8,128)(2,1)} %place.1), calls=%async_computation | async-start | bytes 1048576 | tf_op jit(solution)/shard_map/all_to_all | solution.py:555
  17.7 0.9 reshape_reshape.4.docs_ref
  18.6 2.2 place_meta.1
  20.8 7.1 %all-to-all-done = bf16[16,32,512]{2,1,0:T(8,128)(2,1)S(1)} async-done(((bf16[16,32,512]{2,1,0:T(8,128)(2,1)}), bf16[16,32,512]{2,1,0:T(8,128)(2,1)S(1)}, u32[]{:S(2)}, u32[]{:S(2)}) %all-to-all-start) | async-done | bytes 524320 | tf_op jit(solution)/shard_map/all_to_all | solution.py:555
  28.0 3.6 %all-to-all-start.1 = ((bf16[16,32,640]{2,1,0:T(8,128)(2,1)}), bf16[16,32,640]{2,1,0:T(8,128)(2,1)S(1)}, u32[]{:S(2)}, u32[]{:S(2)}) async-start(bf16[16,32,640]{2,1,0:T(8,128)(2,1)} %place_meta.1), calls=%async_computation.1 | async-start | bytes 1310720 | tf_op jit(solution)/shard_map/all_to_all | solution.py:555
  32.2 1.3 collective-permute-start.2
  34.7 1.4 collective-permute-start.3
  36.1 2.6 collective-permute-start.4
  38.8 2.8 %all-to-all-done.1 = bf16[16,32,640]{2,1,0:T(8,128)(2,1)S(1)} async-done(((bf16[16,32,640]{2,1,0:T(8,128)(2,1)}), bf16[16,32,640]{2,1,0:T(8,128)(2,1)S(1)}, u32[]{:S(2)}, u32[]{:S(2)}) %all-to-all-start.1) | async-done | bytes 655392 | tf_op jit(solution)/shard_map/all_to_all | solution.py:555
  41.6 1.4 collective-permute-start
  43.6 1.2 collective-permute-done.2.refs_2_
  45.0 4.9 %collective-permute-start.5 = (bf16[512,512]{1,0:T(8,128)(2,1)S(1)}, bf16[512,512]{1,0:T(8,128)(2,1)S(1)}, u32[]{:S(2)}, u32[]{:S(2)}) collective-permute-start(bf16[512,512]{1,0:T(8,128)(2,1)S(1)} %collective-permute-done.2.refs_2_), channel_id=1, source_target_pairs={{0,1},{1,0},{2,3},{3,2},{4,5},{5,4},{6,7},{7,6},{8,9},{9,8},{10,11... | collective-permute-start | bytes 1572872 | tf_op jit(solution)/shard_map/ppermute | solution.py:527
  50.0 1.0 fusion.12
  51.1 2.7 %collective-permute-start.1 = (bf16[512,512]{1,0:T(8,128)(2,1)S(1)}, bf16[512,512]{1,0:T(8,128)(2,1)S(1)}, u32[]{:S(2)}, u32[]{:S(2)}) collective-permute-start(bf16[512,512]{1,0:T(8,128)(2,1)S(1)} %bitcast.78), channel_id=1, source_target_pairs={{0,6},{2,0},{4,2},{6,4},{1,7},{3,1},{5,3},{7,5},{8,14},{10,8},{12,... | collective-permute-start | bytes 1572872 | tf_op jit(solution)/shard_map/ppermute | solution.py:523
  53.8 7.8 %collective-permute-done.14.refs_1_ = bf16[256,512]{1,0:T(8,128)(2,1)S(1)} collective-permute-done((bf16[256,512]{1,0:T(8,128)(2,1)S(1)}, bf16[256,512]{1,0:T(8,128)(2,1)S(1)}, u32[]{:S(2)}, u32[]{:S(2)}) %collective-permute-start.14) | collective-permute-done | bytes 262176 | tf_op jit(solution)/shard_map/ppermute | solution.py:523
  61.6 1.4 collective-permute-start.15
  63.0 0.8 pad_maximum_fusion.6.refs_12_
  63.9 5.7 %collective-permute-done.15.refs_2_ = bf16[256,512]{1,0:T(8,128)(2,1)S(1)} collective-permute-done((bf16[256,512]{1,0:T(8,128)(2,1)S(1)}, bf16[256,512]{1,0:T(8,128)(2,1)S(1)}, u32[]{:S(2)}, u32[]{:S(2)}) %collective-permute-start.15) | collective-permute-done | bytes 262176 | tf_op jit(solution)/shard_map/ppermute | solution.py:523
  69.6 2.0 collective-permute-start.16
  71.7 0.7 copy-done.13
  72.3 0.8 copy-done.14
  73.1 9.0 %project_near.1 = (bf16[3,1024,512]{2,1,0:T(8,128)(2,1)}, f32[512,768]{1,0:T(8,128)}, f32[512,128]{1,0:T(8,128)}) custom-call(s32[5]{0:T(128)} %pad_add_fusion.1.refs_0_, bf16[512,512]{1,0:T(8,128)(2,1)} %bitcast.76, bf16[512,512]{1,0:T(8,128)(2,1)} %copy-done.7, bf16[512,512]{1,0:T(8,128)(2,1)} %copy-done.8, ...), custom_call_target="tpu_custom_call" | custom-call | flops 2415919104 | bytes 11010048 | tf_op jit(solution)/shard_map/project_near/pallas_call | solution.py:183
  83.0 0.7 slice.83
  83.7 0.7 slice.82
  84.5 3.4 %collective-permute-start.8 = (bf16[256,512]{1,0:T(8,128)(2,1)}, bf16[256,512]{1,0:T(8,128)(2,1)S(1)}, u32[]{:S(2)}, u32[]{:S(2)}) collective-permute-start(bf16[256,512]{1,0:T(8,128)(2,1)} %slice.83), channel_id=1, source_target_pairs={{0,6},{2,0},{4,2},{6,4},{1,7},{3,1},{5,3},{7,5},{8,14},{10,8},{12,... | collective-permute-start | bytes 786440 | tf_op jit(solution)/shard_map/ppermute | solution.py:523
  89.3 0.9 copy.20.refs_13_
  90.1 0.8 fusion.22
  91.0 0.8 pad_maximum_fusion.2.refs_16_
  91.8 1.7 collective-permute-done.8.refs_2_
  93.5 1.2 collective-permute-start.10
  94.8 1.9 collective-permute-done.7.refs_1_
  96.7 1.6 collective-permute-start.9
  98.2 8.5 %attend.1 = (bf16[1,1024,512]{2,1,0:T(8,128)(2,1)}, f32[512,768]{1,0:T(8,128)}, f32[512,128]{1,0:T(8,128)}, bf16[512,512]{1,0:T(8,128)(2,1)}, bf16[512,128]{1,0:...) custom-call(s32[5]{0:T(128)} %pad_add_fusion.1.refs_0_, ...), custom_call_target="tpu_custom_call" | custom-call | flops 1342177280 | bytes 3670016 | tf_op jit(solution)/shard_map/attend/pallas_call | solution.py:266
  106.8 0.8 copy-done.11
  107.8 6.0 %back_near.1.refs_6_ = f32[512,512]{1,0:T(8,128)} custom-call(s32[5]{0:T(128)} %pad_add_fusion.1.refs_0_, bf16[512,512]{1,0:T(8,128)(2,1)} %bitcast.80, bf16[512,512]{1,0:T(8,128)(2,1)} %copy-done.5, bf16[512,512]{1,0:T(8,128)(2,1)} %copy-done.6, bf16[512,512]{1,0:T(8,128)(2,1)} %collective-permute-done.11.refs_4_, bf16[512,512]{1,0:T(8,128)(2,1)} %copy-done.11, ...), custom_call_target="tpu_custom_call" | custom-call | flops 1610612736 | bytes 6291456 | tf_op jit(solution)/shard_map/back_near/pallas_call | solution.py:305
  113.8 0.7 copy-done.27
  114.6 13.2 %back.1 = (bf16[512,768]{1,0:T(8,128)(2,1)}, f32[8,512]{1,0:T(8,128)}, bf16[4096,512]{1,0:T(8,128)(2,1)}, bf16[4096,128]{1,0:T(8,128)(2,1)}, bf16[4096,128]{1,0:T(8,128)(2,1)}) custom-call(s32[5]{0:T(128)} %pad_add_fusion.1.refs_0_, bf16[256,512]{1,0:T(8,128)(2,1)} %collective-permute-done.7.refs_1_, bf16[256,512]{1,0:T(8,128)(2,1)} %copy-done.26, ...), custom_call_target="tpu_custom_call" | custom-call | flops 4831838208 | bytes 8388608 | tf_op jit(solution)/shard_map/back/pallas_call | solution.py:425
  128.7 0.8 collective-permute-done.18._
  130.1 5.5 %out_terms.3 = bf16[4,512,512]{2,1,0:T(8,128)(2,1)} custom-call(s32[4]{0:T(128)} %broadcast_add_fusion.idx_ref, f32[8,512]{1,0:T(8,128)} %copy-done.29, bf16[512,512]{1,0:T(8,128)(2,1)} %get-tuple-element.56.attended_ref, bf16[512,4096]{1,0:T(8,128)(2,1)} %wo_ref.3), custom_call_target="tpu_custom_call" | custom-call | flops 21474836480 | bytes 83886080 | tf_op jit(solution)/shard_map/out_terms/pallas_call | solution.py:469
  135.7 7.0 %input_terms.3 = bf16[4,528,512]{2,1,0:T(8,128)(2,1)} custom-call(s32[4]{0:T(128)} %broadcast_add_fusion.idx_ref, f32[8,512]{1,0:T(8,128)} %copy-done.29, bf16[512,768]{1,0:T(8,128)(2,1)} %get-tuple-element.57.grad_ref, f32[8,512]{1,0:T(8,128)} %get-tuple-element.55.dots_ref, bf16[4096,512]{1,0:T(8,128)(2,1)} %wq_ref.3, bf16[4096,128]{1,0:T(8,128)(2,1)} %wk_ref.3, ...), custom_call_target="tpu_custom_call" | custom-call | flops 32212254720 | bytes 104857600 | tf_op jit(solution)/shard_map/input_terms/pallas_call | solution.py:511
  143.0 6.5 %input_terms.2 = bf16[4,528,512]{2,1,0:T(8,128)(2,1)} custom-call(s32[4]{0:T(128)} %get-tuple-element.64.idx_ref, f32[8,512]{1,0:T(8,128)} %copy-done.29, bf16[512,768]{1,0:T(8,128)(2,1)} %get-tuple-element.57.grad_ref, f32[8,512]{1,0:T(8,128)} %get-tuple-element.55.dots_ref, bf16[4096,512]{1,0:T(8,128)(2,1)} %wq_ref.3, bf16[4096,128]{1,0:T(8,128)(2,1)} %wk_ref.3, ...), custom_call_target="tpu_custom_call" | custom-call | flops 32212254720 | bytes 104857600 | tf_op jit(solution)/shard_map/input_terms/pallas_call | solution.py:511
  149.6 5.5 %out_terms.2 = bf16[4,512,512]{2,1,0:T(8,128)(2,1)} custom-call(s32[4]{0:T(128)} %get-tuple-element.64.idx_ref, f32[8,512]{1,0:T(8,128)} %copy-done.29, bf16[512,512]{1,0:T(8,128)(2,1)} %get-tuple-element.56.attended_ref, bf16[512,4096]{1,0:T(8,128)(2,1)} %wo_ref.3), custom_call_target="tpu_custom_call" | custom-call | flops 21474836480 | bytes 83886080 | tf_op jit(solution)/shard_map/out_terms/pallas_call | solution.py:469
  155.0 2.4 add_convert_fusion.1
  158.4 2.7 %collective-permute-start.22 = (bf16[256,512]{1,0:T(8,128)(2,1)S(1)}, bf16[256,512]{1,0:T(8,128)(2,1)S(1)}, u32[]{:S(2)}, u32[]{:S(2)}) collective-permute-start(bf16[256,512]{1,0:T(8,128)(2,1)S(1)} %get-tuple-element.73), channel_id=1, source_target_pairs={{0,6},{2,0},{4,2},{6,4},{1,7},{3,1},{5,3},{7,5},{8,14},{10,8},{12,... | collective-permute-start | bytes 786440 | tf_op jit(solution)/shard_map/ppermute | solution.py:523
  161.1 1.5 collective-permute-start.27
  162.6 4.4 %collective-permute-done.25 = bf16[256,512]{1,0:T(8,128)(2,1)S(1)} collective-permute-done((bf16[256,512]{1,0:T(8,128)(2,1)S(1)}, bf16[256,512]{1,0:T(8,128)(2,1)S(1)}, u32[]{:S(2)}, u32[]{:S(2)}) %collective-permute-start.25) | collective-permute-done | bytes 262176 | tf_op jit(solution)/shard_map/ppermute | solution.py:523
  167.2 5.0 %collective-permute-done.27 = bf16[272,512]{1,0:T(8,128)(2,1)S(1)} collective-permute-done((bf16[272,512]{1,0:T(8,128)(2,1)S(1)}, bf16[272,512]{1,0:T(8,128)(2,1)S(1)}, u32[]{:S(2)}, u32[]{:S(2)}) %collective-permute-start.27) | collective-permute-done | bytes 278560 | tf_op jit(solution)/shard_map/ppermute | solution.py:523
  172.3 3.5 %collective-permute-start.28 = (bf16[528,512]{1,0:T(8,128)(2,1)S(1)}, bf16[528,512]{1,0:T(8,128)(2,1)S(1)}, u32[]{:S(2)}, u32[]{:S(2)}) collective-permute-start(bf16[528,512]{1,0:T(8,128)(2,1)S(1)} %pad_maximum_fusion.1), channel_id=1, source_target_pairs={{0,6},{2,0},{4,2},{6,4},{1,7},{3,1},{5,3},{7,5},{8,14},{10,8},{12,... | collective-permute-start | bytes 1622024 | tf_op jit(solution)/shard_map/ppermute | solution.py:523
  176.2 2.7 %collective-permute-start.23 = (bf16[512,512]{1,0:T(8,128)(2,1)S(1)}, bf16[512,512]{1,0:T(8,128)(2,1)S(1)}, u32[]{:S(2)}, u32[]{:S(2)}) collective-permute-start(bf16[512,512]{1,0:T(8,128)(2,1)S(1)} %pad_maximum_fusion.4), channel_id=1, source_target_pairs={{0,6},{2,0},{4,2},{6,4},{1,7},{3,1},{5,3},{7,5},{8,14},{10,8},{12,... | collective-permute-start | bytes 1572872 | tf_op jit(solution)/shard_map/ppermute | solution.py:523
  179.0 5.3 %collective-permute-done.26 = bf16[528,512]{1,0:T(8,128)(2,1)S(1)} collective-permute-done((bf16[528,512]{1,0:T(8,128)(2,1)S(1)}, bf16[528,512]{1,0:T(8,128)(2,1)S(1)}, u32[]{:S(2)}, u32[]{:S(2)}) %collective-permute-start.26) | collective-permute-done | bytes 540704 | tf_op jit(solution)/shard_map/ppermute | solution.py:523
  184.4 1.6 collective-permute-done.28
  186.2 9.3 %collective-permute-done.21 = bf16[512,512]{1,0:T(8,128)(2,1)S(1)} collective-permute-done((bf16[512,512]{1,0:T(8,128)(2,1)S(1)}, bf16[512,512]{1,0:T(8,128)(2,1)S(1)}, u32[]{:S(2)}, u32[]{:S(2)}) %collective-permute-start.21) | collective-permute-done | bytes 524320 | tf_op jit(solution)/shard_map/ppermute | solution.py:523
  195.5 1.8 collective-permute-done.23
  197.2 1.4 fusion.6
  198.6 17.1 %all_to_all.20 = bf16[16,32,512]{2,1,0:T(8,128)(2,1)S(1)} all-to-all(bf16[16,32,512]{2,1,0:T(8,128)(2,1)S(1)} %bitcast.81), channel_id=1, replica_groups=mesh['x'=4,'z'=4,'y'=4,'core'=2] {'x','z'}, dimensions={0} | all-to-all | bytes 1048576 | tf_op jit(solution)/shard_map/all_to_all | solution.py:555
  215.7 4.4 %all-to-all-start.3 = ((bf16[16,32,512]{2,1,0:T(8,128)(2,1)}), bf16[16,32,512]{2,1,0:T(8,128)(2,1)S(1)}, u32[]{:S(2)}, u32[]{:S(2)}) async-start(bf16[16,32,512]{2,1,0:T(8,128)(2,1)} %bitcast.29), calls=%async_computation.3 | async-start | bytes 1048576 | tf_op jit(solution)/shard_map/all_to_all | solution.py:555
  220.2 1.4 gather_fusion
  221.6 7.5 %all-to-all-done.3 = bf16[16,32,512]{2,1,0:T(8,128)(2,1)S(1)} async-done(((bf16[16,32,512]{2,1,0:T(8,128)(2,1)}), bf16[16,32,512]{2,1,0:T(8,128)(2,1)S(1)}, u32[]{:S(2)}, u32[]{:S(2)}) %all-to-all-start.3) | async-done | bytes 524320 | tf_op jit(solution)/shard_map/all_to_all | solution.py:555
  229.1 1.4 gather_fusion.1
  230.5 26.9 %all-reduce.3.cloned.1.call-done = (bf16[4096,512]{1,0:T(8,128)(2,1)}, bf16[4096,128]{1,0:T(8,128)(2,1)}, bf16[4096,128]{1,0:T(8,128)(2,1)}) async-done(((bf16[4096,512]{1,0:T(8,128)(2,1)}, bf16[4096,128]{1,0:T(8,128)(2,1)}, bf16[4096,128]{1,0:T(8,128)(2,1)}), (bf16[4096,512]{1,0:T(8,128)(2,1)}, bf16[4096,128]{1,0:T(8,128)(2,1)}, bf16[4096,128]{1,0:T(8,128)(2,1)})) %all-reduce.3.cloned.1.call-update) | async-done | bytes 6291472 | tf_op jit(solution)/shard_map/psum | solution.py:609
  257.4 4.6 %copy.27 = bf16[4096,512]{1,0:T(8,128)(2,1)} copy(bf16[4096,512]{1,0:T(8,128)(2,1)} %get-tuple-element.92) | data formatting | bytes 8388608
  261.9 1.0 copy.28
  263.5 1.0 copy.29
  (124 shorter events, 10.0 us)
Async XLA Ops:
  7.2 10.5 %copy-start.21 = (s32[512]{0:T(512)S(1)}, s32[512]{0:T(512)}, u32[]{:S(2)}) copy-start(s32[512]{0:T(512)} %param.12) | copy-start | bytes 6148
  9.1 22.6 %copy-start.25 = (s32[4]{0:T(128)S(1)}, s32[4]{0:T(128)}, u32[]{:S(2)}) copy-start(s32[4]{0:T(128)} %constant.89.clone) | copy-start | bytes 52
  9.1 25.0 %copy-start.20 = (f32[4096]{0:T(1024)S(1)}, f32[4096]{0:T(1024)}, u32[]{:S(2)}) copy-start(f32[4096]{0:T(1024)} %param.11) | copy-start | bytes 49156
  9.1 18.9 %all-to-all-start = ((bf16[16,32,512]{2,1,0:T(8,128)(2,1)}), bf16[16,32,512]{2,1,0:T(8,128)(2,1)S(1)}, u32[]{:S(2)}, u32[]{:S(2)}) async-start(bf16[16,32,512]{2,1,0:T(8,128)(2,1)} %place.1), calls=%async_computation | async-start | bytes 1048576 | tf_op jit(solution)/shard_map/all_to_all | solution.py:555
  28.0 15.3 %copy-start = (bf16[16,32,512]{2,1,0:T(8,128)(2,1)}, bf16[16,32,512]{2,1,0:T(8,128)(2,1)S(1)}, u32[]{:S(2)}) copy-start(bf16[16,32,512]{2,1,0:T(8,128)(2,1)S(1)} %all-to-all-done) | copy-start | bytes 1572868
  28.0 13.5 %all-to-all-start.1 = ((bf16[16,32,640]{2,1,0:T(8,128)(2,1)}), bf16[16,32,640]{2,1,0:T(8,128)(2,1)S(1)}, u32[]{:S(2)}, u32[]{:S(2)}) async-start(bf16[16,32,640]{2,1,0:T(8,128)(2,1)} %place_meta.1), calls=%async_computation.1 | async-start | bytes 1310720 | tf_op jit(solution)/shard_map/all_to_all | solution.py:555
  31.6 225.8 %all-reduce.3.cloned.1.call-start = ((), (), s32[]{:S(2)}) async-start(), calls=%async_computation.4 | async-start | bytes 12582912 | tf_op jit(solution)/shard_map/psum | solution.py:609
  32.2 9.4 %copy-start.23 = (s32[4]{0:T(128)}, s32[4]{0:T(128)S(1)}, u32[]{:S(2)}) copy-start(s32[4]{0:T(128)S(1)} %get-tuple-element.65) | copy-start | bytes 52
  32.2 12.6 %collective-permute-start.2 = (bf16[512,512]{1,0:T(8,128)(2,1)S(1)}, bf16[512,512]{1,0:T(8,128)(2,1)S(1)}, u32[]{:S(2)}, u32[]{:S(2)}) collective-permute-start(bf16[512,512]{1,0:T(8,128)(2,1)S(1)} %bitcast.73), channel_id=1, source_target_pairs={{0,2},{2,4},{4,6},{6,0},{1,3},{3,5},{5,7},{7,1},{8,10},{10,12},{12... | collective-permute-start | bytes 1572872 | tf_op jit(solution)/shard_map/ppermute | solution.py:523
  34.7 15.3 %collective-permute-start.3 = (bf16[512,512]{1,0:T(8,128)(2,1)S(1)}, bf16[512,512]{1,0:T(8,128)(2,1)S(1)}, u32[]{:S(2)}, u32[]{:S(2)}) collective-permute-start(bf16[512,512]{1,0:T(8,128)(2,1)S(1)} %bitcast.74), channel_id=1, source_target_pairs={{0,6},{2,0},{4,2},{6,4},{1,7},{3,1},{5,3},{7,5},{8,14},{10,8},{12,... | collective-permute-start | bytes 1572872 | tf_op jit(solution)/shard_map/ppermute | solution.py:523
  36.1 15.0 %collective-permute-start.4 = (bf16[512,512]{1,0:T(8,128)(2,1)S(1)}, bf16[512,512]{1,0:T(8,128)(2,1)}, u32[]{:S(2)}, u32[]{:S(2)}) collective-permute-start(bf16[512,512]{1,0:T(8,128)(2,1)S(1)} %bitcast.75), channel_id=1, source_target_pairs={{0,1},{1,0},{2,3},{3,2},{4,5},{5,4},{6,7},{7,6},{8,9},{9,8},{10,11... | collective-permute-start | bytes 1572872 | tf_op jit(solution)/shard_map/ppermute | solution.py:527
  41.6 41.2 %copy-start.2 = (bf16[16,32,512]{2,1,0:T(8,128)(2,1)}, bf16[16,32,512]{2,1,0:T(8,128)(2,1)S(1)}, u32[]{:S(2)}) copy-start(bf16[16,32,512]{2,1,0:T(8,128)(2,1)S(1)} %slice.112) | copy-start | bytes 1572868
  41.6 40.6 %collective-permute-start = (bf16[512,512]{1,0:T(8,128)(2,1)S(1)}, bf16[512,512]{1,0:T(8,128)(2,1)S(1)}, u32[]{:S(2)}, u32[]{:S(2)}) collective-permute-start(bf16[512,512]{1,0:T(8,128)(2,1)S(1)} %bitcast.77), channel_id=1, source_target_pairs={{0,2},{2,4},{4,6},{6,0},{1,3},{3,5},{5,7},{7,1},{8,10},{10,12},{12... | collective-permute-start | bytes 1572872 | tf_op jit(solution)/shard_map/ppermute | solution.py:523
  44.8 26.9 %copy-start.7 = (bf16[512,512]{1,0:T(8,128)(2,1)}, bf16[512,512]{1,0:T(8,128)(2,1)S(1)}, u32[]{:S(2)}) copy-start(bf16[512,512]{1,0:T(8,128)(2,1)S(1)} %collective-permute-done.2.refs_2_) | copy-start | bytes 1572868
  44.8 16.8 %collective-permute-start.14 = (bf16[256,512]{1,0:T(8,128)(2,1)S(1)}, bf16[256,512]{1,0:T(8,128)(2,1)S(1)}, u32[]{:S(2)}, u32[]{:S(2)}) collective-permute-start(bf16[256,512]{1,0:T(8,128)(2,1)S(1)} %slice.113), channel_id=1, source_target_pairs={{0,2},{2,4},{4,6},{6,0},{1,3},{3,5},{5,7},{7,1},{8,10},{10,12},{12... | collective-permute-start | bytes 786440 | tf_op jit(solution)/shard_map/ppermute | solution.py:523
  45.0 26.5 %collective-permute-start.5 = (bf16[512,512]{1,0:T(8,128)(2,1)S(1)}, bf16[512,512]{1,0:T(8,128)(2,1)S(1)}, u32[]{:S(2)}, u32[]{:S(2)}) collective-permute-start(bf16[512,512]{1,0:T(8,128)(2,1)S(1)} %collective-permute-done.2.refs_2_), channel_id=1, source_target_pairs={{0,1},{1,0},{2,3},{3,2},{4,5},{5,4},{6,7},{7,6},{8,9},{9,8},{10,11... | collective-permute-start | bytes 1572872 | tf_op jit(solution)/shard_map/ppermute | solution.py:527
  49.9 21.7 %copy-start.8 = (bf16[512,512]{1,0:T(8,128)(2,1)}, bf16[512,512]{1,0:T(8,128)(2,1)S(1)}, u32[]{:S(2)}) copy-start(bf16[512,512]{1,0:T(8,128)(2,1)S(1)} %collective-permute-done.3.refs_3_) | copy-start | bytes 1572868
  49.9 21.7 %collective-permute-start.6 = (bf16[512,512]{1,0:T(8,128)(2,1)S(1)}, bf16[512,512]{1,0:T(8,128)(2,1)S(1)}, u32[]{:S(2)}, u32[]{:S(2)}) collective-permute-start(bf16[512,512]{1,0:T(8,128)(2,1)S(1)} %collective-permute-done.3.refs_3_), channel_id=1, source_target_pairs={{0,1},{1,0},{2,3},{3,2},{4,5},{5,4},{6,7},{7,6},{8,9},{9,8},{10,11... | collective-permute-start | bytes 1572872 | tf_op jit(solution)/shard_map/ppermute | solution.py:527
  51.1 31.1 %collective-permute-start.1 = (bf16[512,512]{1,0:T(8,128)(2,1)S(1)}, bf16[512,512]{1,0:T(8,128)(2,1)S(1)}, u32[]{:S(2)}, u32[]{:S(2)}) collective-permute-start(bf16[512,512]{1,0:T(8,128)(2,1)S(1)} %bitcast.78), channel_id=1, source_target_pairs={{0,6},{2,0},{4,2},{6,4},{1,7},{3,1},{5,3},{7,5},{8,14},{10,8},{12,... | collective-permute-start | bytes 1572872 | tf_op jit(solution)/shard_map/ppermute | solution.py:523
  61.6 20.5 %copy-start.15 = (bf16[256,512]{1,0:T(8,128)(2,1)}, bf16[256,512]{1,0:T(8,128)(2,1)S(1)}, u32[]{:S(2)}) copy-start(bf16[256,512]{1,0:T(8,128)(2,1)S(1)} %collective-permute-done.14.refs_1_) | copy-start | bytes 786436
  61.6 7.9 %collective-permute-start.15 = (bf16[256,512]{1,0:T(8,128)(2,1)S(1)}, bf16[256,512]{1,0:T(8,128)(2,1)S(1)}, u32[]{:S(2)}, u32[]{:S(2)}) collective-permute-start(bf16[256,512]{1,0:T(8,128)(2,1)S(1)} %slice.114), channel_id=1, source_target_pairs={{0,6},{2,0},{4,2},{6,4},{1,7},{3,1},{5,3},{7,5},{8,14},{10,8},{12,... | collective-permute-start | bytes 786440 | tf_op jit(solution)/shard_map/ppermute | solution.py:523
  69.6 14.9 %copy-start.16 = (bf16[256,512]{1,0:T(8,128)(2,1)}, bf16[256,512]{1,0:T(8,128)(2,1)S(1)}, u32[]{:S(2)}) copy-start(bf16[256,512]{1,0:T(8,128)(2,1)S(1)} %collective-permute-done.15.refs_2_) | copy-start | bytes 786436
  69.6 14.9 %collective-permute-start.16 = (bf16[256,512]{1,0:T(8,128)(2,1)S(1)}, bf16[256,512]{1,0:T(8,128)(2,1)S(1)}, u32[]{:S(2)}, u32[]{:S(2)}) collective-permute-start(bf16[256,512]{1,0:T(8,128)(2,1)S(1)} %collective-permute-done.14.refs_1_), channel_id=1, source_target_pairs={{0,1},{1,0},{2,3},{3,2},{4,5},{5,4},{6,7},{7,6},{8,9},{9,8},{10,11... | collective-permute-start | bytes 786440 | tf_op jit(solution)/shard_map/ppermute | solution.py:527
  71.6 0.8 copy-start.13
  71.6 16.4 %collective-permute-start.17 = (bf16[256,512]{1,0:T(8,128)(2,1)S(1)}, bf16[256,512]{1,0:T(8,128)(2,1)S(1)}, u32[]{:S(2)}, u32[]{:S(2)}) collective-permute-start(bf16[256,512]{1,0:T(8,128)(2,1)S(1)} %collective-permute-done.15.refs_2_), channel_id=1, source_target_pairs={{0,1},{1,0},{2,3},{3,2},{4,5},{5,4},{6,7},{7,6},{8,9},{9,8},{10,11... | collective-permute-start | bytes 786440 | tf_op jit(solution)/shard_map/ppermute | solution.py:527
  72.3 0.8 copy-start.14
  82.2 24.6 %copy-start.5 = (bf16[512,512]{1,0:T(8,128)(2,1)}, bf16[512,512]{1,0:T(8,128)(2,1)S(1)}, u32[]{:S(2)}) copy-start(bf16[512,512]{1,0:T(8,128)(2,1)S(1)} %collective-permute-done.refs_2_) | copy-start | bytes 1572868
  82.2 24.6 %copy-start.6 = (bf16[512,512]{1,0:T(8,128)(2,1)}, bf16[512,512]{1,0:T(8,128)(2,1)S(1)}, u32[]{:S(2)}) copy-start(bf16[512,512]{1,0:T(8,128)(2,1)S(1)} %collective-permute-done.1.refs_3_) | copy-start | bytes 1572868
  82.2 24.6 %collective-permute-start.12 = (bf16[512,512]{1,0:T(8,128)(2,1)S(1)}, bf16[512,512]{1,0:T(8,128)(2,1)S(1)}, u32[]{:S(2)}, u32[]{:S(2)}) collective-permute-start(bf16[512,512]{1,0:T(8,128)(2,1)S(1)} %collective-permute-done.refs_2_), channel_id=1, source_target_pairs={{0,1},{1,0},{2,3},{3,2},{4,5},{5,4},{6,7},{7,6},{8,9},{9,8},{10,11... | collective-permute-start | bytes 1572872 | tf_op jit(solution)/shard_map/ppermute | solution.py:527
  82.3 24.5 %collective-permute-start.13 = (bf16[512,512]{1,0:T(8,128)(2,1)S(1)}, bf16[512,512]{1,0:T(8,128)(2,1)S(1)}, u32[]{:S(2)}, u32[]{:S(2)}) collective-permute-start(bf16[512,512]{1,0:T(8,128)(2,1)S(1)} %collective-permute-done.1.refs_3_), channel_id=1, source_target_pairs={{0,1},{1,0},{2,3},{3,2},{4,5},{5,4},{6,7},{7,6},{8,9},{9,8},{10,11... | collective-permute-start | bytes 1572872 | tf_op jit(solution)/shard_map/ppermute | solution.py:527
  82.8 24.1 %collective-permute-start.11 = (bf16[512,512]{1,0:T(8,128)(2,1)S(1)}, bf16[512,512]{1,0:T(8,128)(2,1)}, u32[]{:S(2)}, u32[]{:S(2)}) collective-permute-start(bf16[512,512]{1,0:T(8,128)(2,1)S(1)} %bitcast.79), channel_id=1, source_target_pairs={{0,1},{1,0},{2,3},{3,2},{4,5},{5,4},{6,7},{7,6},{8,9},{9,8},{10,11... | collective-permute-start | bytes 1572872 | tf_op jit(solution)/shard_map/ppermute | solution.py:527
  84.5 3.5 %copy-start.17 = (bf16[256,512]{1,0:T(8,128)(2,1)}, bf16[256,512]{1,0:T(8,128)(2,1)S(1)}, u32[]{:S(2)}) copy-start(bf16[256,512]{1,0:T(8,128)(2,1)S(1)} %collective-permute-done.16.refs_3_) | copy-start | bytes 786436
  84.5 9.0 %collective-permute-start.8 = (bf16[256,512]{1,0:T(8,128)(2,1)}, bf16[256,512]{1,0:T(8,128)(2,1)S(1)}, u32[]{:S(2)}, u32[]{:S(2)}) collective-permute-start(bf16[256,512]{1,0:T(8,128)(2,1)} %slice.83), channel_id=1, source_target_pairs={{0,6},{2,0},{4,2},{6,4},{1,7},{3,1},{5,3},{7,5},{8,14},{10,8},{12,... | collective-permute-start | bytes 786440 | tf_op jit(solution)/shard_map/ppermute | solution.py:523
  87.9 0.7 copy-start.18
  87.9 8.7 %collective-permute-start.7 = (bf16[256,512]{1,0:T(8,128)(2,1)}, bf16[256,512]{1,0:T(8,128)(2,1)}, u32[]{:S(2)}, u32[]{:S(2)}) collective-permute-start(bf16[256,512]{1,0:T(8,128)(2,1)} %slice.82), channel_id=1, source_target_pairs={{0,2},{2,4},{4,6},{6,0},{1,3},{3,5},{5,7},{7,1},{8,10},{10,12},{12... | collective-permute-start | bytes 786440 | tf_op jit(solution)/shard_map/ppermute | solution.py:523
  93.5 13.3 %copy-start.26 = (bf16[256,512]{1,0:T(8,128)(2,1)}, bf16[256,512]{1,0:T(8,128)(2,1)S(1)}, u32[]{:S(2)}) copy-start(bf16[256,512]{1,0:T(8,128)(2,1)S(1)} %collective-permute-done.8.refs_2_) | copy-start | bytes 786436
  93.5 20.3 %collective-permute-start.10 = (bf16[256,512]{1,0:T(8,128)(2,1)S(1)}, bf16[256,512]{1,0:T(8,128)(2,1)S(1)}, u32[]{:S(2)}, u32[]{:S(2)}) collective-permute-start(bf16[256,512]{1,0:T(8,128)(2,1)S(1)} %collective-permute-done.8.refs_2_), channel_id=1, source_target_pairs={{0,1},{1,0},{2,3},{3,2},{4,5},{5,4},{6,7},{7,6},{8,9},{9,8},{10,11... | collective-permute-start | bytes 786440 | tf_op jit(solution)/shard_map/ppermute | solution.py:527
  96.7 17.1 %collective-permute-start.9 = (bf16[256,512]{1,0:T(8,128)(2,1)}, bf16[256,512]{1,0:T(8,128)(2,1)S(1)}, u32[]{:S(2)}, u32[]{:S(2)}) collective-permute-start(bf16[256,512]{1,0:T(8,128)(2,1)} %collective-permute-done.7.refs_1_), channel_id=1, source_target_pairs={{0,1},{1,0},{2,3},{3,2},{4,5},{5,4},{6,7},{7,6},{8,9},{9,8},{10,11... | collective-permute-start | bytes 786440 | tf_op jit(solution)/shard_map/ppermute | solution.py:527
  106.8 0.8 copy-start.11
  106.8 1.0 copy-start.12
  113.8 0.7 copy-start.27
  113.8 0.8 copy-start.28
  114.6 13.5 %copy-start.24 = (s32[4]{0:T(128)S(1)}, s32[4]{0:T(128)}, u32[]{:S(2)}) copy-start(s32[4]{0:T(128)} %copy-done.23) | copy-start | bytes 52
  127.8 1.7 collective-permute-start.18
  129.5 0.6 copy-start.29
  135.5 19.5 %collective-permute-start.19 = (bf16[4,512,512]{2,1,0:T(8,128)(2,1)}, bf16[4,512,512]{2,1,0:T(8,128)(2,1)S(1)}, u32[]{:S(2)}, u32[]{:S(2)}) collective-permute-start(bf16[4,512,512]{2,1,0:T(8,128)(2,1)} %out_terms.3), channel_id=1, source_target_pairs={{0,1},{1,0},{2,3},{3,2},{4,5},{5,4},{6,7},{7,6},{8,9},{9,8},{10,11... | collective-permute-start | bytes 6291464 | tf_op jit(solution)/shard_map/ppermute | solution.py:527
  142.7 14.7 %collective-permute-start.24 = (bf16[4,528,512]{2,1,0:T(8,128)(2,1)}, bf16[4,528,512]{2,1,0:T(8,128)(2,1)S(1)}, u32[]{:S(2)}, u32[]{:S(2)}) collective-permute-start(bf16[4,528,512]{2,1,0:T(8,128)(2,1)} %input_terms.3), channel_id=1, source_target_pairs={{0,1},{1,0},{2,3},{3,2},{4,5},{5,4},{6,7},{7,6},{8,9},{9,8},{10,11... | collective-permute-start | bytes 6488072 | tf_op jit(solution)/shard_map/ppermute | solution.py:527
  155.0 2.4 copy-start.4
  158.1 8.9 %collective-permute-start.25 = (bf16[256,512]{1,0:T(8,128)(2,1)S(1)}, bf16[256,512]{1,0:T(8,128)(2,1)S(1)}, u32[]{:S(2)}, u32[]{:S(2)}) collective-permute-start(bf16[256,512]{1,0:T(8,128)(2,1)S(1)} %get-tuple-element.66), channel_id=1, source_target_pairs={{0,2},{2,4},{4,6},{6,0},{1,3},{3,5},{5,7},{7,1},{8,10},{10,12},{12... | collective-permute-start | bytes 786440 | tf_op jit(solution)/shard_map/ppermute | solution.py:523
  158.3 17.5 %collective-permute-start.20 = (bf16[256,512]{1,0:T(8,128)(2,1)S(1)}, bf16[256,512]{1,0:T(8,128)(2,1)S(1)}, u32[]{:S(2)}, u32[]{:S(2)}) collective-permute-start(bf16[256,512]{1,0:T(8,128)(2,1)S(1)} %get-tuple-element.72), channel_id=1, source_target_pairs={{0,2},{2,4},{4,6},{6,0},{1,3},{3,5},{5,7},{7,1},{8,10},{10,12},{12... | collective-permute-start | bytes 786440 | tf_op jit(solution)/shard_map/ppermute | solution.py:523
  158.4 17.4 %collective-permute-start.22 = (bf16[256,512]{1,0:T(8,128)(2,1)S(1)}, bf16[256,512]{1,0:T(8,128)(2,1)S(1)}, u32[]{:S(2)}, u32[]{:S(2)}) collective-permute-start(bf16[256,512]{1,0:T(8,128)(2,1)S(1)} %get-tuple-element.73), channel_id=1, source_target_pairs={{0,6},{2,0},{4,2},{6,4},{1,7},{3,1},{5,3},{7,5},{8,14},{10,8},{12,... | collective-permute-start | bytes 786440 | tf_op jit(solution)/shard_map/ppermute | solution.py:523
  161.1 11.1 %collective-permute-start.27 = (bf16[272,512]{1,0:T(8,128)(2,1)S(1)}, bf16[272,512]{1,0:T(8,128)(2,1)S(1)}, u32[]{:S(2)}, u32[]{:S(2)}) collective-permute-start(bf16[272,512]{1,0:T(8,128)(2,1)S(1)} %get-tuple-element.69), channel_id=1, source_target_pairs={{0,6},{2,0},{4,2},{6,4},{1,7},{3,1},{5,3},{7,5},{8,14},{10,8},{12,... | collective-permute-start | bytes 835592 | tf_op jit(solution)/shard_map/ppermute | solution.py:523
  167.2 17.2 %collective-permute-start.26 = (bf16[528,512]{1,0:T(8,128)(2,1)S(1)}, bf16[528,512]{1,0:T(8,128)(2,1)S(1)}, u32[]{:S(2)}, u32[]{:S(2)}) collective-permute-start(bf16[528,512]{1,0:T(8,128)(2,1)S(1)} %pad_maximum_fusion), channel_id=1, source_target_pairs={{0,2},{2,4},{4,6},{6,0},{1,3},{3,5},{5,7},{7,1},{8,10},{10,12},{12... | collective-permute-start | bytes 1622024 | tf_op jit(solution)/shard_map/ppermute | solution.py:523
  172.3 6.6 %copy-start.19 = (f32[512,128]{1,0:T(8,128)S(1)}, f32[512,128]{1,0:T(8,128)}, u32[]{:S(2)}) copy-start(f32[512,128]{1,0:T(8,128)} %get-tuple-element.54.refs_15_) | copy-start | bytes 786436
  172.3 13.7 %collective-permute-start.28 = (bf16[528,512]{1,0:T(8,128)(2,1)S(1)}, bf16[528,512]{1,0:T(8,128)(2,1)S(1)}, u32[]{:S(2)}, u32[]{:S(2)}) collective-permute-start(bf16[528,512]{1,0:T(8,128)(2,1)S(1)} %pad_maximum_fusion.1), channel_id=1, source_target_pairs={{0,6},{2,0},{4,2},{6,4},{1,7},{3,1},{5,3},{7,5},{8,14},{10,8},{12,... | collective-permute-start | bytes 1622024 | tf_op jit(solution)/shard_map/ppermute | solution.py:523
  176.0 21.2 %copy-start.1 = (bf16[16,32,512]{2,1,0:T(8,128)(2,1)S(1)}, bf16[16,32,512]{2,1,0:T(8,128)(2,1)}, u32[]{:S(2)}) copy-start(bf16[16,32,512]{2,1,0:T(8,128)(2,1)} %copy-done) | copy-start | bytes 1572868
  176.0 21.2 %copy-start.3 = (bf16[16,32,512]{2,1,0:T(8,128)(2,1)S(1)}, bf16[16,32,512]{2,1,0:T(8,128)(2,1)}, u32[]{:S(2)}) copy-start(bf16[16,32,512]{2,1,0:T(8,128)(2,1)} %copy-done.2) | copy-start | bytes 1572868
  176.0 19.5 %collective-permute-start.21 = (bf16[512,512]{1,0:T(8,128)(2,1)S(1)}, bf16[512,512]{1,0:T(8,128)(2,1)S(1)}, u32[]{:S(2)}, u32[]{:S(2)}) collective-permute-start(bf16[512,512]{1,0:T(8,128)(2,1)S(1)} %pad_maximum_fusion.3), channel_id=1, source_target_pairs={{0,2},{2,4},{4,6},{6,0},{1,3},{3,5},{5,7},{7,1},{8,10},{10,12},{12... | collective-permute-start | bytes 1572872 | tf_op jit(solution)/shard_map/ppermute | solution.py:523
  176.2 21.1 %collective-permute-start.23 = (bf16[512,512]{1,0:T(8,128)(2,1)S(1)}, bf16[512,512]{1,0:T(8,128)(2,1)S(1)}, u32[]{:S(2)}, u32[]{:S(2)}) collective-permute-start(bf16[512,512]{1,0:T(8,128)(2,1)S(1)} %pad_maximum_fusion.4), channel_id=1, source_target_pairs={{0,6},{2,0},{4,2},{6,4},{1,7},{3,1},{5,3},{7,5},{8,14},{10,8},{12,... | collective-permute-start | bytes 1572872 | tf_op jit(solution)/shard_map/ppermute | solution.py:523
  198.6 21.6 %copy-start.22 = (s32[16]{0:T(128)S(1)}, s32[16]{0:T(128)}, u32[]{:S(2)}) copy-start(s32[16]{0:T(128)} %plan_ref.3) | copy-start | bytes 196
  215.7 13.4 %all-to-all-start.3 = ((bf16[16,32,512]{2,1,0:T(8,128)(2,1)}), bf16[16,32,512]{2,1,0:T(8,128)(2,1)S(1)}, u32[]{:S(2)}, u32[]{:S(2)}) async-start(bf16[16,32,512]{2,1,0:T(8,128)(2,1)} %bitcast.29), calls=%async_computation.3 | async-start | bytes 1048576 | tf_op jit(solution)/shard_map/all_to_all | solution.py:555
  257.4 4.6 %copy-start.10 = (bf16[4096,128]{1,0:T(8,128)(2,1)S(1)}, bf16[4096,128]{1,0:T(8,128)(2,1)}, u32[]{:S(2)}) copy-start(bf16[4096,128]{1,0:T(8,128)(2,1)} %get-tuple-element.93) | copy-start | bytes 3145732
  261.9 1.6 copy-start.9
Sparse Core Ops, SparseCore 0:
  128.8 128.4 all-reduce.2

commit v3 on v2

--- a/solution.py
+++ b/solution.py
@@ -518,25 +518,27 @@
     )(idx, after, grad, dots, wq, wk, wv)
 
 
-def shift(array, step):
-    size = lax.axis_size("y")
-    return lax.ppermute(array, "y", [(i, (i + step) % size) for i in range(size)])
+def shift(array, step, axis="y"):
+    size = lax.axis_size(axis)
+    return lax.ppermute(array, axis, [(i, (i + step) % size) for i in range(size)])
 
 
 def swap(array):
     return lax.ppermute(array, "core", [(0, 1), (1, 0)])
 
 
-def start_gather(piece):
+def gather_near(piece):
     return piece, shift(piece, 1), shift(piece, -1)
 
 
-def end_gather(piece, below, above):
-    half = piece.shape[0] // 2
-    far = (shift(below[:half], 1), shift(above[half:], -1))
-    near = (piece, below, above)
-    near = near + tuple(swap(a) for a in near)
-    return near, far + tuple(swap(a) for a in far)
+def gather_far(near):
+    _, below, above = near
+    half = below.shape[0] // 2
+    return shift(below[:half], 1), shift(above[half:], -1)
+
+
+def both_cores(pieces):
+    return tuple(pieces) + tuple(swap(a) for a in pieces)
 
 
 def sum_pieces(mine_terms, other_terms):
@@ -568,7 +570,10 @@
     features = norm_gain.shape[0]
 
     around = (y + jnp.array(STEPS, jnp.int32)) % ys
-    idx = jnp.concatenate([around * cores, core[None]])
+    steps = jnp.array(STEPS, jnp.int32)
+    idx = jnp.concatenate(
+        [around * cores, core[None], (lax.axis_index("x") + steps) % 4, (lax.axis_index("z") + steps) % 4]
+    )
 
     here_tokens = exchange(place(panel_plan, tokens.reshape(count, panel, width))).reshape(rows, width)
     arrived = exchange(
@@ -587,27 +592,27 @@
     where_row = jnp.stack([docs, at])
     where_col = where_row.T
 
-    tok_near = start_gather(here_tokens)
-    cot_near = start_gather(here_cot)
-    tok_pieces = end_gather(*tok_near)
+    tok_near = gather_near(here_tokens)
+    cot_near = gather_near(here_cot)
+    tok_far = gather_far(tok_near)
     gain = norm_gain.reshape(features // width, width)
-    near_turned, near_raw, near_squares = project_near(idx, tok_pieces[0], gain, wq, wk, wv)
-    cot_near, near_raw = lax.optimization_barrier((cot_near, near_raw))
-    cot_pieces = end_gather(*cot_near)
+    near_turned, near_raw, near_squares = project_near(idx, both_cores(tok_near), gain, wq, wk, wv)
+    tok_far, cot_near, near_raw = lax.optimization_barrier((tok_far, cot_near, near_raw))
+    cot_far = gather_far(cot_near)
     far_turned, raw, inverse, q, k, k_turned, v, shares, attended = attend(
-        idx, tok_pieces[1], gain, wq, wk, wv, near_raw, near_squares, cosine, sine, where_col, where_row
+        idx, both_cores(tok_far), gain, wq, wk, wv, near_raw, near_squares, cosine, sine, where_col, where_row
     )
 
     scale = (rows * dp) ** (-0.5)
-    cot_nears, shares = lax.optimization_barrier((cot_pieces[0], shares))
-    near = back_near(idx, cot_nears, wo)
+    cot_near, shares = lax.optimization_barrier((both_cores(cot_near), shares))
+    near = back_near(idx, cot_near, wo)
+    cot_far, near = lax.optimization_barrier((cot_far, near))
     rotary = jnp.stack([cosine, sine])
     grad, dots, *grads = back(
-        idx, cot_pieces[1], wo, near, far_turned, near_turned, q, k, k_turned, v, shares,
+        idx, both_cores(cot_far), wo, near, far_turned, near_turned, q, k, k_turned, v, shares,
         raw, inverse, rotary, scale,
     )
     grad_query, grad_key, grad_value = lax.psum(tuple(grads), ("x", "z"))
-
     after = swap(dots)
     idx_mine, idx_other = around * cores + core, around * cores + (1 - core)
     out_sum = sum_pieces(

time: 272 us -> 249 us (0.915)
  waiting for transfers between devices: 90.8 us -> 74.5 us
  starting transfers between devices: 53.3 us -> 49.3 us
  local copies, waits for them, and re-layouts: 19.3 us -> 16.4 us
    ppermute x16, waiting for transfers between devices: 45.7 us -> 29.7 us  [shift(): lax.ppermute(array, axis, [(i, (i + step) % size) for i in range(size)])]
    unnamed x66 -> x52, local copies, waits for them, and re-layouts: 12 us -> 9.64 us
  transfers between devices with their start and end apart: 33 -> 33, of which waited for: 16 -> 13; matrix products, arithmetic and copies ran while one was open for 7% -> 7% of each run, Pallas kernels for 18% -> 20%
where the time goes in v3:
time: 249 us; the launch traced here: 248 us
  waiting for transfers between devices  74.5 us (30%)
  Pallas kernels  64.8 us (26%)
  starting transfers between devices  49.3 us (20%)
  blocking collectives  17.3 us (7%)
  local copies, waits for them, and re-layouts  16.4 us (7%)
  between operations  14.6 us (6%)
  other arithmetic  11 us (4%)
    ppermute x16, waiting for transfers between devices, shift(): lax.ppermute(array, axis, [(i, (i + step) % size) for i in range(size)])  29.7 us
    psum x1, waiting for transfers between devices, per_device(): grad_query, grad_key, grad_value = lax.psum(tuple(grads), ('x', 'z'))  26.3 us
    ppermute x16, starting transfers between devices, shift(): lax.ppermute(array, axis, [(i, (i + step) % size) for i in range(size)])  20.4 us
    all_to_all x3, waiting for transfers between devices, exchange(): lax.all_to_all(panels, ('x', 'z'), split_axis=0, concat_axis=0, tiled=True)  17.6 us
    all_to_all x3, starting transfers between devices, exchange(): lax.all_to_all(panels, ('x', 'z'), split_axis=0, concat_axis=0, tiled=True)  17.6 us
    all_to_all x1, blocking collectives, exchange(): lax.all_to_all(panels, ('x', 'z'), split_axis=0, concat_axis=0, tiled=True)  17.3 us
    pallas_call x2, Pallas kernels, input_terms(): pl.pallas_call(input_term_kernel, grid_spec=grid_spec, out_shape=jax.Shap...  13.1 us
    pallas_call x1, Pallas kernels, back(): pl.pallas_call(functools.partial(back_kernel, scale=scale), grid=(1,), in...  13.1 us
  transfers between devices with their start and end apart: 33, of which 13 were waited for; matrix products, arithmetic and copies ran while one was open for 7% of the time, Pallas kernels for 20%

profile of v3, /device:TPU:1, one launch (start us, length us, event | category | flops | bytes accessed | tf_op | source)
XLA Modules:
  0.0 247.9 jit_solution(5664900765226400238)
XLA Ops:
  7.2 1.9 place.1
  9.1 8.6 %all-to-all-start = ((bf16[16,32,512]{2,1,0:T(8,128)(2,1)}), bf16[16,32,512]{2,1,0:T(8,128)(2,1)S(1)}, u32[]{:S(2)}, u32[]{:S(2)}) async-start(bf16[16,32,512]{2,1,0:T(8,128)(2,1)} %place.1), calls=%async_computation | async-start | bytes 1048576 | tf_op jit(solution)/shard_map/all_to_all | solution.py:557
  17.7 0.9 reshape_reshape.4.docs_ref
  18.6 2.2 place_meta.1
  20.8 7.1 %all-to-all-done = bf16[16,32,512]{2,1,0:T(8,128)(2,1)S(1)} async-done(((bf16[16,32,512]{2,1,0:T(8,128)(2,1)}), bf16[16,32,512]{2,1,0:T(8,128)(2,1)S(1)}, u32[]{:S(2)}, u32[]{:S(2)}) %all-to-all-start) | async-done | bytes 524320 | tf_op jit(solution)/shard_map/all_to_all | solution.py:557
  28.0 3.6 %all-to-all-start.1 = ((bf16[16,32,640]{2,1,0:T(8,128)(2,1)}), bf16[16,32,640]{2,1,0:T(8,128)(2,1)S(1)}, u32[]{:S(2)}, u32[]{:S(2)}) async-start(bf16[16,32,640]{2,1,0:T(8,128)(2,1)} %place_meta.1), calls=%async_computation.1 | async-start | bytes 1310720 | tf_op jit(solution)/shard_map/all_to_all | solution.py:557
  31.6 1.4 collective-permute-start
  33.0 0.6 reshape.162.refs_7_.refs_5_
  33.6 1.5 collective-permute-start.2
  35.1 0.5 broadcast_add_fusion.1
  35.6 0.6 pad_add_fusion.1.refs_0_
  36.2 2.6 %collective-permute-start.6 = (bf16[512,512]{1,0:T(8,128)(2,1)S(1)}, bf16[512,512]{1,0:T(8,128)(2,1)}, u32[]{:S(2)}, u32[]{:S(2)}) collective-permute-start(bf16[512,512]{1,0:T(8,128)(2,1)S(1)} %bitcast.75), channel_id=1, source_target_pairs={{0,1},{1,0},{2,3},{3,2},{4,5},{5,4},{6,7},{7,6},{8,9},{9,8},{10,11... | collective-permute-start | bytes 1572872 | tf_op jit(solution)/shard_map/ppermute | solution.py:527
  38.8 2.7 %all-to-all-done.1 = bf16[16,32,640]{2,1,0:T(8,128)(2,1)S(1)} async-done(((bf16[16,32,640]{2,1,0:T(8,128)(2,1)}), bf16[16,32,640]{2,1,0:T(8,128)(2,1)S(1)}, u32[]{:S(2)}, u32[]{:S(2)}) %all-to-all-start.1) | async-done | bytes 655392 | tf_op jit(solution)/shard_map/all_to_all | solution.py:557
  41.6 1.4 collective-permute-start.4
  43.0 1.5 collective-permute-start.5
  44.5 4.4 %collective-permute-start.7 = (bf16[512,512]{1,0:T(8,128)(2,1)S(1)}, bf16[512,512]{1,0:T(8,128)(2,1)}, u32[]{:S(2)}, u32[]{:S(2)}) collective-permute-start(bf16[512,512]{1,0:T(8,128)(2,1)S(1)} %collective-permute-done.refs_2_), channel_id=1, source_target_pairs={{0,1},{1,0},{2,3},{3,2},{4,5},{5,4},{6,7},{7,6},{8,9},{9,8},{10,11... | collective-permute-start | bytes 1572872 | tf_op jit(solution)/shard_map/ppermute | solution.py:527
  49.0 0.9 collective-permute-start.8
  50.5 1.0 slice.113
  51.5 1.4 collective-permute-start.1
  52.9 1.4 collective-permute-start.3
  54.3 1.0 fusion.12
  55.3 8.9 %project_near.1 = (bf16[3,1024,512]{2,1,0:T(8,128)(2,1)}, f32[512,768]{1,0:T(8,128)}, f32[512,128]{1,0:T(8,128)}) custom-call(s32[13]{0:T(128)} %pad_add_fusion.1.refs_0_, bf16[512,512]{1,0:T(8,128)(2,1)} %bitcast.76, bf16[512,512]{1,0:T(8,128)(2,1)} %copy-done.7, bf16[512,512]{1,0:T(8,128)(2,1)} %collective-permute-done.2.refs_3_, ...), custom_call_target="tpu_custom_call" | custom-call | flops 2415919104 | bytes 11010048 | tf_op jit(solution)/shard_map/project_near/pallas_call | solution.py:183
  64.3 0.6 collective-permute-start.12
  66.0 0.6 pad_add_fusion
  66.6 0.9 copy.21.refs_13_
  67.4 0.8 fusion.24
  68.3 0.8 pad_maximum_fusion.6.refs_12_
  69.2 2.7 %collective-permute-start.10 = (bf16[256,512]{1,0:T(8,128)(2,1)S(1)}, bf16[256,512]{1,0:T(8,128)(2,1)S(1)}, u32[]{:S(2)}, u32[]{:S(2)}) collective-permute-start(bf16[256,512]{1,0:T(8,128)(2,1)S(1)} %slice.85), channel_id=1, source_target_pairs={{0,6},{2,0},{4,2},{6,4},{1,7},{3,1},{5,3},{7,5},{8,14},{10,8},{12,... | collective-permute-start | bytes 786440 | tf_op jit(solution)/shard_map/ppermute | solution.py:523
  71.9 8.5 %attend.1 = (bf16[1,1024,512]{2,1,0:T(8,128)(2,1)}, f32[512,768]{1,0:T(8,128)}, f32[512,128]{1,0:T(8,128)}, bf16[512,512]{1,0:T(8,128)(2,1)}, bf16[512,128]{1,0:...) custom-call(s32[13]{0:T(128)} %pad_add_fusion.1.refs_0_, ...), custom_call_target="tpu_custom_call" | custom-call | flops 1342177280 | bytes 3670016 | tf_op jit(solution)/shard_map/attend/pallas_call | solution.py:266
  80.5 0.8 copy-done.10
  81.3 6.0 %back_near.1.refs_6_ = f32[512,512]{1,0:T(8,128)} custom-call(s32[13]{0:T(128)} %pad_add_fusion.1.refs_0_, bf16[512,512]{1,0:T(8,128)(2,1)} %bitcast.80, bf16[512,512]{1,0:T(8,128)(2,1)} %copy-done.5, bf16[512,512]{1,0:T(8,128)(2,1)} %copy-done.6, bf16[512,512]{1,0:T(8,128)(2,1)} %collective-permute-done.11.refs_4_, bf16[512,512]{1,0:T(8,128)(2,1)} %copy-done.10, ...), custom_call_target="tpu_custom_call" | custom-call | flops 1610612736 | bytes 6291456 | tf_op jit(solution)/shard_map/back_near/pallas_call | solution.py:305
  88.0 0.8 pad_maximum_fusion.2.refs_16_
  89.3 0.5 copy-done.20
  90.0 13.1 %back.1 = (bf16[512,768]{1,0:T(8,128)(2,1)}, f32[8,512]{1,0:T(8,128)}, bf16[4096,512]{1,0:T(8,128)(2,1)}, bf16[4096,128]{1,0:T(8,128)(2,1)}, bf16[4096,128]{1,0:T(8,128)(2,1)}) custom-call(s32[13]{0:T(128)} %pad_add_fusion.1.refs_0_, bf16[256,512]{1,0:T(8,128)(2,1)} %collective-permute-done.9.refs_1_, bf16[256,512]{1,0:T(8,128)(2,1)} %copy-done.19, ...), custom_call_target="tpu_custom_call" | custom-call | flops 4831838208 | bytes 8388608 | tf_op jit(solution)/shard_map/back/pallas_call | solution.py:425
  103.1 0.7 collective-permute-start.18
  104.8 0.6 copy-done.22
  105.4 5.4 %out_terms.3 = bf16[4,512,512]{2,1,0:T(8,128)(2,1)} custom-call(s32[4]{0:T(128)} %broadcast_add_fusion.idx_ref, f32[8,512]{1,0:T(8,128)} %copy-done.22, bf16[512,512]{1,0:T(8,128)(2,1)} %get-tuple-element.66.attended_ref, bf16[512,4096]{1,0:T(8,128)(2,1)} %wo_ref.3), custom_call_target="tpu_custom_call" | custom-call | flops 21474836480 | bytes 83886080 | tf_op jit(solution)/shard_map/out_terms/pallas_call | solution.py:469
  111.2 6.6 %input_terms.3 = bf16[4,528,512]{2,1,0:T(8,128)(2,1)} custom-call(s32[4]{0:T(128)} %broadcast_add_fusion.idx_ref, f32[8,512]{1,0:T(8,128)} %copy-done.22, bf16[512,768]{1,0:T(8,128)(2,1)} %get-tuple-element.67.grad_ref, f32[8,512]{1,0:T(8,128)} %get-tuple-element.65.dots_ref, bf16[4096,512]{1,0:T(8,128)(2,1)} %wq_ref.3, bf16[4096,128]{1,0:T(8,128)(2,1)} %wk_ref.3, ...), custom_call_target="tpu_custom_call" | custom-call | flops 32212254720 | bytes 104857600 | tf_op jit(solution)/shard_map/input_terms/pallas_call | solution.py:511
  118.1 6.5 %input_terms.2 = bf16[4,528,512]{2,1,0:T(8,128)(2,1)} custom-call(s32[4]{0:T(128)} %get-tuple-element.74.idx_ref, f32[8,512]{1,0:T(8,128)} %copy-done.22, bf16[512,768]{1,0:T(8,128)(2,1)} %get-tuple-element.67.grad_ref, f32[8,512]{1,0:T(8,128)} %get-tuple-element.65.dots_ref, bf16[4096,512]{1,0:T(8,128)(2,1)} %wq_ref.3, bf16[4096,128]{1,0:T(8,128)(2,1)} %wk_ref.3, ...), custom_call_target="tpu_custom_call" | custom-call | flops 32212254720 | bytes 104857600 | tf_op jit(solution)/shard_map/input_terms/pallas_call | solution.py:511
  124.6 5.5 %out_terms.2 = bf16[4,512,512]{2,1,0:T(8,128)(2,1)} custom-call(s32[4]{0:T(128)} %get-tuple-element.74.idx_ref, f32[8,512]{1,0:T(8,128)} %copy-done.22, bf16[512,512]{1,0:T(8,128)(2,1)} %get-tuple-element.66.attended_ref, bf16[512,4096]{1,0:T(8,128)(2,1)} %wo_ref.3), custom_call_target="tpu_custom_call" | custom-call | flops 21474836480 | bytes 83886080 | tf_op jit(solution)/shard_map/out_terms/pallas_call | solution.py:469
  130.0 2.4 add_convert_fusion.1
  132.5 0.6 add_convert_fusion
  133.7 1.1 collective-permute-start.20
  134.8 1.6 collective-permute-start.22
  136.5 1.4 collective-permute-start.27
  137.9 4.7 %collective-permute-done.25 = bf16[256,512]{1,0:T(8,128)(2,1)S(1)} collective-permute-done((bf16[256,512]{1,0:T(8,128)(2,1)S(1)}, bf16[256,512]{1,0:T(8,128)(2,1)S(1)}, u32[]{:S(2)}, u32[]{:S(2)}) %collective-permute-start.25) | collective-permute-done | bytes 262176 | tf_op jit(solution)/shard_map/ppermute | solution.py:523
  142.8 6.2 %collective-permute-done.27 = bf16[272,512]{1,0:T(8,128)(2,1)S(1)} collective-permute-done((bf16[272,512]{1,0:T(8,128)(2,1)S(1)}, bf16[272,512]{1,0:T(8,128)(2,1)S(1)}, u32[]{:S(2)}, u32[]{:S(2)}) %collective-permute-start.27) | collective-permute-done | bytes 278560 | tf_op jit(solution)/shard_map/ppermute | solution.py:523
  149.2 1.5 collective-permute-start.28
  151.0 2.8 %collective-permute-start.23 = (bf16[512,512]{1,0:T(8,128)(2,1)S(1)}, bf16[512,512]{1,0:T(8,128)(2,1)S(1)}, u32[]{:S(2)}, u32[]{:S(2)}) collective-permute-start(bf16[512,512]{1,0:T(8,128)(2,1)S(1)} %pad_maximum_fusion.4), channel_id=1, source_target_pairs={{0,6},{2,0},{4,2},{6,4},{1,7},{3,1},{5,3},{7,5},{8,14},{10,8},{12,... | collective-permute-start | bytes 1572872 | tf_op jit(solution)/shard_map/ppermute | solution.py:523
  153.9 5.8 %collective-permute-done.26 = bf16[528,512]{1,0:T(8,128)(2,1)S(1)} collective-permute-done((bf16[528,512]{1,0:T(8,128)(2,1)S(1)}, bf16[528,512]{1,0:T(8,128)(2,1)S(1)}, u32[]{:S(2)}, u32[]{:S(2)}) %collective-permute-start.26) | collective-permute-done | bytes 540704 | tf_op jit(solution)/shard_map/ppermute | solution.py:523
  159.7 2.0 collective-permute-done.28
  162.0 9.0 %collective-permute-done.21 = bf16[512,512]{1,0:T(8,128)(2,1)S(1)} collective-permute-done((bf16[512,512]{1,0:T(8,128)(2,1)S(1)}, bf16[512,512]{1,0:T(8,128)(2,1)S(1)}, u32[]{:S(2)}, u32[]{:S(2)}) %collective-permute-start.21) | collective-permute-done | bytes 524320 | tf_op jit(solution)/shard_map/ppermute | solution.py:523
  171.0 1.9 collective-permute-done.23
  172.9 1.4 fusion.6
  174.3 17.3 %all_to_all.20 = bf16[16,32,512]{2,1,0:T(8,128)(2,1)S(1)} all-to-all(bf16[16,32,512]{2,1,0:T(8,128)(2,1)S(1)} %bitcast.81), channel_id=1, replica_groups=mesh['x'=4,'z'=4,'y'=4,'core'=2] {'x','z'}, dimensions={0} | all-to-all | bytes 1048576 | tf_op jit(solution)/shard_map/all_to_all | solution.py:557
  191.6 5.4 %all-to-all-start.3 = ((bf16[16,32,512]{2,1,0:T(8,128)(2,1)}), bf16[16,32,512]{2,1,0:T(8,128)(2,1)S(1)}, u32[]{:S(2)}, u32[]{:S(2)}) async-start(bf16[16,32,512]{2,1,0:T(8,128)(2,1)} %bitcast.29), calls=%async_computation.3 | async-start | bytes 1048576 | tf_op jit(solution)/shard_map/all_to_all | solution.py:557
  197.0 1.4 gather_fusion
  198.4 7.8 %all-to-all-done.3 = bf16[16,32,512]{2,1,0:T(8,128)(2,1)S(1)} async-done(((bf16[16,32,512]{2,1,0:T(8,128)(2,1)}), bf16[16,32,512]{2,1,0:T(8,128)(2,1)S(1)}, u32[]{:S(2)}, u32[]{:S(2)}) %all-to-all-start.3) | async-done | bytes 524320 | tf_op jit(solution)/shard_map/all_to_all | solution.py:557
  206.2 1.4 gather_fusion.1
  207.6 26.3 %all-reduce.3.cloned.1.call-done = (bf16[4096,512]{1,0:T(8,128)(2,1)}, bf16[4096,128]{1,0:T(8,128)(2,1)}, bf16[4096,128]{1,0:T(8,128)(2,1)}) async-done(((bf16[4096,512]{1,0:T(8,128)(2,1)}, bf16[4096,128]{1,0:T(8,128)(2,1)}, bf16[4096,128]{1,0:T(8,128)(2,1)}), (bf16[4096,512]{1,0:T(8,128)(2,1)}, bf16[4096,128]{1,0:T(8,128)(2,1)}, bf16[4096,128]{1,0:T(8,128)(2,1)})) %all-reduce.3.cloned.1.call-update) | async-done | bytes 6291472 | tf_op jit(solution)/shard_map/psum | solution.py:615
  233.9 4.6 %copy.28 = bf16[4096,512]{1,0:T(8,128)(2,1)} copy(bf16[4096,512]{1,0:T(8,128)(2,1)} %get-tuple-element.104) | data formatting | bytes 8388608
  238.5 1.0 copy.29
  239.4 0.6 copy-done.8
  240.1 1.0 copy.30
  (110 shorter events, 6.5 us)
Async XLA Ops:
  7.2 10.5 %copy-start.14 = (s32[512]{0:T(512)S(1)}, s32[512]{0:T(512)}, u32[]{:S(2)}) copy-start(s32[512]{0:T(512)} %param.13) | copy-start | bytes 6148
  9.1 23.9 %copy-start.13 = (f32[4096]{0:T(1024)S(1)}, f32[4096]{0:T(1024)}, u32[]{:S(2)}) copy-start(f32[4096]{0:T(1024)} %param.12) | copy-start | bytes 49156
  9.1 26.0 %copy-start.18 = (s32[4]{0:T(128)S(1)}, s32[4]{0:T(128)}, u32[]{:S(2)}) copy-start(s32[4]{0:T(128)} %constant.99.clone) | copy-start | bytes 52
  9.1 18.9 %all-to-all-start = ((bf16[16,32,512]{2,1,0:T(8,128)(2,1)}), bf16[16,32,512]{2,1,0:T(8,128)(2,1)S(1)}, u32[]{:S(2)}, u32[]{:S(2)}) async-start(bf16[16,32,512]{2,1,0:T(8,128)(2,1)} %place.1), calls=%async_computation | async-start | bytes 1048576 | tf_op jit(solution)/shard_map/all_to_all | solution.py:557
  28.0 22.1 %copy-start = (bf16[16,32,512]{2,1,0:T(8,128)(2,1)}, bf16[16,32,512]{2,1,0:T(8,128)(2,1)S(1)}, u32[]{:S(2)}) copy-start(bf16[16,32,512]{2,1,0:T(8,128)(2,1)S(1)} %all-to-all-done) | copy-start | bytes 1572868
  28.0 13.5 %all-to-all-start.1 = ((bf16[16,32,640]{2,1,0:T(8,128)(2,1)}), bf16[16,32,640]{2,1,0:T(8,128)(2,1)S(1)}, u32[]{:S(2)}, u32[]{:S(2)}) async-start(bf16[16,32,640]{2,1,0:T(8,128)(2,1)} %place_meta.1), calls=%async_computation.1 | async-start | bytes 1310720 | tf_op jit(solution)/shard_map/all_to_all | solution.py:557
  31.6 202.3 %all-reduce.3.cloned.1.call-start = ((), (), s32[]{:S(2)}) async-start(), calls=%async_computation.4 | async-start | bytes 12582912 | tf_op jit(solution)/shard_map/psum | solution.py:615
  31.6 12.9 %collective-permute-start = (bf16[512,512]{1,0:T(8,128)(2,1)S(1)}, bf16[512,512]{1,0:T(8,128)(2,1)S(1)}, u32[]{:S(2)}, u32[]{:S(2)}) collective-permute-start(bf16[512,512]{1,0:T(8,128)(2,1)S(1)} %bitcast.73), channel_id=1, source_target_pairs={{0,2},{2,4},{4,6},{6,0},{1,3},{3,5},{5,7},{7,1},{8,10},{10,12},{12... | collective-permute-start | bytes 1572872 | tf_op jit(solution)/shard_map/ppermute | solution.py:523
  33.6 15.3 %collective-permute-start.2 = (bf16[512,512]{1,0:T(8,128)(2,1)S(1)}, bf16[512,512]{1,0:T(8,128)(2,1)}, u32[]{:S(2)}, u32[]{:S(2)}) collective-permute-start(bf16[512,512]{1,0:T(8,128)(2,1)S(1)} %bitcast.74), channel_id=1, source_target_pairs={{0,6},{2,0},{4,2},{6,4},{1,7},{3,1},{5,3},{7,5},{8,14},{10,8},{12,... | collective-permute-start | bytes 1572872 | tf_op jit(solution)/shard_map/ppermute | solution.py:523
  35.6 13.3 %copy-start.16 = (s32[4]{0:T(128)}, s32[4]{0:T(128)S(1)}, u32[]{:S(2)}) copy-start(s32[4]{0:T(128)S(1)} %get-tuple-element.75) | copy-start | bytes 52
  36.2 15.3 %collective-permute-start.6 = (bf16[512,512]{1,0:T(8,128)(2,1)S(1)}, bf16[512,512]{1,0:T(8,128)(2,1)}, u32[]{:S(2)}, u32[]{:S(2)}) collective-permute-start(bf16[512,512]{1,0:T(8,128)(2,1)S(1)} %bitcast.75), channel_id=1, source_target_pairs={{0,1},{1,0},{2,3},{3,2},{4,5},{5,4},{6,7},{7,6},{8,9},{9,8},{10,11... | collective-permute-start | bytes 1572872 | tf_op jit(solution)/shard_map/ppermute | solution.py:527
  41.6 23.5 %copy-start.2 = (bf16[16,32,512]{2,1,0:T(8,128)(2,1)}, bf16[16,32,512]{2,1,0:T(8,128)(2,1)S(1)}, u32[]{:S(2)}) copy-start(bf16[16,32,512]{2,1,0:T(8,128)(2,1)S(1)} %slice.114) | copy-start | bytes 1572868
  41.6 22.7 %collective-permute-start.4 = (bf16[512,512]{1,0:T(8,128)(2,1)S(1)}, bf16[512,512]{1,0:T(8,128)(2,1)S(1)}, u32[]{:S(2)}, u32[]{:S(2)}) collective-permute-start(bf16[512,512]{1,0:T(8,128)(2,1)S(1)} %bitcast.77), channel_id=1, source_target_pairs={{0,2},{2,4},{4,6},{6,0},{1,3},{3,5},{5,7},{7,1},{8,10},{10,12},{12... | collective-permute-start | bytes 1572872 | tf_op jit(solution)/shard_map/ppermute | solution.py:523
  43.0 21.3 %collective-permute-start.5 = (bf16[512,512]{1,0:T(8,128)(2,1)S(1)}, bf16[512,512]{1,0:T(8,128)(2,1)S(1)}, u32[]{:S(2)}, u32[]{:S(2)}) collective-permute-start(bf16[512,512]{1,0:T(8,128)(2,1)S(1)} %bitcast.78), channel_id=1, source_target_pairs={{0,6},{2,0},{4,2},{6,4},{1,7},{3,1},{5,3},{7,5},{8,14},{10,8},{12,... | collective-permute-start | bytes 1572872 | tf_op jit(solution)/shard_map/ppermute | solution.py:523
  44.5 10.8 %copy-start.7 = (bf16[512,512]{1,0:T(8,128)(2,1)}, bf16[512,512]{1,0:T(8,128)(2,1)S(1)}, u32[]{:S(2)}) copy-start(bf16[512,512]{1,0:T(8,128)(2,1)S(1)} %collective-permute-done.refs_2_) | copy-start | bytes 1572868
  44.5 8.3 %collective-permute-start.7 = (bf16[512,512]{1,0:T(8,128)(2,1)S(1)}, bf16[512,512]{1,0:T(8,128)(2,1)}, u32[]{:S(2)}, u32[]{:S(2)}) collective-permute-start(bf16[512,512]{1,0:T(8,128)(2,1)S(1)} %collective-permute-done.refs_2_), channel_id=1, source_target_pairs={{0,1},{1,0},{2,3},{3,2},{4,5},{5,4},{6,7},{7,6},{8,9},{9,8},{10,11... | collective-permute-start | bytes 1572872 | tf_op jit(solution)/shard_map/ppermute | solution.py:527
  49.0 6.3 %collective-permute-start.8 = (bf16[512,512]{1,0:T(8,128)(2,1)}, bf16[512,512]{1,0:T(8,128)(2,1)}, u32[]{:S(2)}, u32[]{:S(2)}) collective-permute-start(bf16[512,512]{1,0:T(8,128)(2,1)} %collective-permute-done.2.refs_3_), channel_id=1, source_target_pairs={{0,1},{1,0},{2,3},{3,2},{4,5},{5,4},{6,7},{7,6},{8,9},{9,8},{10,11... | collective-permute-start | bytes 1572872 | tf_op jit(solution)/shard_map/ppermute | solution.py:527
  51.5 12.8 %collective-permute-start.1 = (bf16[256,512]{1,0:T(8,128)(2,1)S(1)}, bf16[256,512]{1,0:T(8,128)(2,1)S(1)}, u32[]{:S(2)}, u32[]{:S(2)}) collective-permute-start(bf16[256,512]{1,0:T(8,128)(2,1)S(1)} %slice.112), channel_id=1, source_target_pairs={{0,2},{2,4},{4,6},{6,0},{1,3},{3,5},{5,7},{7,1},{8,10},{10,12},{12... | collective-permute-start | bytes 786440 | tf_op jit(solution)/shard_map/ppermute | solution.py:523
  52.9 11.5 %collective-permute-start.3 = (bf16[256,512]{1,0:T(8,128)(2,1)S(1)}, bf16[256,512]{1,0:T(8,128)(2,1)}, u32[]{:S(2)}, u32[]{:S(2)}) collective-permute-start(bf16[256,512]{1,0:T(8,128)(2,1)S(1)} %slice.113), channel_id=1, source_target_pairs={{0,6},{2,0},{4,2},{6,4},{1,7},{3,1},{5,3},{7,5},{8,14},{10,8},{12,... | collective-permute-start | bytes 786440 | tf_op jit(solution)/shard_map/ppermute | solution.py:523
  64.3 16.2 %copy-start.5 = (bf16[512,512]{1,0:T(8,128)(2,1)}, bf16[512,512]{1,0:T(8,128)(2,1)S(1)}, u32[]{:S(2)}) copy-start(bf16[512,512]{1,0:T(8,128)(2,1)S(1)} %collective-permute-done.4.refs_2_) | copy-start | bytes 1572868
  64.3 16.2 %copy-start.6 = (bf16[512,512]{1,0:T(8,128)(2,1)}, bf16[512,512]{1,0:T(8,128)(2,1)S(1)}, u32[]{:S(2)}) copy-start(bf16[512,512]{1,0:T(8,128)(2,1)S(1)} %collective-permute-done.5.refs_3_) | copy-start | bytes 1572868
  64.3 7.6 %copy-start.11 = (bf16[256,512]{1,0:T(8,128)(2,1)}, bf16[256,512]{1,0:T(8,128)(2,1)S(1)}, u32[]{:S(2)}) copy-start(bf16[256,512]{1,0:T(8,128)(2,1)S(1)} %collective-permute-done.1.refs_1_) | copy-start | bytes 786436
  64.3 16.2 %collective-permute-start.12 = (bf16[512,512]{1,0:T(8,128)(2,1)S(1)}, bf16[512,512]{1,0:T(8,128)(2,1)S(1)}, u32[]{:S(2)}, u32[]{:S(2)}) collective-permute-start(bf16[512,512]{1,0:T(8,128)(2,1)S(1)} %collective-permute-done.4.refs_2_), channel_id=1, source_target_pairs={{0,1},{1,0},{2,3},{3,2},{4,5},{5,4},{6,7},{7,6},{8,9},{9,8},{10,11... | collective-permute-start | bytes 1572872 | tf_op jit(solution)/shard_map/ppermute | solution.py:527
  64.9 15.6 %collective-permute-start.13 = (bf16[512,512]{1,0:T(8,128)(2,1)S(1)}, bf16[512,512]{1,0:T(8,128)(2,1)}, u32[]{:S(2)}, u32[]{:S(2)}) collective-permute-start(bf16[512,512]{1,0:T(8,128)(2,1)S(1)} %collective-permute-done.5.refs_3_), channel_id=1, source_target_pairs={{0,1},{1,0},{2,3},{3,2},{4,5},{5,4},{6,7},{7,6},{8,9},{9,8},{10,11... | collective-permute-start | bytes 1572872 | tf_op jit(solution)/shard_map/ppermute | solution.py:527
  65.0 15.5 %collective-permute-start.11 = (bf16[512,512]{1,0:T(8,128)(2,1)S(1)}, bf16[512,512]{1,0:T(8,128)(2,1)}, u32[]{:S(2)}, u32[]{:S(2)}) collective-permute-start(bf16[512,512]{1,0:T(8,128)(2,1)S(1)} %bitcast.79), channel_id=1, source_target_pairs={{0,1},{1,0},{2,3},{3,2},{4,5},{5,4},{6,7},{7,6},{8,9},{9,8},{10,11... | collective-permute-start | bytes 1572872 | tf_op jit(solution)/shard_map/ppermute | solution.py:527
  65.5 3.7 %collective-permute-start.14 = (bf16[256,512]{1,0:T(8,128)(2,1)S(1)}, bf16[256,512]{1,0:T(8,128)(2,1)}, u32[]{:S(2)}, u32[]{:S(2)}) collective-permute-start(bf16[256,512]{1,0:T(8,128)(2,1)S(1)} %collective-permute-done.1.refs_1_), channel_id=1, source_target_pairs={{0,1},{1,0},{2,3},{3,2},{4,5},{5,4},{6,7},{7,6},{8,9},{9,8},{10,11... | collective-permute-start | bytes 786440 | tf_op jit(solution)/shard_map/ppermute | solution.py:527
  65.6 6.3 %collective-permute-start.15 = (bf16[256,512]{1,0:T(8,128)(2,1)}, bf16[256,512]{1,0:T(8,128)(2,1)}, u32[]{:S(2)}, u32[]{:S(2)}) collective-permute-start(bf16[256,512]{1,0:T(8,128)(2,1)} %collective-permute-done.3.refs_2_), channel_id=1, source_target_pairs={{0,1},{1,0},{2,3},{3,2},{4,5},{5,4},{6,7},{7,6},{8,9},{9,8},{10,11... | collective-permute-start | bytes 786440 | tf_op jit(solution)/shard_map/ppermute | solution.py:527
  69.2 18.1 %collective-permute-start.10 = (bf16[256,512]{1,0:T(8,128)(2,1)S(1)}, bf16[256,512]{1,0:T(8,128)(2,1)S(1)}, u32[]{:S(2)}, u32[]{:S(2)}) collective-permute-start(bf16[256,512]{1,0:T(8,128)(2,1)S(1)} %slice.85), channel_id=1, source_target_pairs={{0,6},{2,0},{4,2},{6,4},{1,7},{3,1},{5,3},{7,5},{8,14},{10,8},{12,... | collective-permute-start | bytes 786440 | tf_op jit(solution)/shard_map/ppermute | solution.py:523
  71.9 15.4 %collective-permute-start.9 = (bf16[256,512]{1,0:T(8,128)(2,1)S(1)}, bf16[256,512]{1,0:T(8,128)(2,1)}, u32[]{:S(2)}, u32[]{:S(2)}) collective-permute-start(bf16[256,512]{1,0:T(8,128)(2,1)S(1)} %slice.84), channel_id=1, source_target_pairs={{0,2},{2,4},{4,6},{6,0},{1,3},{3,5},{5,7},{7,1},{8,10},{10,12},{12... | collective-permute-start | bytes 786440 | tf_op jit(solution)/shard_map/ppermute | solution.py:523
  80.5 0.8 copy-start.10
  87.3 2.0 copy-start.19
  87.3 1.8 collective-permute-start.16
  87.7 1.6 collective-permute-start.17
  89.1 0.7 copy-start.20
  89.3 0.7 copy-start.21
  90.0 13.8 %copy-start.17 = (s32[4]{0:T(128)S(1)}, s32[4]{0:T(128)}, u32[]{:S(2)}) copy-start(s32[4]{0:T(128)} %copy-done.16) | copy-start | bytes 52
  103.1 1.7 collective-permute-start.18
  104.8 0.6 copy-start.22
  110.9 19.1 %collective-permute-start.19 = (bf16[4,512,512]{2,1,0:T(8,128)(2,1)}, bf16[4,512,512]{2,1,0:T(8,128)(2,1)S(1)}, u32[]{:S(2)}, u32[]{:S(2)}) collective-permute-start(bf16[4,512,512]{2,1,0:T(8,128)(2,1)} %out_terms.3), channel_id=1, source_target_pairs={{0,1},{1,0},{2,3},{3,2},{4,5},{5,4},{6,7},{7,6},{8,9},{9,8},{10,11... | collective-permute-start | bytes 6291464 | tf_op jit(solution)/shard_map/ppermute | solution.py:527
  117.8 14.6 %collective-permute-start.24 = (bf16[4,528,512]{2,1,0:T(8,128)(2,1)}, bf16[4,528,512]{2,1,0:T(8,128)(2,1)S(1)}, u32[]{:S(2)}, u32[]{:S(2)}) collective-permute-start(bf16[4,528,512]{2,1,0:T(8,128)(2,1)} %input_terms.3), channel_id=1, source_target_pairs={{0,1},{1,0},{2,3},{3,2},{4,5},{5,4},{6,7},{7,6},{8,9},{9,8},{10,11... | collective-permute-start | bytes 6488072 | tf_op jit(solution)/shard_map/ppermute | solution.py:527
  130.0 2.4 copy-start.4
  133.1 9.5 %collective-permute-start.25 = (bf16[256,512]{1,0:T(8,128)(2,1)S(1)}, bf16[256,512]{1,0:T(8,128)(2,1)S(1)}, u32[]{:S(2)}, u32[]{:S(2)}) collective-permute-start(bf16[256,512]{1,0:T(8,128)(2,1)S(1)} %get-tuple-element.76), channel_id=1, source_target_pairs={{0,2},{2,4},{4,6},{6,0},{1,3},{3,5},{5,7},{7,1},{8,10},{10,12},{12... | collective-permute-start | bytes 786440 | tf_op jit(solution)/shard_map/ppermute | solution.py:523
  133.7 17.0 %collective-permute-start.20 = (bf16[256,512]{1,0:T(8,128)(2,1)S(1)}, bf16[256,512]{1,0:T(8,128)(2,1)S(1)}, u32[]{:S(2)}, u32[]{:S(2)}) collective-permute-start(bf16[256,512]{1,0:T(8,128)(2,1)S(1)} %get-tuple-element.82), channel_id=1, source_target_pairs={{0,2},{2,4},{4,6},{6,0},{1,3},{3,5},{5,7},{7,1},{8,10},{10,12},{12... | collective-permute-start | bytes 786440 | tf_op jit(solution)/shard_map/ppermute | solution.py:523
  134.8 15.9 %collective-permute-start.22 = (bf16[256,512]{1,0:T(8,128)(2,1)S(1)}, bf16[256,512]{1,0:T(8,128)(2,1)S(1)}, u32[]{:S(2)}, u32[]{:S(2)}) collective-permute-start(bf16[256,512]{1,0:T(8,128)(2,1)S(1)} %get-tuple-element.83), channel_id=1, source_target_pairs={{0,6},{2,0},{4,2},{6,4},{1,7},{3,1},{5,3},{7,5},{8,14},{10,8},{12,... | collective-permute-start | bytes 786440 | tf_op jit(solution)/shard_map/ppermute | solution.py:523
  136.5 12.5 %collective-permute-start.27 = (bf16[272,512]{1,0:T(8,128)(2,1)S(1)}, bf16[272,512]{1,0:T(8,128)(2,1)S(1)}, u32[]{:S(2)}, u32[]{:S(2)}) collective-permute-start(bf16[272,512]{1,0:T(8,128)(2,1)S(1)} %get-tuple-element.79), channel_id=1, source_target_pairs={{0,6},{2,0},{4,2},{6,4},{1,7},{3,1},{5,3},{7,5},{8,14},{10,8},{12,... | collective-permute-start | bytes 835592 | tf_op jit(solution)/shard_map/ppermute | solution.py:523
  142.8 17.0 %collective-permute-start.26 = (bf16[528,512]{1,0:T(8,128)(2,1)S(1)}, bf16[528,512]{1,0:T(8,128)(2,1)S(1)}, u32[]{:S(2)}, u32[]{:S(2)}) collective-permute-start(bf16[528,512]{1,0:T(8,128)(2,1)S(1)} %pad_maximum_fusion), channel_id=1, source_target_pairs={{0,2},{2,4},{4,6},{6,0},{1,3},{3,5},{5,7},{7,1},{8,10},{10,12},{12... | collective-permute-start | bytes 1622024 | tf_op jit(solution)/shard_map/ppermute | solution.py:523
  149.2 4.6 %copy-start.12 = (f32[512,128]{1,0:T(8,128)S(1)}, f32[512,128]{1,0:T(8,128)}, u32[]{:S(2)}) copy-start(f32[512,128]{1,0:T(8,128)} %get-tuple-element.64.refs_15_) | copy-start | bytes 786436
  149.2 12.6 %collective-permute-start.28 = (bf16[528,512]{1,0:T(8,128)(2,1)S(1)}, bf16[528,512]{1,0:T(8,128)(2,1)S(1)}, u32[]{:S(2)}, u32[]{:S(2)}) collective-permute-start(bf16[528,512]{1,0:T(8,128)(2,1)S(1)} %pad_maximum_fusion.1), channel_id=1, source_target_pairs={{0,6},{2,0},{4,2},{6,4},{1,7},{3,1},{5,3},{7,5},{8,14},{10,8},{12,... | collective-permute-start | bytes 1622024 | tf_op jit(solution)/shard_map/ppermute | solution.py:523
  150.9 22.0 %copy-start.1 = (bf16[16,32,512]{2,1,0:T(8,128)(2,1)S(1)}, bf16[16,32,512]{2,1,0:T(8,128)(2,1)}, u32[]{:S(2)}) copy-start(bf16[16,32,512]{2,1,0:T(8,128)(2,1)} %copy-done) | copy-start | bytes 1572868
  150.9 22.0 %copy-start.3 = (bf16[16,32,512]{2,1,0:T(8,128)(2,1)S(1)}, bf16[16,32,512]{2,1,0:T(8,128)(2,1)}, u32[]{:S(2)}) copy-start(bf16[16,32,512]{2,1,0:T(8,128)(2,1)} %copy-done.2) | copy-start | bytes 1572868
  150.9 20.1 %collective-permute-start.21 = (bf16[512,512]{1,0:T(8,128)(2,1)S(1)}, bf16[512,512]{1,0:T(8,128)(2,1)S(1)}, u32[]{:S(2)}, u32[]{:S(2)}) collective-permute-start(bf16[512,512]{1,0:T(8,128)(2,1)S(1)} %pad_maximum_fusion.3), channel_id=1, source_target_pairs={{0,2},{2,4},{4,6},{6,0},{1,3},{3,5},{5,7},{7,1},{8,10},{10,12},{12... | collective-permute-start | bytes 1572872 | tf_op jit(solution)/shard_map/ppermute | solution.py:523
  151.0 21.9 %collective-permute-start.23 = (bf16[512,512]{1,0:T(8,128)(2,1)S(1)}, bf16[512,512]{1,0:T(8,128)(2,1)S(1)}, u32[]{:S(2)}, u32[]{:S(2)}) collective-permute-start(bf16[512,512]{1,0:T(8,128)(2,1)S(1)} %pad_maximum_fusion.4), channel_id=1, source_target_pairs={{0,6},{2,0},{4,2},{6,4},{1,7},{3,1},{5,3},{7,5},{8,14},{10,8},{12,... | collective-permute-start | bytes 1572872 | tf_op jit(solution)/shard_map/ppermute | solution.py:523
  174.3 22.7 %copy-start.15 = (s32[16]{0:T(128)S(1)}, s32[16]{0:T(128)}, u32[]{:S(2)}) copy-start(s32[16]{0:T(128)} %plan_ref.3) | copy-start | bytes 196
  191.6 14.7 %all-to-all-start.3 = ((bf16[16,32,512]{2,1,0:T(8,128)(2,1)}), bf16[16,32,512]{2,1,0:T(8,128)(2,1)S(1)}, u32[]{:S(2)}, u32[]{:S(2)}) async-start(bf16[16,32,512]{2,1,0:T(8,128)(2,1)} %bitcast.29), calls=%async_computation.3 | async-start | bytes 1048576 | tf_op jit(solution)/shard_map/all_to_all | solution.py:557
  233.9 4.6 %copy-start.9 = (bf16[4096,128]{1,0:T(8,128)(2,1)S(1)}, bf16[4096,128]{1,0:T(8,128)(2,1)}, u32[]{:S(2)}) copy-start(bf16[4096,128]{1,0:T(8,128)(2,1)} %get-tuple-element.105) | copy-start | bytes 3145732
  238.5 1.6 copy-start.8
Sparse Core Ops, SparseCore 0:
  104.5 129.3 all-reduce.2

commit v4 on v3

--- a/solution.py
+++ b/solution.py
@@ -132,7 +132,7 @@
 
 
 def project_steps(
-    idx_ref, places, arrivals, copies, buffer, gain_ref, weights, held, turned_ref, raw_ref, fresh
+    idx_ref, places, arrivals, copies, buffer, gain_ref, weights, held, stage, turned_ref, raw_ref, fresh
 ):
     rows, width = buffer.shape[1:]
     for n, (step, other) in enumerate(places):
@@ -140,6 +140,7 @@
         for ref, target in zip(weights, held):
             arrivals[n].append(copies.start(ref.at[part], target.at[n]))
     squares = jnp.zeros((rows, 1), F32)
+    sent = []
     for n, (step, other) in enumerate(places):
         core = idx_ref[4] if not other else 1 - idx_ref[4]
         for copy in arrivals[n]:
@@ -147,7 +148,9 @@
         wide = buffer[n].astype(F32)
         squares += jnp.sum(wide * wide, axis=1, keepdims=True)
         gained = (wide * gain_ref[pl.ds(idx_ref[step] + core, 1)]).astype(BF)
-        turned_ref[step % 3, pl.ds(pl.multiple_of(core * width, width), width)] = gained.T
+        stage[n] = gained.T
+        here = pl.ds(pl.multiple_of(core * width, width), width)
+        sent.append(copies.start(stage.at[n], turned_ref.at[step % 3, here]))
         at = 0
         for target in held:
             cols = slice(at, at + target.shape[2])
@@ -156,19 +159,21 @@
                 raw_ref[:, cols] = nn(gained, target[n])
             else:
                 raw_ref[:, cols] += nn(gained, target[n])
-    return squares
+    return squares, sent
 
 
 def project_near_kernel(*refs):
     idx_ref, pieces = refs[0], refs[1:7]
-    gain_ref, wq, wk, wv, turned_ref, raw_ref, squares_ref, buffer, hq, hk, hv, sems = refs[7:]
+    gain_ref, wq, wk, wv, turned_ref, raw_ref, squares_ref, buffer, stage, hq, hk, hv, sems = refs[7:]
     copies = Copies(sems)
     arrivals = fetch_near(copies, pieces, buffer)
-    squares = project_steps(
+    squares, sent = project_steps(
         idx_ref, NEAR, arrivals, copies, buffer, gain_ref, (wq, wk, wv), (hq, hk, hv),
-        turned_ref, raw_ref, True,
+        stage, turned_ref, raw_ref, True,
     )
     squares_ref[...] = jnp.broadcast_to(squares, squares_ref.shape)
+    for copy in sent:
+        copy.wait()
 
 
 def project_near(idx, pieces, gain, wq, wk, wv):
@@ -184,11 +189,11 @@
         project_near_kernel,
         grid=(1,),
         in_specs=[SMEM_SPEC] + [HBM_SPEC] * 6 + [whole(gain.shape)] + [HBM_SPEC] * 3,
-        out_specs=[whole(a.shape) for a in shapes],
+        out_specs=[HBM_SPEC] + [whole(a.shape) for a in shapes[1:]],
         out_shape=shapes,
-        scratch_shapes=[pltpu.VMEM((6, rows, width), BF)]
+        scratch_shapes=[pltpu.VMEM((6, rows, width), BF), pltpu.VMEM((6, width, rows), BF)]
         + [pltpu.VMEM((6, width, w.shape[1]), BF) for w in weights]
-        + [pltpu.SemaphoreType.DMA((24,))],
+        + [pltpu.SemaphoreType.DMA((30,))],
         compiler_params=params(),
         cost_estimate=cost(12 * rows * width * cols, 12 * width * (2 * rows + cols)),
         name="project_near",
@@ -198,27 +203,25 @@
 def attend_kernel(*refs):
     idx_ref, pieces = refs[0], refs[1:5]
     (
-        gain_ref, wq, wk, wv, near_raw_ref, near_squares_ref,
-        cosine_ref, sine_ref, where_col_ref, where_row_ref,
-        turned_ref, raw_ref, inverse_ref, q_ref, k_ref, k_turned_ref, v_ref, shares_ref, attended_ref,
-        buffer, hq, hk, hv, sems,
+        gain_ref, wq, wk, wv, near_raw_ref, near_squares_ref, rotary_ref, where_ref,
+        turned_ref, inverse_ref, q_ref, k_ref, k_turned_ref, v_ref, shares_ref, attended_ref,
+        raw_ref, shares_stage, buffer, stage, hq, hk, hv, sems,
     ) = refs[5:]
     rows, width = buffer.shape[1:]
     copies = Copies(sems)
     arrivals = fetch_far(copies, pieces, buffer)
     raw_ref[...] = near_raw_ref[...]
-    squares = project_steps(
+    squares, sent = project_steps(
         idx_ref, FAR, arrivals, copies, buffer, gain_ref, (wq, wk, wv), (hq, hk, hv),
-        turned_ref, raw_ref, False,
+        stage, turned_ref, raw_ref, False,
     )
     features = wq.shape[0]
     inverse = lax.rsqrt((squares + near_squares_ref[:, 0:1]) / features + NORM_EPSILON)
     inverse_ref[...] = jnp.broadcast_to(inverse, inverse_ref.shape)
-    raw_ref[...] = raw_ref[...] * inverse
-
-    cosine = cosine_ref[...]
-    sine = sine_ref[...]
-    heads = shares_ref.shape[0]
+
+    cosine = rotary_ref[0] * inverse
+    sine = rotary_ref[1] * inverse
+    heads = shares_stage.shape[0]
 
     def rotate(u):
         return u * cosine + pltpu.roll(u, HD // 2, 1) * sine
@@ -226,13 +229,14 @@
     key = rotate(raw_ref[:, heads * HD : (heads + 1) * HD])
     k_ref[...] = key.astype(BF)
     k_turned_ref[...] = key.T.astype(BF)
-    value = raw_ref[:, (heads + 1) * HD :]
+    value = raw_ref[:, (heads + 1) * HD :] * inverse
     v_ref[...] = value.astype(BF)
     v_turned = value.T.astype(BF)
-    doc_s = where_col_ref[:, 0:1]
-    at_s = where_col_ref[:, 1:2]
-    doc_g = where_row_ref[0:1, :]
-    at_g = where_row_ref[1:2, :]
+    down = where_ref[...].T
+    doc_s = down[:, 0:1]
+    at_s = down[:, 1:2]
+    doc_g = where_ref[0:1, :]
+    at_g = where_ref[1:2, :]
     allowed = (doc_s == doc_g) & (at_s <= at_g)
     for h in range(heads):
         cols = slice(h * HD, (h + 1) * HD)
@@ -242,18 +246,20 @@
         weights = jnp.where(allowed, jnp.exp(scores), 0.0)
         total = jnp.sum(weights, axis=0, keepdims=True)
         shares = (weights * (1.0 / total)).astype(BF)
-        shares_ref[h] = shares
+        shares_stage[h] = shares
+        sent.append(copies.start(shares_stage.at[h], shares_ref.at[h]))
         attended_ref[:, cols] = nn(v_turned, shares).T.astype(BF)
-
-
-def attend(idx, pieces, gain, wq, wk, wv, near_raw, near_squares, cosine, sine, where_col, where_row):
+    for copy in sent:
+        copy.wait()
+
+
+def attend(idx, pieces, gain, wq, wk, wv, near_raw, near_squares, rotary, where):
     width = pieces[0].shape[1]
     rows, cols = near_raw.shape
     weights = (wq, wk, wv)
     heads = wq.shape[1] // HD
     shapes = [
         jax.ShapeDtypeStruct((1, 2 * width, rows), BF),
-        jax.ShapeDtypeStruct((rows, cols), F32),
         jax.ShapeDtypeStruct((rows, HD), F32),
         jax.ShapeDtypeStruct((rows, heads * HD), BF),
         jax.ShapeDtypeStruct((rows, HD), BF),
@@ -262,17 +268,24 @@
         jax.ShapeDtypeStruct((heads, rows, rows), BF),
         jax.ShapeDtypeStruct((rows, heads * HD), BF),
     ]
-    extras = (near_raw, near_squares, cosine, sine, where_col, where_row)
+    extras = (near_raw, near_squares, rotary, where)
+    out_specs = [whole(a.shape) for a in shapes]
+    out_specs[0] = out_specs[6] = HBM_SPEC
     return pl.pallas_call(
         attend_kernel,
         grid=(1,),
         in_specs=[SMEM_SPEC] + [HBM_SPEC] * 4 + [whole(gain.shape)] + [HBM_SPEC] * 3
         + [whole(a.shape) for a in extras],
-        out_specs=[whole(a.shape) for a in shapes],
+        out_specs=out_specs,
         out_shape=shapes,
-        scratch_shapes=[pltpu.VMEM((2, rows, width), BF)]
+        scratch_shapes=[
+            pltpu.VMEM((rows, cols), F32),
+            pltpu.VMEM((heads, rows, rows), BF),
+            pltpu.VMEM((2, rows, width), BF),
+            pltpu.VMEM((2, width, rows), BF),
+        ]
         + [pltpu.VMEM((2, width, w.shape[1]), BF) for w in weights]
-        + [pltpu.SemaphoreType.DMA((10,))],
+        + [pltpu.SemaphoreType.DMA((16,))],
         compiler_params=params(),
         cost_estimate=cost(
             4 * rows * width * cols + 4 * heads * rows * rows * HD, 4 * width * (2 * rows + cols)
@@ -321,10 +334,10 @@
 
 def back_kernel(*refs, scale):
     idx_ref, pieces = refs[0], refs[1:5]
-    inputs = refs[5:17]
-    grad_ref, dots_ref, gq_ref, gk_ref, gv_ref = refs[17:22]
-    buffer, held, scaled_ref, gq, gk, gv, sems = refs[22:29]
-    targets = refs[29:]
+    inputs = refs[5:16]
+    grad_ref, dots_ref, gq_ref, gk_ref, gv_ref = refs[16:21]
+    buffer, held, scaled_ref, gq, gk, gv, sems = refs[21:28]
+    targets = refs[28:]
     wo_ref, near_ref, far_turned, near_turned = inputs[:4]
     copies = Copies(sems)
     arrivals = fetch_far(copies, pieces, buffer)
@@ -339,7 +352,7 @@
         copies.start(near_turned, turned_ref.at[:3]),
         copies.start(far_turned, turned_ref.at[3:]),
     ]
-    q_ref, k_ref, k_turned_ref, v_ref, shares_ref, raw_ref, inverse_ref, rotary_ref = targets[2:]
+    q_ref, k_ref, k_turned_ref, v_ref, shares_ref, inverse_ref, rotary_ref = targets[2:]
     acc_copy.wait()
     for n in range(2):
         for copy in arrivals[n]:
@@ -360,10 +373,8 @@
 
     def emit(at, grad):
         cols = slice(at * HD, (at + 1) * HD)
-        rounded = grad.astype(BF)
-        grad_ref[:, cols] = rounded
+        grad_ref[:, cols] = grad.astype(BF)
         scaled_ref[:, cols] = (grad * factor).astype(BF)
-        return rounded.astype(F32) * raw_ref[:, cols]
 
     parts = turned_ref.shape[0]
     outs = []
@@ -388,9 +399,12 @@
         dscore = (wide * (share_grad - row_dot) * SCORE_SCALE).astype(BF)
         key_grad += nn(dscore, q_ref[:, cols])
         value_grad += nn(shares, grad_attended)
-        products += emit(h, rotate_back(nn(k_turned_ref[...], dscore).T))
-    products += emit(heads, rotate_back(key_grad))
-    products += emit(heads + 1, value_grad)
+        query_grad = nn(k_turned_ref[...], dscore).T
+        products += query_grad * q_ref[:, cols].astype(F32)
+        emit(h, rotate_back(query_grad))
+    products += key_grad * k_ref[...].astype(F32) + value_grad * v_ref[...].astype(F32)
+    emit(heads, rotate_back(key_grad))
+    emit(heads + 1, value_grad)
     for copy in turned_loads:
         copy.wait()
     send(gq, gq_ref, 0)
@@ -411,27 +425,28 @@
         copy.wait()
 
 
-def back(idx, pieces, wo, near, far_turned, near_turned, q, k, k_turned, v, shares, raw, inverse, rotary, scale):
+def back(idx, pieces, wo, near, far_turned, near_turned, q, k, k_turned, v, shares, inverse, rotary, scale):
     width = pieces[0].shape[1]
     cols, features = wo.shape
     rows = near.shape[0]
     kv_cols = k.shape[1]
-    inputs = (wo, near, far_turned, near_turned, q, k, k_turned, v, shares, raw, inverse, rotary)
-    loaded = (q, k, k_turned, v, shares, raw, inverse, rotary)
+    grad_shape = (rows, cols + 2 * kv_cols)
+    inputs = (wo, near, far_turned, near_turned, q, k, k_turned, v, shares, inverse, rotary)
+    loaded = (q, k, k_turned, v, shares, inverse, rotary)
     weight_shapes = [
         jax.ShapeDtypeStruct((features, w), BF) for w in (cols, kv_cols, kv_cols)
     ]
-    shapes = [jax.ShapeDtypeStruct(raw.shape, BF), jax.ShapeDtypeStruct((8, rows), F32)]
+    shapes = [jax.ShapeDtypeStruct(grad_shape, BF), jax.ShapeDtypeStruct((8, rows), F32)]
     return pl.pallas_call(
         functools.partial(back_kernel, scale=scale),
         grid=(1,),
-        in_specs=[SMEM_SPEC] + [HBM_SPEC] * 16,
+        in_specs=[SMEM_SPEC] + [HBM_SPEC] * 15,
         out_specs=[whole(a.shape) for a in shapes] + [HBM_SPEC] * 3,
         out_shape=shapes + weight_shapes,
         scratch_shapes=[
             pltpu.VMEM((2, rows, width), BF),
             pltpu.VMEM((2, cols, width), BF),
-            pltpu.VMEM(raw.shape, BF),
+            pltpu.VMEM(grad_shape, BF),
         ]
         + [pltpu.VMEM((4, features // 4, w.shape[1]), BF) for w in weight_shapes]
         + [
@@ -447,6 +462,26 @@
         ),
         name="back",
     )(idx, *pieces, *inputs)
+
+
+def finish_kernel(*refs):
+    for source, target in zip(refs[:3], refs[3:]):
+        target[...] = source[...]
+
+
+def finish(arrays):
+    parts = 4
+    specs = [pl.BlockSpec((a.shape[0] // parts, a.shape[1]), lambda j: (j, 0)) for a in arrays]
+    return pl.pallas_call(
+        finish_kernel,
+        grid=(parts,),
+        in_specs=specs,
+        out_specs=specs,
+        out_shape=[jax.ShapeDtypeStruct(a.shape, a.dtype) for a in arrays],
+        compiler_params=params(),
+        cost_estimate=cost(0, 4 * sum(a.size for a in arrays)),
+        name="finish",
+    )(*arrays)
 
 
 def out_term_kernel(idx_ref, _, attended_ref, wo_ref, out_ref):
@@ -587,10 +622,10 @@
     frequency = ROPE_THETA ** (-2.0 * jnp.arange(HD // 2, dtype=F32) / HD)
     angles = positions[:, None] * frequency[None, :]
     cosine, sine = jnp.cos(angles), jnp.sin(angles)
-    cosine = jnp.concatenate([cosine, cosine], axis=1)
-    sine = jnp.concatenate([-sine, sine], axis=1)
-    where_row = jnp.stack([docs, at])
-    where_col = where_row.T
+    rotary = jnp.stack(
+        [jnp.concatenate([cosine, cosine], axis=1), jnp.concatenate([-sine, sine], axis=1)]
+    )
+    where = jnp.pad(jnp.stack([docs, at]).astype(F32), ((0, 6), (0, 0)))
 
     tok_near = gather_near(here_tokens)
     cot_near = gather_near(here_cot)
@@ -599,20 +634,19 @@
     near_turned, near_raw, near_squares = project_near(idx, both_cores(tok_near), gain, wq, wk, wv)
     tok_far, cot_near, near_raw = lax.optimization_barrier((tok_far, cot_near, near_raw))
     cot_far = gather_far(cot_near)
-    far_turned, raw, inverse, q, k, k_turned, v, shares, attended = attend(
-        idx, both_cores(tok_far), gain, wq, wk, wv, near_raw, near_squares, cosine, sine, where_col, where_row
+    far_turned, inverse, q, k, k_turned, v, shares, attended = attend(
+        idx, both_cores(tok_far), gain, wq, wk, wv, near_raw, near_squares, rotary, where
     )
 
     scale = (rows * dp) ** (-0.5)
     cot_near, shares = lax.optimization_barrier((both_cores(cot_near), shares))
     near = back_near(idx, cot_near, wo)
     cot_far, near = lax.optimization_barrier((cot_far, near))
-    rotary = jnp.stack([cosine, sine])
     grad, dots, *grads = back(
         idx, both_cores(cot_far), wo, near, far_turned, near_turned, q, k, k_turned, v, shares,
-        raw, inverse, rotary, scale,
-    )
-    grad_query, grad_key, grad_value = lax.psum(tuple(grads), ("x", "z"))
+        inverse, rotary, scale,
+    )
+    grad_query, grad_key, grad_value = finish(lax.psum(tuple(grads), ("x", "z")))
     after = swap(dots)
     idx_mine, idx_other = around * cores + core, around * cores + (1 - core)
     out_sum = sum_pieces(

time: 249 us -> 247 us (level)
  local copies, waits for them, and re-layouts: 16.4 us -> 10 us
  Pallas kernels: 64.8 us -> 70.4 us
    unnamed x52 -> x57, local copies, waits for them, and re-layouts: 9.64 us -> 3.49 us
    pallas_call x0 -> x1, Pallas kernels: none -> 5.8 us  [finish(): pl.pallas_call(finish_kernel, grid=(parts,), in_specs=specs, out_specs=sp...]
  transfers between devices with their start and end apart: 33 -> 33, of which waited for: 13 -> 14; matrix products, arithmetic and copies ran while one was open for 7% -> 6% of each run, Pallas kernels for 20% -> 20%
where the time goes in v4:
time: 247 us; the launch traced here: 246 us
  waiting for transfers between devices  75.2 us (30%)
  Pallas kernels  70.4 us (29%)
  starting transfers between devices  49.4 us (20%)
  blocking collectives  17.4 us (7%)
  between operations  14.6 us (6%)
  local copies, waits for them, and re-layouts  10 us (4%)
  other arithmetic  8.89 us (4%)
    ppermute x16, waiting for transfers between devices, shift(): lax.ppermute(array, axis, [(i, (i + step) % size) for i in range(size)])  28.7 us
    psum x1, waiting for transfers between devices, per_device(): lax.psum(tuple(grads), ('x', 'z'))  26.4 us
    ppermute x16, starting transfers between devices, shift(): lax.ppermute(array, axis, [(i, (i + step) % size) for i in range(size)])  20.5 us
    all_to_all x3, waiting for transfers between devices, exchange(): lax.all_to_all(panels, ('x', 'z'), split_axis=0, concat_axis=0, tiled=True)  17.6 us
    all_to_all x3, starting transfers between devices, exchange(): lax.all_to_all(panels, ('x', 'z'), split_axis=0, concat_axis=0, tiled=True)  17.4 us
    all_to_all x1, blocking collectives, exchange(): lax.all_to_all(panels, ('x', 'z'), split_axis=0, concat_axis=0, tiled=True)  17.4 us
    pallas_call x2, Pallas kernels, input_terms(): pl.pallas_call(input_term_kernel, grid_spec=grid_spec, out_shape=jax.Shap...  13.2 us
    pallas_call x1, Pallas kernels, back(): pl.pallas_call(functools.partial(back_kernel, scale=scale), grid=(1,), in...  12.6 us
  transfers between devices with their start and end apart: 33, of which 14 were waited for; matrix products, arithmetic and copies ran while one was open for 6% of the time, Pallas kernels for 20%

profile of v4, /device:TPU:1, one launch (start us, length us, event | category | flops | bytes accessed | tf_op | source)
XLA Modules:
  0.0 245.9 jit_solution(13799399354833947352)
XLA Ops:
  7.2 1.9 place.1
  9.1 8.6 %all-to-all-start = ((bf16[16,32,512]{2,1,0:T(8,128)(2,1)}), bf16[16,32,512]{2,1,0:T(8,128)(2,1)S(1)}, u32[]{:S(2)}, u32[]{:S(2)}) async-start(bf16[16,32,512]{2,1,0:T(8,128)(2,1)} %place.1), calls=%async_computation | async-start | bytes 1048576 | tf_op jit(solution)/shard_map/all_to_all | solution.py:592
  17.7 0.9 reshape_reshape.4.docs_ref
  18.6 2.2 place_meta.1
  20.8 7.1 %all-to-all-done = bf16[16,32,512]{2,1,0:T(8,128)(2,1)S(1)} async-done(((bf16[16,32,512]{2,1,0:T(8,128)(2,1)}), bf16[16,32,512]{2,1,0:T(8,128)(2,1)S(1)}, u32[]{:S(2)}, u32[]{:S(2)}) %all-to-all-start) | async-done | bytes 524320 | tf_op jit(solution)/shard_map/all_to_all | solution.py:592
  28.0 3.6 %all-to-all-start.1 = ((bf16[16,32,640]{2,1,0:T(8,128)(2,1)}), bf16[16,32,640]{2,1,0:T(8,128)(2,1)S(1)}, u32[]{:S(2)}, u32[]{:S(2)}) async-start(bf16[16,32,640]{2,1,0:T(8,128)(2,1)} %place_meta.1), calls=%async_computation.1 | async-start | bytes 1310720 | tf_op jit(solution)/shard_map/all_to_all | solution.py:592
  31.6 1.4 collective-permute-start
  33.0 0.6 reshape.162.refs_7_.refs_5_
  33.6 1.5 collective-permute-start.2
  35.1 0.6 broadcast_add_fusion.1
  35.7 0.6 pad_add_fusion.refs_0_
  36.3 2.6 %collective-permute-start.6 = (bf16[512,512]{1,0:T(8,128)(2,1)S(1)}, bf16[512,512]{1,0:T(8,128)(2,1)}, u32[]{:S(2)}, u32[]{:S(2)}) collective-permute-start(bf16[512,512]{1,0:T(8,128)(2,1)S(1)} %bitcast.73), channel_id=1, source_target_pairs={{0,1},{1,0},{2,3},{3,2},{4,5},{5,4},{6,7},{7,6},{8,9},{9,8},{10,11... | collective-permute-start | bytes 1572872 | tf_op jit(solution)/shard_map/ppermute | solution.py:562
  38.9 2.6 %all-to-all-done.1 = bf16[16,32,640]{2,1,0:T(8,128)(2,1)S(1)} async-done(((bf16[16,32,640]{2,1,0:T(8,128)(2,1)}), bf16[16,32,640]{2,1,0:T(8,128)(2,1)S(1)}, u32[]{:S(2)}, u32[]{:S(2)}) %all-to-all-start.1) | async-done | bytes 655392 | tf_op jit(solution)/shard_map/all_to_all | solution.py:592
  41.6 1.4 collective-permute-start.4
  43.0 1.5 collective-permute-start.5
  44.5 4.4 %collective-permute-start.7 = (bf16[512,512]{1,0:T(8,128)(2,1)S(1)}, bf16[512,512]{1,0:T(8,128)(2,1)}, u32[]{:S(2)}, u32[]{:S(2)}) collective-permute-start(bf16[512,512]{1,0:T(8,128)(2,1)S(1)} %collective-permute-done.refs_2_), channel_id=1, source_target_pairs={{0,1},{1,0},{2,3},{3,2},{4,5},{5,4},{6,7},{7,6},{8,9},{9,8},{10,11... | collective-permute-start | bytes 1572872 | tf_op jit(solution)/shard_map/ppermute | solution.py:562
  49.0 0.9 collective-permute-start.8
  50.5 1.0 slice.113
  51.5 1.4 collective-permute-start.1
  52.9 1.4 collective-permute-start.3
  54.3 1.0 multiply_cosine_fusion
  55.3 8.8 %project_near.1 = (bf16[3,1024,512]{2,1,0:T(8,128)(2,1)}, f32[512,768]{1,0:T(8,128)}, f32[512,128]{1,0:T(8,128)}) custom-call(s32[13]{0:T(128)} %pad_add_fusion.refs_0_, bf16[512,512]{1,0:T(8,128)(2,1)} %bitcast.74, bf16[512,512]{1,0:T(8,128)(2,1)} %copy-done.7, bf16[512,512]{1,0:T(8,128)(2,1)} %collective-permute-done.2.refs_3_, ...), custom_call_target="tpu_custom_call" | custom-call | flops 2415919104 | bytes 11010048 | tf_op jit(solution)/shard_map/project_near/pallas_call | solution.py:188
  64.2 0.7 collective-permute-start.12
  64.8 0.5 collective-permute-start.11
  65.9 0.6 pad.4.refs_12_
  66.7 0.9 pad_maximum_fusion.2.refs_11_.refs_15_
  67.6 0.7 collective-permute-done.14.refs_3_
  68.2 2.7 %collective-permute-start.10 = (bf16[256,512]{1,0:T(8,128)(2,1)S(1)}, bf16[256,512]{1,0:T(8,128)(2,1)S(1)}, u32[]{:S(2)}, u32[]{:S(2)}) collective-permute-start(bf16[256,512]{1,0:T(8,128)(2,1)S(1)} %slice.85), channel_id=1, source_target_pairs={{0,6},{2,0},{4,2},{6,4},{1,7},{3,1},{5,3},{7,5},{8,14},{10,8},{12,... | collective-permute-start | bytes 786440 | tf_op jit(solution)/shard_map/ppermute | solution.py:558
  70.9 0.7 copy-done.14
  71.6 9.0 %attend.1 = (bf16[1,1024,512]{2,1,0:T(8,128)(2,1)}, f32[512,128]{1,0:T(8,128)}, bf16[512,512]{1,0:T(8,128)(2,1)}, bf16[512,128]{1,0:T(8,128)(2,1)}, bf16[128,512...) custom-call(s32[13]{0:T(128)} %pad_add_fusion.refs_0_, ...), custom_call_target="tpu_custom_call" | custom-call | flops 1342177280 | bytes 3670016 | tf_op jit(solution)/shard_map/attend/pallas_call | solution.py:274
  80.7 0.7 copy-done.8
  81.7 6.0 %back_near.1.refs_6_ = f32[512,512]{1,0:T(8,128)} custom-call(s32[13]{0:T(128)} %pad_add_fusion.refs_0_, bf16[512,512]{1,0:T(8,128)(2,1)} %bitcast.78, bf16[512,512]{1,0:T(8,128)(2,1)} %copy-done.5, bf16[512,512]{1,0:T(8,128)(2,1)} %copy-done.6, bf16[512,512]{1,0:T(8,128)(2,1)} %copy-done.10, bf16[512,512]{1,0:T(8,128)(2,1)} %copy-done.8, ...), custom_call_target="tpu_custom_call" | custom-call | flops 1610612736 | bytes 6291456 | tf_op jit(solution)/shard_map/back_near/pallas_call | solution.py:318
  87.8 0.7 collective-permute-start.16
  88.6 1.1 collective-permute-done.16.refs_3_
  90.7 12.6 %back.1 = (bf16[512,768]{1,0:T(8,128)(2,1)}, f32[8,512]{1,0:T(8,128)}, bf16[4096,512]{1,0:T(8,128)(2,1)}, bf16[4096,128]{1,0:T(8,128)(2,1)}, bf16[4096,128]{1,0:T(8,128)(2,1)}) custom-call(s32[13]{0:T(128)} %pad_add_fusion.refs_0_, bf16[256,512]{1,0:T(8,128)(2,1)} %copy-done.23, bf16[256,512]{1,0:T(8,128)(2,1)} %copy-done.22, bf16[256,512]{1,0:T(8,128)(2,1)} %copy-done.24, ...), custom_call_target="tpu_custom_call" | custom-call | flops 4831838208 | bytes 8388608 | tf_op jit(solution)/shard_map/back/pallas_call | solution.py:440
  103.4 0.7 collective-permute-start.18
  104.1 0.5 broadcast_add_fusion.idx_ref
  104.7 0.4 collective-permute-done.18._
  105.1 0.6 copy-done.26
  105.7 5.4 %out_terms.3 = bf16[4,512,512]{2,1,0:T(8,128)(2,1)} custom-call(s32[4]{0:T(128)} %broadcast_add_fusion.idx_ref, f32[8,512]{1,0:T(8,128)} %copy-done.26, bf16[512,512]{1,0:T(8,128)(2,1)} %get-tuple-element.67.attended_ref, bf16[512,4096]{1,0:T(8,128)(2,1)} %wo_ref.3), custom_call_target="tpu_custom_call" | custom-call | flops 21474836480 | bytes 83886080 | tf_op jit(solution)/shard_map/out_terms/pallas_call | solution.py:504
  111.5 6.7 %input_terms.3 = bf16[4,528,512]{2,1,0:T(8,128)(2,1)} custom-call(s32[4]{0:T(128)} %broadcast_add_fusion.idx_ref, f32[8,512]{1,0:T(8,128)} %copy-done.26, bf16[512,768]{1,0:T(8,128)(2,1)} %get-tuple-element.68.grad_ref, f32[8,512]{1,0:T(8,128)} %get-tuple-element.66.dots_ref, bf16[4096,512]{1,0:T(8,128)(2,1)} %wq_ref.3, bf16[4096,128]{1,0:T(8,128)(2,1)} %wk_ref.3, ...), custom_call_target="tpu_custom_call" | custom-call | flops 32212254720 | bytes 104857600 | tf_op jit(solution)/shard_map/input_terms/pallas_call | solution.py:546
  118.2 6.5 %input_terms.2 = bf16[4,528,512]{2,1,0:T(8,128)(2,1)} custom-call(s32[4]{0:T(128)} %get-tuple-element.78.idx_ref, f32[8,512]{1,0:T(8,128)} %copy-done.26, bf16[512,768]{1,0:T(8,128)(2,1)} %get-tuple-element.68.grad_ref, f32[8,512]{1,0:T(8,128)} %get-tuple-element.66.dots_ref, bf16[4096,512]{1,0:T(8,128)(2,1)} %wq_ref.3, bf16[4096,128]{1,0:T(8,128)(2,1)} %wk_ref.3, ...), custom_call_target="tpu_custom_call" | custom-call | flops 32212254720 | bytes 104857600 | tf_op jit(solution)/shard_map/input_terms/pallas_call | solution.py:546
  124.7 5.5 %out_terms.2 = bf16[4,512,512]{2,1,0:T(8,128)(2,1)} custom-call(s32[4]{0:T(128)} %get-tuple-element.78.idx_ref, f32[8,512]{1,0:T(8,128)} %copy-done.26, bf16[512,512]{1,0:T(8,128)(2,1)} %get-tuple-element.67.attended_ref, bf16[512,4096]{1,0:T(8,128)(2,1)} %wo_ref.3), custom_call_target="tpu_custom_call" | custom-call | flops 21474836480 | bytes 83886080 | tf_op jit(solution)/shard_map/out_terms/pallas_call | solution.py:504
  130.2 2.4 add_convert_fusion.1
  132.6 0.6 add_convert_fusion
  133.5 0.9 collective-permute-start.20
  134.3 1.9 collective-permute-start.22
  136.3 1.5 collective-permute-start.27
  137.8 4.3 %collective-permute-done.25 = bf16[256,512]{1,0:T(8,128)(2,1)S(1)} collective-permute-done((bf16[256,512]{1,0:T(8,128)(2,1)S(1)}, bf16[256,512]{1,0:T(8,128)(2,1)S(1)}, u32[]{:S(2)}, u32[]{:S(2)}) %collective-permute-start.25) | collective-permute-done | bytes 262176 | tf_op jit(solution)/shard_map/ppermute | solution.py:558
  142.3 6.2 %collective-permute-done.27 = bf16[272,512]{1,0:T(8,128)(2,1)S(1)} collective-permute-done((bf16[272,512]{1,0:T(8,128)(2,1)S(1)}, bf16[272,512]{1,0:T(8,128)(2,1)S(1)}, u32[]{:S(2)}, u32[]{:S(2)}) %collective-permute-start.27) | collective-permute-done | bytes 278560 | tf_op jit(solution)/shard_map/ppermute | solution.py:558
  148.6 2.1 collective-permute-start.28
  151.1 2.7 %collective-permute-start.23 = (bf16[512,512]{1,0:T(8,128)(2,1)S(1)}, bf16[512,512]{1,0:T(8,128)(2,1)S(1)}, u32[]{:S(2)}, u32[]{:S(2)}) collective-permute-start(bf16[512,512]{1,0:T(8,128)(2,1)S(1)} %pad_maximum_fusion.4), channel_id=1, source_target_pairs={{0,6},{2,0},{4,2},{6,4},{1,7},{3,1},{5,3},{7,5},{8,14},{10,8},{12,... | collective-permute-start | bytes 1572872 | tf_op jit(solution)/shard_map/ppermute | solution.py:558
  154.0 5.2 %collective-permute-done.26 = bf16[528,512]{1,0:T(8,128)(2,1)S(1)} collective-permute-done((bf16[528,512]{1,0:T(8,128)(2,1)S(1)}, bf16[528,512]{1,0:T(8,128)(2,1)S(1)}, u32[]{:S(2)}, u32[]{:S(2)}) %collective-permute-start.26) | collective-permute-done | bytes 540704 | tf_op jit(solution)/shard_map/ppermute | solution.py:558
  159.2 2.0 collective-permute-done.28
  161.4 9.0 %collective-permute-done.21 = bf16[512,512]{1,0:T(8,128)(2,1)S(1)} collective-permute-done((bf16[512,512]{1,0:T(8,128)(2,1)S(1)}, bf16[512,512]{1,0:T(8,128)(2,1)S(1)}, u32[]{:S(2)}, u32[]{:S(2)}) %collective-permute-start.21) | collective-permute-done | bytes 524320 | tf_op jit(solution)/shard_map/ppermute | solution.py:558
  170.4 1.9 collective-permute-done.23
  172.3 1.4 fusion.6
  173.7 17.4 %all_to_all.20 = bf16[16,32,512]{2,1,0:T(8,128)(2,1)S(1)} all-to-all(bf16[16,32,512]{2,1,0:T(8,128)(2,1)S(1)} %bitcast.79), channel_id=1, replica_groups=mesh['x'=4,'z'=4,'y'=4,'core'=2] {'x','z'}, dimensions={0} | all-to-all | bytes 1048576 | tf_op jit(solution)/shard_map/all_to_all | solution.py:592
  191.0 5.2 %all-to-all-start.3 = ((bf16[16,32,512]{2,1,0:T(8,128)(2,1)}), bf16[16,32,512]{2,1,0:T(8,128)(2,1)S(1)}, u32[]{:S(2)}, u32[]{:S(2)}) async-start(bf16[16,32,512]{2,1,0:T(8,128)(2,1)} %bitcast.28), calls=%async_computation.3 | async-start | bytes 1048576 | tf_op jit(solution)/shard_map/all_to_all | solution.py:592
  196.3 1.4 gather_fusion
  197.7 7.8 %all-to-all-done.3 = bf16[16,32,512]{2,1,0:T(8,128)(2,1)S(1)} async-done(((bf16[16,32,512]{2,1,0:T(8,128)(2,1)}), bf16[16,32,512]{2,1,0:T(8,128)(2,1)S(1)}, u32[]{:S(2)}, u32[]{:S(2)}) %all-to-all-start.3) | async-done | bytes 524320 | tf_op jit(solution)/shard_map/all_to_all | solution.py:592
  205.5 1.4 gather_fusion.1
  206.9 26.4 %all-reduce.4.cloned.1.call-done = (bf16[4096,512]{1,0:T(8,128)(2,1)}, bf16[4096,128]{1,0:T(8,128)(2,1)}, bf16[4096,128]{1,0:T(8,128)(2,1)}) async-done(((bf16[4096,512]{1,0:T(8,128)(2,1)}, bf16[4096,128]{1,0:T(8,128)(2,1)}, bf16[4096,128]{1,0:T(8,128)(2,1)}), (bf16[4096,512]{1,0:T(8,128)(2,1)}, bf16[4096,128]{1,0:T(8,128)(2,1)}, bf16[4096,128]{1,0:T(8,128)(2,1)})) %all-reduce.4.cloned.1.call-update) | async-done | bytes 6291472 | tf_op jit(solution)/shard_map/psum | solution.py:649
  233.3 5.8 %finish.1 = (bf16[4096,512]{1,0:T(8,128)(2,1)}, bf16[4096,128]{1,0:T(8,128)(2,1)}, bf16[4096,128]{1,0:T(8,128)(2,1)}) custom-call(bf16[4096,512]{1,0:T(8,128)(2,1)} %get-tuple-element.75.refs_0_, bf16[4096,128]{1,0:T(8,128)(2,1)} %get-tuple-element.76.refs_1_, bf16[4096,128]{1,0:T(8,128)(2,1)} %get-tuple-element.77.refs_2_), custom_call_target="tpu_custom_call" | custom-call | bytes 12582912 | tf_op jit(solution)/shard_map/finish/pallas_call | solution.py:475
  (114 shorter events, 4.8 us)
Async XLA Ops:
  7.2 10.5 %copy-start.17 = (s32[512]{0:T(512)S(1)}, s32[512]{0:T(512)}, u32[]{:S(2)}) copy-start(s32[512]{0:T(512)} %param.13) | copy-start | bytes 6148
  9.1 23.9 %copy-start.16 = (f32[4096]{0:T(1024)S(1)}, f32[4096]{0:T(1024)}, u32[]{:S(2)}) copy-start(f32[4096]{0:T(1024)} %param.12) | copy-start | bytes 49156
  9.1 26.0 %copy-start.21 = (s32[4]{0:T(128)S(1)}, s32[4]{0:T(128)}, u32[]{:S(2)}) copy-start(s32[4]{0:T(128)} %constant.101.clone) | copy-start | bytes 52
  9.1 18.9 %all-to-all-start = ((bf16[16,32,512]{2,1,0:T(8,128)(2,1)}), bf16[16,32,512]{2,1,0:T(8,128)(2,1)S(1)}, u32[]{:S(2)}, u32[]{:S(2)}) async-start(bf16[16,32,512]{2,1,0:T(8,128)(2,1)} %place.1), calls=%async_computation | async-start | bytes 1048576 | tf_op jit(solution)/shard_map/all_to_all | solution.py:592
  28.0 22.1 %copy-start = (bf16[16,32,512]{2,1,0:T(8,128)(2,1)}, bf16[16,32,512]{2,1,0:T(8,128)(2,1)S(1)}, u32[]{:S(2)}) copy-start(bf16[16,32,512]{2,1,0:T(8,128)(2,1)S(1)} %all-to-all-done) | copy-start | bytes 1572868
  28.0 13.5 %all-to-all-start.1 = ((bf16[16,32,640]{2,1,0:T(8,128)(2,1)}), bf16[16,32,640]{2,1,0:T(8,128)(2,1)S(1)}, u32[]{:S(2)}, u32[]{:S(2)}) async-start(bf16[16,32,640]{2,1,0:T(8,128)(2,1)} %place_meta.1), calls=%async_computation.1 | async-start | bytes 1310720 | tf_op jit(solution)/shard_map/all_to_all | solution.py:592
  31.6 201.7 %all-reduce.4.cloned.1.call-start = ((), (), s32[]{:S(2)}) async-start(), calls=%async_computation.4 | async-start | bytes 12582912 | tf_op jit(solution)/shard_map/psum | solution.py:649
  31.6 12.9 %collective-permute-start = (bf16[512,512]{1,0:T(8,128)(2,1)S(1)}, bf16[512,512]{1,0:T(8,128)(2,1)S(1)}, u32[]{:S(2)}, u32[]{:S(2)}) collective-permute-start(bf16[512,512]{1,0:T(8,128)(2,1)S(1)} %bitcast.71), channel_id=1, source_target_pairs={{0,2},{2,4},{4,6},{6,0},{1,3},{3,5},{5,7},{7,1},{8,10},{10,12},{12... | collective-permute-start | bytes 1572872 | tf_op jit(solution)/shard_map/ppermute | solution.py:558
  33.6 15.3 %collective-permute-start.2 = (bf16[512,512]{1,0:T(8,128)(2,1)S(1)}, bf16[512,512]{1,0:T(8,128)(2,1)}, u32[]{:S(2)}, u32[]{:S(2)}) collective-permute-start(bf16[512,512]{1,0:T(8,128)(2,1)S(1)} %bitcast.72), channel_id=1, source_target_pairs={{0,6},{2,0},{4,2},{6,4},{1,7},{3,1},{5,3},{7,5},{8,14},{10,8},{12,... | collective-permute-start | bytes 1572872 | tf_op jit(solution)/shard_map/ppermute | solution.py:558
  35.7 13.3 %copy-start.19 = (s32[4]{0:T(128)}, s32[4]{0:T(128)S(1)}, u32[]{:S(2)}) copy-start(s32[4]{0:T(128)S(1)} %get-tuple-element.79) | copy-start | bytes 52
  36.3 15.2 %collective-permute-start.6 = (bf16[512,512]{1,0:T(8,128)(2,1)S(1)}, bf16[512,512]{1,0:T(8,128)(2,1)}, u32[]{:S(2)}, u32[]{:S(2)}) collective-permute-start(bf16[512,512]{1,0:T(8,128)(2,1)S(1)} %bitcast.73), channel_id=1, source_target_pairs={{0,1},{1,0},{2,3},{3,2},{4,5},{5,4},{6,7},{7,6},{8,9},{9,8},{10,11... | collective-permute-start | bytes 1572872 | tf_op jit(solution)/shard_map/ppermute | solution.py:562
  41.6 23.3 %copy-start.2 = (bf16[16,32,512]{2,1,0:T(8,128)(2,1)}, bf16[16,32,512]{2,1,0:T(8,128)(2,1)S(1)}, u32[]{:S(2)}) copy-start(bf16[16,32,512]{2,1,0:T(8,128)(2,1)S(1)} %slice.114) | copy-start | bytes 1572868
  41.6 22.5 %collective-permute-start.4 = (bf16[512,512]{1,0:T(8,128)(2,1)S(1)}, bf16[512,512]{1,0:T(8,128)(2,1)S(1)}, u32[]{:S(2)}, u32[]{:S(2)}) collective-permute-start(bf16[512,512]{1,0:T(8,128)(2,1)S(1)} %bitcast.75), channel_id=1, source_target_pairs={{0,2},{2,4},{4,6},{6,0},{1,3},{3,5},{5,7},{7,1},{8,10},{10,12},{12... | collective-permute-start | bytes 1572872 | tf_op jit(solution)/shard_map/ppermute | solution.py:558
  43.0 21.1 %collective-permute-start.5 = (bf16[512,512]{1,0:T(8,128)(2,1)S(1)}, bf16[512,512]{1,0:T(8,128)(2,1)S(1)}, u32[]{:S(2)}, u32[]{:S(2)}) collective-permute-start(bf16[512,512]{1,0:T(8,128)(2,1)S(1)} %bitcast.76), channel_id=1, source_target_pairs={{0,6},{2,0},{4,2},{6,4},{1,7},{3,1},{5,3},{7,5},{8,14},{10,8},{12,... | collective-permute-start | bytes 1572872 | tf_op jit(solution)/shard_map/ppermute | solution.py:558
  44.5 10.8 %copy-start.7 = (bf16[512,512]{1,0:T(8,128)(2,1)}, bf16[512,512]{1,0:T(8,128)(2,1)S(1)}, u32[]{:S(2)}) copy-start(bf16[512,512]{1,0:T(8,128)(2,1)S(1)} %collective-permute-done.refs_2_) | copy-start | bytes 1572868
  44.5 8.3 %collective-permute-start.7 = (bf16[512,512]{1,0:T(8,128)(2,1)S(1)}, bf16[512,512]{1,0:T(8,128)(2,1)}, u32[]{:S(2)}, u32[]{:S(2)}) collective-permute-start(bf16[512,512]{1,0:T(8,128)(2,1)S(1)} %collective-permute-done.refs_2_), channel_id=1, source_target_pairs={{0,1},{1,0},{2,3},{3,2},{4,5},{5,4},{6,7},{7,6},{8,9},{9,8},{10,11... | collective-permute-start | bytes 1572872 | tf_op jit(solution)/shard_map/ppermute | solution.py:562
  49.0 6.3 %collective-permute-start.8 = (bf16[512,512]{1,0:T(8,128)(2,1)}, bf16[512,512]{1,0:T(8,128)(2,1)}, u32[]{:S(2)}, u32[]{:S(2)}) collective-permute-start(bf16[512,512]{1,0:T(8,128)(2,1)} %collective-permute-done.2.refs_3_), channel_id=1, source_target_pairs={{0,1},{1,0},{2,3},{3,2},{4,5},{5,4},{6,7},{7,6},{8,9},{9,8},{10,11... | collective-permute-start | bytes 1572872 | tf_op jit(solution)/shard_map/ppermute | solution.py:562
  51.5 12.6 %collective-permute-start.1 = (bf16[256,512]{1,0:T(8,128)(2,1)S(1)}, bf16[256,512]{1,0:T(8,128)(2,1)S(1)}, u32[]{:S(2)}, u32[]{:S(2)}) collective-permute-start(bf16[256,512]{1,0:T(8,128)(2,1)S(1)} %slice.112), channel_id=1, source_target_pairs={{0,2},{2,4},{4,6},{6,0},{1,3},{3,5},{5,7},{7,1},{8,10},{10,12},{12... | collective-permute-start | bytes 786440 | tf_op jit(solution)/shard_map/ppermute | solution.py:558
  52.9 11.3 %collective-permute-start.3 = (bf16[256,512]{1,0:T(8,128)(2,1)S(1)}, bf16[256,512]{1,0:T(8,128)(2,1)S(1)}, u32[]{:S(2)}, u32[]{:S(2)}) collective-permute-start(bf16[256,512]{1,0:T(8,128)(2,1)S(1)} %slice.113), channel_id=1, source_target_pairs={{0,6},{2,0},{4,2},{6,4},{1,7},{3,1},{5,3},{7,5},{8,14},{10,8},{12,... | collective-permute-start | bytes 786440 | tf_op jit(solution)/shard_map/ppermute | solution.py:558
  64.1 16.5 %copy-start.5 = (bf16[512,512]{1,0:T(8,128)(2,1)}, bf16[512,512]{1,0:T(8,128)(2,1)S(1)}, u32[]{:S(2)}) copy-start(bf16[512,512]{1,0:T(8,128)(2,1)S(1)} %collective-permute-done.4.refs_2_) | copy-start | bytes 1572868
  64.1 16.5 %copy-start.6 = (bf16[512,512]{1,0:T(8,128)(2,1)}, bf16[512,512]{1,0:T(8,128)(2,1)S(1)}, u32[]{:S(2)}) copy-start(bf16[512,512]{1,0:T(8,128)(2,1)S(1)} %collective-permute-done.5.refs_3_) | copy-start | bytes 1572868
  64.1 6.8 %copy-start.11 = (bf16[256,512]{1,0:T(8,128)(2,1)}, bf16[256,512]{1,0:T(8,128)(2,1)S(1)}, u32[]{:S(2)}) copy-start(bf16[256,512]{1,0:T(8,128)(2,1)S(1)} %collective-permute-done.1.refs_1_) | copy-start | bytes 786436
  64.1 6.8 %copy-start.12 = (bf16[256,512]{1,0:T(8,128)(2,1)}, bf16[256,512]{1,0:T(8,128)(2,1)S(1)}, u32[]{:S(2)}) copy-start(bf16[256,512]{1,0:T(8,128)(2,1)S(1)} %collective-permute-done.3.refs_2_) | copy-start | bytes 786436
  64.2 16.4 %collective-permute-start.12 = (bf16[512,512]{1,0:T(8,128)(2,1)S(1)}, bf16[512,512]{1,0:T(8,128)(2,1)S(1)}, u32[]{:S(2)}, u32[]{:S(2)}) collective-permute-start(bf16[512,512]{1,0:T(8,128)(2,1)S(1)} %collective-permute-done.4.refs_2_), channel_id=1, source_target_pairs={{0,1},{1,0},{2,3},{3,2},{4,5},{5,4},{6,7},{7,6},{8,9},{9,8},{10,11... | collective-permute-start | bytes 1572872 | tf_op jit(solution)/shard_map/ppermute | solution.py:562
  64.8 15.8 %collective-permute-start.13 = (bf16[512,512]{1,0:T(8,128)(2,1)S(1)}, bf16[512,512]{1,0:T(8,128)(2,1)S(1)}, u32[]{:S(2)}, u32[]{:S(2)}) collective-permute-start(bf16[512,512]{1,0:T(8,128)(2,1)S(1)} %collective-permute-done.5.refs_3_), channel_id=1, source_target_pairs={{0,1},{1,0},{2,3},{3,2},{4,5},{5,4},{6,7},{7,6},{8,9},{9,8},{10,11... | collective-permute-start | bytes 1572872 | tf_op jit(solution)/shard_map/ppermute | solution.py:562
  64.8 15.8 %collective-permute-start.11 = (bf16[512,512]{1,0:T(8,128)(2,1)S(1)}, bf16[512,512]{1,0:T(8,128)(2,1)S(1)}, u32[]{:S(2)}, u32[]{:S(2)}) collective-permute-start(bf16[512,512]{1,0:T(8,128)(2,1)S(1)} %bitcast.77), channel_id=1, source_target_pairs={{0,1},{1,0},{2,3},{3,2},{4,5},{5,4},{6,7},{7,6},{8,9},{9,8},{10,11... | collective-permute-start | bytes 1572872 | tf_op jit(solution)/shard_map/ppermute | solution.py:562
  65.3 2.9 %collective-permute-start.14 = (bf16[256,512]{1,0:T(8,128)(2,1)S(1)}, bf16[256,512]{1,0:T(8,128)(2,1)S(1)}, u32[]{:S(2)}, u32[]{:S(2)}) collective-permute-start(bf16[256,512]{1,0:T(8,128)(2,1)S(1)} %collective-permute-done.1.refs_1_), channel_id=1, source_target_pairs={{0,1},{1,0},{2,3},{3,2},{4,5},{5,4},{6,7},{7,6},{8,9},{9,8},{10,11... | collective-permute-start | bytes 786440 | tf_op jit(solution)/shard_map/ppermute | solution.py:562
  65.4 5.5 %collective-permute-start.15 = (bf16[256,512]{1,0:T(8,128)(2,1)S(1)}, bf16[256,512]{1,0:T(8,128)(2,1)S(1)}, u32[]{:S(2)}, u32[]{:S(2)}) collective-permute-start(bf16[256,512]{1,0:T(8,128)(2,1)S(1)} %collective-permute-done.3.refs_2_), channel_id=1, source_target_pairs={{0,1},{1,0},{2,3},{3,2},{4,5},{5,4},{6,7},{7,6},{8,9},{9,8},{10,11... | collective-permute-start | bytes 786440 | tf_op jit(solution)/shard_map/ppermute | solution.py:562
  68.2 2.7 %copy-start.13 = (bf16[256,512]{1,0:T(8,128)(2,1)}, bf16[256,512]{1,0:T(8,128)(2,1)S(1)}, u32[]{:S(2)}) copy-start(bf16[256,512]{1,0:T(8,128)(2,1)S(1)} %collective-permute-done.14.refs_3_) | copy-start | bytes 786436
  68.2 19.5 %collective-permute-start.10 = (bf16[256,512]{1,0:T(8,128)(2,1)S(1)}, bf16[256,512]{1,0:T(8,128)(2,1)S(1)}, u32[]{:S(2)}, u32[]{:S(2)}) collective-permute-start(bf16[256,512]{1,0:T(8,128)(2,1)S(1)} %slice.85), channel_id=1, source_target_pairs={{0,6},{2,0},{4,2},{6,4},{1,7},{3,1},{5,3},{7,5},{8,14},{10,8},{12,... | collective-permute-start | bytes 786440 | tf_op jit(solution)/shard_map/ppermute | solution.py:558
  70.9 0.7 copy-start.14
  70.9 16.8 %collective-permute-start.9 = (bf16[256,512]{1,0:T(8,128)(2,1)S(1)}, bf16[256,512]{1,0:T(8,128)(2,1)S(1)}, u32[]{:S(2)}, u32[]{:S(2)}) collective-permute-start(bf16[256,512]{1,0:T(8,128)(2,1)S(1)} %slice.84), channel_id=1, source_target_pairs={{0,2},{2,4},{4,6},{6,0},{1,3},{3,5},{5,7},{7,1},{8,10},{10,12},{12... | collective-permute-start | bytes 786440 | tf_op jit(solution)/shard_map/ppermute | solution.py:558
  80.6 0.8 copy-start.8
  80.6 1.0 copy-start.9
  80.7 1.1 copy-start.10
  87.7 2.3 copy-start.22
  87.7 2.3 copy-start.23
  87.8 1.9 collective-permute-start.16
  88.5 1.5 collective-permute-start.17
  89.7 0.7 copy-start.24
  90.0 0.7 copy-start.25
  90.7 13.3 %copy-start.20 = (s32[4]{0:T(128)S(1)}, s32[4]{0:T(128)}, u32[]{:S(2)}) copy-start(s32[4]{0:T(128)} %copy-done.19) | copy-start | bytes 52
  103.4 1.7 collective-permute-start.18
  105.1 0.6 copy-start.26
  111.1 19.0 %collective-permute-start.19 = (bf16[4,512,512]{2,1,0:T(8,128)(2,1)}, bf16[4,512,512]{2,1,0:T(8,128)(2,1)S(1)}, u32[]{:S(2)}, u32[]{:S(2)}) collective-permute-start(bf16[4,512,512]{2,1,0:T(8,128)(2,1)} %out_terms.3), channel_id=1, source_target_pairs={{0,1},{1,0},{2,3},{3,2},{4,5},{5,4},{6,7},{7,6},{8,9},{9,8},{10,11... | collective-permute-start | bytes 6291464 | tf_op jit(solution)/shard_map/ppermute | solution.py:562
  118.1 14.5 %collective-permute-start.24 = (bf16[4,528,512]{2,1,0:T(8,128)(2,1)}, bf16[4,528,512]{2,1,0:T(8,128)(2,1)S(1)}, u32[]{:S(2)}, u32[]{:S(2)}) collective-permute-start(bf16[4,528,512]{2,1,0:T(8,128)(2,1)} %input_terms.3), channel_id=1, source_target_pairs={{0,1},{1,0},{2,3},{3,2},{4,5},{5,4},{6,7},{7,6},{8,9},{9,8},{10,11... | collective-permute-start | bytes 6488072 | tf_op jit(solution)/shard_map/ppermute | solution.py:562
  130.2 2.5 copy-start.4
  133.3 8.8 %collective-permute-start.25 = (bf16[256,512]{1,0:T(8,128)(2,1)S(1)}, bf16[256,512]{1,0:T(8,128)(2,1)S(1)}, u32[]{:S(2)}, u32[]{:S(2)}) collective-permute-start(bf16[256,512]{1,0:T(8,128)(2,1)S(1)} %get-tuple-element.80), channel_id=1, source_target_pairs={{0,2},{2,4},{4,6},{6,0},{1,3},{3,5},{5,7},{7,1},{8,10},{10,12},{12... | collective-permute-start | bytes 786440 | tf_op jit(solution)/shard_map/ppermute | solution.py:558
  133.5 17.3 %collective-permute-start.20 = (bf16[256,512]{1,0:T(8,128)(2,1)S(1)}, bf16[256,512]{1,0:T(8,128)(2,1)S(1)}, u32[]{:S(2)}, u32[]{:S(2)}) collective-permute-start(bf16[256,512]{1,0:T(8,128)(2,1)S(1)} %get-tuple-element.86), channel_id=1, source_target_pairs={{0,2},{2,4},{4,6},{6,0},{1,3},{3,5},{5,7},{7,1},{8,10},{10,12},{12... | collective-permute-start | bytes 786440 | tf_op jit(solution)/shard_map/ppermute | solution.py:558
  134.3 16.4 %collective-permute-start.22 = (bf16[256,512]{1,0:T(8,128)(2,1)S(1)}, bf16[256,512]{1,0:T(8,128)(2,1)S(1)}, u32[]{:S(2)}, u32[]{:S(2)}) collective-permute-start(bf16[256,512]{1,0:T(8,128)(2,1)S(1)} %get-tuple-element.87), channel_id=1, source_target_pairs={{0,6},{2,0},{4,2},{6,4},{1,7},{3,1},{5,3},{7,5},{8,14},{10,8},{12,... | collective-permute-start | bytes 786440 | tf_op jit(solution)/shard_map/ppermute | solution.py:558
  136.3 12.2 %collective-permute-start.27 = (bf16[272,512]{1,0:T(8,128)(2,1)S(1)}, bf16[272,512]{1,0:T(8,128)(2,1)S(1)}, u32[]{:S(2)}, u32[]{:S(2)}) collective-permute-start(bf16[272,512]{1,0:T(8,128)(2,1)S(1)} %get-tuple-element.83), channel_id=1, source_target_pairs={{0,6},{2,0},{4,2},{6,4},{1,7},{3,1},{5,3},{7,5},{8,14},{10,8},{12,... | collective-permute-start | bytes 835592 | tf_op jit(solution)/shard_map/ppermute | solution.py:558
  142.2 17.0 %collective-permute-start.26 = (bf16[528,512]{1,0:T(8,128)(2,1)S(1)}, bf16[528,512]{1,0:T(8,128)(2,1)S(1)}, u32[]{:S(2)}, u32[]{:S(2)}) collective-permute-start(bf16[528,512]{1,0:T(8,128)(2,1)S(1)} %pad_maximum_fusion), channel_id=1, source_target_pairs={{0,2},{2,4},{4,6},{6,0},{1,3},{3,5},{5,7},{7,1},{8,10},{10,12},{12... | collective-permute-start | bytes 1622024 | tf_op jit(solution)/shard_map/ppermute | solution.py:558
  148.6 5.2 %copy-start.15 = (f32[512,128]{1,0:T(8,128)S(1)}, f32[512,128]{1,0:T(8,128)}, u32[]{:S(2)}) copy-start(f32[512,128]{1,0:T(8,128)} %get-tuple-element.65.refs_14_) | copy-start | bytes 786436
  148.6 12.5 %collective-permute-start.28 = (bf16[528,512]{1,0:T(8,128)(2,1)S(1)}, bf16[528,512]{1,0:T(8,128)(2,1)S(1)}, u32[]{:S(2)}, u32[]{:S(2)}) collective-permute-start(bf16[528,512]{1,0:T(8,128)(2,1)S(1)} %pad_maximum_fusion.1), channel_id=1, source_target_pairs={{0,6},{2,0},{4,2},{6,4},{1,7},{3,1},{5,3},{7,5},{8,14},{10,8},{12,... | collective-permute-start | bytes 1622024 | tf_op jit(solution)/shard_map/ppermute | solution.py:558
  150.9 21.4 %copy-start.1 = (bf16[16,32,512]{2,1,0:T(8,128)(2,1)S(1)}, bf16[16,32,512]{2,1,0:T(8,128)(2,1)}, u32[]{:S(2)}) copy-start(bf16[16,32,512]{2,1,0:T(8,128)(2,1)} %copy-done) | copy-start | bytes 1572868
  150.9 21.4 %copy-start.3 = (bf16[16,32,512]{2,1,0:T(8,128)(2,1)S(1)}, bf16[16,32,512]{2,1,0:T(8,128)(2,1)}, u32[]{:S(2)}) copy-start(bf16[16,32,512]{2,1,0:T(8,128)(2,1)} %copy-done.2) | copy-start | bytes 1572868
  151.0 19.5 %collective-permute-start.21 = (bf16[512,512]{1,0:T(8,128)(2,1)S(1)}, bf16[512,512]{1,0:T(8,128)(2,1)S(1)}, u32[]{:S(2)}, u32[]{:S(2)}) collective-permute-start(bf16[512,512]{1,0:T(8,128)(2,1)S(1)} %pad_maximum_fusion.3), channel_id=1, source_target_pairs={{0,2},{2,4},{4,6},{6,0},{1,3},{3,5},{5,7},{7,1},{8,10},{10,12},{12... | collective-permute-start | bytes 1572872 | tf_op jit(solution)/shard_map/ppermute | solution.py:558
  151.1 21.2 %collective-permute-start.23 = (bf16[512,512]{1,0:T(8,128)(2,1)S(1)}, bf16[512,512]{1,0:T(8,128)(2,1)S(1)}, u32[]{:S(2)}, u32[]{:S(2)}) collective-permute-start(bf16[512,512]{1,0:T(8,128)(2,1)S(1)} %pad_maximum_fusion.4), channel_id=1, source_target_pairs={{0,6},{2,0},{4,2},{6,4},{1,7},{3,1},{5,3},{7,5},{8,14},{10,8},{12,... | collective-permute-start | bytes 1572872 | tf_op jit(solution)/shard_map/ppermute | solution.py:558
  173.7 22.6 %copy-start.18 = (s32[16]{0:T(128)S(1)}, s32[16]{0:T(128)}, u32[]{:S(2)}) copy-start(s32[16]{0:T(128)} %plan_ref.3) | copy-start | bytes 196
  191.0 14.5 %all-to-all-start.3 = ((bf16[16,32,512]{2,1,0:T(8,128)(2,1)}), bf16[16,32,512]{2,1,0:T(8,128)(2,1)S(1)}, u32[]{:S(2)}, u32[]{:S(2)}) async-start(bf16[16,32,512]{2,1,0:T(8,128)(2,1)} %bitcast.28), calls=%async_computation.3 | async-start | bytes 1048576 | tf_op jit(solution)/shard_map/all_to_all | solution.py:592
Sparse Core Ops, SparseCore 0:
  104.8 128.4 all-reduce.3

commit v5 on v4

--- a/solution.py
+++ b/solution.py
@@ -15,6 +15,7 @@
 STEPS = (0, -1, 1, 2)
 BF = jnp.bfloat16
 F32 = jnp.float32
+COSTLY = 40
 VMEM_LIMIT = 56 * 1024 * 1024
 
 
@@ -335,9 +336,9 @@
 def back_kernel(*refs, scale):
     idx_ref, pieces = refs[0], refs[1:5]
     inputs = refs[5:16]
-    grad_ref, dots_ref, gq_ref, gk_ref, gv_ref = refs[16:21]
-    buffer, held, scaled_ref, gq, gk, gv, sems = refs[21:28]
-    targets = refs[28:]
+    grad_ref, dots_ref, gq_ref, gkv_ref = refs[16:20]
+    buffer, held, scaled_ref, gq, gkv, sems = refs[20:26]
+    targets = refs[26:]
     wo_ref, near_ref, far_turned, near_turned = inputs[:4]
     copies = Copies(sems)
     arrivals = fetch_far(copies, pieces, buffer)
@@ -348,10 +349,10 @@
     acc_ref, turned_ref = targets[:2]
     acc_copy = copies.start(near_ref, acc_ref)
     loads = [copies.start(source, target) for source, target in zip(inputs[4:], targets[2:])]
+    tall = 2 * width
     turned_loads = [
-        copies.start(near_turned, turned_ref.at[:3]),
-        copies.start(far_turned, turned_ref.at[3:]),
-    ]
+        copies.start(near_turned.at[n], turned_ref.at[n * tall : (n + 1) * tall]) for n in range(3)
+    ] + [copies.start(far_turned.at[0], turned_ref.at[3 * tall :])]
     q_ref, k_ref, k_turned_ref, v_ref, shares_ref, inverse_ref, rotary_ref = targets[2:]
     acc_copy.wait()
     for n in range(2):
@@ -375,17 +376,6 @@
         cols = slice(at * HD, (at + 1) * HD)
         grad_ref[:, cols] = grad.astype(BF)
         scaled_ref[:, cols] = (grad * factor).astype(BF)
-
-    parts = turned_ref.shape[0]
-    outs = []
-
-    def send(held_ref, out_ref, at):
-        tall = turned_ref.shape[1]
-        wide = held_ref.shape[2]
-        for j in range(parts):
-            held_ref[j] = nn(turned_ref[j], scaled_ref[:, at : at + wide]).astype(BF)
-            start = pl.multiple_of(idx_ref[j] * width, tall)
-            outs.append(copies.start(held_ref.at[j], out_ref.at[pl.ds(start, tall)]))
 
     key_grad = jnp.zeros((rows, HD), F32)
     value_grad = jnp.zeros((rows, HD), F32)
@@ -407,16 +397,19 @@
     emit(heads + 1, value_grad)
     for copy in turned_loads:
         copy.wait()
-    send(gq, gq_ref, 0)
-    kv = gk.shape[2]
-    for j in range(parts):
-        both = nn(turned_ref[j], scaled_ref[:, heads * HD :]).astype(BF)
-        gk[j] = both[:, :kv]
-        gv[j] = both[:, kv:]
-        tall = turned_ref.shape[1]
+    outs = []
+    q_cols = gq.shape[2]
+    share = gkv.shape[2]
+    for j in range(4):
+        gq[j] = nn(turned_ref[j * tall : (j + 1) * tall], scaled_ref[:, :q_cols]).astype(BF)
         start = pl.multiple_of(idx_ref[j] * width, tall)
-        outs.append(copies.start(gk.at[j], gk_ref.at[pl.ds(start, tall)]))
-        outs.append(copies.start(gv.at[j], gv_ref.at[pl.ds(start, tall)]))
+        outs.append(copies.start(gq.at[j], gq_ref.at[pl.ds(start, tall)]))
+    for first in range(4):
+        for n in range(4):
+            at = (idx_ref[5 + first] * 4 + idx_ref[9 + n]) * share
+            block = turned_ref[pl.ds(pl.multiple_of(at, share), share)]
+            gkv[first, n] = nn(block, scaled_ref[:, q_cols:]).astype(BF)
+        outs.append(copies.start(gkv.at[first], gkv_ref.at[first]))
     dots_ref[...] = lax.dot_general(
         jnp.ones((8, HD), F32), products, (((1,), (1,)), ((), ())),
         preferred_element_type=F32, precision=lax.Precision.HIGHEST,
@@ -434,25 +427,27 @@
     inputs = (wo, near, far_turned, near_turned, q, k, k_turned, v, shares, inverse, rotary)
     loaded = (q, k, k_turned, v, shares, inverse, rotary)
     weight_shapes = [
-        jax.ShapeDtypeStruct((features, w), BF) for w in (cols, kv_cols, kv_cols)
+        jax.ShapeDtypeStruct((features, cols), BF),
+        jax.ShapeDtypeStruct((4, 4, features // 16, 2 * kv_cols), BF),
     ]
     shapes = [jax.ShapeDtypeStruct(grad_shape, BF), jax.ShapeDtypeStruct((8, rows), F32)]
     return pl.pallas_call(
         functools.partial(back_kernel, scale=scale),
         grid=(1,),
         in_specs=[SMEM_SPEC] + [HBM_SPEC] * 15,
-        out_specs=[whole(a.shape) for a in shapes] + [HBM_SPEC] * 3,
+        out_specs=[whole(a.shape) for a in shapes] + [HBM_SPEC] * 2,
         out_shape=shapes + weight_shapes,
         scratch_shapes=[
             pltpu.VMEM((2, rows, width), BF),
             pltpu.VMEM((2, cols, width), BF),
             pltpu.VMEM(grad_shape, BF),
         ]
-        + [pltpu.VMEM((4, features // 4, w.shape[1]), BF) for w in weight_shapes]
         + [
+            pltpu.VMEM((4, features // 4, cols), BF),
+            pltpu.VMEM(weight_shapes[1].shape, BF),
             pltpu.SemaphoreType.DMA((40,)),
             pltpu.VMEM(near.shape, F32),
-            pltpu.VMEM((4, features // 4, rows), BF),
+            pltpu.VMEM((features, rows), BF),
         ]
         + [pltpu.VMEM(a.shape, a.dtype) for a in loaded],
         compiler_params=params(),
@@ -464,57 +459,73 @@
     )(idx, *pieces, *inputs)
 
 
+def sum_wide(chunks, axis):
+    total = chunks[0].astype(F32)
+    for n, step in ((1, -1), (2, 1), (3, 2)):
+        total = total + shift(chunks[n], step, axis).astype(F32)
+    return total
+
+
+def sum_direct(chunks, axis):
+    return sum_wide(chunks, axis).astype(BF)
+
+
+def spread_direct(piece, axis):
+    return [piece, shift(piece, 1, axis), shift(piece, -1, axis), shift(piece, 2, axis)]
+
+
+def assemble_kernel(*refs):
+    idx_ref, pieces, k_ref, v_ref = refs[0], refs[1:5], refs[5], refs[6]
+    share = pieces[0].shape[1]
+    kv = k_ref.shape[1]
+    for first in range(4):
+        for n in range(4):
+            owner = idx_ref[5 + first] * 4 + idx_ref[9 + n]
+            row = idx_ref[owner // 4] * 2 * share + owner % 4 * share
+            rows = pl.ds(pl.multiple_of(row, share), share)
+            k_ref[rows] = pieces[first][n, :, :kv]
+            v_ref[rows] = pieces[first][n, :, kv:]
+
+
+def assemble(idx, pieces, features, kv):
+    return pl.pallas_call(
+        assemble_kernel,
+        grid=(1,),
+        in_specs=[SMEM_SPEC] + [whole(a.shape) for a in pieces],
+        out_specs=[whole((features, kv))] * 2,
+        out_shape=[jax.ShapeDtypeStruct((features, kv), BF)] * 2,
+        compiler_params=params(),
+        cost_estimate=cost(0, 8 * features * kv),
+        name="assemble",
+    )(idx, *pieces)
+
+
 def finish_kernel(*refs):
-    for source, target in zip(refs[:3], refs[3:]):
-        target[...] = source[...]
-
-
-def finish(arrays):
+    refs[-1][...] = refs[-2][...]
+
+
+def finish(after, array):
     parts = 4
-    specs = [pl.BlockSpec((a.shape[0] // parts, a.shape[1]), lambda j: (j, 0)) for a in arrays]
+    spec = pl.BlockSpec((array.shape[0] // parts, array.shape[1]), lambda j: (j, 0))
     return pl.pallas_call(
         finish_kernel,
         grid=(parts,),
-        in_specs=specs,
-        out_specs=specs,
-        out_shape=[jax.ShapeDtypeStruct(a.shape, a.dtype) for a in arrays],
-        compiler_params=params(),
-        cost_estimate=cost(0, 4 * sum(a.size for a in arrays)),
+        in_specs=[HBM_SPEC] * len(after) + [spec],
+        out_specs=spec,
+        out_shape=jax.ShapeDtypeStruct(array.shape, array.dtype),
+        compiler_params=params(),
+        cost_estimate=cost(0, 4 * array.size),
         name="finish",
-    )(*arrays)
-
-
-def out_term_kernel(idx_ref, _, attended_ref, wo_ref, out_ref):
-    out_ref[0] = nn(attended_ref[...], wo_ref[...]).astype(BF)
-
-
-def out_terms(idx, after, attended, wo, width):
-    rows, cols = attended.shape
-    parts = 4
-    grid_spec = pltpu.PrefetchScalarGridSpec(
-        num_scalar_prefetch=1,
-        grid=(parts,),
-        in_specs=[
-            HBM_SPEC,
-            pl.BlockSpec((rows, cols), lambda j, idx: (0, 0)),
-            pl.BlockSpec((cols, width), lambda j, idx: (0, idx[j])),
-        ],
-        out_specs=pl.BlockSpec((1, rows, width), lambda j, idx: (j, 0, 0)),
-    )
-    return pl.pallas_call(
-        out_term_kernel,
-        grid_spec=grid_spec,
-        out_shape=jax.ShapeDtypeStruct((parts, rows, width), BF),
-        compiler_params=params(),
-        cost_estimate=cost(40 * parts * rows * cols * width, 40 * parts * width * (rows + cols)),
-        name="out_terms",
-    )(idx, after, attended, wo)
-
-
-def input_term_kernel(idx_ref, _, grad_ref, dots_ref, wq_ref, wk_ref, wv_ref, out_ref):
+    )(*after, array)
+
+
+def term_kernel(
+    idx_ref, _, attended_ref, wo_ref, grad_ref, dots_ref, wq_ref, wk_ref, wv_ref, out_ref
+):
     q_cols = wq_ref.shape[1]
     kv_cols = wk_ref.shape[1]
     rows = grad_ref.shape[0]
+    out_ref[0, :rows] = nn(attended_ref[...], wo_ref[...]).astype(BF)
     dots = dots_ref[0:1, :]
     high = dots.astype(BF).astype(F32)
     line = lax.broadcasted_iota(jnp.int32, (16, dots.shape[1]), 0)
@@ -522,35 +533,37 @@
     term = nt(grad_ref[:, :q_cols], wq_ref[...])
     term += nt(grad_ref[:, q_cols : q_cols + kv_cols], wk_ref[...])
     term += nt(grad_ref[:, q_cols + kv_cols :], wv_ref[...])
-    out_ref[0, :rows] = term.astype(BF)
-    out_ref[0, rows:] = extra.astype(BF)
-
-
-def input_terms(idx, after, grad, dots, wq, wk, wv, width):
+    out_ref[0, rows : 2 * rows] = term.astype(BF)
+    out_ref[0, 2 * rows :] = extra.astype(BF)
+
+
+def terms(idx, after, attended, wo, grad, dots, wq, wk, wv, width):
     rows, cols = grad.shape
+    heads = attended.shape[1]
     parts = 4
     grid_spec = pltpu.PrefetchScalarGridSpec(
         num_scalar_prefetch=1,
         grid=(parts,),
         in_specs=[
             HBM_SPEC,
+            pl.BlockSpec((rows, heads), lambda j, idx: (0, 0)),
+            pl.BlockSpec((heads, width), lambda j, idx: (0, idx[j])),
             pl.BlockSpec((rows, cols), lambda j, idx: (0, 0)),
             pl.BlockSpec(dots.shape, lambda j, idx: (0, 0)),
         ]
-        + [
-            pl.BlockSpec((width, w.shape[1]), lambda j, idx: (idx[j], 0))
-            for w in (wq, wk, wv)
-        ],
-        out_specs=pl.BlockSpec((1, rows + 16, width), lambda j, idx: (j, 0, 0)),
-    )
-    return pl.pallas_call(
-        input_term_kernel,
+        + [pl.BlockSpec((width, w.shape[1]), lambda j, idx: (idx[j], 0)) for w in (wq, wk, wv)],
+        out_specs=pl.BlockSpec((1, 2 * rows + 16, width), lambda j, idx: (j, 0, 0)),
+    )
+    return pl.pallas_call(
+        term_kernel,
         grid_spec=grid_spec,
-        out_shape=jax.ShapeDtypeStruct((parts, rows + 16, width), BF),
-        compiler_params=params(),
-        cost_estimate=cost(40 * parts * rows * cols * width, 40 * parts * width * (rows + cols)),
-        name="input_terms",
-    )(idx, after, grad, dots, wq, wk, wv)
+        out_shape=jax.ShapeDtypeStruct((parts, 2 * rows + 16, width), BF),
+        compiler_params=params(),
+        cost_estimate=cost(
+            COSTLY * parts * rows * (cols + heads) * width, COSTLY * parts * width * (rows + cols)
+        ),
+        name="terms",
+    )(idx, after, attended, wo, grad, dots, wq, wk, wv)
 
 
 def shift(array, step, axis="y"):
@@ -576,16 +589,8 @@
     return tuple(pieces) + tuple(swap(a) for a in pieces)
 
 
-def sum_pieces(mine_terms, other_terms):
-    wide = lambda a: a.astype(F32)
-    sums = (wide(mine_terms) + wide(swap(other_terms))).astype(BF)
-    rows = sums.shape[1]
-    half = rows // 32 * 16
-    relay_top = shift(sums[3, :half], 1)
-    relay_end = shift(sums[3, half:], -1)
-    up = jnp.concatenate([(wide(sums[2, :half]) + wide(relay_top)).astype(BF), sums[2, half:]], axis=0)
-    down = jnp.concatenate([sums[1, :half], (wide(sums[1, half:]) + wide(relay_end)).astype(BF)], axis=0)
-    return wide(sums[0]) + wide(shift(up, 1)) + wide(shift(down, -1))
+def add_cores(mine_terms, other_terms):
+    return (mine_terms.astype(F32) + swap(other_terms).astype(F32)).astype(BF)
 
 
 def exchange(panels):
@@ -642,20 +647,28 @@
     cot_near, shares = lax.optimization_barrier((both_cores(cot_near), shares))
     near = back_near(idx, cot_near, wo)
     cot_far, near = lax.optimization_barrier((cot_far, near))
-    grad, dots, *grads = back(
+    grad, dots, grad_q, grad_kv = back(
         idx, both_cores(cot_far), wo, near, far_turned, near_turned, q, k, k_turned, v, shares,
         inverse, rotary, scale,
     )
-    grad_query, grad_key, grad_value = finish(lax.psum(tuple(grads), ("x", "z")))
+    grad_query = lax.psum(grad_q, ("x", "z"))
+    tie = lax.optimization_barrier
+
     after = swap(dots)
+    grad_kv = sum_direct(grad_kv, "x")
     idx_mine, idx_other = around * cores + core, around * cores + (1 - core)
-    out_sum = sum_pieces(
-        *[out_terms(i, after, attended, wo, width) for i in (idx_mine, idx_other)]
-    )
-    output_rows = (here_tokens.astype(F32) + out_sum).astype(BF)
-    in_sum = sum_pieces(
-        *[input_terms(i, after, grad, dots, wq, wk, wv, width) for i in (idx_mine, idx_other)]
-    )
+    sums = add_cores(
+        *[terms(i, after, attended, wo, grad, dots, wq, wk, wv, width) for i in (idx_mine, idx_other)]
+    )
+    grad_kv, sums = tie((grad_kv, sums))
+    grad_kv = sum_direct(grad_kv, "z")
+    sums = sum_wide(sums, "y")
+    grad_kv, sums = tie((grad_kv, sums))
+    grad_kv = jnp.stack(spread_direct(grad_kv, "z"))
+    grad_key, grad_value = assemble(idx, spread_direct(grad_kv, "x"), features, wk.shape[1])
+
+    output_rows = (here_tokens.astype(F32) + sums[:rows]).astype(BF)
+    in_sum = sums[rows:]
     inverse = inverse[:, 0:1]
     mean_term = ((in_sum[rows] + in_sum[rows + 1]) / features)[:, None]
     own = y * cores + core
@@ -665,8 +678,10 @@
     grad_rows = grad_rows.astype(BF)
 
     targets = panel_plan // count
-    output = exchange(output_rows.reshape(dp, panel, width))[targets].reshape(rows, width)
-    grad_tokens = exchange(grad_rows.reshape(dp, panel, width))[targets].reshape(rows, width)
+    both = jnp.concatenate([output_rows, grad_rows], axis=1).reshape(dp, panel, 2 * width)
+    both = exchange(both)[targets].reshape(rows, 2 * width)
+    output, grad_tokens = both[:, :width], both[:, width:]
+    grad_query = finish((output, grad_tokens, grad_key), grad_query)
     return output, grad_tokens, grad_query, grad_key, grad_value
 
 

time: 247 us -> 286 us (1.16)
  waiting for transfers between devices: 75.2 us -> 114 us
  blocking collectives: 17.4 us -> 0 us
  starting transfers between devices: 49.4 us -> 63.6 us
  Pallas kernels: 70.4 us -> 64.9 us
  local copies, waits for them, and re-layouts: 10 us -> 14.5 us
  other arithmetic: 8.89 us -> 12.9 us
    ppermute x16 -> x23, waiting for transfers between devices: 28.7 us -> 103 us  [shift(): lax.ppermute(array, axis, [(i, (i + step) % size) for i in range(size)])]
    psum x1, waiting for transfers between devices: 26.4 us -> 0.01 us  [per_device(): grad_query = lax.psum(grad_q, ('x', 'z'))]
    all_to_all x1 -> x0, blocking collectives: 17.4 us -> none  [exchange(): lax.all_to_all(panels, ('x', 'z'), split_axis=0, concat_axis=0, tiled=True)]
    ppermute x16 -> x23, starting transfers between devices: 20.5 us -> 33.6 us  [shift(): lax.ppermute(array, axis, [(i, (i + step) % size) for i in range(size)])]
    all_to_all x3, waiting for transfers between devices: 17.6 us -> 9.18 us  [exchange(): lax.all_to_all(panels, ('x', 'z'), split_axis=0, concat_axis=0, tiled=True)]
    pallas_call x5 -> x4, Pallas kernels: 29.9 us -> 24.6 us  [the longest x2 16.6 us: terms(): pl.pallas_call(term_kernel, grid_spec=grid_spec, out_shape=jax.ShapeDtype...]
    squeeze x3, local copies, waits for them, and re-layouts: 0.17 us -> 3.75 us  [sum_wide(): total = total + shift(chunks[n], step, axis).astype(F32)]
    ppermute x13 -> x12, starting transfers between devices: 11.5 us -> 12.1 us  [swap(): return lax.ppermute(array, 'core', [(0, 1), (1, 0)])]
  transfers between devices with their start and end apart: 33 -> 39, of which waited for: 14 -> 16; matrix products, arithmetic and copies ran while one was open for 6% -> 8% of each run, Pallas kernels for 20% -> 16%
where the time goes in v5:
time: 286 us; the launch traced here: 284 us
  waiting for transfers between devices  114 us (40%)
  Pallas kernels  64.9 us (23%)
  starting transfers between devices  63.6 us (22%)
  between operations  14.6 us (5%)
  local copies, waits for them, and re-layouts  14.5 us (5%)
  other arithmetic  12.9 us (5%)
    ppermute x23, waiting for transfers between devices, shift(): lax.ppermute(array, axis, [(i, (i + step) % size) for i in range(size)])  103 us
    ppermute x23, starting transfers between devices, shift(): lax.ppermute(array, axis, [(i, (i + step) % size) for i in range(size)])  33.6 us
    all_to_all x3, starting transfers between devices, exchange(): lax.all_to_all(panels, ('x', 'z'), split_axis=0, concat_axis=0, tiled=True)  17.9 us
    pallas_call x2, Pallas kernels, terms(): pl.pallas_call(term_kernel, grid_spec=grid_spec, out_shape=jax.ShapeDtype...  16.6 us
    pallas_call x1, Pallas kernels, back(): pl.pallas_call(functools.partial(back_kernel, scale=scale), grid=(1,), in...  12.3 us
    ppermute x12, starting transfers between devices, swap(): return lax.ppermute(array, 'core', [(0, 1), (1, 0)])  12.1 us
    all_to_all x3, waiting for transfers between devices, exchange(): lax.all_to_all(panels, ('x', 'z'), split_axis=0, concat_axis=0, tiled=True)  9.18 us
    pallas_call x1, Pallas kernels, attend(): pl.pallas_call(attend_kernel, grid=(1,), in_specs=[SMEM_SPEC] + [HBM_SPEC...  8.98 us
  transfers between devices with their start and end apart: 39, of which 16 were waited for; matrix products, arithmetic and copies ran while one was open for 8% of the time, Pallas kernels for 16%

profile of v5, /device:TPU:1, one launch (start us, length us, event | category | flops | bytes accessed | tf_op | source)
XLA Modules:
  0.0 284.2 jit_solution(14574107741574418819)
XLA Ops:
  7.2 1.9 place.1
  9.1 8.6 %all-to-all-start = ((bf16[16,32,512]{2,1,0:T(8,128)(2,1)}), bf16[16,32,512]{2,1,0:T(8,128)(2,1)S(1)}, u32[]{:S(2)}, u32[]{:S(2)}) async-start(bf16[16,32,512]{2,1,0:T(8,128)(2,1)} %place.1), calls=%async_computation | async-start | bytes 1048576 | tf_op jit(solution)/shard_map/all_to_all | solution.py:597
  17.7 1.6 reshape_reshape.4.docs_ref
  19.3 2.2 place_meta.1
  21.5 6.5 %all-to-all-done = bf16[16,32,512]{2,1,0:T(8,128)(2,1)S(1)} async-done(((bf16[16,32,512]{2,1,0:T(8,128)(2,1)}), bf16[16,32,512]{2,1,0:T(8,128)(2,1)S(1)}, u32[]{:S(2)}, u32[]{:S(2)}) %all-to-all-start) | async-done | bytes 524320 | tf_op jit(solution)/shard_map/all_to_all | solution.py:597
  28.0 3.6 %all-to-all-start.1 = ((bf16[16,32,640]{2,1,0:T(8,128)(2,1)}), bf16[16,32,640]{2,1,0:T(8,128)(2,1)S(1)}, u32[]{:S(2)}, u32[]{:S(2)}) async-start(bf16[16,32,640]{2,1,0:T(8,128)(2,1)} %place_meta.1), calls=%async_computation.1 | async-start | bytes 1310720 | tf_op jit(solution)/shard_map/all_to_all | solution.py:597
  31.6 1.4 collective-permute-start
  33.6 1.5 collective-permute-start.2
  36.2 2.6 collective-permute-start.6
  38.8 2.7 all-to-all-done.1
  41.6 1.4 collective-permute-start.4
  42.9 1.5 collective-permute-start.5
  44.5 4.4 %collective-permute-start.7 = (bf16[512,512]{1,0:T(8,128)(2,1)S(1)}, bf16[512,512]{1,0:T(8,128)(2,1)}, u32[]{:S(2)}, u32[]{:S(2)}) collective-permute-start(bf16[512,512]{1,0:T(8,128)(2,1)S(1)} %collective-permute-done.refs_2_), channel_id=1, source_target_pairs={{0,1},{1,0},{2,3},{3,2},{4,5},{5,4},{6,7},{7,6},{8,9},{9,8},{10,11... | collective-permute-start | bytes 1572872 | tf_op jit(solution)/shard_map/ppermute | solution.py:575
  49.0 0.9 collective-permute-start.8
  50.5 1.0 slice.119
  51.5 1.4 collective-permute-start.1
  52.8 1.4 collective-permute-start.3
  54.3 1.0 multiply_cosine_fusion
  55.3 8.8 %project_near.1 = (bf16[3,1024,512]{2,1,0:T(8,128)(2,1)}, f32[512,768]{1,0:T(8,128)}, f32[512,128]{1,0:T(8,128)}) custom-call(s32[13]{0:T(128)} %pad_add_fusion.refs_0_, bf16[512,512]{1,0:T(8,128)(2,1)} %bitcast.57, bf16[512,512]{1,0:T(8,128)(2,1)} %copy-done.8, bf16[512,512]{1,0:T(8,128)(2,1)} %collective-permute-done.2.refs_3_, ...), custom_call_target="tpu_custom_call" | custom-call | flops 2415919104 | bytes 11010048 | tf_op jit(solution)/shard_map/project_near/pallas_call | solution.py:189
  66.7 0.8 pad_maximum_fusion.1.refs_11_.refs_15_
  67.5 0.7 collective-permute-done.14.refs_3_
  68.2 1.3 collective-permute-start.9
  69.5 1.8 collective-permute-start.10
  71.3 9.0 %attend.1 = (bf16[1,1024,512]{2,1,0:T(8,128)(2,1)}, f32[512,128]{1,0:T(8,128)}, bf16[512,512]{1,0:T(8,128)(2,1)}, bf16[512,128]{1,0:T(8,128)(2,1)}, bf16[128,512...) custom-call(s32[13]{0:T(128)} %pad_add_fusion.refs_0_, ...), custom_call_target="tpu_custom_call" | custom-call | flops 1342177280 | bytes 3670016 | tf_op jit(solution)/shard_map/attend/pallas_call | solution.py:275
  80.4 0.7 copy-done.9
  81.5 6.1 %back_near.1.refs_6_ = f32[512,512]{1,0:T(8,128)} custom-call(s32[13]{0:T(128)} %pad_add_fusion.refs_0_, bf16[512,512]{1,0:T(8,128)(2,1)} %bitcast.61, bf16[512,512]{1,0:T(8,128)(2,1)} %copy-done.6, bf16[512,512]{1,0:T(8,128)(2,1)} %copy-done.7, bf16[512,512]{1,0:T(8,128)(2,1)} %copy-done.9, bf16[512,512]{1,0:T(8,128)(2,1)} %copy-done.10, ...), custom_call_target="tpu_custom_call" | custom-call | flops 1610612736 | bytes 6291456 | tf_op jit(solution)/shard_map/back_near/pallas_call | solution.py:319
  87.6 0.7 collective-permute-start.16
  90.6 12.3 %back.1 = (bf16[512,768]{1,0:T(8,128)(2,1)}, f32[8,512]{1,0:T(8,128)}, bf16[4096,512]{1,0:T(8,128)(2,1)}, bf16[4,4,256,256]{3,2,1,0:T(8,128)(2,1)}) custom-call(s32[13]{0:T(128)} %pad_add_fusion.refs_0_, bf16[256,512]{1,0:T(8,128)(2,1)} %copy-done.25, bf16[256,512]{1,0:T(8,128)(2,1)} %copy-done.26, bf16[256,512]{1,0:T(8,128)(2,1)} %copy-done.27, ...), custom_call_target="tpu_custom_call" | custom-call | flops 4831838208 | bytes 8388608 | tf_op jit(solution)/shard_map/back/pallas_call | solution.py:434
  103.0 0.7 collective-permute-start.21
  103.6 1.5 slice_bitcast_fusion.5
  105.1 4.2 %collective-permute-start.20 = (bf16[4,256,256]{2,1,0:T(8,128)(2,1)S(1)}, bf16[4,256,256]{2,1,0:T(8,128)(2,1)S(1)}, u32[]{:S(2)}, u32[]{:S(2)}) collective-permute-start(bf16[4,256,256]{2,1,0:T(8,128)(2,1)S(1)} %get-tuple-element.87), channel_id=1, source_target_pairs={{0,64},{32,96},{64,0},{96,32},{1,65},{33,97},{65,1},{97,33},{2,66}... | collective-permute-start | bytes 1572872 | tf_op jit(solution)/shard_map/ppermute | solution.py:571
  109.3 2.6 collective-permute-start.18
  112.6 8.3 %terms.3 = bf16[4,1040,512]{2,1,0:T(8,128)(2,1)} custom-call(s32[4]{0:T(128)} %broadcast_add_fusion.idx_ref, f32[8,512]{1,0:T(8,128)} %copy-done.29, bf16[512,512]{1,0:T(8,128)(2,1)} %get-tuple-element.70.attended_ref, bf16[512,4096]{1,0:T(8,128)(2,1)} %wo_ref.3, bf16[512,768]{1,0:T(8,128)(2,1)} %get-tuple-element.71.grad_ref, ...), custom_call_target="tpu_custom_call" | custom-call | flops 53687091200 | bytes 104857600 | tf_op jit(solution)/shard_map/terms/pallas_call | solution.py:557
  120.9 1.0 collective-permute-start.22
  121.9 8.3 %terms.2 = bf16[4,1040,512]{2,1,0:T(8,128)(2,1)} custom-call(s32[4]{0:T(128)} %get-tuple-element.79.idx_ref, f32[8,512]{1,0:T(8,128)} %copy-done.29, bf16[512,512]{1,0:T(8,128)(2,1)} %get-tuple-element.70.attended_ref, bf16[512,4096]{1,0:T(8,128)(2,1)} %wo_ref.3, bf16[512,768]{1,0:T(8,128)(2,1)} %get-tuple-element.71.grad_ref, ...), custom_call_target="tpu_custom_call" | custom-call | flops 53687091200 | bytes 104857600 | tf_op jit(solution)/shard_map/terms/pallas_call | solution.py:557
  130.2 16.3 %collective-permute-done.19 = bf16[4,256,256]{2,1,0:T(8,128)(2,1)S(1)} collective-permute-done((bf16[4,256,256]{2,1,0:T(8,128)(2,1)S(1)}, bf16[4,256,256]{2,1,0:T(8,128)(2,1)S(1)}, u32[]{:S(2)}, u32[]{:S(2)}) %collective-permute-start.19) | collective-permute-done | bytes 524320 | tf_op jit(solution)/shard_map/ppermute | solution.py:571
  146.5 1.3 fusion.10
  147.8 3.5 %add_convert_fusion = bf16[4,1040,512]{2,1,0:T(8,128)(2,1)S(1)} fusion(bf16[4,1040,512]{2,1,0:T(8,128)(2,1)S(1)} %collective-permute-done.22, bf16[4,1040,512]{2,1,0:T(8,128)(2,1)} %terms.2), kind=kLoop, calls=%fused_computation.1 | loop fusion | flops 8519680 | bytes 12779520 | tf_op jit(solution)/shard_map/convert_element_type | solution.py:593
  151.3 1.6 slice_bitcast_fusion.2
  153.0 1.0 copy-done
  154.0 2.7 collective-permute-start.26
  156.7 0.7 slice_bitcast_fusion.8
  157.4 2.6 collective-permute-start.25
  160.2 4.1 %collective-permute-done.25 = bf16[256,256]{1,0:T(8,128)(2,1)S(1)} collective-permute-done((bf16[256,256]{1,0:T(8,128)(2,1)S(1)}, bf16[256,256]{1,0:T(8,128)(2,1)S(1)}, u32[]{:S(2)}, u32[]{:S(2)}) %collective-permute-start.25) | collective-permute-done | bytes 131104 | tf_op jit(solution)/shard_map/ppermute | solution.py:571
  164.3 0.9 collective-permute-start.23
  165.4 2.6 collective-permute-done.24
  168.7 10.0 %collective-permute-done.28 = bf16[1040,512]{1,0:T(8,128)(2,1)S(1)} collective-permute-done((bf16[1040,512]{1,0:T(8,128)(2,1)}, bf16[1040,512]{1,0:T(8,128)(2,1)S(1)}, u32[]{:S(2)}, u32[]{:S(2)}) %collective-permute-start.28) | collective-permute-done | bytes 1064992 | tf_op jit(solution)/shard_map/ppermute | solution.py:571
  178.8 24.7 %collective-permute-done.27 = bf16[1040,512]{1,0:T(8,128)(2,1)} collective-permute-done((bf16[1040,512]{1,0:T(8,128)(2,1)}, bf16[1040,512]{1,0:T(8,128)(2,1)}, u32[]{:S(2)}, u32[]{:S(2)}) %collective-permute-start.27) | collective-permute-done | bytes 1064992 | tf_op jit(solution)/shard_map/ppermute | solution.py:571
  203.4 2.6 fusion.1
  206.6 1.2 pad_maximum_fusion
  207.7 5.7 %all-to-all-start.2 = ((bf16[16,32,1024]{2,1,0:T(8,128)(2,1)}), bf16[16,32,1024]{2,1,0:T(8,128)(2,1)S(1)}, u32[]{:S(2)}, u32[]{:S(2)}) async-start(bf16[16,32,1024]{2,1,0:T(8,128)(2,1)} %bitcast.24), calls=%async_computation.2 | async-start | bytes 2097152 | tf_op jit(solution)/shard_map/all_to_all | solution.py:597
  213.5 2.9 %collective-permute-start.31 = (bf16[256,256]{1,0:T(8,128)(2,1)S(1)}, bf16[256,256]{1,0:T(8,128)(2,1)S(1)}, u32[]{:S(2)}, u32[]{:S(2)}) collective-permute-start(bf16[256,256]{1,0:T(8,128)(2,1)S(1)} %fusion.13), channel_id=1, source_target_pairs={{0,16},{8,24},{16,0},{24,8},{1,17},{9,25},{17,1},{25,9},{2,18},{10... | collective-permute-start | bytes 393224 | tf_op jit(solution)/shard_map/ppermute | solution.py:571
  216.3 0.9 collective-permute-start.30
  217.8 15.3 %collective-permute-done.31 = bf16[256,256]{1,0:T(8,128)(2,1)S(1)} collective-permute-done((bf16[256,256]{1,0:T(8,128)(2,1)S(1)}, bf16[256,256]{1,0:T(8,128)(2,1)S(1)}, u32[]{:S(2)}, u32[]{:S(2)}) %collective-permute-start.31) | collective-permute-done | bytes 131104 | tf_op jit(solution)/shard_map/ppermute | solution.py:571
  233.1 7.6 %collective-permute-done.30 = bf16[256,256]{1,0:T(8,128)(2,1)S(1)} collective-permute-done((bf16[256,256]{1,0:T(8,128)(2,1)S(1)}, bf16[256,256]{1,0:T(8,128)(2,1)S(1)}, u32[]{:S(2)}, u32[]{:S(2)}) %collective-permute-start.30) | collective-permute-done | bytes 131104 | tf_op jit(solution)/shard_map/ppermute | solution.py:571
  240.8 1.5 collective-permute-start.32
  242.3 1.3 collective-permute-start.33
  243.6 1.7 collective-permute-start.34
  245.3 9.1 %collective-permute-done.32.refs_2_ = bf16[4,256,256]{2,1,0:T(8,128)(2,1)S(1)} collective-permute-done((bf16[4,256,256]{2,1,0:T(8,128)(2,1)S(1)}, bf16[4,256,256]{2,1,0:T(8,128)(2,1)S(1)}, u32[]{:S(2)}, u32[]{:S(2)}) %collective-permute-start.32) | collective-permute-done | bytes 524320 | tf_op jit(solution)/shard_map/ppermute | solution.py:571
  254.5 12.5 %collective-permute-done.34.refs_4_ = bf16[4,256,256]{2,1,0:T(8,128)(2,1)S(1)} collective-permute-done((bf16[4,256,256]{2,1,0:T(8,128)(2,1)S(1)}, bf16[4,256,256]{2,1,0:T(8,128)(2,1)S(1)}, u32[]{:S(2)}, u32[]{:S(2)}) %collective-permute-start.34) | collective-permute-done | bytes 524320 | tf_op jit(solution)/shard_map/ppermute | solution.py:571
  266.9 0.8 copy-done.14
  267.7 3.2 %assemble.1 = (bf16[4096,128]{1,0:T(8,128)(2,1)}, bf16[4096,128]{1,0:T(8,128)(2,1)}) custom-call(s32[13]{0:T(128)} %pad_add_fusion.refs_0_, bf16[4,256,256]{2,1,0:T(8,128)(2,1)} %copy-done.5, bf16[4,256,256]{2,1,0:T(8,128)(2,1)} %copy-done.12, bf16[4,256,256]{2,1,0:T(8,128)(2,1)} %copy-done.13, bf16[4,256,256]{2,1,0:T(8,128)(2,1)} %copy-done.14), custom_call_target="tpu_custom_call" | custom-call | bytes 4194304 | tf_op jit(solution)/shard_map/assemble/pallas_call | solution.py:491
  271.6 1.0 fusion.25
  272.6 4.7 %finish.1 = bf16[4096,512]{1,0:T(8,128)(2,1)} custom-call(bf16[512,512]{1,0:T(8,128)(2,1)} %get-tuple-element.90.refs_0_, bf16[512,512]{1,0:T(8,128)(2,1)} %get-tuple-element.89.refs_1_, bf16[4096,128]{1,0:T(8,128)(2,1)} %get-tuple-element.40.refs_2_, bf16[4096,512]{1,0:T(8,128)(2,1)} %all-reduce.3.cloned.1.call-done.refs_3_), custom_call_target="tpu_custom_call" | custom-call | bytes 8388608 | tf_op jit(solution)/shard_map/finish/pallas_call | solution.py:510
  (126 shorter events, 11.5 us)
Async XLA Ops:
  9.1 23.9 %copy-start.20 = (f32[4096]{0:T(1024)S(1)}, f32[4096]{0:T(1024)}, u32[]{:S(2)}) copy-start(f32[4096]{0:T(1024)} %param.12) | copy-start | bytes 49156
  9.1 26.0 %copy-start.24 = (s32[4]{0:T(128)S(1)}, s32[4]{0:T(128)}, u32[]{:S(2)}) copy-start(s32[4]{0:T(128)} %constant.101.clone) | copy-start | bytes 52
  9.1 18.9 %all-to-all-start = ((bf16[16,32,512]{2,1,0:T(8,128)(2,1)}), bf16[16,32,512]{2,1,0:T(8,128)(2,1)S(1)}, u32[]{:S(2)}, u32[]{:S(2)}) async-start(bf16[16,32,512]{2,1,0:T(8,128)(2,1)} %place.1), calls=%async_computation | async-start | bytes 1048576 | tf_op jit(solution)/shard_map/all_to_all | solution.py:597
  28.0 22.1 %copy-start.1 = (bf16[16,32,512]{2,1,0:T(8,128)(2,1)}, bf16[16,32,512]{2,1,0:T(8,128)(2,1)S(1)}, u32[]{:S(2)}) copy-start(bf16[16,32,512]{2,1,0:T(8,128)(2,1)S(1)} %all-to-all-done) | copy-start | bytes 1572868
  28.0 13.5 %all-to-all-start.1 = ((bf16[16,32,640]{2,1,0:T(8,128)(2,1)}), bf16[16,32,640]{2,1,0:T(8,128)(2,1)S(1)}, u32[]{:S(2)}, u32[]{:S(2)}) async-start(bf16[16,32,640]{2,1,0:T(8,128)(2,1)} %place_meta.1), calls=%async_computation.1 | async-start | bytes 1310720 | tf_op jit(solution)/shard_map/all_to_all | solution.py:597
  31.6 241.0 %all-reduce.3.cloned.1.call-start = ((), (), s32[]{:S(2)}) async-start(), calls=%async_computation.3 | async-start | bytes 8388608 | tf_op jit(solution)/shard_map/psum | solution.py:654
  31.6 12.9 %collective-permute-start = (bf16[512,512]{1,0:T(8,128)(2,1)S(1)}, bf16[512,512]{1,0:T(8,128)(2,1)S(1)}, u32[]{:S(2)}, u32[]{:S(2)}) collective-permute-start(bf16[512,512]{1,0:T(8,128)(2,1)S(1)} %bitcast.54), channel_id=1, source_target_pairs={{0,2},{2,4},{4,6},{6,0},{1,3},{3,5},{5,7},{7,1},{8,10},{10,12},{12... | collective-permute-start | bytes 1572872 | tf_op jit(solution)/shard_map/ppermute | solution.py:571
  33.6 15.3 %collective-permute-start.2 = (bf16[512,512]{1,0:T(8,128)(2,1)S(1)}, bf16[512,512]{1,0:T(8,128)(2,1)}, u32[]{:S(2)}, u32[]{:S(2)}) collective-permute-start(bf16[512,512]{1,0:T(8,128)(2,1)S(1)} %bitcast.55), channel_id=1, source_target_pairs={{0,6},{2,0},{4,2},{6,4},{1,7},{3,1},{5,3},{7,5},{8,14},{10,8},{12,... | collective-permute-start | bytes 1572872 | tf_op jit(solution)/shard_map/ppermute | solution.py:571
  35.6 13.4 %copy-start.22 = (s32[4]{0:T(128)}, s32[4]{0:T(128)S(1)}, u32[]{:S(2)}) copy-start(s32[4]{0:T(128)S(1)} %get-tuple-element.80) | copy-start | bytes 52
  36.2 15.3 %collective-permute-start.6 = (bf16[512,512]{1,0:T(8,128)(2,1)S(1)}, bf16[512,512]{1,0:T(8,128)(2,1)}, u32[]{:S(2)}, u32[]{:S(2)}) collective-permute-start(bf16[512,512]{1,0:T(8,128)(2,1)S(1)} %bitcast.56), channel_id=1, source_target_pairs={{0,1},{1,0},{2,3},{3,2},{4,5},{5,4},{6,7},{7,6},{8,9},{9,8},{10,11... | collective-permute-start | bytes 1572872 | tf_op jit(solution)/shard_map/ppermute | solution.py:575
  41.6 22.6 %copy-start.3 = (bf16[16,32,512]{2,1,0:T(8,128)(2,1)}, bf16[16,32,512]{2,1,0:T(8,128)(2,1)S(1)}, u32[]{:S(2)}) copy-start(bf16[16,32,512]{2,1,0:T(8,128)(2,1)S(1)} %slice.120) | copy-start | bytes 1572868
  41.6 22.5 %collective-permute-start.4 = (bf16[512,512]{1,0:T(8,128)(2,1)S(1)}, bf16[512,512]{1,0:T(8,128)(2,1)S(1)}, u32[]{:S(2)}, u32[]{:S(2)}) collective-permute-start(bf16[512,512]{1,0:T(8,128)(2,1)S(1)} %bitcast.58), channel_id=1, source_target_pairs={{0,2},{2,4},{4,6},{6,0},{1,3},{3,5},{5,7},{7,1},{8,10},{10,12},{12... | collective-permute-start | bytes 1572872 | tf_op jit(solution)/shard_map/ppermute | solution.py:571
  42.9 21.2 %collective-permute-start.5 = (bf16[512,512]{1,0:T(8,128)(2,1)S(1)}, bf16[512,512]{1,0:T(8,128)(2,1)S(1)}, u32[]{:S(2)}, u32[]{:S(2)}) collective-permute-start(bf16[512,512]{1,0:T(8,128)(2,1)S(1)} %bitcast.59), channel_id=1, source_target_pairs={{0,6},{2,0},{4,2},{6,4},{1,7},{3,1},{5,3},{7,5},{8,14},{10,8},{12,... | collective-permute-start | bytes 1572872 | tf_op jit(solution)/shard_map/ppermute | solution.py:571
  44.5 10.8 %copy-start.8 = (bf16[512,512]{1,0:T(8,128)(2,1)}, bf16[512,512]{1,0:T(8,128)(2,1)S(1)}, u32[]{:S(2)}) copy-start(bf16[512,512]{1,0:T(8,128)(2,1)S(1)} %collective-permute-done.refs_2_) | copy-start | bytes 1572868
  44.5 8.3 %collective-permute-start.7 = (bf16[512,512]{1,0:T(8,128)(2,1)S(1)}, bf16[512,512]{1,0:T(8,128)(2,1)}, u32[]{:S(2)}, u32[]{:S(2)}) collective-permute-start(bf16[512,512]{1,0:T(8,128)(2,1)S(1)} %collective-permute-done.refs_2_), channel_id=1, source_target_pairs={{0,1},{1,0},{2,3},{3,2},{4,5},{5,4},{6,7},{7,6},{8,9},{9,8},{10,11... | collective-permute-start | bytes 1572872 | tf_op jit(solution)/shard_map/ppermute | solution.py:575
  49.0 6.3 %collective-permute-start.8 = (bf16[512,512]{1,0:T(8,128)(2,1)}, bf16[512,512]{1,0:T(8,128)(2,1)}, u32[]{:S(2)}, u32[]{:S(2)}) collective-permute-start(bf16[512,512]{1,0:T(8,128)(2,1)} %collective-permute-done.2.refs_3_), channel_id=1, source_target_pairs={{0,1},{1,0},{2,3},{3,2},{4,5},{5,4},{6,7},{7,6},{8,9},{9,8},{10,11... | collective-permute-start | bytes 1572872 | tf_op jit(solution)/shard_map/ppermute | solution.py:575
  51.5 12.7 %collective-permute-start.1 = (bf16[256,512]{1,0:T(8,128)(2,1)S(1)}, bf16[256,512]{1,0:T(8,128)(2,1)S(1)}, u32[]{:S(2)}, u32[]{:S(2)}) collective-permute-start(bf16[256,512]{1,0:T(8,128)(2,1)S(1)} %slice.118), channel_id=1, source_target_pairs={{0,2},{2,4},{4,6},{6,0},{1,3},{3,5},{5,7},{7,1},{8,10},{10,12},{12... | collective-permute-start | bytes 786440 | tf_op jit(solution)/shard_map/ppermute | solution.py:571
  52.8 11.3 %collective-permute-start.3 = (bf16[256,512]{1,0:T(8,128)(2,1)S(1)}, bf16[256,512]{1,0:T(8,128)(2,1)S(1)}, u32[]{:S(2)}, u32[]{:S(2)}) collective-permute-start(bf16[256,512]{1,0:T(8,128)(2,1)S(1)} %slice.119), channel_id=1, source_target_pairs={{0,6},{2,0},{4,2},{6,4},{1,7},{3,1},{5,3},{7,5},{8,14},{10,8},{12,... | collective-permute-start | bytes 786440 | tf_op jit(solution)/shard_map/ppermute | solution.py:571
  64.1 16.2 %copy-start.6 = (bf16[512,512]{1,0:T(8,128)(2,1)}, bf16[512,512]{1,0:T(8,128)(2,1)S(1)}, u32[]{:S(2)}) copy-start(bf16[512,512]{1,0:T(8,128)(2,1)S(1)} %collective-permute-done.4.refs_2_) | copy-start | bytes 1572868
  64.1 16.2 %copy-start.7 = (bf16[512,512]{1,0:T(8,128)(2,1)}, bf16[512,512]{1,0:T(8,128)(2,1)S(1)}, u32[]{:S(2)}) copy-start(bf16[512,512]{1,0:T(8,128)(2,1)S(1)} %collective-permute-done.5.refs_3_) | copy-start | bytes 1572868
  64.1 7.1 %copy-start.15 = (bf16[256,512]{1,0:T(8,128)(2,1)}, bf16[256,512]{1,0:T(8,128)(2,1)S(1)}, u32[]{:S(2)}) copy-start(bf16[256,512]{1,0:T(8,128)(2,1)S(1)} %collective-permute-done.1.refs_1_) | copy-start | bytes 786436
  64.2 7.1 %copy-start.16 = (bf16[256,512]{1,0:T(8,128)(2,1)}, bf16[256,512]{1,0:T(8,128)(2,1)S(1)}, u32[]{:S(2)}) copy-start(bf16[256,512]{1,0:T(8,128)(2,1)S(1)} %collective-permute-done.3.refs_2_) | copy-start | bytes 786436
  64.2 16.1 %collective-permute-start.11 = (bf16[512,512]{1,0:T(8,128)(2,1)S(1)}, bf16[512,512]{1,0:T(8,128)(2,1)S(1)}, u32[]{:S(2)}, u32[]{:S(2)}) collective-permute-start(bf16[512,512]{1,0:T(8,128)(2,1)S(1)} %bitcast.60), channel_id=1, source_target_pairs={{0,1},{1,0},{2,3},{3,2},{4,5},{5,4},{6,7},{7,6},{8,9},{9,8},{10,11... | collective-permute-start | bytes 1572872 | tf_op jit(solution)/shard_map/ppermute | solution.py:575
  64.8 15.5 %collective-permute-start.12 = (bf16[512,512]{1,0:T(8,128)(2,1)S(1)}, bf16[512,512]{1,0:T(8,128)(2,1)S(1)}, u32[]{:S(2)}, u32[]{:S(2)}) collective-permute-start(bf16[512,512]{1,0:T(8,128)(2,1)S(1)} %collective-permute-done.4.refs_2_), channel_id=1, source_target_pairs={{0,1},{1,0},{2,3},{3,2},{4,5},{5,4},{6,7},{7,6},{8,9},{9,8},{10,11... | collective-permute-start | bytes 1572872 | tf_op jit(solution)/shard_map/ppermute | solution.py:575
  64.9 15.4 %collective-permute-start.13 = (bf16[512,512]{1,0:T(8,128)(2,1)S(1)}, bf16[512,512]{1,0:T(8,128)(2,1)S(1)}, u32[]{:S(2)}, u32[]{:S(2)}) collective-permute-start(bf16[512,512]{1,0:T(8,128)(2,1)S(1)} %collective-permute-done.5.refs_3_), channel_id=1, source_target_pairs={{0,1},{1,0},{2,3},{3,2},{4,5},{5,4},{6,7},{7,6},{8,9},{9,8},{10,11... | collective-permute-start | bytes 1572872 | tf_op jit(solution)/shard_map/ppermute | solution.py:575
  65.3 2.9 %collective-permute-start.14 = (bf16[256,512]{1,0:T(8,128)(2,1)S(1)}, bf16[256,512]{1,0:T(8,128)(2,1)S(1)}, u32[]{:S(2)}, u32[]{:S(2)}) collective-permute-start(bf16[256,512]{1,0:T(8,128)(2,1)S(1)} %collective-permute-done.1.refs_1_), channel_id=1, source_target_pairs={{0,1},{1,0},{2,3},{3,2},{4,5},{5,4},{6,7},{7,6},{8,9},{9,8},{10,11... | collective-permute-start | bytes 786440 | tf_op jit(solution)/shard_map/ppermute | solution.py:575
  65.5 4.1 %collective-permute-start.15 = (bf16[256,512]{1,0:T(8,128)(2,1)S(1)}, bf16[256,512]{1,0:T(8,128)(2,1)S(1)}, u32[]{:S(2)}, u32[]{:S(2)}) collective-permute-start(bf16[256,512]{1,0:T(8,128)(2,1)S(1)} %collective-permute-done.3.refs_2_), channel_id=1, source_target_pairs={{0,1},{1,0},{2,3},{3,2},{4,5},{5,4},{6,7},{7,6},{8,9},{9,8},{10,11... | collective-permute-start | bytes 786440 | tf_op jit(solution)/shard_map/ppermute | solution.py:575
  68.2 3.1 %copy-start.17 = (bf16[256,512]{1,0:T(8,128)(2,1)}, bf16[256,512]{1,0:T(8,128)(2,1)S(1)}, u32[]{:S(2)}) copy-start(bf16[256,512]{1,0:T(8,128)(2,1)S(1)} %collective-permute-done.14.refs_3_) | copy-start | bytes 786436
  68.2 19.4 %collective-permute-start.9 = (bf16[256,512]{1,0:T(8,128)(2,1)S(1)}, bf16[256,512]{1,0:T(8,128)(2,1)S(1)}, u32[]{:S(2)}, u32[]{:S(2)}) collective-permute-start(bf16[256,512]{1,0:T(8,128)(2,1)S(1)} %slice.91), channel_id=1, source_target_pairs={{0,2},{2,4},{4,6},{6,0},{1,3},{3,5},{5,7},{7,1},{8,10},{10,12},{12... | collective-permute-start | bytes 786440 | tf_op jit(solution)/shard_map/ppermute | solution.py:571
  69.5 1.8 copy-start.18
  69.5 18.1 %collective-permute-start.10 = (bf16[256,512]{1,0:T(8,128)(2,1)S(1)}, bf16[256,512]{1,0:T(8,128)(2,1)S(1)}, u32[]{:S(2)}, u32[]{:S(2)}) collective-permute-start(bf16[256,512]{1,0:T(8,128)(2,1)S(1)} %slice.92), channel_id=1, source_target_pairs={{0,6},{2,0},{4,2},{6,4},{1,7},{3,1},{5,3},{7,5},{8,14},{10,8},{12,... | collective-permute-start | bytes 786440 | tf_op jit(solution)/shard_map/ppermute | solution.py:571
  80.3 1.0 copy-start.10
  80.3 1.1 copy-start.11
  81.5 7.0 %copy-start.23 = (s32[4]{0:T(128)S(1)}, s32[4]{0:T(128)}, u32[]{:S(2)}) copy-start(s32[4]{0:T(128)} %copy-done.22) | copy-start | bytes 52
  87.6 2.3 copy-start.25
  87.6 2.3 copy-start.26
  87.6 1.9 collective-permute-start.16
  88.4 1.5 collective-permute-start.17
  103.0 9.0 %collective-permute-start.21 = (f32[8,512]{1,0:T(8,128)}, f32[8,512]{1,0:T(8,128)S(1)}, u32[]{:S(2)}, u32[]{:S(2)}) collective-permute-start(f32[8,512]{1,0:T(8,128)} %get-tuple-element.69.dots_ref), channel_id=1, source_target_pairs={{0,1},{1,0},{2,3},{3,2},{4,5},{5,4},{6,7},{7,6},{8,9},{9,8},{10,11... | collective-permute-start | bytes 49160 | tf_op jit(solution)/shard_map/ppermute | solution.py:575
  105.1 25.1 %collective-permute-start.20 = (bf16[4,256,256]{2,1,0:T(8,128)(2,1)S(1)}, bf16[4,256,256]{2,1,0:T(8,128)(2,1)S(1)}, u32[]{:S(2)}, u32[]{:S(2)}) collective-permute-start(bf16[4,256,256]{2,1,0:T(8,128)(2,1)S(1)} %get-tuple-element.87), channel_id=1, source_target_pairs={{0,64},{32,96},{64,0},{96,32},{1,65},{33,97},{65,1},{97,33},{2,66}... | collective-permute-start | bytes 1572872 | tf_op jit(solution)/shard_map/ppermute | solution.py:571
  109.3 37.2 %collective-permute-start.19 = (bf16[4,256,256]{2,1,0:T(8,128)(2,1)S(1)}, bf16[4,256,256]{2,1,0:T(8,128)(2,1)S(1)}, u32[]{:S(2)}, u32[]{:S(2)}) collective-permute-start(bf16[4,256,256]{2,1,0:T(8,128)(2,1)S(1)} %get-tuple-element.88), channel_id=1, source_target_pairs={{0,32},{32,64},{64,96},{96,0},{1,33},{33,65},{65,97},{97,1},{2,34}... | collective-permute-start | bytes 1572872 | tf_op jit(solution)/shard_map/ppermute | solution.py:571
  109.3 37.1 %collective-permute-start.18 = (bf16[4,256,256]{2,1,0:T(8,128)(2,1)S(1)}, bf16[4,256,256]{2,1,0:T(8,128)(2,1)S(1)}, u32[]{:S(2)}, u32[]{:S(2)}) collective-permute-start(bf16[4,256,256]{2,1,0:T(8,128)(2,1)S(1)} %get-tuple-element.86), channel_id=1, source_target_pairs={{0,96},{32,0},{64,32},{96,64},{1,97},{33,1},{65,33},{97,65},{2,98}... | collective-permute-start | bytes 1572872 | tf_op jit(solution)/shard_map/ppermute | solution.py:571
  120.9 26.9 %collective-permute-start.22 = (bf16[4,1040,512]{2,1,0:T(8,128)(2,1)}, bf16[4,1040,512]{2,1,0:T(8,128)(2,1)S(1)}, u32[]{:S(2)}, u32[]{:S(2)}) collective-permute-start(bf16[4,1040,512]{2,1,0:T(8,128)(2,1)} %terms.3), channel_id=1, source_target_pairs={{0,1},{1,0},{2,3},{3,2},{4,5},{5,4},{6,7},{7,6},{8,9},{9,8},{10,11... | collective-permute-start | bytes 12779528 | tf_op jit(solution)/shard_map/ppermute | solution.py:575
  151.3 2.7 copy-start
  151.3 13.9 %copy-start.19 = (f32[512,128]{1,0:T(8,128)S(1)}, f32[512,128]{1,0:T(8,128)}, u32[]{:S(2)}) copy-start(f32[512,128]{1,0:T(8,128)} %get-tuple-element.67.refs_14_) | copy-start | bytes 786436
  154.0 24.8 %collective-permute-start.28 = (bf16[1040,512]{1,0:T(8,128)(2,1)}, bf16[1040,512]{1,0:T(8,128)(2,1)S(1)}, u32[]{:S(2)}, u32[]{:S(2)}) collective-permute-start(bf16[1040,512]{1,0:T(8,128)(2,1)} %get-tuple-element.82), channel_id=1, source_target_pairs={{0,4},{2,6},{4,0},{6,2},{1,5},{3,7},{5,1},{7,3},{8,12},{10,14},{12... | collective-permute-start | bytes 3194888 | tf_op jit(solution)/shard_map/ppermute | solution.py:571
  154.0 49.4 %collective-permute-start.27 = (bf16[1040,512]{1,0:T(8,128)(2,1)}, bf16[1040,512]{1,0:T(8,128)(2,1)}, u32[]{:S(2)}, u32[]{:S(2)}) collective-permute-start(bf16[1040,512]{1,0:T(8,128)(2,1)} %get-tuple-element.83), channel_id=1, source_target_pairs={{0,2},{2,4},{4,6},{6,0},{1,3},{3,5},{5,7},{7,1},{8,10},{10,12},{12... | collective-permute-start | bytes 3194888 | tf_op jit(solution)/shard_map/ppermute | solution.py:571
  154.0 49.4 %collective-permute-start.26 = (bf16[1040,512]{1,0:T(8,128)(2,1)S(1)}, bf16[1040,512]{1,0:T(8,128)(2,1)}, u32[]{:S(2)}, u32[]{:S(2)}) collective-permute-start(bf16[1040,512]{1,0:T(8,128)(2,1)S(1)} %get-tuple-element.81), channel_id=1, source_target_pairs={{0,6},{2,0},{4,2},{6,4},{1,7},{3,1},{5,3},{7,5},{8,14},{10,8},{12,... | collective-permute-start | bytes 3194888 | tf_op jit(solution)/shard_map/ppermute | solution.py:571
  157.4 6.9 %collective-permute-start.25 = (bf16[256,256]{1,0:T(8,128)(2,1)S(1)}, bf16[256,256]{1,0:T(8,128)(2,1)S(1)}, u32[]{:S(2)}, u32[]{:S(2)}) collective-permute-start(bf16[256,256]{1,0:T(8,128)(2,1)S(1)} %get-tuple-element.92), channel_id=1, source_target_pairs={{0,16},{8,24},{16,0},{24,8},{1,17},{9,25},{17,1},{25,9},{2,18},{10... | collective-permute-start | bytes 393224 | tf_op jit(solution)/shard_map/ppermute | solution.py:571
  159.9 8.1 %collective-permute-start.24 = (bf16[256,256]{1,0:T(8,128)(2,1)}, bf16[256,256]{1,0:T(8,128)(2,1)S(1)}, u32[]{:S(2)}, u32[]{:S(2)}) collective-permute-start(bf16[256,256]{1,0:T(8,128)(2,1)} %get-tuple-element.93), channel_id=1, source_target_pairs={{0,8},{8,16},{16,24},{24,0},{1,9},{9,17},{17,25},{25,1},{2,10},{10... | collective-permute-start | bytes 393224 | tf_op jit(solution)/shard_map/ppermute | solution.py:571
  164.3 4.4 %collective-permute-start.23 = (bf16[256,256]{1,0:T(8,128)(2,1)S(1)}, bf16[256,256]{1,0:T(8,128)(2,1)S(1)}, u32[]{:S(2)}, u32[]{:S(2)}) collective-permute-start(bf16[256,256]{1,0:T(8,128)(2,1)S(1)} %get-tuple-element.91), channel_id=1, source_target_pairs={{0,24},{8,0},{16,8},{24,16},{1,25},{9,1},{17,9},{25,17},{2,26},{10... | collective-permute-start | bytes 393224 | tf_op jit(solution)/shard_map/ppermute | solution.py:571
  168.7 37.3 %copy-start.2 = (bf16[16,32,512]{2,1,0:T(8,128)(2,1)S(1)}, bf16[16,32,512]{2,1,0:T(8,128)(2,1)}, u32[]{:S(2)}) copy-start(bf16[16,32,512]{2,1,0:T(8,128)(2,1)} %copy-done.1) | copy-start | bytes 1572868
  168.7 37.3 %copy-start.4 = (bf16[16,32,512]{2,1,0:T(8,128)(2,1)S(1)}, bf16[16,32,512]{2,1,0:T(8,128)(2,1)}, u32[]{:S(2)}) copy-start(bf16[16,32,512]{2,1,0:T(8,128)(2,1)} %copy-done.3) | copy-start | bytes 1572868
  206.5 38.7 %copy-start.21 = (s32[16]{0:T(128)S(1)}, s32[16]{0:T(128)}, u32[]{:S(2)}) copy-start(s32[16]{0:T(128)} %plan_ref.3) | copy-start | bytes 196
  207.7 63.3 %all-to-all-start.2 = ((bf16[16,32,1024]{2,1,0:T(8,128)(2,1)}), bf16[16,32,1024]{2,1,0:T(8,128)(2,1)S(1)}, u32[]{:S(2)}, u32[]{:S(2)}) async-start(bf16[16,32,1024]{2,1,0:T(8,128)(2,1)} %bitcast.24), calls=%async_computation.2 | async-start | bytes 2097152 | tf_op jit(solution)/shard_map/all_to_all | solution.py:597
  213.5 19.7 %collective-permute-start.31 = (bf16[256,256]{1,0:T(8,128)(2,1)S(1)}, bf16[256,256]{1,0:T(8,128)(2,1)S(1)}, u32[]{:S(2)}, u32[]{:S(2)}) collective-permute-start(bf16[256,256]{1,0:T(8,128)(2,1)S(1)} %fusion.13), channel_id=1, source_target_pairs={{0,16},{8,24},{16,0},{24,8},{1,17},{9,25},{17,1},{25,9},{2,18},{10... | collective-permute-start | bytes 393224 | tf_op jit(solution)/shard_map/ppermute | solution.py:571
  216.3 24.4 %collective-permute-start.30 = (bf16[256,256]{1,0:T(8,128)(2,1)S(1)}, bf16[256,256]{1,0:T(8,128)(2,1)S(1)}, u32[]{:S(2)}, u32[]{:S(2)}) collective-permute-start(bf16[256,256]{1,0:T(8,128)(2,1)S(1)} %fusion.13), channel_id=1, source_target_pairs={{0,24},{8,0},{16,8},{24,16},{1,25},{9,1},{17,9},{25,17},{2,26},{10... | collective-permute-start | bytes 393224 | tf_op jit(solution)/shard_map/ppermute | solution.py:571
  217.2 23.5 %collective-permute-start.29 = (bf16[256,256]{1,0:T(8,128)(2,1)S(1)}, bf16[256,256]{1,0:T(8,128)(2,1)S(1)}, u32[]{:S(2)}, u32[]{:S(2)}) collective-permute-start(bf16[256,256]{1,0:T(8,128)(2,1)S(1)} %fusion.13), channel_id=1, source_target_pairs={{0,8},{8,16},{16,24},{24,0},{1,9},{9,17},{17,25},{25,1},{2,10},{10... | collective-permute-start | bytes 393224 | tf_op jit(solution)/shard_map/ppermute | solution.py:571
  240.8 26.1 %copy-start.5 = (bf16[4,256,256]{2,1,0:T(8,128)(2,1)}, bf16[4,256,256]{2,1,0:T(8,128)(2,1)S(1)}, u32[]{:S(2)}) copy-start(bf16[4,256,256]{2,1,0:T(8,128)(2,1)S(1)} %pad_maximum_fusion.2.refs_1_) | copy-start | bytes 1572868
  240.8 13.5 %collective-permute-start.32 = (bf16[4,256,256]{2,1,0:T(8,128)(2,1)S(1)}, bf16[4,256,256]{2,1,0:T(8,128)(2,1)S(1)}, u32[]{:S(2)}, u32[]{:S(2)}) collective-permute-start(bf16[4,256,256]{2,1,0:T(8,128)(2,1)S(1)} %pad_maximum_fusion.2.refs_1_), channel_id=1, source_target_pairs={{0,32},{32,64},{64,96},{96,0},{1,33},{33,65},{65,97},{97,1},{2,34}... | collective-permute-start | bytes 1572872 | tf_op jit(solution)/shard_map/ppermute | solution.py:571
  242.3 12.2 %collective-permute-start.33 = (bf16[4,256,256]{2,1,0:T(8,128)(2,1)S(1)}, bf16[4,256,256]{2,1,0:T(8,128)(2,1)S(1)}, u32[]{:S(2)}, u32[]{:S(2)}) collective-permute-start(bf16[4,256,256]{2,1,0:T(8,128)(2,1)S(1)} %pad_maximum_fusion.2.refs_1_), channel_id=1, source_target_pairs={{0,96},{32,0},{64,32},{96,64},{1,97},{33,1},{65,33},{97,65},{2,98}... | collective-permute-start | bytes 1572872 | tf_op jit(solution)/shard_map/ppermute | solution.py:571
  243.6 23.3 %collective-permute-start.34 = (bf16[4,256,256]{2,1,0:T(8,128)(2,1)S(1)}, bf16[4,256,256]{2,1,0:T(8,128)(2,1)S(1)}, u32[]{:S(2)}, u32[]{:S(2)}) collective-permute-start(bf16[4,256,256]{2,1,0:T(8,128)(2,1)S(1)} %pad_maximum_fusion.2.refs_1_), channel_id=1, source_target_pairs={{0,64},{32,96},{64,0},{96,32},{1,65},{33,97},{65,1},{97,33},{2,66}... | collective-permute-start | bytes 1572872 | tf_op jit(solution)/shard_map/ppermute | solution.py:571
  254.3 12.6 %copy-start.12 = (bf16[4,256,256]{2,1,0:T(8,128)(2,1)}, bf16[4,256,256]{2,1,0:T(8,128)(2,1)S(1)}, u32[]{:S(2)}) copy-start(bf16[4,256,256]{2,1,0:T(8,128)(2,1)S(1)} %collective-permute-done.32.refs_2_) | copy-start | bytes 1572868
  254.5 12.5 %copy-start.13 = (bf16[4,256,256]{2,1,0:T(8,128)(2,1)}, bf16[4,256,256]{2,1,0:T(8,128)(2,1)S(1)}, u32[]{:S(2)}) copy-start(bf16[4,256,256]{2,1,0:T(8,128)(2,1)S(1)} %collective-permute-done.33.refs_3_) | copy-start | bytes 1572868
  (5 other events, 3.6 us)
Sparse Core Ops, SparseCore 0:
  112.1 130.6 all-reduce.2

commit v6 on v4

--- a/solution.py
+++ b/solution.py
@@ -55,7 +55,7 @@
     )(plan, panels)
 
 
-def place_meta_kernel(plan_ref, rows_ref, docs_ref, out_ref):
+def place_meta_kernel(plan_ref, _, rows_ref, docs_ref, out_ref):
     count, rows, width = rows_ref.shape
     for panel in range(count):
         target = plan_ref[panel] // count
@@ -71,13 +71,14 @@
         out_ref[target, :, width:] = extra.astype(BF)
 
 
-def place_meta(plan, panels, docs):
+def place_meta(plan, after, panels, docs):
     count, rows, width = panels.shape
     return pl.pallas_call(
         place_meta_kernel,
         out_shape=jax.ShapeDtypeStruct((count, rows, width + 128), panels.dtype),
         in_specs=[
             pl.BlockSpec(memory_space=pltpu.SMEM),
+            pl.BlockSpec(memory_space=pltpu.HBM),
             pl.BlockSpec(memory_space=pltpu.VMEM),
             pl.BlockSpec(memory_space=pltpu.VMEM),
         ],
@@ -85,7 +86,7 @@
         compiler_params=params(),
         cost_estimate=cost(0, 2 * panels.size * 2),
         name="place_meta",
-    )(plan, panels, docs.reshape(count, rows, 1))
+    )(plan, after, panels, docs.reshape(count, rows, 1))
 
 
 NEAR = tuple((step, other) for step in range(3) for other in (0, 1))
@@ -488,16 +489,23 @@
     out_ref[0] = nn(attended_ref[...], wo_ref[...]).astype(BF)
 
 
-def out_terms(idx, after, attended, wo, width):
+def place_of(other):
+    if other:
+        return lambda j, idx: idx[j] + 1 - idx[4]
+    return lambda j, idx: idx[j] + idx[4]
+
+
+def out_terms(idx, other, after, attended, wo, width):
     rows, cols = attended.shape
     parts = 4
+    at = place_of(other)
     grid_spec = pltpu.PrefetchScalarGridSpec(
         num_scalar_prefetch=1,
         grid=(parts,),
         in_specs=[
             HBM_SPEC,
             pl.BlockSpec((rows, cols), lambda j, idx: (0, 0)),
-            pl.BlockSpec((cols, width), lambda j, idx: (0, idx[j])),
+            pl.BlockSpec((cols, width), lambda j, idx: (0, at(j, idx))),
         ],
         out_specs=pl.BlockSpec((1, rows, width), lambda j, idx: (j, 0, 0)),
     )
@@ -526,9 +534,10 @@
     out_ref[0, rows:] = extra.astype(BF)
 
 
-def input_terms(idx, after, grad, dots, wq, wk, wv, width):
+def input_terms(idx, other, after, grad, dots, wq, wk, wv, width):
     rows, cols = grad.shape
     parts = 4
+    at = place_of(other)
     grid_spec = pltpu.PrefetchScalarGridSpec(
         num_scalar_prefetch=1,
         grid=(parts,),
@@ -538,7 +547,7 @@
             pl.BlockSpec(dots.shape, lambda j, idx: (0, 0)),
         ]
         + [
-            pl.BlockSpec((width, w.shape[1]), lambda j, idx: (idx[j], 0))
+            pl.BlockSpec((width, w.shape[1]), lambda j, idx: (at(j, idx), 0))
             for w in (wq, wk, wv)
         ],
         out_specs=pl.BlockSpec((1, rows + 16, width), lambda j, idx: (j, 0, 0)),
@@ -612,7 +621,9 @@
 
     here_tokens = exchange(place(panel_plan, tokens.reshape(count, panel, width))).reshape(rows, width)
     arrived = exchange(
-        place_meta(panel_plan, cotangent.reshape(count, panel, width), doc_ids.reshape(count, panel))
+        place_meta(
+            panel_plan, here_tokens, cotangent.reshape(count, panel, width), doc_ids.reshape(count, panel)
+        )
     )
     here_cot = arrived[:, :, :width].reshape(rows, width)
     meta = arrived[:, :, width : width + 3].reshape(rows, 3).astype(jnp.int32)
@@ -648,13 +659,12 @@
     )
     grad_query, grad_key, grad_value = finish(lax.psum(tuple(grads), ("x", "z")))
     after = swap(dots)
-    idx_mine, idx_other = around * cores + core, around * cores + (1 - core)
     out_sum = sum_pieces(
-        *[out_terms(i, after, attended, wo, width) for i in (idx_mine, idx_other)]
+        *[out_terms(idx, other, after, attended, wo, width) for other in (False, True)]
     )
     output_rows = (here_tokens.astype(F32) + out_sum).astype(BF)
     in_sum = sum_pieces(
-        *[input_terms(i, after, grad, dots, wq, wk, wv, width) for i in (idx_mine, idx_other)]
+        *[input_terms(idx, other, after, grad, dots, wq, wk, wv, width) for other in (False, True)]
     )
     inverse = inverse[:, 0:1]
     mean_term = ((in_sum[rows] + in_sum[rows + 1]) / features)[:, None]

time: 247 us -> 256 us (1.036)
  waiting for transfers between devices: 75.2 us -> 84.7 us
    ppermute x16, waiting for transfers between devices: 28.7 us -> 38 us  [shift(): lax.ppermute(array, axis, [(i, (i + step) % size) for i in range(size)])]
  transfers between devices with their start and end apart: 33 -> 33, of which waited for: 14 -> 15; matrix products, arithmetic and copies ran while one was open for 6% -> 6% of each run, Pallas kernels for 20% -> 19%
where the time goes in v6:
time: 256 us; the launch traced here: 254 us
  waiting for transfers between devices  84.7 us (33%)
  Pallas kernels  70.7 us (28%)
  starting transfers between devices  48 us (19%)
  blocking collectives  17.3 us (7%)
  between operations  14.6 us (6%)
  local copies, waits for them, and re-layouts  11.4 us (4%)
  other arithmetic  7.72 us (3%)
    ppermute x16, waiting for transfers between devices, shift(): lax.ppermute(array, axis, [(i, (i + step) % size) for i in range(size)])  38 us
    psum x1, waiting for transfers between devices, per_device(): lax.psum(tuple(grads), ('x', 'z'))  26.4 us
    ppermute x16, starting transfers between devices, shift(): lax.ppermute(array, axis, [(i, (i + step) % size) for i in range(size)])  20.9 us
    all_to_all x3, starting transfers between devices, exchange(): lax.all_to_all(panels, ('x', 'z'), split_axis=0, concat_axis=0, tiled=True)  17.3 us
    all_to_all x1, blocking collectives, exchange(): lax.all_to_all(panels, ('x', 'z'), split_axis=0, concat_axis=0, tiled=True)  17.3 us
    all_to_all x3, waiting for transfers between devices, exchange(): lax.all_to_all(panels, ('x', 'z'), split_axis=0, concat_axis=0, tiled=True)  17.2 us
    pallas_call x2, Pallas kernels, input_terms(): pl.pallas_call(input_term_kernel, grid_spec=grid_spec, out_shape=jax.Shap...  13.6 us
    pallas_call x1, Pallas kernels, back(): pl.pallas_call(functools.partial(back_kernel, scale=scale), grid=(1,), in...  12.5 us
  transfers between devices with their start and end apart: 33, of which 15 were waited for; matrix products, arithmetic and copies ran while one was open for 6% of the time, Pallas kernels for 19%

profile of v6, /device:TPU:1, one launch (start us, length us, event | category | flops | bytes accessed | tf_op | source)
XLA Modules:
  0.0 254.5 jit_solution(13116442658766635096)
XLA Ops:
  7.2 1.9 place.1
  9.1 8.6 %all-to-all-start = ((bf16[16,32,512]{2,1,0:T(8,128)(2,1)}), bf16[16,32,512]{2,1,0:T(8,128)(2,1)S(1)}, u32[]{:S(2)}, u32[]{:S(2)}) async-start(bf16[16,32,512]{2,1,0:T(8,128)(2,1)} %place.1), calls=%async_computation | async-start | bytes 1048576 | tf_op jit(solution)/shard_map/all_to_all | solution.py:601
  17.7 0.9 reshape_reshape.4.docs_ref
  18.6 9.4 %all-to-all-done = bf16[16,32,512]{2,1,0:T(8,128)(2,1)S(1)} async-done(((bf16[16,32,512]{2,1,0:T(8,128)(2,1)}), bf16[16,32,512]{2,1,0:T(8,128)(2,1)S(1)}, u32[]{:S(2)}, u32[]{:S(2)}) %all-to-all-start) | async-done | bytes 524320 | tf_op jit(solution)/shard_map/all_to_all | solution.py:601
  28.0 0.8 copy-done
  28.8 2.2 place_meta.1
  31.0 3.6 %all-to-all-start.1 = ((bf16[16,32,640]{2,1,0:T(8,128)(2,1)}), bf16[16,32,640]{2,1,0:T(8,128)(2,1)S(1)}, u32[]{:S(2)}, u32[]{:S(2)}) async-start(bf16[16,32,640]{2,1,0:T(8,128)(2,1)} %place_meta.1), calls=%async_computation.1 | async-start | bytes 1310720 | tf_op jit(solution)/shard_map/all_to_all | solution.py:601
  34.7 1.4 collective-permute-start
  36.0 1.5 collective-permute-start.2
  37.6 0.6 reshape.162.refs_7_.refs_5_
  38.2 0.6 pad_add_fusion.refs_0_.idx_ref
  38.8 2.6 %collective-permute-start.6 = (bf16[512,512]{1,0:T(8,128)(2,1)}, bf16[512,512]{1,0:T(8,128)(2,1)}, u32[]{:S(2)}, u32[]{:S(2)}) collective-permute-start(bf16[512,512]{1,0:T(8,128)(2,1)} %bitcast.74), channel_id=1, source_target_pairs={{0,1},{1,0},{2,3},{3,2},{4,5},{5,4},{6,7},{7,6},{8,9},{9,8},{10,11... | collective-permute-start | bytes 1572872 | tf_op jit(solution)/shard_map/ppermute | solution.py:571
  41.4 6.2 %collective-permute-done.refs_2_ = bf16[512,512]{1,0:T(8,128)(2,1)S(1)} collective-permute-done((bf16[512,512]{1,0:T(8,128)(2,1)}, bf16[512,512]{1,0:T(8,128)(2,1)S(1)}, u32[]{:S(2)}, u32[]{:S(2)}) %collective-permute-start) | collective-permute-done | bytes 524320 | tf_op jit(solution)/shard_map/ppermute | solution.py:567
  47.6 3.0 %collective-permute-start.7 = (bf16[512,512]{1,0:T(8,128)(2,1)S(1)}, bf16[512,512]{1,0:T(8,128)(2,1)}, u32[]{:S(2)}, u32[]{:S(2)}) collective-permute-start(bf16[512,512]{1,0:T(8,128)(2,1)S(1)} %collective-permute-done.refs_2_), channel_id=1, source_target_pairs={{0,1},{1,0},{2,3},{3,2},{4,5},{5,4},{6,7},{7,6},{8,9},{9,8},{10,11... | collective-permute-start | bytes 1572872 | tf_op jit(solution)/shard_map/ppermute | solution.py:571
  50.6 0.7 slice.112
  51.4 0.8 slice.113
  52.3 0.5 collective-permute-start.4
  52.7 2.3 collective-permute-start.5
  55.8 2.7 %collective-permute-start.3 = (bf16[256,512]{1,0:T(8,128)(2,1)}, bf16[256,512]{1,0:T(8,128)(2,1)S(1)}, u32[]{:S(2)}, u32[]{:S(2)}) collective-permute-start(bf16[256,512]{1,0:T(8,128)(2,1)} %slice.113), channel_id=1, source_target_pairs={{0,6},{2,0},{4,2},{6,4},{1,7},{3,1},{5,3},{7,5},{8,14},{10,8},{12,... | collective-permute-start | bytes 786440 | tf_op jit(solution)/shard_map/ppermute | solution.py:567
  58.4 1.0 multiply_cosine_fusion
  59.4 8.8 %project_near.1 = (bf16[3,1024,512]{2,1,0:T(8,128)(2,1)}, f32[512,768]{1,0:T(8,128)}, f32[512,128]{1,0:T(8,128)}) custom-call(s32[13]{0:T(128)} %pad_add_fusion.refs_0_.idx_ref, bf16[512,512]{1,0:T(8,128)(2,1)} %bitcast.75, bf16[512,512]{1,0:T(8,128)(2,1)} %copy-done.7, bf16[512,512]{1,0:T(8,128)(2,1)} %copy-done.8, ...), custom_call_target="tpu_custom_call" | custom-call | flops 2415919104 | bytes 11010048 | tf_op jit(solution)/shard_map/project_near/pallas_call | solution.py:189
  68.2 4.1 %collective-permute-done.1.refs_1_ = bf16[256,512]{1,0:T(8,128)(2,1)S(1)} collective-permute-done((bf16[256,512]{1,0:T(8,128)(2,1)}, bf16[256,512]{1,0:T(8,128)(2,1)S(1)}, u32[]{:S(2)}, u32[]{:S(2)}) %collective-permute-start.1) | collective-permute-done | bytes 262176 | tf_op jit(solution)/shard_map/ppermute | solution.py:567
  72.4 1.2 collective-permute-start.12
  73.7 0.4 collective-permute-start.11
  74.7 0.6 pad.4.refs_12_
  75.5 0.9 pad_maximum_fusion.2.refs_11_.refs_15_
  76.4 0.7 collective-permute-done.14.refs_3_
  77.0 2.7 %collective-permute-start.10 = (bf16[256,512]{1,0:T(8,128)(2,1)S(1)}, bf16[256,512]{1,0:T(8,128)(2,1)S(1)}, u32[]{:S(2)}, u32[]{:S(2)}) collective-permute-start(bf16[256,512]{1,0:T(8,128)(2,1)S(1)} %slice.85), channel_id=1, source_target_pairs={{0,6},{2,0},{4,2},{6,4},{1,7},{3,1},{5,3},{7,5},{8,14},{10,8},{12,... | collective-permute-start | bytes 786440 | tf_op jit(solution)/shard_map/ppermute | solution.py:567
  79.7 0.7 copy-done.15
  80.4 9.0 %attend.1 = (bf16[1,1024,512]{2,1,0:T(8,128)(2,1)}, f32[512,128]{1,0:T(8,128)}, bf16[512,512]{1,0:T(8,128)(2,1)}, bf16[512,128]{1,0:T(8,128)(2,1)}, bf16[128,512...) custom-call(s32[13]{0:T(128)} %pad_add_fusion.refs_0_.idx_ref, ...), custom_call_target="tpu_custom_call" | custom-call | flops 1342177280 | bytes 3670016 | tf_op jit(solution)/shard_map/attend/pallas_call | solution.py:275
  89.5 0.8 copy-done.9
  90.5 6.0 %back_near.1.refs_6_ = f32[512,512]{1,0:T(8,128)} custom-call(s32[13]{0:T(128)} %pad_add_fusion.refs_0_.idx_ref, bf16[512,512]{1,0:T(8,128)(2,1)} %bitcast.79, bf16[512,512]{1,0:T(8,128)(2,1)} %copy-done.5, bf16[512,512]{1,0:T(8,128)(2,1)} %copy-done.6, bf16[512,512]{1,0:T(8,128)(2,1)} %copy-done.11, bf16[512,512]{1,0:T(8,128)(2,1)} %copy-done.9, ...), custom_call_target="tpu_custom_call" | custom-call | flops 1610612736 | bytes 6291456 | tf_op jit(solution)/shard_map/back_near/pallas_call | solution.py:319
  96.6 0.7 collective-permute-start.16
  97.4 1.1 collective-permute-done.16.refs_3_
  98.5 0.4 collective-permute-done.17.refs_4_
  99.2 0.4 copy-done.24
  99.6 12.5 %back.1 = (bf16[512,768]{1,0:T(8,128)(2,1)}, f32[8,512]{1,0:T(8,128)}, bf16[4096,512]{1,0:T(8,128)(2,1)}, bf16[4096,128]{1,0:T(8,128)(2,1)}, bf16[4096,128]{1,0:T(8,128)(2,1)}) custom-call(s32[13]{0:T(128)} %pad_add_fusion.refs_0_.idx_ref, bf16[256,512]{1,0:T(8,128)(2,1)} %copy-done.22, bf16[256,512]{1,0:T(8,128)(2,1)} %copy-done.21, ...), custom_call_target="tpu_custom_call" | custom-call | flops 4831838208 | bytes 8388608 | tf_op jit(solution)/shard_map/back/pallas_call | solution.py:441
  112.1 0.7 collective-permute-start.18
  112.9 1.0 collective-permute-done.18._
  113.8 0.6 copy-done.25
  114.4 5.5 %out_terms.3 = bf16[4,512,512]{2,1,0:T(8,128)(2,1)} custom-call(s32[13]{0:T(128)} %pad_add_fusion.refs_0_.idx_ref, f32[8,512]{1,0:T(8,128)} %copy-done.25, bf16[512,512]{1,0:T(8,128)(2,1)} %get-tuple-element.67.attended_ref, bf16[512,4096]{1,0:T(8,128)(2,1)} %wo_ref.3), custom_call_target="tpu_custom_call" | custom-call | flops 21474836480 | bytes 83886080 | tf_op jit(solution)/shard_map/out_terms/pallas_call | solution.py:512
  120.2 7.0 %input_terms.3 = bf16[4,528,512]{2,1,0:T(8,128)(2,1)} custom-call(s32[13]{0:T(128)} %pad_add_fusion.refs_0_.idx_ref, f32[8,512]{1,0:T(8,128)} %copy-done.25, bf16[512,768]{1,0:T(8,128)(2,1)} %get-tuple-element.68.grad_ref, f32[8,512]{1,0:T(8,128)} %get-tuple-element.66.dots_ref, bf16[4096,512]{1,0:T(8,128)(2,1)} %wq_ref.3, bf16[4096,128]{1,0:T(8,128)(2,1)} %wk_ref.3, ...), custom_call_target="tpu_custom_call" | custom-call | flops 32212254720 | bytes 104857600 | tf_op jit(solution)/shard_map/input_terms/pallas_call | solution.py:555
  127.3 6.6 %input_terms.2 = bf16[4,528,512]{2,1,0:T(8,128)(2,1)} custom-call(s32[13]{0:T(128)} %pad_add_fusion.refs_0_.idx_ref, f32[8,512]{1,0:T(8,128)} %copy-done.25, bf16[512,768]{1,0:T(8,128)(2,1)} %get-tuple-element.68.grad_ref, f32[8,512]{1,0:T(8,128)} %get-tuple-element.66.dots_ref, bf16[4096,512]{1,0:T(8,128)(2,1)} %wq_ref.3, bf16[4096,128]{1,0:T(8,128)(2,1)} %wk_ref.3, ...), custom_call_target="tpu_custom_call" | custom-call | flops 32212254720 | bytes 104857600 | tf_op jit(solution)/shard_map/input_terms/pallas_call | solution.py:555
  133.9 5.5 %out_terms.2 = bf16[4,512,512]{2,1,0:T(8,128)(2,1)} custom-call(s32[13]{0:T(128)} %pad_add_fusion.refs_0_.idx_ref, f32[8,512]{1,0:T(8,128)} %copy-done.25, bf16[512,512]{1,0:T(8,128)(2,1)} %get-tuple-element.67.attended_ref, bf16[512,4096]{1,0:T(8,128)(2,1)} %wo_ref.3), custom_call_target="tpu_custom_call" | custom-call | flops 21474836480 | bytes 83886080 | tf_op jit(solution)/shard_map/out_terms/pallas_call | solution.py:512
  139.4 2.4 add_convert_fusion.1
  141.8 0.6 add_convert_fusion
  142.9 2.5 collective-permute-start.22
  145.4 1.5 collective-permute-start.27
  146.9 4.2 %collective-permute-done.25 = bf16[256,512]{1,0:T(8,128)(2,1)S(1)} collective-permute-done((bf16[256,512]{1,0:T(8,128)(2,1)S(1)}, bf16[256,512]{1,0:T(8,128)(2,1)S(1)}, u32[]{:S(2)}, u32[]{:S(2)}) %collective-permute-start.25) | collective-permute-done | bytes 262176 | tf_op jit(solution)/shard_map/ppermute | solution.py:567
  151.3 5.8 %collective-permute-done.27 = bf16[272,512]{1,0:T(8,128)(2,1)S(1)} collective-permute-done((bf16[272,512]{1,0:T(8,128)(2,1)S(1)}, bf16[272,512]{1,0:T(8,128)(2,1)S(1)}, u32[]{:S(2)}, u32[]{:S(2)}) %collective-permute-start.27) | collective-permute-done | bytes 278560 | tf_op jit(solution)/shard_map/ppermute | solution.py:567
  157.2 2.6 %collective-permute-start.28 = (bf16[528,512]{1,0:T(8,128)(2,1)S(1)}, bf16[528,512]{1,0:T(8,128)(2,1)S(1)}, u32[]{:S(2)}, u32[]{:S(2)}) collective-permute-start(bf16[528,512]{1,0:T(8,128)(2,1)S(1)} %pad_maximum_fusion.1), channel_id=1, source_target_pairs={{0,6},{2,0},{4,2},{6,4},{1,7},{3,1},{5,3},{7,5},{8,14},{10,8},{12,... | collective-permute-start | bytes 1622024 | tf_op jit(solution)/shard_map/ppermute | solution.py:567
  160.2 2.7 %collective-permute-start.23 = (bf16[512,512]{1,0:T(8,128)(2,1)S(1)}, bf16[512,512]{1,0:T(8,128)(2,1)S(1)}, u32[]{:S(2)}, u32[]{:S(2)}) collective-permute-start(bf16[512,512]{1,0:T(8,128)(2,1)S(1)} %pad_maximum_fusion.4), channel_id=1, source_target_pairs={{0,6},{2,0},{4,2},{6,4},{1,7},{3,1},{5,3},{7,5},{8,14},{10,8},{12,... | collective-permute-start | bytes 1572872 | tf_op jit(solution)/shard_map/ppermute | solution.py:567
  163.1 5.3 %collective-permute-done.26 = bf16[528,512]{1,0:T(8,128)(2,1)S(1)} collective-permute-done((bf16[528,512]{1,0:T(8,128)(2,1)S(1)}, bf16[528,512]{1,0:T(8,128)(2,1)S(1)}, u32[]{:S(2)}, u32[]{:S(2)}) %collective-permute-start.26) | collective-permute-done | bytes 540704 | tf_op jit(solution)/shard_map/ppermute | solution.py:567
  168.4 1.4 collective-permute-done.28
  170.0 9.6 %collective-permute-done.21 = bf16[512,512]{1,0:T(8,128)(2,1)S(1)} collective-permute-done((bf16[512,512]{1,0:T(8,128)(2,1)S(1)}, bf16[512,512]{1,0:T(8,128)(2,1)S(1)}, u32[]{:S(2)}, u32[]{:S(2)}) %collective-permute-start.21) | collective-permute-done | bytes 524320 | tf_op jit(solution)/shard_map/ppermute | solution.py:567
  179.5 1.5 collective-permute-done.23
  181.0 1.4 fusion.6
  182.4 17.3 %all_to_all.20 = bf16[16,32,512]{2,1,0:T(8,128)(2,1)S(1)} all-to-all(bf16[16,32,512]{2,1,0:T(8,128)(2,1)S(1)} %bitcast.80), channel_id=1, replica_groups=mesh['x'=4,'z'=4,'y'=4,'core'=2] {'x','z'}, dimensions={0} | all-to-all | bytes 1048576 | tf_op jit(solution)/shard_map/all_to_all | solution.py:601
  199.7 5.1 %all-to-all-start.3 = ((bf16[16,32,512]{2,1,0:T(8,128)(2,1)}), bf16[16,32,512]{2,1,0:T(8,128)(2,1)S(1)}, u32[]{:S(2)}, u32[]{:S(2)}) async-start(bf16[16,32,512]{2,1,0:T(8,128)(2,1)} %bitcast.28), calls=%async_computation.3 | async-start | bytes 1048576 | tf_op jit(solution)/shard_map/all_to_all | solution.py:601
  204.9 1.4 gather_fusion
  206.3 7.8 %all-to-all-done.3 = bf16[16,32,512]{2,1,0:T(8,128)(2,1)S(1)} async-done(((bf16[16,32,512]{2,1,0:T(8,128)(2,1)}), bf16[16,32,512]{2,1,0:T(8,128)(2,1)S(1)}, u32[]{:S(2)}, u32[]{:S(2)}) %all-to-all-start.3) | async-done | bytes 524320 | tf_op jit(solution)/shard_map/all_to_all | solution.py:601
  214.1 1.4 gather_fusion.1
  215.4 26.4 %all-reduce.4.cloned.1.call-done = (bf16[4096,512]{1,0:T(8,128)(2,1)}, bf16[4096,128]{1,0:T(8,128)(2,1)}, bf16[4096,128]{1,0:T(8,128)(2,1)}) async-done(((bf16[4096,512]{1,0:T(8,128)(2,1)}, bf16[4096,128]{1,0:T(8,128)(2,1)}, bf16[4096,128]{1,0:T(8,128)(2,1)}), (bf16[4096,512]{1,0:T(8,128)(2,1)}, bf16[4096,128]{1,0:T(8,128)(2,1)}, bf16[4096,128]{1,0:T(8,128)(2,1)})) %all-reduce.4.cloned.1.call-update) | async-done | bytes 6291472 | tf_op jit(solution)/shard_map/psum | solution.py:660
  241.8 5.8 %finish.1 = (bf16[4096,512]{1,0:T(8,128)(2,1)}, bf16[4096,128]{1,0:T(8,128)(2,1)}, bf16[4096,128]{1,0:T(8,128)(2,1)}) custom-call(bf16[4096,512]{1,0:T(8,128)(2,1)} %get-tuple-element.75.refs_0_, bf16[4096,128]{1,0:T(8,128)(2,1)} %get-tuple-element.76.refs_1_, bf16[4096,128]{1,0:T(8,128)(2,1)} %get-tuple-element.77.refs_2_), custom_call_target="tpu_custom_call" | custom-call | bytes 12582912 | tf_op jit(solution)/shard_map/finish/pallas_call | solution.py:476
  (111 shorter events, 4.6 us)
Async XLA Ops:
  7.2 10.5 %copy-start.18 = (s32[512]{0:T(512)S(1)}, s32[512]{0:T(512)}, u32[]{:S(2)}) copy-start(s32[512]{0:T(512)} %param.13) | copy-start | bytes 6148
  9.1 28.4 %copy-start.17 = (f32[4096]{0:T(1024)S(1)}, f32[4096]{0:T(1024)}, u32[]{:S(2)}) copy-start(f32[4096]{0:T(1024)} %param.12) | copy-start | bytes 49156
  9.1 29.1 %copy-start.20 = (s32[4]{0:T(128)S(1)}, s32[4]{0:T(128)}, u32[]{:S(2)}) copy-start(s32[4]{0:T(128)} %constant.100.clone) | copy-start | bytes 52
  9.1 18.9 %all-to-all-start = ((bf16[16,32,512]{2,1,0:T(8,128)(2,1)}), bf16[16,32,512]{2,1,0:T(8,128)(2,1)S(1)}, u32[]{:S(2)}, u32[]{:S(2)}) async-start(bf16[16,32,512]{2,1,0:T(8,128)(2,1)} %place.1), calls=%async_computation | async-start | bytes 1048576 | tf_op jit(solution)/shard_map/all_to_all | solution.py:601
  28.0 0.8 copy-start
  31.0 21.2 %all-to-all-start.1 = ((bf16[16,32,640]{2,1,0:T(8,128)(2,1)}), bf16[16,32,640]{2,1,0:T(8,128)(2,1)S(1)}, u32[]{:S(2)}, u32[]{:S(2)}) async-start(bf16[16,32,640]{2,1,0:T(8,128)(2,1)} %place_meta.1), calls=%async_computation.1 | async-start | bytes 1310720 | tf_op jit(solution)/shard_map/all_to_all | solution.py:601
  34.6 207.2 %all-reduce.4.cloned.1.call-start = ((), (), s32[]{:S(2)}) async-start(), calls=%async_computation.4 | async-start | bytes 12582912 | tf_op jit(solution)/shard_map/psum | solution.py:660
  34.7 12.9 %collective-permute-start = (bf16[512,512]{1,0:T(8,128)(2,1)}, bf16[512,512]{1,0:T(8,128)(2,1)S(1)}, u32[]{:S(2)}, u32[]{:S(2)}) collective-permute-start(bf16[512,512]{1,0:T(8,128)(2,1)} %bitcast.72), channel_id=1, source_target_pairs={{0,2},{2,4},{4,6},{6,0},{1,3},{3,5},{5,7},{7,1},{8,10},{10,12},{12... | collective-permute-start | bytes 1572872 | tf_op jit(solution)/shard_map/ppermute | solution.py:567
  36.0 15.3 %collective-permute-start.2 = (bf16[512,512]{1,0:T(8,128)(2,1)}, bf16[512,512]{1,0:T(8,128)(2,1)S(1)}, u32[]{:S(2)}, u32[]{:S(2)}) collective-permute-start(bf16[512,512]{1,0:T(8,128)(2,1)} %bitcast.73), channel_id=1, source_target_pairs={{0,6},{2,0},{4,2},{6,4},{1,7},{3,1},{5,3},{7,5},{8,14},{10,8},{12,... | collective-permute-start | bytes 1572872 | tf_op jit(solution)/shard_map/ppermute | solution.py:567
  38.8 16.9 %collective-permute-start.6 = (bf16[512,512]{1,0:T(8,128)(2,1)}, bf16[512,512]{1,0:T(8,128)(2,1)}, u32[]{:S(2)}, u32[]{:S(2)}) collective-permute-start(bf16[512,512]{1,0:T(8,128)(2,1)} %bitcast.74), channel_id=1, source_target_pairs={{0,1},{1,0},{2,3},{3,2},{4,5},{5,4},{6,7},{7,6},{8,9},{9,8},{10,11... | collective-permute-start | bytes 1572872 | tf_op jit(solution)/shard_map/ppermute | solution.py:571
  47.6 7.7 %copy-start.7 = (bf16[512,512]{1,0:T(8,128)(2,1)}, bf16[512,512]{1,0:T(8,128)(2,1)S(1)}, u32[]{:S(2)}) copy-start(bf16[512,512]{1,0:T(8,128)(2,1)S(1)} %collective-permute-done.refs_2_) | copy-start | bytes 1572868
  47.6 8.2 %collective-permute-start.7 = (bf16[512,512]{1,0:T(8,128)(2,1)S(1)}, bf16[512,512]{1,0:T(8,128)(2,1)}, u32[]{:S(2)}, u32[]{:S(2)}) collective-permute-start(bf16[512,512]{1,0:T(8,128)(2,1)S(1)} %collective-permute-done.refs_2_), channel_id=1, source_target_pairs={{0,1},{1,0},{2,3},{3,2},{4,5},{5,4},{6,7},{7,6},{8,9},{9,8},{10,11... | collective-permute-start | bytes 1572872 | tf_op jit(solution)/shard_map/ppermute | solution.py:571
  51.3 4.2 %copy-start.8 = (bf16[512,512]{1,0:T(8,128)(2,1)}, bf16[512,512]{1,0:T(8,128)(2,1)S(1)}, u32[]{:S(2)}) copy-start(bf16[512,512]{1,0:T(8,128)(2,1)S(1)} %collective-permute-done.2.refs_3_) | copy-start | bytes 1572868
  51.3 8.1 %collective-permute-start.8 = (bf16[512,512]{1,0:T(8,128)(2,1)S(1)}, bf16[512,512]{1,0:T(8,128)(2,1)}, u32[]{:S(2)}, u32[]{:S(2)}) collective-permute-start(bf16[512,512]{1,0:T(8,128)(2,1)S(1)} %collective-permute-done.2.refs_3_), channel_id=1, source_target_pairs={{0,1},{1,0},{2,3},{3,2},{4,5},{5,4},{6,7},{7,6},{8,9},{9,8},{10,11... | collective-permute-start | bytes 1572872 | tf_op jit(solution)/shard_map/ppermute | solution.py:571
  52.3 21.5 %copy-start.2 = (bf16[16,32,512]{2,1,0:T(8,128)(2,1)}, bf16[16,32,512]{2,1,0:T(8,128)(2,1)S(1)}, u32[]{:S(2)}) copy-start(bf16[16,32,512]{2,1,0:T(8,128)(2,1)S(1)} %slice.114) | copy-start | bytes 1572868
  52.3 20.1 %collective-permute-start.4 = (bf16[512,512]{1,0:T(8,128)(2,1)S(1)}, bf16[512,512]{1,0:T(8,128)(2,1)S(1)}, u32[]{:S(2)}, u32[]{:S(2)}) collective-permute-start(bf16[512,512]{1,0:T(8,128)(2,1)S(1)} %bitcast.76), channel_id=1, source_target_pairs={{0,2},{2,4},{4,6},{6,0},{1,3},{3,5},{5,7},{7,1},{8,10},{10,12},{12... | collective-permute-start | bytes 1572872 | tf_op jit(solution)/shard_map/ppermute | solution.py:567
  52.7 19.6 %collective-permute-start.5 = (bf16[512,512]{1,0:T(8,128)(2,1)S(1)}, bf16[512,512]{1,0:T(8,128)(2,1)S(1)}, u32[]{:S(2)}, u32[]{:S(2)}) collective-permute-start(bf16[512,512]{1,0:T(8,128)(2,1)S(1)} %bitcast.77), channel_id=1, source_target_pairs={{0,6},{2,0},{4,2},{6,4},{1,7},{3,1},{5,3},{7,5},{8,14},{10,8},{12,... | collective-permute-start | bytes 1572872 | tf_op jit(solution)/shard_map/ppermute | solution.py:567
  55.7 16.7 %collective-permute-start.1 = (bf16[256,512]{1,0:T(8,128)(2,1)}, bf16[256,512]{1,0:T(8,128)(2,1)S(1)}, u32[]{:S(2)}, u32[]{:S(2)}) collective-permute-start(bf16[256,512]{1,0:T(8,128)(2,1)} %slice.112), channel_id=1, source_target_pairs={{0,2},{2,4},{4,6},{6,0},{1,3},{3,5},{5,7},{7,1},{8,10},{10,12},{12... | collective-permute-start | bytes 786440 | tf_op jit(solution)/shard_map/ppermute | solution.py:567
  55.8 16.6 %collective-permute-start.3 = (bf16[256,512]{1,0:T(8,128)(2,1)}, bf16[256,512]{1,0:T(8,128)(2,1)S(1)}, u32[]{:S(2)}, u32[]{:S(2)}) collective-permute-start(bf16[256,512]{1,0:T(8,128)(2,1)} %slice.113), channel_id=1, source_target_pairs={{0,6},{2,0},{4,2},{6,4},{1,7},{3,1},{5,3},{7,5},{8,14},{10,8},{12,... | collective-permute-start | bytes 786440 | tf_op jit(solution)/shard_map/ppermute | solution.py:567
  72.3 7.4 %copy-start.12 = (bf16[256,512]{1,0:T(8,128)(2,1)}, bf16[256,512]{1,0:T(8,128)(2,1)S(1)}, u32[]{:S(2)}) copy-start(bf16[256,512]{1,0:T(8,128)(2,1)S(1)} %collective-permute-done.1.refs_1_) | copy-start | bytes 786436
  72.4 7.4 %copy-start.13 = (bf16[256,512]{1,0:T(8,128)(2,1)}, bf16[256,512]{1,0:T(8,128)(2,1)S(1)}, u32[]{:S(2)}) copy-start(bf16[256,512]{1,0:T(8,128)(2,1)S(1)} %collective-permute-done.3.refs_2_) | copy-start | bytes 786436
  72.4 17.0 %copy-start.5 = (bf16[512,512]{1,0:T(8,128)(2,1)}, bf16[512,512]{1,0:T(8,128)(2,1)S(1)}, u32[]{:S(2)}) copy-start(bf16[512,512]{1,0:T(8,128)(2,1)S(1)} %collective-permute-done.4.refs_2_) | copy-start | bytes 1572868
  72.4 17.0 %copy-start.6 = (bf16[512,512]{1,0:T(8,128)(2,1)}, bf16[512,512]{1,0:T(8,128)(2,1)S(1)}, u32[]{:S(2)}) copy-start(bf16[512,512]{1,0:T(8,128)(2,1)S(1)} %collective-permute-done.5.refs_3_) | copy-start | bytes 1572868
  72.4 17.0 %collective-permute-start.12 = (bf16[512,512]{1,0:T(8,128)(2,1)S(1)}, bf16[512,512]{1,0:T(8,128)(2,1)S(1)}, u32[]{:S(2)}, u32[]{:S(2)}) collective-permute-start(bf16[512,512]{1,0:T(8,128)(2,1)S(1)} %collective-permute-done.4.refs_2_), channel_id=1, source_target_pairs={{0,1},{1,0},{2,3},{3,2},{4,5},{5,4},{6,7},{7,6},{8,9},{9,8},{10,11... | collective-permute-start | bytes 1572872 | tf_op jit(solution)/shard_map/ppermute | solution.py:571
  73.6 15.8 %collective-permute-start.13 = (bf16[512,512]{1,0:T(8,128)(2,1)S(1)}, bf16[512,512]{1,0:T(8,128)(2,1)S(1)}, u32[]{:S(2)}, u32[]{:S(2)}) collective-permute-start(bf16[512,512]{1,0:T(8,128)(2,1)S(1)} %collective-permute-done.5.refs_3_), channel_id=1, source_target_pairs={{0,1},{1,0},{2,3},{3,2},{4,5},{5,4},{6,7},{7,6},{8,9},{9,8},{10,11... | collective-permute-start | bytes 1572872 | tf_op jit(solution)/shard_map/ppermute | solution.py:571
  73.7 15.7 %collective-permute-start.11 = (bf16[512,512]{1,0:T(8,128)(2,1)S(1)}, bf16[512,512]{1,0:T(8,128)(2,1)S(1)}, u32[]{:S(2)}, u32[]{:S(2)}) collective-permute-start(bf16[512,512]{1,0:T(8,128)(2,1)S(1)} %bitcast.78), channel_id=1, source_target_pairs={{0,1},{1,0},{2,3},{3,2},{4,5},{5,4},{6,7},{7,6},{8,9},{9,8},{10,11... | collective-permute-start | bytes 1572872 | tf_op jit(solution)/shard_map/ppermute | solution.py:571
  74.1 2.9 %collective-permute-start.14 = (bf16[256,512]{1,0:T(8,128)(2,1)S(1)}, bf16[256,512]{1,0:T(8,128)(2,1)S(1)}, u32[]{:S(2)}, u32[]{:S(2)}) collective-permute-start(bf16[256,512]{1,0:T(8,128)(2,1)S(1)} %collective-permute-done.1.refs_1_), channel_id=1, source_target_pairs={{0,1},{1,0},{2,3},{3,2},{4,5},{5,4},{6,7},{7,6},{8,9},{9,8},{10,11... | collective-permute-start | bytes 786440 | tf_op jit(solution)/shard_map/ppermute | solution.py:571
  74.3 5.4 %collective-permute-start.15 = (bf16[256,512]{1,0:T(8,128)(2,1)S(1)}, bf16[256,512]{1,0:T(8,128)(2,1)S(1)}, u32[]{:S(2)}, u32[]{:S(2)}) collective-permute-start(bf16[256,512]{1,0:T(8,128)(2,1)S(1)} %collective-permute-done.3.refs_2_), channel_id=1, source_target_pairs={{0,1},{1,0},{2,3},{3,2},{4,5},{5,4},{6,7},{7,6},{8,9},{9,8},{10,11... | collective-permute-start | bytes 786440 | tf_op jit(solution)/shard_map/ppermute | solution.py:571
  77.0 2.7 %copy-start.14 = (bf16[256,512]{1,0:T(8,128)(2,1)}, bf16[256,512]{1,0:T(8,128)(2,1)S(1)}, u32[]{:S(2)}) copy-start(bf16[256,512]{1,0:T(8,128)(2,1)S(1)} %collective-permute-done.14.refs_3_) | copy-start | bytes 786436
  77.0 19.5 %collective-permute-start.10 = (bf16[256,512]{1,0:T(8,128)(2,1)S(1)}, bf16[256,512]{1,0:T(8,128)(2,1)S(1)}, u32[]{:S(2)}, u32[]{:S(2)}) collective-permute-start(bf16[256,512]{1,0:T(8,128)(2,1)S(1)} %slice.85), channel_id=1, source_target_pairs={{0,6},{2,0},{4,2},{6,4},{1,7},{3,1},{5,3},{7,5},{8,14},{10,8},{12,... | collective-permute-start | bytes 786440 | tf_op jit(solution)/shard_map/ppermute | solution.py:567
  79.7 0.7 copy-start.15
  79.7 16.8 %collective-permute-start.9 = (bf16[256,512]{1,0:T(8,128)(2,1)S(1)}, bf16[256,512]{1,0:T(8,128)(2,1)S(1)}, u32[]{:S(2)}, u32[]{:S(2)}) collective-permute-start(bf16[256,512]{1,0:T(8,128)(2,1)S(1)} %slice.84), channel_id=1, source_target_pairs={{0,2},{2,4},{4,6},{6,0},{1,3},{3,5},{5,7},{7,1},{8,10},{10,12},{12... | collective-permute-start | bytes 786440 | tf_op jit(solution)/shard_map/ppermute | solution.py:567
  89.4 0.8 copy-start.9
  89.4 1.0 copy-start.10
  89.5 1.1 copy-start.11
  96.5 2.3 copy-start.21
  96.6 2.3 copy-start.22
  96.6 1.9 collective-permute-start.16
  97.3 1.5 collective-permute-start.17
  98.5 0.7 copy-start.23
  98.8 0.7 copy-start.24
  112.1 1.7 collective-permute-start.18
  113.8 0.6 copy-start.25
  119.9 19.5 %collective-permute-start.19 = (bf16[4,512,512]{2,1,0:T(8,128)(2,1)}, bf16[4,512,512]{2,1,0:T(8,128)(2,1)S(1)}, u32[]{:S(2)}, u32[]{:S(2)}) collective-permute-start(bf16[4,512,512]{2,1,0:T(8,128)(2,1)} %out_terms.3), channel_id=1, source_target_pairs={{0,1},{1,0},{2,3},{3,2},{4,5},{5,4},{6,7},{7,6},{8,9},{9,8},{10,11... | collective-permute-start | bytes 6291464 | tf_op jit(solution)/shard_map/ppermute | solution.py:571
  127.2 14.5 %collective-permute-start.24 = (bf16[4,528,512]{2,1,0:T(8,128)(2,1)}, bf16[4,528,512]{2,1,0:T(8,128)(2,1)S(1)}, u32[]{:S(2)}, u32[]{:S(2)}) collective-permute-start(bf16[4,528,512]{2,1,0:T(8,128)(2,1)} %input_terms.3), channel_id=1, source_target_pairs={{0,1},{1,0},{2,3},{3,2},{4,5},{5,4},{6,7},{7,6},{8,9},{9,8},{10,11... | collective-permute-start | bytes 6488072 | tf_op jit(solution)/shard_map/ppermute | solution.py:571
  139.4 2.4 copy-start.4
  142.4 8.7 %collective-permute-start.25 = (bf16[256,512]{1,0:T(8,128)(2,1)S(1)}, bf16[256,512]{1,0:T(8,128)(2,1)S(1)}, u32[]{:S(2)}, u32[]{:S(2)}) collective-permute-start(bf16[256,512]{1,0:T(8,128)(2,1)S(1)} %get-tuple-element.78), channel_id=1, source_target_pairs={{0,2},{2,4},{4,6},{6,0},{1,3},{3,5},{5,7},{7,1},{8,10},{10,12},{12... | collective-permute-start | bytes 786440 | tf_op jit(solution)/shard_map/ppermute | solution.py:567
  142.6 17.3 %collective-permute-start.20 = (bf16[256,512]{1,0:T(8,128)(2,1)S(1)}, bf16[256,512]{1,0:T(8,128)(2,1)S(1)}, u32[]{:S(2)}, u32[]{:S(2)}) collective-permute-start(bf16[256,512]{1,0:T(8,128)(2,1)S(1)} %get-tuple-element.84), channel_id=1, source_target_pairs={{0,2},{2,4},{4,6},{6,0},{1,3},{3,5},{5,7},{7,1},{8,10},{10,12},{12... | collective-permute-start | bytes 786440 | tf_op jit(solution)/shard_map/ppermute | solution.py:567
  142.9 17.0 %collective-permute-start.22 = (bf16[256,512]{1,0:T(8,128)(2,1)S(1)}, bf16[256,512]{1,0:T(8,128)(2,1)S(1)}, u32[]{:S(2)}, u32[]{:S(2)}) collective-permute-start(bf16[256,512]{1,0:T(8,128)(2,1)S(1)} %get-tuple-element.85), channel_id=1, source_target_pairs={{0,6},{2,0},{4,2},{6,4},{1,7},{3,1},{5,3},{7,5},{8,14},{10,8},{12,... | collective-permute-start | bytes 786440 | tf_op jit(solution)/shard_map/ppermute | solution.py:567
  145.4 11.6 %collective-permute-start.27 = (bf16[272,512]{1,0:T(8,128)(2,1)S(1)}, bf16[272,512]{1,0:T(8,128)(2,1)S(1)}, u32[]{:S(2)}, u32[]{:S(2)}) collective-permute-start(bf16[272,512]{1,0:T(8,128)(2,1)S(1)} %get-tuple-element.81), channel_id=1, source_target_pairs={{0,6},{2,0},{4,2},{6,4},{1,7},{3,1},{5,3},{7,5},{8,14},{10,8},{12,... | collective-permute-start | bytes 835592 | tf_op jit(solution)/shard_map/ppermute | solution.py:567
  151.2 17.2 %collective-permute-start.26 = (bf16[528,512]{1,0:T(8,128)(2,1)S(1)}, bf16[528,512]{1,0:T(8,128)(2,1)S(1)}, u32[]{:S(2)}, u32[]{:S(2)}) collective-permute-start(bf16[528,512]{1,0:T(8,128)(2,1)S(1)} %pad_maximum_fusion), channel_id=1, source_target_pairs={{0,2},{2,4},{4,6},{6,0},{1,3},{3,5},{5,7},{7,1},{8,10},{10,12},{12... | collective-permute-start | bytes 1622024 | tf_op jit(solution)/shard_map/ppermute | solution.py:567
  157.2 5.7 %copy-start.16 = (f32[512,128]{1,0:T(8,128)S(1)}, f32[512,128]{1,0:T(8,128)}, u32[]{:S(2)}) copy-start(f32[512,128]{1,0:T(8,128)} %get-tuple-element.65.refs_14_) | copy-start | bytes 786436
  157.2 12.5 %collective-permute-start.28 = (bf16[528,512]{1,0:T(8,128)(2,1)S(1)}, bf16[528,512]{1,0:T(8,128)(2,1)S(1)}, u32[]{:S(2)}, u32[]{:S(2)}) collective-permute-start(bf16[528,512]{1,0:T(8,128)(2,1)S(1)} %pad_maximum_fusion.1), channel_id=1, source_target_pairs={{0,6},{2,0},{4,2},{6,4},{1,7},{3,1},{5,3},{7,5},{8,14},{10,8},{12,... | collective-permute-start | bytes 1622024 | tf_op jit(solution)/shard_map/ppermute | solution.py:567
  160.0 21.0 %copy-start.1 = (bf16[16,32,512]{2,1,0:T(8,128)(2,1)S(1)}, bf16[16,32,512]{2,1,0:T(8,128)(2,1)}, u32[]{:S(2)}) copy-start(bf16[16,32,512]{2,1,0:T(8,128)(2,1)} %copy-done) | copy-start | bytes 1572868
  160.1 21.0 %copy-start.3 = (bf16[16,32,512]{2,1,0:T(8,128)(2,1)S(1)}, bf16[16,32,512]{2,1,0:T(8,128)(2,1)}, u32[]{:S(2)}) copy-start(bf16[16,32,512]{2,1,0:T(8,128)(2,1)} %copy-done.2) | copy-start | bytes 1572868
  160.1 19.5 %collective-permute-start.21 = (bf16[512,512]{1,0:T(8,128)(2,1)S(1)}, bf16[512,512]{1,0:T(8,128)(2,1)S(1)}, u32[]{:S(2)}, u32[]{:S(2)}) collective-permute-start(bf16[512,512]{1,0:T(8,128)(2,1)S(1)} %pad_maximum_fusion.3), channel_id=1, source_target_pairs={{0,2},{2,4},{4,6},{6,0},{1,3},{3,5},{5,7},{7,1},{8,10},{10,12},{12... | collective-permute-start | bytes 1572872 | tf_op jit(solution)/shard_map/ppermute | solution.py:567
  160.2 20.8 %collective-permute-start.23 = (bf16[512,512]{1,0:T(8,128)(2,1)S(1)}, bf16[512,512]{1,0:T(8,128)(2,1)S(1)}, u32[]{:S(2)}, u32[]{:S(2)}) collective-permute-start(bf16[512,512]{1,0:T(8,128)(2,1)S(1)} %pad_maximum_fusion.4), channel_id=1, source_target_pairs={{0,6},{2,0},{4,2},{6,4},{1,7},{3,1},{5,3},{7,5},{8,14},{10,8},{12,... | collective-permute-start | bytes 1572872 | tf_op jit(solution)/shard_map/ppermute | solution.py:567
  182.4 22.5 %copy-start.19 = (s32[16]{0:T(128)S(1)}, s32[16]{0:T(128)}, u32[]{:S(2)}) copy-start(s32[16]{0:T(128)} %plan_ref.3) | copy-start | bytes 196
  199.7 14.4 %all-to-all-start.3 = ((bf16[16,32,512]{2,1,0:T(8,128)(2,1)}), bf16[16,32,512]{2,1,0:T(8,128)(2,1)S(1)}, u32[]{:S(2)}, u32[]{:S(2)}) async-start(bf16[16,32,512]{2,1,0:T(8,128)(2,1)} %bitcast.28), calls=%async_computation.3 | async-start | bytes 1048576 | tf_op jit(solution)/shard_map/all_to_all | solution.py:601
Sparse Core Ops, SparseCore 0:
  113.0 128.8 all-reduce.3

commit v7 on v6

--- a/solution.py
+++ b/solution.py
@@ -15,7 +15,7 @@
 STEPS = (0, -1, 1, 2)
 BF = jnp.bfloat16
 F32 = jnp.float32
-VMEM_LIMIT = 56 * 1024 * 1024
+VMEM_LIMIT = 60 * 1024 * 1024
 
 
 def params():
@@ -55,7 +55,7 @@
     )(plan, panels)
 
 
-def place_meta_kernel(plan_ref, _, rows_ref, docs_ref, out_ref):
+def place_meta_kernel(plan_ref, rows_ref, docs_ref, out_ref):
     count, rows, width = rows_ref.shape
     for panel in range(count):
         target = plan_ref[panel] // count
@@ -71,14 +71,13 @@
         out_ref[target, :, width:] = extra.astype(BF)
 
 
-def place_meta(plan, after, panels, docs):
+def place_meta(plan, panels, docs):
     count, rows, width = panels.shape
     return pl.pallas_call(
         place_meta_kernel,
         out_shape=jax.ShapeDtypeStruct((count, rows, width + 128), panels.dtype),
         in_specs=[
             pl.BlockSpec(memory_space=pltpu.SMEM),
-            pl.BlockSpec(memory_space=pltpu.HBM),
             pl.BlockSpec(memory_space=pltpu.VMEM),
             pl.BlockSpec(memory_space=pltpu.VMEM),
         ],
@@ -86,7 +85,7 @@
         compiler_params=params(),
         cost_estimate=cost(0, 2 * panels.size * 2),
         name="place_meta",
-    )(plan, after, panels, docs.reshape(count, rows, 1))
+    )(plan, panels, docs.reshape(count, rows, 1))
 
 
 NEAR = tuple((step, other) for step in range(3) for other in (0, 1))
@@ -621,9 +620,7 @@
 
     here_tokens = exchange(place(panel_plan, tokens.reshape(count, panel, width))).reshape(rows, width)
     arrived = exchange(
-        place_meta(
-            panel_plan, here_tokens, cotangent.reshape(count, panel, width), doc_ids.reshape(count, panel)
-        )
+        place_meta(panel_plan, cotangent.reshape(count, panel, width), doc_ids.reshape(count, panel))
     )
     here_cot = arrived[:, :, :width].reshape(rows, width)
     meta = arrived[:, :, width : width + 3].reshape(rows, 3).astype(jnp.int32)

time: 256 us -> 247 us (0.965)
  waiting for transfers between devices: 84.7 us -> 76.1 us
    ppermute x16, waiting for transfers between devices: 38 us -> 28.9 us  [shift(): lax.ppermute(array, axis, [(i, (i + step) % size) for i in range(size)])]
  transfers between devices with their start and end apart: 33 -> 33, of which waited for: 15 -> 14; matrix products, arithmetic and copies ran while one was open for 6% -> 7% of each run, Pallas kernels for 19% -> 20%
where the time goes in v7:
time: 247 us; the launch traced here: 245 us
  waiting for transfers between devices  76.1 us (31%)
  Pallas kernels  70.3 us (28%)
  starting transfers between devices  49.1 us (20%)
  blocking collectives  16.7 us (7%)
  between operations  14.6 us (6%)
  local copies, waits for them, and re-layouts  10.2 us (4%)
  other arithmetic  8.52 us (3%)
    ppermute x16, waiting for transfers between devices, shift(): lax.ppermute(array, axis, [(i, (i + step) % size) for i in range(size)])  28.9 us
    psum x1, waiting for transfers between devices, per_device(): lax.psum(tuple(grads), ('x', 'z'))  26.6 us
    ppermute x16, starting transfers between devices, shift(): lax.ppermute(array, axis, [(i, (i + step) % size) for i in range(size)])  20 us
    all_to_all x3, waiting for transfers between devices, exchange(): lax.all_to_all(panels, ('x', 'z'), split_axis=0, concat_axis=0, tiled=True)  18.1 us
    all_to_all x3, starting transfers between devices, exchange(): lax.all_to_all(panels, ('x', 'z'), split_axis=0, concat_axis=0, tiled=True)  17.6 us
    all_to_all x1, blocking collectives, exchange(): lax.all_to_all(panels, ('x', 'z'), split_axis=0, concat_axis=0, tiled=True)  16.7 us
    pallas_call x2, Pallas kernels, input_terms(): pl.pallas_call(input_term_kernel, grid_spec=grid_spec, out_shape=jax.Shap...  13.2 us
    pallas_call x1, Pallas kernels, back(): pl.pallas_call(functools.partial(back_kernel, scale=scale), grid=(1,), in...  12.5 us
  transfers between devices with their start and end apart: 33, of which 14 were waited for; matrix products, arithmetic and copies ran while one was open for 7% of the time, Pallas kernels for 20%

profile of v7, /device:TPU:1, one launch (start us, length us, event | category | flops | bytes accessed | tf_op | source)
XLA Modules:
  0.0 245.5 jit_solution(3440575789857216312)
XLA Ops:
  7.2 1.9 place.1
  9.1 8.6 %all-to-all-start = ((bf16[16,32,512]{2,1,0:T(8,128)(2,1)}), bf16[16,32,512]{2,1,0:T(8,128)(2,1)S(1)}, u32[]{:S(2)}, u32[]{:S(2)}) async-start(bf16[16,32,512]{2,1,0:T(8,128)(2,1)} %place.1), calls=%async_computation | async-start | bytes 1048576 | tf_op jit(solution)/shard_map/all_to_all | solution.py:600
  17.7 0.9 reshape_reshape.4.docs_ref
  18.6 2.2 place_meta.1
  20.8 7.1 %all-to-all-done = bf16[16,32,512]{2,1,0:T(8,128)(2,1)S(1)} async-done(((bf16[16,32,512]{2,1,0:T(8,128)(2,1)}), bf16[16,32,512]{2,1,0:T(8,128)(2,1)S(1)}, u32[]{:S(2)}, u32[]{:S(2)}) %all-to-all-start) | async-done | bytes 524320 | tf_op jit(solution)/shard_map/all_to_all | solution.py:600
  28.0 3.6 %all-to-all-start.1 = ((bf16[16,32,640]{2,1,0:T(8,128)(2,1)}), bf16[16,32,640]{2,1,0:T(8,128)(2,1)S(1)}, u32[]{:S(2)}, u32[]{:S(2)}) async-start(bf16[16,32,640]{2,1,0:T(8,128)(2,1)} %place_meta.1), calls=%async_computation.1 | async-start | bytes 1310720 | tf_op jit(solution)/shard_map/all_to_all | solution.py:600
  31.6 1.4 collective-permute-start
  33.0 0.6 reshape.162.refs_7_.refs_5_
  33.6 1.5 collective-permute-start.2
  35.1 0.7 pad_add_fusion.refs_0_.idx_ref
  35.7 2.6 %collective-permute-start.6 = (bf16[512,512]{1,0:T(8,128)(2,1)S(1)}, bf16[512,512]{1,0:T(8,128)(2,1)}, u32[]{:S(2)}, u32[]{:S(2)}) collective-permute-start(bf16[512,512]{1,0:T(8,128)(2,1)S(1)} %bitcast.73), channel_id=1, source_target_pairs={{0,1},{1,0},{2,3},{3,2},{4,5},{5,4},{6,7},{7,6},{8,9},{9,8},{10,11... | collective-permute-start | bytes 1572872 | tf_op jit(solution)/shard_map/ppermute | solution.py:570
  38.4 3.2 %all-to-all-done.1 = bf16[16,32,640]{2,1,0:T(8,128)(2,1)S(1)} async-done(((bf16[16,32,640]{2,1,0:T(8,128)(2,1)}), bf16[16,32,640]{2,1,0:T(8,128)(2,1)S(1)}, u32[]{:S(2)}, u32[]{:S(2)}) %all-to-all-start.1) | async-done | bytes 655392 | tf_op jit(solution)/shard_map/all_to_all | solution.py:600
  41.6 1.4 collective-permute-start.4
  43.0 1.5 collective-permute-start.5
  44.5 4.4 %collective-permute-start.7 = (bf16[512,512]{1,0:T(8,128)(2,1)S(1)}, bf16[512,512]{1,0:T(8,128)(2,1)}, u32[]{:S(2)}, u32[]{:S(2)}) collective-permute-start(bf16[512,512]{1,0:T(8,128)(2,1)S(1)} %collective-permute-done.refs_2_), channel_id=1, source_target_pairs={{0,1},{1,0},{2,3},{3,2},{4,5},{5,4},{6,7},{7,6},{8,9},{9,8},{10,11... | collective-permute-start | bytes 1572872 | tf_op jit(solution)/shard_map/ppermute | solution.py:570
  49.0 0.9 collective-permute-start.8
  50.5 0.7 slice.112
  51.2 1.0 slice.113
  52.2 1.4 collective-permute-start.1
  53.5 1.4 collective-permute-start.3
  55.0 1.0 multiply_cosine_fusion
  56.0 8.8 %project_near.1 = (bf16[3,1024,512]{2,1,0:T(8,128)(2,1)}, f32[512,768]{1,0:T(8,128)}, f32[512,128]{1,0:T(8,128)}) custom-call(s32[13]{0:T(128)} %pad_add_fusion.refs_0_.idx_ref, bf16[512,512]{1,0:T(8,128)(2,1)} %bitcast.74, bf16[512,512]{1,0:T(8,128)(2,1)} %copy-done.7, bf16[512,512]{1,0:T(8,128)(2,1)} %collective-permute-done.2.refs_3_, ...), custom_call_target="tpu_custom_call" | custom-call | flops 2415919104 | bytes 11010048 | tf_op jit(solution)/shard_map/project_near/pallas_call | solution.py:188
  64.8 0.6 collective-permute-start.12
  65.5 0.4 collective-permute-start.11
  66.1 0.4 collective-permute-start.15
  66.5 0.6 pad.4.refs_12_
  67.3 0.9 pad_maximum_fusion.2.refs_11_.refs_15_
  68.4 2.1 collective-permute-start.10
  70.8 0.5 copy-done.12
  71.2 8.9 %attend.1 = (bf16[1,1024,512]{2,1,0:T(8,128)(2,1)}, f32[512,128]{1,0:T(8,128)}, bf16[512,512]{1,0:T(8,128)(2,1)}, bf16[512,128]{1,0:T(8,128)(2,1)}, bf16[128,512...) custom-call(s32[13]{0:T(128)} %pad_add_fusion.refs_0_.idx_ref, ...), custom_call_target="tpu_custom_call" | custom-call | flops 1342177280 | bytes 3670016 | tf_op jit(solution)/shard_map/attend/pallas_call | solution.py:274
  80.2 0.8 copy-done.8
  81.0 6.0 %back_near.1.refs_6_ = f32[512,512]{1,0:T(8,128)} custom-call(s32[13]{0:T(128)} %pad_add_fusion.refs_0_.idx_ref, bf16[512,512]{1,0:T(8,128)(2,1)} %bitcast.78, bf16[512,512]{1,0:T(8,128)(2,1)} %copy-done.5, bf16[512,512]{1,0:T(8,128)(2,1)} %copy-done.6, bf16[512,512]{1,0:T(8,128)(2,1)} %collective-permute-done.11.refs_4_, bf16[512,512]{1,0:T(8,128)(2,1)} %copy-done.8, ...), custom_call_target="tpu_custom_call" | custom-call | flops 1610612736 | bytes 6291456 | tf_op jit(solution)/shard_map/back_near/pallas_call | solution.py:318
  87.0 0.7 collective-permute-start.16
  87.8 1.3 collective-permute-done.16.refs_3_
  89.3 0.5 copy-done.19
  90.0 12.5 %back.1 = (bf16[512,768]{1,0:T(8,128)(2,1)}, f32[8,512]{1,0:T(8,128)}, bf16[4096,512]{1,0:T(8,128)(2,1)}, bf16[4096,128]{1,0:T(8,128)(2,1)}, bf16[4096,128]{1,0:T(8,128)(2,1)}) custom-call(s32[13]{0:T(128)} %pad_add_fusion.refs_0_.idx_ref, bf16[256,512]{1,0:T(8,128)(2,1)} %collective-permute-done.9.refs_1_, bf16[256,512]{1,0:T(8,128)(2,1)} %copy-done.18, ...), custom_call_target="tpu_custom_call" | custom-call | flops 4831838208 | bytes 8388608 | tf_op jit(solution)/shard_map/back/pallas_call | solution.py:440
  102.5 0.7 collective-permute-start.18
  103.3 1.0 collective-permute-done.18._
  104.3 0.6 copy-done.21
  104.9 5.4 %out_terms.3 = bf16[4,512,512]{2,1,0:T(8,128)(2,1)} custom-call(s32[13]{0:T(128)} %pad_add_fusion.refs_0_.idx_ref, f32[8,512]{1,0:T(8,128)} %copy-done.21, bf16[512,512]{1,0:T(8,128)(2,1)} %get-tuple-element.67.attended_ref, bf16[512,4096]{1,0:T(8,128)(2,1)} %wo_ref.3), custom_call_target="tpu_custom_call" | custom-call | flops 21474836480 | bytes 83886080 | tf_op jit(solution)/shard_map/out_terms/pallas_call | solution.py:511
  110.6 6.6 %input_terms.3 = bf16[4,528,512]{2,1,0:T(8,128)(2,1)} custom-call(s32[13]{0:T(128)} %pad_add_fusion.refs_0_.idx_ref, f32[8,512]{1,0:T(8,128)} %copy-done.21, bf16[512,768]{1,0:T(8,128)(2,1)} %get-tuple-element.68.grad_ref, f32[8,512]{1,0:T(8,128)} %get-tuple-element.66.dots_ref, bf16[4096,512]{1,0:T(8,128)(2,1)} %wq_ref.3, bf16[4096,128]{1,0:T(8,128)(2,1)} %wk_ref.3, ...), custom_call_target="tpu_custom_call" | custom-call | flops 32212254720 | bytes 104857600 | tf_op jit(solution)/shard_map/input_terms/pallas_call | solution.py:554
  117.3 6.6 %input_terms.2 = bf16[4,528,512]{2,1,0:T(8,128)(2,1)} custom-call(s32[13]{0:T(128)} %pad_add_fusion.refs_0_.idx_ref, f32[8,512]{1,0:T(8,128)} %copy-done.21, bf16[512,768]{1,0:T(8,128)(2,1)} %get-tuple-element.68.grad_ref, f32[8,512]{1,0:T(8,128)} %get-tuple-element.66.dots_ref, bf16[4096,512]{1,0:T(8,128)(2,1)} %wq_ref.3, bf16[4096,128]{1,0:T(8,128)(2,1)} %wk_ref.3, ...), custom_call_target="tpu_custom_call" | custom-call | flops 32212254720 | bytes 104857600 | tf_op jit(solution)/shard_map/input_terms/pallas_call | solution.py:554
  123.9 5.5 %out_terms.2 = bf16[4,512,512]{2,1,0:T(8,128)(2,1)} custom-call(s32[13]{0:T(128)} %pad_add_fusion.refs_0_.idx_ref, f32[8,512]{1,0:T(8,128)} %copy-done.21, bf16[512,512]{1,0:T(8,128)(2,1)} %get-tuple-element.67.attended_ref, bf16[512,4096]{1,0:T(8,128)(2,1)} %wo_ref.3), custom_call_target="tpu_custom_call" | custom-call | flops 21474836480 | bytes 83886080 | tf_op jit(solution)/shard_map/out_terms/pallas_call | solution.py:511
  129.4 3.1 %add_convert_fusion.1 = bf16[4,512,512]{2,1,0:T(8,128)(2,1)S(1)} fusion(bf16[4,512,512]{2,1,0:T(8,128)(2,1)} %collective-permute-done.19, bf16[4,512,512]{2,1,0:T(8,128)(2,1)} %out_terms.2), kind=kLoop, calls=%fused_computation.3 | loop fusion | flops 4194304 | bytes 6291456 | tf_op jit(solution)/shard_map/convert_element_type | solution.py:589
  132.5 0.7 add_convert_fusion
  133.4 1.0 collective-permute-start.20
  134.5 1.7 collective-permute-start.22
  136.2 1.5 collective-permute-start.27
  137.7 4.2 %collective-permute-done.25 = bf16[256,512]{1,0:T(8,128)(2,1)S(1)} collective-permute-done((bf16[256,512]{1,0:T(8,128)(2,1)S(1)}, bf16[256,512]{1,0:T(8,128)(2,1)S(1)}, u32[]{:S(2)}, u32[]{:S(2)}) %collective-permute-start.25) | collective-permute-done | bytes 262176 | tf_op jit(solution)/shard_map/ppermute | solution.py:566
  142.1 6.4 %collective-permute-done.27 = bf16[272,512]{1,0:T(8,128)(2,1)S(1)} collective-permute-done((bf16[272,512]{1,0:T(8,128)(2,1)S(1)}, bf16[272,512]{1,0:T(8,128)(2,1)S(1)}, u32[]{:S(2)}, u32[]{:S(2)}) %collective-permute-start.27) | collective-permute-done | bytes 278560 | tf_op jit(solution)/shard_map/ppermute | solution.py:566
  148.6 1.9 collective-permute-start.28
  150.8 2.7 %collective-permute-start.23 = (bf16[512,512]{1,0:T(8,128)(2,1)S(1)}, bf16[512,512]{1,0:T(8,128)(2,1)S(1)}, u32[]{:S(2)}, u32[]{:S(2)}) collective-permute-start(bf16[512,512]{1,0:T(8,128)(2,1)S(1)} %pad_maximum_fusion.4), channel_id=1, source_target_pairs={{0,6},{2,0},{4,2},{6,4},{1,7},{3,1},{5,3},{7,5},{8,14},{10,8},{12,... | collective-permute-start | bytes 1572872 | tf_op jit(solution)/shard_map/ppermute | solution.py:566
  153.7 5.4 %collective-permute-done.26 = bf16[528,512]{1,0:T(8,128)(2,1)S(1)} collective-permute-done((bf16[528,512]{1,0:T(8,128)(2,1)S(1)}, bf16[528,512]{1,0:T(8,128)(2,1)S(1)}, u32[]{:S(2)}, u32[]{:S(2)}) %collective-permute-start.26) | collective-permute-done | bytes 540704 | tf_op jit(solution)/shard_map/ppermute | solution.py:566
  159.1 1.9 collective-permute-done.28
  161.3 9.1 %collective-permute-done.21 = bf16[512,512]{1,0:T(8,128)(2,1)S(1)} collective-permute-done((bf16[512,512]{1,0:T(8,128)(2,1)S(1)}, bf16[512,512]{1,0:T(8,128)(2,1)S(1)}, u32[]{:S(2)}, u32[]{:S(2)}) %collective-permute-start.21) | collective-permute-done | bytes 524320 | tf_op jit(solution)/shard_map/ppermute | solution.py:566
  170.3 1.8 collective-permute-done.23
  172.2 1.4 fusion.6
  173.5 16.7 %all_to_all.20 = bf16[16,32,512]{2,1,0:T(8,128)(2,1)S(1)} all-to-all(bf16[16,32,512]{2,1,0:T(8,128)(2,1)S(1)} %bitcast.79), channel_id=1, replica_groups=mesh['x'=4,'z'=4,'y'=4,'core'=2] {'x','z'}, dimensions={0} | all-to-all | bytes 1048576 | tf_op jit(solution)/shard_map/all_to_all | solution.py:600
  190.3 5.4 %all-to-all-start.3 = ((bf16[16,32,512]{2,1,0:T(8,128)(2,1)}), bf16[16,32,512]{2,1,0:T(8,128)(2,1)S(1)}, u32[]{:S(2)}, u32[]{:S(2)}) async-start(bf16[16,32,512]{2,1,0:T(8,128)(2,1)} %bitcast.28), calls=%async_computation.3 | async-start | bytes 1048576 | tf_op jit(solution)/shard_map/all_to_all | solution.py:600
  195.8 1.4 gather_fusion
  197.1 7.8 %all-to-all-done.3 = bf16[16,32,512]{2,1,0:T(8,128)(2,1)S(1)} async-done(((bf16[16,32,512]{2,1,0:T(8,128)(2,1)}), bf16[16,32,512]{2,1,0:T(8,128)(2,1)S(1)}, u32[]{:S(2)}, u32[]{:S(2)}) %all-to-all-start.3) | async-done | bytes 524320 | tf_op jit(solution)/shard_map/all_to_all | solution.py:600
  204.9 1.4 gather_fusion.1
  206.3 26.6 %all-reduce.4.cloned.1.call-done = (bf16[4096,512]{1,0:T(8,128)(2,1)}, bf16[4096,128]{1,0:T(8,128)(2,1)}, bf16[4096,128]{1,0:T(8,128)(2,1)}) async-done(((bf16[4096,512]{1,0:T(8,128)(2,1)}, bf16[4096,128]{1,0:T(8,128)(2,1)}, bf16[4096,128]{1,0:T(8,128)(2,1)}), (bf16[4096,512]{1,0:T(8,128)(2,1)}, bf16[4096,128]{1,0:T(8,128)(2,1)}, bf16[4096,128]{1,0:T(8,128)(2,1)})) %all-reduce.4.cloned.1.call-update) | async-done | bytes 6291472 | tf_op jit(solution)/shard_map/psum | solution.py:657
  232.9 5.8 %finish.1 = (bf16[4096,512]{1,0:T(8,128)(2,1)}, bf16[4096,128]{1,0:T(8,128)(2,1)}, bf16[4096,128]{1,0:T(8,128)(2,1)}) custom-call(bf16[4096,512]{1,0:T(8,128)(2,1)} %get-tuple-element.75.refs_0_, bf16[4096,128]{1,0:T(8,128)(2,1)} %get-tuple-element.76.refs_1_, bf16[4096,128]{1,0:T(8,128)(2,1)} %get-tuple-element.77.refs_2_), custom_call_target="tpu_custom_call" | custom-call | bytes 12582912 | tf_op jit(solution)/shard_map/finish/pallas_call | solution.py:475
  (103 shorter events, 3.9 us)
Async XLA Ops:
  7.2 10.5 %copy-start.15 = (s32[512]{0:T(512)S(1)}, s32[512]{0:T(512)}, u32[]{:S(2)}) copy-start(s32[512]{0:T(512)} %param.13) | copy-start | bytes 6148
  9.1 23.9 %copy-start.14 = (f32[4096]{0:T(1024)S(1)}, f32[4096]{0:T(1024)}, u32[]{:S(2)}) copy-start(f32[4096]{0:T(1024)} %param.12) | copy-start | bytes 49156
  9.1 26.0 %copy-start.17 = (s32[4]{0:T(128)S(1)}, s32[4]{0:T(128)}, u32[]{:S(2)}) copy-start(s32[4]{0:T(128)} %constant.100.clone) | copy-start | bytes 52
  9.1 18.9 %all-to-all-start = ((bf16[16,32,512]{2,1,0:T(8,128)(2,1)}), bf16[16,32,512]{2,1,0:T(8,128)(2,1)S(1)}, u32[]{:S(2)}, u32[]{:S(2)}) async-start(bf16[16,32,512]{2,1,0:T(8,128)(2,1)} %place.1), calls=%async_computation | async-start | bytes 1048576 | tf_op jit(solution)/shard_map/all_to_all | solution.py:600
  28.0 22.1 %copy-start = (bf16[16,32,512]{2,1,0:T(8,128)(2,1)}, bf16[16,32,512]{2,1,0:T(8,128)(2,1)S(1)}, u32[]{:S(2)}) copy-start(bf16[16,32,512]{2,1,0:T(8,128)(2,1)S(1)} %all-to-all-done) | copy-start | bytes 1572868
  28.0 13.5 %all-to-all-start.1 = ((bf16[16,32,640]{2,1,0:T(8,128)(2,1)}), bf16[16,32,640]{2,1,0:T(8,128)(2,1)S(1)}, u32[]{:S(2)}, u32[]{:S(2)}) async-start(bf16[16,32,640]{2,1,0:T(8,128)(2,1)} %place_meta.1), calls=%async_computation.1 | async-start | bytes 1310720 | tf_op jit(solution)/shard_map/all_to_all | solution.py:600
  31.6 201.3 %all-reduce.4.cloned.1.call-start = ((), (), s32[]{:S(2)}) async-start(), calls=%async_computation.4 | async-start | bytes 12582912 | tf_op jit(solution)/shard_map/psum | solution.py:657
  31.6 12.9 %collective-permute-start = (bf16[512,512]{1,0:T(8,128)(2,1)S(1)}, bf16[512,512]{1,0:T(8,128)(2,1)S(1)}, u32[]{:S(2)}, u32[]{:S(2)}) collective-permute-start(bf16[512,512]{1,0:T(8,128)(2,1)S(1)} %bitcast.71), channel_id=1, source_target_pairs={{0,2},{2,4},{4,6},{6,0},{1,3},{3,5},{5,7},{7,1},{8,10},{10,12},{12... | collective-permute-start | bytes 1572872 | tf_op jit(solution)/shard_map/ppermute | solution.py:566
  33.6 15.3 %collective-permute-start.2 = (bf16[512,512]{1,0:T(8,128)(2,1)S(1)}, bf16[512,512]{1,0:T(8,128)(2,1)}, u32[]{:S(2)}, u32[]{:S(2)}) collective-permute-start(bf16[512,512]{1,0:T(8,128)(2,1)S(1)} %bitcast.72), channel_id=1, source_target_pairs={{0,6},{2,0},{4,2},{6,4},{1,7},{3,1},{5,3},{7,5},{8,14},{10,8},{12,... | collective-permute-start | bytes 1572872 | tf_op jit(solution)/shard_map/ppermute | solution.py:566
  35.7 16.4 %collective-permute-start.6 = (bf16[512,512]{1,0:T(8,128)(2,1)S(1)}, bf16[512,512]{1,0:T(8,128)(2,1)}, u32[]{:S(2)}, u32[]{:S(2)}) collective-permute-start(bf16[512,512]{1,0:T(8,128)(2,1)S(1)} %bitcast.73), channel_id=1, source_target_pairs={{0,1},{1,0},{2,3},{3,2},{4,5},{5,4},{6,7},{7,6},{8,9},{9,8},{10,11... | collective-permute-start | bytes 1572872 | tf_op jit(solution)/shard_map/ppermute | solution.py:570
  41.6 24.0 %copy-start.2 = (bf16[16,32,512]{2,1,0:T(8,128)(2,1)}, bf16[16,32,512]{2,1,0:T(8,128)(2,1)S(1)}, u32[]{:S(2)}) copy-start(bf16[16,32,512]{2,1,0:T(8,128)(2,1)S(1)} %slice.114) | copy-start | bytes 1572868
  41.6 23.2 %collective-permute-start.4 = (bf16[512,512]{1,0:T(8,128)(2,1)S(1)}, bf16[512,512]{1,0:T(8,128)(2,1)S(1)}, u32[]{:S(2)}, u32[]{:S(2)}) collective-permute-start(bf16[512,512]{1,0:T(8,128)(2,1)S(1)} %bitcast.75), channel_id=1, source_target_pairs={{0,2},{2,4},{4,6},{6,0},{1,3},{3,5},{5,7},{7,1},{8,10},{10,12},{12... | collective-permute-start | bytes 1572872 | tf_op jit(solution)/shard_map/ppermute | solution.py:566
  43.0 21.8 %collective-permute-start.5 = (bf16[512,512]{1,0:T(8,128)(2,1)S(1)}, bf16[512,512]{1,0:T(8,128)(2,1)S(1)}, u32[]{:S(2)}, u32[]{:S(2)}) collective-permute-start(bf16[512,512]{1,0:T(8,128)(2,1)S(1)} %bitcast.76), channel_id=1, source_target_pairs={{0,6},{2,0},{4,2},{6,4},{1,7},{3,1},{5,3},{7,5},{8,14},{10,8},{12,... | collective-permute-start | bytes 1572872 | tf_op jit(solution)/shard_map/ppermute | solution.py:566
  44.5 11.4 %copy-start.7 = (bf16[512,512]{1,0:T(8,128)(2,1)}, bf16[512,512]{1,0:T(8,128)(2,1)S(1)}, u32[]{:S(2)}) copy-start(bf16[512,512]{1,0:T(8,128)(2,1)S(1)} %collective-permute-done.refs_2_) | copy-start | bytes 1572868
  44.5 9.0 %collective-permute-start.7 = (bf16[512,512]{1,0:T(8,128)(2,1)S(1)}, bf16[512,512]{1,0:T(8,128)(2,1)}, u32[]{:S(2)}, u32[]{:S(2)}) collective-permute-start(bf16[512,512]{1,0:T(8,128)(2,1)S(1)} %collective-permute-done.refs_2_), channel_id=1, source_target_pairs={{0,1},{1,0},{2,3},{3,2},{4,5},{5,4},{6,7},{7,6},{8,9},{9,8},{10,11... | collective-permute-start | bytes 1572872 | tf_op jit(solution)/shard_map/ppermute | solution.py:570
  49.0 7.0 %collective-permute-start.8 = (bf16[512,512]{1,0:T(8,128)(2,1)}, bf16[512,512]{1,0:T(8,128)(2,1)}, u32[]{:S(2)}, u32[]{:S(2)}) collective-permute-start(bf16[512,512]{1,0:T(8,128)(2,1)} %collective-permute-done.2.refs_3_), channel_id=1, source_target_pairs={{0,1},{1,0},{2,3},{3,2},{4,5},{5,4},{6,7},{7,6},{8,9},{9,8},{10,11... | collective-permute-start | bytes 1572872 | tf_op jit(solution)/shard_map/ppermute | solution.py:570
  52.2 12.6 %collective-permute-start.1 = (bf16[256,512]{1,0:T(8,128)(2,1)}, bf16[256,512]{1,0:T(8,128)(2,1)S(1)}, u32[]{:S(2)}, u32[]{:S(2)}) collective-permute-start(bf16[256,512]{1,0:T(8,128)(2,1)} %slice.112), channel_id=1, source_target_pairs={{0,2},{2,4},{4,6},{6,0},{1,3},{3,5},{5,7},{7,1},{8,10},{10,12},{12... | collective-permute-start | bytes 786440 | tf_op jit(solution)/shard_map/ppermute | solution.py:566
  53.5 11.3 %collective-permute-start.3 = (bf16[256,512]{1,0:T(8,128)(2,1)S(1)}, bf16[256,512]{1,0:T(8,128)(2,1)S(1)}, u32[]{:S(2)}, u32[]{:S(2)}) collective-permute-start(bf16[256,512]{1,0:T(8,128)(2,1)S(1)} %slice.113), channel_id=1, source_target_pairs={{0,6},{2,0},{4,2},{6,4},{1,7},{3,1},{5,3},{7,5},{8,14},{10,8},{12,... | collective-permute-start | bytes 786440 | tf_op jit(solution)/shard_map/ppermute | solution.py:566
  64.8 15.4 %copy-start.5 = (bf16[512,512]{1,0:T(8,128)(2,1)}, bf16[512,512]{1,0:T(8,128)(2,1)S(1)}, u32[]{:S(2)}) copy-start(bf16[512,512]{1,0:T(8,128)(2,1)S(1)} %collective-permute-done.4.refs_2_) | copy-start | bytes 1572868
  64.8 15.4 %copy-start.6 = (bf16[512,512]{1,0:T(8,128)(2,1)}, bf16[512,512]{1,0:T(8,128)(2,1)S(1)}, u32[]{:S(2)}) copy-start(bf16[512,512]{1,0:T(8,128)(2,1)S(1)} %collective-permute-done.5.refs_3_) | copy-start | bytes 1572868
  64.8 6.4 %copy-start.9 = (bf16[256,512]{1,0:T(8,128)(2,1)}, bf16[256,512]{1,0:T(8,128)(2,1)S(1)}, u32[]{:S(2)}) copy-start(bf16[256,512]{1,0:T(8,128)(2,1)S(1)} %collective-permute-done.1.refs_1_) | copy-start | bytes 786436
  64.8 6.4 %copy-start.10 = (bf16[256,512]{1,0:T(8,128)(2,1)}, bf16[256,512]{1,0:T(8,128)(2,1)S(1)}, u32[]{:S(2)}) copy-start(bf16[256,512]{1,0:T(8,128)(2,1)S(1)} %collective-permute-done.3.refs_2_) | copy-start | bytes 786436
  64.8 15.4 %collective-permute-start.12 = (bf16[512,512]{1,0:T(8,128)(2,1)S(1)}, bf16[512,512]{1,0:T(8,128)(2,1)S(1)}, u32[]{:S(2)}, u32[]{:S(2)}) collective-permute-start(bf16[512,512]{1,0:T(8,128)(2,1)S(1)} %collective-permute-done.4.refs_2_), channel_id=1, source_target_pairs={{0,1},{1,0},{2,3},{3,2},{4,5},{5,4},{6,7},{7,6},{8,9},{9,8},{10,11... | collective-permute-start | bytes 1572872 | tf_op jit(solution)/shard_map/ppermute | solution.py:570
  65.5 14.8 %collective-permute-start.13 = (bf16[512,512]{1,0:T(8,128)(2,1)S(1)}, bf16[512,512]{1,0:T(8,128)(2,1)}, u32[]{:S(2)}, u32[]{:S(2)}) collective-permute-start(bf16[512,512]{1,0:T(8,128)(2,1)S(1)} %collective-permute-done.5.refs_3_), channel_id=1, source_target_pairs={{0,1},{1,0},{2,3},{3,2},{4,5},{5,4},{6,7},{7,6},{8,9},{9,8},{10,11... | collective-permute-start | bytes 1572872 | tf_op jit(solution)/shard_map/ppermute | solution.py:570
  65.5 14.7 %collective-permute-start.11 = (bf16[512,512]{1,0:T(8,128)(2,1)S(1)}, bf16[512,512]{1,0:T(8,128)(2,1)}, u32[]{:S(2)}, u32[]{:S(2)}) collective-permute-start(bf16[512,512]{1,0:T(8,128)(2,1)S(1)} %bitcast.77), channel_id=1, source_target_pairs={{0,1},{1,0},{2,3},{3,2},{4,5},{5,4},{6,7},{7,6},{8,9},{9,8},{10,11... | collective-permute-start | bytes 1572872 | tf_op jit(solution)/shard_map/ppermute | solution.py:570
  66.0 2.4 collective-permute-start.14
  66.1 4.4 %collective-permute-start.15 = (bf16[256,512]{1,0:T(8,128)(2,1)S(1)}, bf16[256,512]{1,0:T(8,128)(2,1)S(1)}, u32[]{:S(2)}, u32[]{:S(2)}) collective-permute-start(bf16[256,512]{1,0:T(8,128)(2,1)S(1)} %collective-permute-done.3.refs_2_), channel_id=1, source_target_pairs={{0,1},{1,0},{2,3},{3,2},{4,5},{5,4},{6,7},{7,6},{8,9},{9,8},{10,11... | collective-permute-start | bytes 786440 | tf_op jit(solution)/shard_map/ppermute | solution.py:570
  68.4 2.1 copy-start.11
  68.4 18.6 %collective-permute-start.10 = (bf16[256,512]{1,0:T(8,128)(2,1)S(1)}, bf16[256,512]{1,0:T(8,128)(2,1)S(1)}, u32[]{:S(2)}, u32[]{:S(2)}) collective-permute-start(bf16[256,512]{1,0:T(8,128)(2,1)S(1)} %slice.85), channel_id=1, source_target_pairs={{0,6},{2,0},{4,2},{6,4},{1,7},{3,1},{5,3},{7,5},{8,14},{10,8},{12,... | collective-permute-start | bytes 786440 | tf_op jit(solution)/shard_map/ppermute | solution.py:566
  70.5 0.7 copy-start.12
  70.5 16.5 %collective-permute-start.9 = (bf16[256,512]{1,0:T(8,128)(2,1)S(1)}, bf16[256,512]{1,0:T(8,128)(2,1)}, u32[]{:S(2)}, u32[]{:S(2)}) collective-permute-start(bf16[256,512]{1,0:T(8,128)(2,1)S(1)} %slice.84), channel_id=1, source_target_pairs={{0,2},{2,4},{4,6},{6,0},{1,3},{3,5},{5,7},{7,1},{8,10},{10,12},{12... | collective-permute-start | bytes 786440 | tf_op jit(solution)/shard_map/ppermute | solution.py:566
  80.2 0.8 copy-start.8
  87.0 2.3 copy-start.18
  87.0 2.1 collective-permute-start.16
  87.7 1.5 collective-permute-start.17
  89.1 0.7 copy-start.19
  89.3 0.7 copy-start.20
  102.5 1.7 collective-permute-start.18
  104.2 0.6 copy-start.21
  110.3 19.1 %collective-permute-start.19 = (bf16[4,512,512]{2,1,0:T(8,128)(2,1)}, bf16[4,512,512]{2,1,0:T(8,128)(2,1)}, u32[]{:S(2)}, u32[]{:S(2)}) collective-permute-start(bf16[4,512,512]{2,1,0:T(8,128)(2,1)} %out_terms.3), channel_id=1, source_target_pairs={{0,1},{1,0},{2,3},{3,2},{4,5},{5,4},{6,7},{7,6},{8,9},{9,8},{10,11... | collective-permute-start | bytes 6291464 | tf_op jit(solution)/shard_map/ppermute | solution.py:570
  117.2 15.2 %collective-permute-start.24 = (bf16[4,528,512]{2,1,0:T(8,128)(2,1)}, bf16[4,528,512]{2,1,0:T(8,128)(2,1)S(1)}, u32[]{:S(2)}, u32[]{:S(2)}) collective-permute-start(bf16[4,528,512]{2,1,0:T(8,128)(2,1)} %input_terms.3), channel_id=1, source_target_pairs={{0,1},{1,0},{2,3},{3,2},{4,5},{5,4},{6,7},{7,6},{8,9},{9,8},{10,11... | collective-permute-start | bytes 6488072 | tf_op jit(solution)/shard_map/ppermute | solution.py:570
  129.4 3.1 %copy-start.4 = (bf16[4,528,512]{2,1,0:T(8,128)(2,1)S(1)}, bf16[4,528,512]{2,1,0:T(8,128)(2,1)}, u32[]{:S(2)}) copy-start(bf16[4,528,512]{2,1,0:T(8,128)(2,1)} %input_terms.2) | copy-start | bytes 6488068
  133.2 8.7 %collective-permute-start.25 = (bf16[256,512]{1,0:T(8,128)(2,1)S(1)}, bf16[256,512]{1,0:T(8,128)(2,1)S(1)}, u32[]{:S(2)}, u32[]{:S(2)}) collective-permute-start(bf16[256,512]{1,0:T(8,128)(2,1)S(1)} %get-tuple-element.78), channel_id=1, source_target_pairs={{0,2},{2,4},{4,6},{6,0},{1,3},{3,5},{5,7},{7,1},{8,10},{10,12},{12... | collective-permute-start | bytes 786440 | tf_op jit(solution)/shard_map/ppermute | solution.py:566
  133.4 17.1 %collective-permute-start.20 = (bf16[256,512]{1,0:T(8,128)(2,1)S(1)}, bf16[256,512]{1,0:T(8,128)(2,1)S(1)}, u32[]{:S(2)}, u32[]{:S(2)}) collective-permute-start(bf16[256,512]{1,0:T(8,128)(2,1)S(1)} %get-tuple-element.84), channel_id=1, source_target_pairs={{0,2},{2,4},{4,6},{6,0},{1,3},{3,5},{5,7},{7,1},{8,10},{10,12},{12... | collective-permute-start | bytes 786440 | tf_op jit(solution)/shard_map/ppermute | solution.py:566
  134.5 16.1 %collective-permute-start.22 = (bf16[256,512]{1,0:T(8,128)(2,1)S(1)}, bf16[256,512]{1,0:T(8,128)(2,1)S(1)}, u32[]{:S(2)}, u32[]{:S(2)}) collective-permute-start(bf16[256,512]{1,0:T(8,128)(2,1)S(1)} %get-tuple-element.85), channel_id=1, source_target_pairs={{0,6},{2,0},{4,2},{6,4},{1,7},{3,1},{5,3},{7,5},{8,14},{10,8},{12,... | collective-permute-start | bytes 786440 | tf_op jit(solution)/shard_map/ppermute | solution.py:566
  136.2 12.3 %collective-permute-start.27 = (bf16[272,512]{1,0:T(8,128)(2,1)S(1)}, bf16[272,512]{1,0:T(8,128)(2,1)S(1)}, u32[]{:S(2)}, u32[]{:S(2)}) collective-permute-start(bf16[272,512]{1,0:T(8,128)(2,1)S(1)} %get-tuple-element.81), channel_id=1, source_target_pairs={{0,6},{2,0},{4,2},{6,4},{1,7},{3,1},{5,3},{7,5},{8,14},{10,8},{12,... | collective-permute-start | bytes 835592 | tf_op jit(solution)/shard_map/ppermute | solution.py:566
  142.0 17.1 %collective-permute-start.26 = (bf16[528,512]{1,0:T(8,128)(2,1)S(1)}, bf16[528,512]{1,0:T(8,128)(2,1)S(1)}, u32[]{:S(2)}, u32[]{:S(2)}) collective-permute-start(bf16[528,512]{1,0:T(8,128)(2,1)S(1)} %pad_maximum_fusion), channel_id=1, source_target_pairs={{0,2},{2,4},{4,6},{6,0},{1,3},{3,5},{5,7},{7,1},{8,10},{10,12},{12... | collective-permute-start | bytes 1622024 | tf_op jit(solution)/shard_map/ppermute | solution.py:566
  148.6 5.0 %copy-start.13 = (f32[512,128]{1,0:T(8,128)S(1)}, f32[512,128]{1,0:T(8,128)}, u32[]{:S(2)}) copy-start(f32[512,128]{1,0:T(8,128)} %get-tuple-element.65.refs_14_) | copy-start | bytes 786436
  148.6 12.4 %collective-permute-start.28 = (bf16[528,512]{1,0:T(8,128)(2,1)S(1)}, bf16[528,512]{1,0:T(8,128)(2,1)S(1)}, u32[]{:S(2)}, u32[]{:S(2)}) collective-permute-start(bf16[528,512]{1,0:T(8,128)(2,1)S(1)} %pad_maximum_fusion.1), channel_id=1, source_target_pairs={{0,6},{2,0},{4,2},{6,4},{1,7},{3,1},{5,3},{7,5},{8,14},{10,8},{12,... | collective-permute-start | bytes 1622024 | tf_op jit(solution)/shard_map/ppermute | solution.py:566
  150.7 21.5 %copy-start.1 = (bf16[16,32,512]{2,1,0:T(8,128)(2,1)S(1)}, bf16[16,32,512]{2,1,0:T(8,128)(2,1)}, u32[]{:S(2)}) copy-start(bf16[16,32,512]{2,1,0:T(8,128)(2,1)} %copy-done) | copy-start | bytes 1572868
  150.7 21.5 %copy-start.3 = (bf16[16,32,512]{2,1,0:T(8,128)(2,1)S(1)}, bf16[16,32,512]{2,1,0:T(8,128)(2,1)}, u32[]{:S(2)}) copy-start(bf16[16,32,512]{2,1,0:T(8,128)(2,1)} %copy-done.2) | copy-start | bytes 1572868
  150.7 19.6 %collective-permute-start.21 = (bf16[512,512]{1,0:T(8,128)(2,1)S(1)}, bf16[512,512]{1,0:T(8,128)(2,1)S(1)}, u32[]{:S(2)}, u32[]{:S(2)}) collective-permute-start(bf16[512,512]{1,0:T(8,128)(2,1)S(1)} %pad_maximum_fusion.3), channel_id=1, source_target_pairs={{0,2},{2,4},{4,6},{6,0},{1,3},{3,5},{5,7},{7,1},{8,10},{10,12},{12... | collective-permute-start | bytes 1572872 | tf_op jit(solution)/shard_map/ppermute | solution.py:566
  150.8 21.3 %collective-permute-start.23 = (bf16[512,512]{1,0:T(8,128)(2,1)S(1)}, bf16[512,512]{1,0:T(8,128)(2,1)S(1)}, u32[]{:S(2)}, u32[]{:S(2)}) collective-permute-start(bf16[512,512]{1,0:T(8,128)(2,1)S(1)} %pad_maximum_fusion.4), channel_id=1, source_target_pairs={{0,6},{2,0},{4,2},{6,4},{1,7},{3,1},{5,3},{7,5},{8,14},{10,8},{12,... | collective-permute-start | bytes 1572872 | tf_op jit(solution)/shard_map/ppermute | solution.py:566
  173.5 22.2 %copy-start.16 = (s32[16]{0:T(128)S(1)}, s32[16]{0:T(128)}, u32[]{:S(2)}) copy-start(s32[16]{0:T(128)} %plan_ref.3) | copy-start | bytes 196
  190.3 14.7 %all-to-all-start.3 = ((bf16[16,32,512]{2,1,0:T(8,128)(2,1)}), bf16[16,32,512]{2,1,0:T(8,128)(2,1)S(1)}, u32[]{:S(2)}, u32[]{:S(2)}) async-start(bf16[16,32,512]{2,1,0:T(8,128)(2,1)} %bitcast.28), calls=%async_computation.3 | async-start | bytes 1048576 | tf_op jit(solution)/shard_map/all_to_all | solution.py:600
Sparse Core Ops, SparseCore 0:
  103.4 129.3 all-reduce.3
